TPU v7x, 32 devices: a whole 2x2x4 slice. The times are simulated.
32 devices in a mesh: groups: 2 (over x), dp: 8 (over z, y), adapter: 2 (over core).
Axes of the slice: x: 2, y: 2, z: 4, core: 2. Of those that a mesh axis runs over, the one named last changes fastest.
Arguments:
- layer_input_rows: bfloat16 [4096, 7168], P(('groups', 'dp', 'adapter')), parts along dimension 0, may hold values from -6 to 6
- output_gradient: bfloat16 [4096, 7168], P(('groups', 'dp', 'adapter')), parts along dimension 0, may hold values from -6 to 6
- routed_adapter_index: int32 [4096, 2], P(('groups', 'dp', 'adapter')), parts along dimension 0, may hold values from 0 to 7, all different within a row; in each aligned block of 128 rows (0 to 127, 128 to 255, ...) at most 64 rows name the same one
- router_gate_weight: float32 [4096, 2], P(('groups', 'dp', 'adapter')), parts along dimension 0, may hold values from 0.1 to 1
- down_factor_weight: bfloat16 [8, 16, 7168], P('adapter'), may hold values from -0.0625 to 0.0625
- up_factor_weight: bfloat16 [8, 16, 7168], P('adapter'), may hold values from -1.5 to 1.5
Outputs:
- input_grad: bfloat16 [4096, 7168], P(('groups', 'dp', 'adapter')), parts along dimension 0
- down_grad: float32 [16, 16, 7168], P(('groups', 'adapter'), None, 'dp'), parts along dimension 0
- up_grad: float32 [16, 16, 7168], P(('groups', 'adapter'), None, 'dp'), parts along dimension 0
There are 2 independent parts, one for each index of `groups`. A program takes and returns all parts, laid end to end along the dimension named above; an argument that names none is the same for every part. Nothing has to cross between parts.
Inputs may be any that keep to these rules, and one draw needn't show every extreme that they name: `routed_adapter_index`: the 2 adapters of a token differ. In each aligned block of 128 rows (the rows of one device) no adapter is named by more than 64 rows, and some adapter reaches 64.
All inputs are finite; a program needn't handle non-finite values.
Results may differ from a plain program's by a relative error of at most 0.013.
Values may be sent and summed in bfloat16 or wider, within the bound.
No kernel may reach another device: no remote copies, remote signals or barrier semaphores. Data moves between devices by JAX's collectives and lax.ppermute only.
A program may use at most 128 MiB of HBM per device.

v0:
```python
import jax
import jax.numpy as jnp
from jax import lax
from jax.sharding import PartitionSpec as P

MOST = 64


def adapter_task(grad_rows, input_rows, down_w, up_w):
    low_grad = jnp.einsum(
        "sacd,ard->sacr", grad_rows, up_w, preferred_element_type=jnp.float32
    ).astype(jnp.bfloat16)
    row_gradients = jnp.einsum(
        "sacr,ard->sacd", low_grad, down_w, preferred_element_type=jnp.float32
    ).astype(jnp.bfloat16)
    down_piece = jnp.einsum(
        "sacr,sacd->ard", low_grad, input_rows, preferred_element_type=jnp.float32
    )
    low_act = jnp.einsum(
        "sacd,ard->sacr", input_rows, down_w, preferred_element_type=jnp.float32
    ).astype(jnp.bfloat16)
    up_piece = jnp.einsum("sacr,sacd->ard", low_act, grad_rows, preferred_element_type=jnp.float32)
    return (row_gradients, down_piece, up_piece)


def shards(
    layer_input_rows,
    output_gradient,
    routed_adapter_index,
    router_gate_weight,
    down_factor_weight,
    up_factor_weight,
):
    tok_count, width = layer_input_rows.shape
    top_count = routed_adapter_index.shape[1]
    owners = lax.axis_size("adapter")
    retained = down_factor_weight.shape[0]
    adapter_count = retained * owners
    capacity = MOST
    routes_count = tok_count * top_count
    flat_ids = routed_adapter_index.reshape(routes_count)
    onehot = (flat_ids[:, None] == jnp.arange(adapter_count, dtype=jnp.int32)[None, :]).astype(
        jnp.int32
    )
    before = jnp.cumsum(onehot, axis=0) - onehot
    position = jnp.sum(before * onehot, axis=1)
    slot_index = flat_ids * capacity + position
    matches = slot_index[None, :] == jnp.arange(adapter_count * capacity, dtype=jnp.int32)[:, None]
    route_range = jnp.arange(routes_count, dtype=jnp.int32)
    source = jnp.sum(jnp.where(matches, route_range[None, :], 0), axis=1)
    filled = jnp.any(matches, axis=1)
    scaled = (
        router_gate_weight[:, :, None] * output_gradient.astype(jnp.float32)[:, None, :]
    ).astype(jnp.bfloat16)
    scaled = scaled.reshape(routes_count, width)
    slots_grad = jnp.where(
        filled[:, None], jnp.take(scaled, source, axis=0), jnp.zeros((), jnp.bfloat16)
    )
    slots_input = jnp.where(
        filled[:, None],
        jnp.take(layer_input_rows, source // top_count, axis=0),
        jnp.zeros((), jnp.bfloat16),
    )
    slots_grad = slots_grad.reshape(owners, retained, capacity, width)
    slots_input = slots_input.reshape(owners, retained, capacity, width)
    received_gradient, received_input = (
        lax.all_to_all(slots_grad, "adapter", split_axis=0, concat_axis=0, tiled=True),
        lax.all_to_all(slots_input, "adapter", split_axis=0, concat_axis=0, tiled=True),
    )
    row_gradients, down_piece, up_piece = adapter_task(
        received_gradient, received_input, down_factor_weight, up_factor_weight
    )
    returned = lax.all_to_all(row_gradients, "adapter", split_axis=0, concat_axis=0, tiled=True)
    flat_back = returned.reshape(adapter_count * capacity, width)
    picked = jnp.take(flat_back, slot_index, axis=0).reshape(tok_count, top_count, width)
    input_grad = jnp.sum(picked.astype(jnp.float32), axis=1).astype(jnp.bfloat16)
    down_grad, up_grad = (
        lax.psum_scatter(down_piece, "dp", scatter_dimension=2, tiled=True),
        lax.psum_scatter(up_piece, "dp", scatter_dimension=2, tiled=True),
    )
    return (input_grad, down_grad, up_grad)


def solution(mesh):
    return jax.shard_map(
        shards,
        mesh=mesh,
        in_specs=(
            P(("groups", "dp", "adapter"), None),
            P(("groups", "dp", "adapter"), None),
            P(("groups", "dp", "adapter"), None),
            P(("groups", "dp", "adapter"), None),
            P("adapter", None, None),
            P("adapter", None, None),
        ),
        out_specs=(
            P(("groups", "dp", "adapter"), None),
            P(("groups", "adapter"), None, "dp"),
            P(("groups", "adapter"), None, "dp"),
        ),
        check_vma=False,
    )
```

profile of v0, /device:TPU:0, one launch (start us, length us, event | category | flops | bytes accessed | tf_op | source)
XLA Modules:
  0.0 240.4 jit_solution(16515571951494953378)
XLA Ops:
  7.2 0.0 copy-start
  7.2 0.0 reduce-scatter.5.cloned.1.call-start
  7.2 0.9 copy.38
  8.1 0.1 eq.39
  8.3 0.1 reshape.187
  8.4 0.6 reduce-window.6
  9.0 0.2 slice_reduce_fusion
  9.3 0.1 fusion.29
  9.4 0.2 select_reduce_fusion
  9.5 0.2 fusion.27
  9.7 0.1 reduce_sum.41
  9.8 6.8 %mul.55 = f32[128,2,7168]{2,1,0:T(2,128)} broadcast(bf16[128,7168]{1,0:T(8,128)(2,1)} %param.7), dimensions={0,2} | broadcast | bytes 9175040 | tf_op jit(solution)/shard_map/mul | solution.py:53
  16.6 9.6 %mul.56 = f32[256,7168]{1,0:T(8,128)} reshape(f32[128,2,7168]{2,1,0:T(2,128)} %mul.55) | data formatting | bytes 14680064 | tf_op jit(solution)/shard_map/mul | solution.py:53
  26.2 0.0 copy-done.5
  26.2 0.1 copy.42
  26.3 0.1 mul.53
  26.5 0.1 broadcast_in_dim.67
  26.6 5.8 %multiply_convert_fusion = bf16[256,7168]{1,0:T(8,128)(2,1)} fusion(f32[256,7168]{1,0:T(8,128)} %mul.56, f32[256]{0:T(256)S(1)} %mul.53), kind=kLoop, calls=%fused_computation.9 | loop fusion | flops 3670016 | bytes 11011072 | tf_op jit(solution)/shard_map/convert_element_type | solution.py:54
  32.3 16.3 %gather_fusion = bf16[512,7168]{1,0:T(8,128)(2,1)} fusion(bf16[256,7168]{1,0:T(8,128)(2,1)} %multiply_convert_fusion, s32[1024]{0:T(1024)S(1)} %pad_clamp_fusion.2), kind=kCustom, calls=%fused_computation | custom fusion | bytes 14682112 | tf_op jit(solution)/shard_map/jit(_take)/gather | solution.py:57
  48.6 0.0 copy-done
  48.6 7.1 %gather_fusion.2 = bf16[512,7168]{1,0:T(8,128)(2,1)} fusion(bf16[128,7168]{1,0:T(8,128)(2,1)S(1)} %copy-done, s32[1024]{0:T(1024)S(1)} %pad_clamp_fusion), kind=kCustom, calls=%fused_computation.2 | custom fusion | bytes 14682112 | tf_op jit(solution)/shard_map/jit(_take)/gather | solution.py:61
  55.8 6.4 %select_select_fusion = (bf16[2,4,64,7168]{3,2,1,0:T(8,128)(2,1)S(1)}, bf16[2,4,64,7168]{3,2,1,0:T(8,128)(2,1)S(1)}) fusion(bf16[2,4,64,7168]{3,2,1,0:T(8,128)(2,1)} %bitcast.47, pred[2,4,64]{2,1,0:T(4,128)(4,1)S(1)} %get-tuple-element.3, pred[2,4,64]{2,1,0:T(4,128)(4,1)S(1)} %broadcast_in_dim.67, bf16[2,4,64,7168]{3,2,1,0:T(8,128)(2,1)} %bitcast.46, ...), kind=kLoop, calls=%fused_computation.7 | loop fusion | flops 14680064 | bytes 29361664 | tf_op jit(solution)/shard_map/jit(_where)/select_n | solution.py:59
  62.2 10.9 %all_to_all.15 = bf16[2,4,64,7168]{3,2,1,0:T(8,128)(2,1)} all-to-all(bf16[2,4,64,7168]{3,2,1,0:T(8,128)(2,1)S(1)} %get-tuple-element.8), channel_id=1, replica_groups=mesh['groups'=2,'dp'=8,'adapter'=2] {'adapter'}, dimensions={0} | all-to-all | bytes 14680064 | tf_op jit(solution)/shard_map/all_to_all | solution.py:67
  73.0 11.3 %all_to_all.16 = bf16[2,4,64,7168]{3,2,1,0:T(8,128)(2,1)} all-to-all(bf16[2,4,64,7168]{3,2,1,0:T(8,128)(2,1)S(1)} %get-tuple-element.7), channel_id=1, replica_groups=mesh['groups'=2,'dp'=8,'adapter'=2] {'adapter'}, dimensions={0} | all-to-all | bytes 14680064 | tf_op jit(solution)/shard_map/all_to_all | solution.py:68
  84.3 0.0 copy-done.3
  84.3 10.4 %convolution_bitcast_fusion = f32[4,16,7168]{2,1,0:T(8,128)} fusion(bf16[2,4,64,7168]{3,2,1,0:T(8,128)(2,1)} %all_to_all.15, bf16[2,4,64,7168]{3,2,1,0:T(8,128)(2,1)} %all_to_all.16, bf16[4,16,7168]{2,1,0:T(8,128)(2,1)S(1)} %copy-done.3), kind=kOutput, calls=%fused_computation.5 | convolution fusion | flops 234889216 | bytes 17432576 | tf_op jit(solution)/shard_map/sacr,sacd->ard/dot_general | solution.py:22
  94.7 0.0 reduce-scatter.5.cloned.1.call-update
  94.7 0.0 reduce-scatter.3.cloned.1.call-start
  94.8 0.0 copy-done.6
  94.8 0.0 copy-start.2
  94.8 6.2 %fusion.17 = bf16[2,4,64,16]{2,3,0,1:T(8,128)(2,1)S(1)} fusion(bf16[2,4,64,7168]{3,2,1,0:T(8,128)(2,1)} %all_to_all.15, bf16[4,16,7168]{2,1,0:T(8,128)(2,1)S(1)} %copy-done.6), kind=kOutput, calls=%fused_computation.21 | convolution fusion | flops 117448704 | bytes 8273920 | tf_op jit(solution)/shard_map/sacd,ard->sacr/dot_general | solution.py:10
  101.0 2.4 convolution_bitcast_fusion.1
  103.4 0.0 reduce-scatter.3.cloned.1.call-update
  103.4 2.1 fusion
  105.5 3.5 %copy.44 = bf16[2,4,64,7168]{3,2,1,0:T(8,128)(2,1)} copy(bf16[2,4,64,7168]{3,2,0,1:T(8,128)(2,1)S(1)} %fusion) | data formatting | bytes 14680064 | tf_op jit(solution)/shard_map/convert_element_type | solution.py:15
  109.0 7.0 %all-to-all-start.1 = ((bf16[2,4,64,7168]{3,2,1,0:T(8,128)(2,1)}), bf16[2,4,64,7168]{3,2,1,0:T(8,128)(2,1)}, u32[]{:S(2)}, u32[]{:S(2)}) async-start(bf16[2,4,64,7168]{3,2,1,0:T(8,128)(2,1)} %copy.44), calls=%async_computation.1 | async-start | bytes 14680064 | tf_op jit(solution)/shard_map/all_to_all | solution.py:73
  116.0 0.1 reduce_sum.39
  116.1 0.0 copy-done.4
  116.1 0.1 copy.45
  116.3 0.1 mul.58
  116.4 6.1 %all-to-all-done.1 = bf16[2,4,64,7168]{3,2,1,0:T(8,128)(2,1)} async-done(((bf16[2,4,64,7168]{3,2,1,0:T(8,128)(2,1)}), bf16[2,4,64,7168]{3,2,1,0:T(8,128)(2,1)}, u32[]{:S(2)}, u32[]{:S(2)}) %all-to-all-start.1) | async-done | bytes 7340064 | tf_op jit(solution)/shard_map/all_to_all | solution.py:73
  122.5 12.3 %gather_fusion.1 = bf16[256,7168]{1,0:T(8,128)(2,1)} fusion(bf16[512,7168]{1,0:T(8,128)(2,1)} %bitcast.11, s32[1024]{0:T(1024)S(1)} %pad_clamp_fusion.1), kind=kCustom, calls=%fused_computation.1 | custom fusion | bytes 7341056 | tf_op jit(solution)/shard_map/jit(_take)/gather | solution.py:75
  134.8 8.1 %gather.21 = bf16[128,2,7168]{2,1,0:T(2,128)(2,1)} reshape(bf16[256,7168]{1,0:T(8,128)(2,1)} %gather_fusion.1) | data formatting | bytes 7340032 | tf_op jit(solution)/shard_map/jit(_take)/gather | solution.py:75
  142.9 0.1 copy.40
  143.0 0.1 copy.41
  143.2 10.7 %fusion.7 = bf16[128,7168]{1,0:T(8,128)(2,1)} fusion(bf16[128,2,7168]{2,1,0:T(2,128)(2,1)} %gather.21, pred[128,2]{1,0:T(8,128)(4,1)S(1)} %copy.41), kind=kLoop, calls=%fused_computation.17 | loop fusion | flops 2752512 | bytes 5505280 | tf_op jit(solution)/shard_map/reduce_sum | solution.py:76
  153.8 10.1 %reduce-scatter.5.cloned.1.call-done = f32[4,16,896]{2,1,0:T(8,128)} async-done(((f32[4,16,7168]{2,1,0:T(8,128)}), f32[4,16,896]{2,1,0:T(8,128)}) %reduce-scatter.5.cloned.1.call-update) | async-done | bytes 229392 | tf_op jit(solution)/shard_map/reduce_scatter | solution.py:79
  163.9 69.6 %reduce-scatter.3.cloned.1.call-done = f32[4,16,896]{2,1,0:T(8,128)} async-done(((f32[4,16,7168]{2,1,0:T(8,128)}), f32[4,16,896]{2,1,0:T(8,128)}) %reduce-scatter.3.cloned.1.call-update) | async-done | bytes 229392 | tf_op jit(solution)/shard_map/reduce_scatter | solution.py:78
  (19 shorter events, 0.1 us)
Async XLA Ops:
  7.2 41.5 %copy-start = (bf16[128,7168]{1,0:T(8,128)(2,1)S(1)}, bf16[128,7168]{1,0:T(8,128)(2,1)}, u32[]{:S(2)}) copy-start(bf16[128,7168]{1,0:T(8,128)(2,1)} %param.6) | copy-start | bytes 5505028
  7.2 156.8 %reduce-scatter.5.cloned.1.call-start = ((), (), s32[]{:S(2)}) async-start(), calls=%async_computation.6 | async-start | bytes 2064384 | tf_op jit(solution)/shard_map/reduce_scatter | solution.py:79
  16.6 9.6 %copy-start.5 = (f32[128,2]{0,1:T(2,128)S(1)}, f32[128,2]{0,1:T(2,128)}, u32[]{:S(2)}) copy-start(f32[128,2]{0,1:T(2,128)} %param.9) | copy-start | bytes 3076
  73.0 11.3 %copy-start.3 = (bf16[4,16,7168]{2,1,0:T(8,128)(2,1)S(1)}, bf16[4,16,7168]{2,1,0:T(8,128)(2,1)}, u32[]{:S(2)}) copy-start(bf16[4,16,7168]{2,1,0:T(8,128)(2,1)} %param.10) | copy-start | bytes 2752516
  84.3 10.5 %copy-start.6 = (bf16[4,16,7168]{2,1,0:T(8,128)(2,1)S(1)}, bf16[4,16,7168]{2,1,0:T(8,128)(2,1)}, u32[]{:S(2)}) copy-start(bf16[4,16,7168]{2,1,0:T(8,128)(2,1)} %param.11) | copy-start | bytes 2752516
  94.7 138.8 %reduce-scatter.3.cloned.1.call-start = ((), (), s32[]{:S(2)}) async-start(), calls=%async_computation.5 | async-start | bytes 2064384 | tf_op jit(solution)/shard_map/reduce_scatter | solution.py:78
  94.8 6.2 %copy-start.2 = (bf16[2,4,64,7168]{3,2,1,0:T(8,128)(2,1)S(1)}, bf16[2,4,64,7168]{3,2,1,0:T(8,128)(2,1)}, u32[]{:S(2)}) copy-start(bf16[2,4,64,7168]{3,2,1,0:T(8,128)(2,1)} %all_to_all.16) | copy-start | bytes 22020100
  109.0 7.1 %copy-start.4 = (s32[128,2]{0,1:T(2,128)S(1)}, s32[128,2]{0,1:T(2,128)}, u32[]{:S(2)}) copy-start(s32[128,2]{0,1:T(2,128)} %param.8) | copy-start | bytes 3076
  109.0 13.5 %all-to-all-start.1 = ((bf16[2,4,64,7168]{3,2,1,0:T(8,128)(2,1)}), bf16[2,4,64,7168]{3,2,1,0:T(8,128)(2,1)}, u32[]{:S(2)}, u32[]{:S(2)}) async-start(bf16[2,4,64,7168]{3,2,1,0:T(8,128)(2,1)} %copy.44), calls=%async_computation.1 | async-start | bytes 14680064 | tf_op jit(solution)/shard_map/all_to_all | solution.py:73
  122.5 111.1 %copy-start.1 = (bf16[128,7168]{1,0:T(8,128)(2,1)S(1)}, bf16[128,7168]{1,0:T(8,128)(2,1)}, u32[]{:S(2)}) copy-start(bf16[128,7168]{1,0:T(8,128)(2,1)} %param.6) | copy-start | bytes 5505028
Sparse Core Ops, SparseCore 0:
  94.9 69.0 reduce-scatter.4
  168.4 65.1 reduce-scatter.2
where the time goes:
time: 241 us; the launch traced here: 240 us
  waiting for transfers between devices  85.8 us (36%)
  local copies, waits for them, and re-layouts  66.2 us (27%)
  other arithmetic  23.9 us (10%)
  blocking collectives  22.1 us (9%)
  matrix products  21.1 us (9%)
  between operations  14.2 us (6%)
  starting transfers between devices  7.05 us (3%)
    reduce_scatter x1, waiting for transfers between devices, shards(): lax.psum_scatter(down_piece, 'dp', scatter_dimension=2, tiled=True)  69.6 us
    gather x2, local copies, waits for them, and re-layouts, shards(): jnp.take(flat_back, slot_index, axis=0).reshape(tok_count, top_count, width)  20.5 us
    mul x3, local copies, waits for them, and re-layouts, shards(): router_gate_weight[:, :, None]  16.5 us
    gather x1, local copies, waits for them, and re-layouts, shards(): jnp.take(scaled, source, axis=0)  16.3 us
    all_to_all x1, blocking collectives, shards(): lax.all_to_all(slots_input, 'adapter', split_axis=0, concat_axis=0, tiled...  11.3 us
    all_to_all x1, blocking collectives, shards(): lax.all_to_all(slots_grad, 'adapter', split_axis=0, concat_axis=0, tiled=...  10.9 us
    reduce_sum x1, other arithmetic, shards(): jnp.sum(picked.astype(jnp.float32), axis=1).astype(jnp.bfloat16)  10.7 us
    dot_general x1, matrix products, adapter_task(): jnp.einsum('sacr,sacd->ard', low_act, grad_rows, preferred_element_type=j...  10.4 us
  transfers between devices with their start and end apart: 3, of which 3 were waited for; matrix products, arithmetic and copies ran while one was open for 19% of the time, Pallas kernels for 0%

commit v1 on v0

v1 whole, which is shorter than its diff:
```python
import jax
import jax.numpy as jnp
from jax import lax
from jax.sharding import PartitionSpec as P

BF16 = jnp.bfloat16
F32 = jnp.float32
SWAP = [(0, 1), (1, 0)]


def routed_weights(ids, gates, first, count, rank):
    column = first + lax.broadcasted_iota(jnp.int32, (1, 1, count), 2)
    weights = jnp.sum(jnp.where(ids[:, :, None] == column, gates[:, :, None], 0.0), axis=1)
    return jnp.repeat(weights, rank, axis=1)


def reduce_over_dp(down, up):
    replicas = lax.axis_size("dp")
    both = jnp.concatenate([down, up], axis=0)
    rows, width = both.shape
    block = width // replicas
    if replicas & (replicas - 1) or replicas < 2:
        return lax.psum_scatter(both.astype(F32), "dp", scatter_dimension=1, tiled=True)
    me = lax.axis_index("dp")
    far, near = me // 2, me % 2
    total = None
    for step in reversed(range(replicas // 2)):
        base = (far ^ step) * 2
        send = lax.dynamic_slice(both, (0, (base + 1 - near) * block), (rows, block))
        keep = lax.dynamic_slice(both, (0, (base + near) * block), (rows, block))
        came = lax.ppermute(send, "dp", [(i, i ^ 1) for i in range(replicas)])
        term = keep.astype(F32) + came.astype(F32)
        if step:
            term = lax.ppermute(
                term.astype(BF16), "dp", [(i, i ^ (2 * step)) for i in range(replicas)]
            ).astype(F32)
        total = term if total is None else total + term
    return total


def shards(x, g, ids, gates, down_w, up_w):
    tokens, width = x.shape
    count, rank, _ = down_w.shape
    core = lax.axis_index("adapter")
    a = down_w.reshape(count * rank, width)
    b = up_w.reshape(count * rank, width)
    own_weight = routed_weights(ids, gates, core * count, count, rank)
    other_weight = routed_weights(ids, gates, (1 - core) * count, count, rank)
    weight_in = lax.ppermute(other_weight, "adapter", SWAP)
    g_in = lax.ppermute(g, "adapter", SWAP)
    x_in = lax.ppermute(x, "adapter", SWAP)
    a_in = lax.ppermute(a, "adapter", SWAP)

    def low(rows, factor, weight):
        z = lax.dot_general(rows, factor, (((1,), (1,)), ((), ())), preferred_element_type=F32)
        return (z * weight).astype(BF16)

    def outer(left, right):
        return lax.dot_general(left, right, (((0,), (0,)), ((), ())), preferred_element_type=F32)

    low_grad = low(g, b, own_weight)
    low_grad_in = low(g_in, b, weight_in)
    low_act = low(x, a, own_weight)
    low_act_in = low(x_in, a, weight_in)
    down = (outer(low_grad, x) + outer(low_grad_in, x_in)).astype(BF16)
    up = (outer(low_act, g) + outer(low_act_in, g_in)).astype(BF16)
    low_grad_back = lax.ppermute(low_grad_in, "adapter", SWAP)
    input_grad = (
        jnp.dot(low_grad, a, preferred_element_type=F32)
        + jnp.dot(low_grad_back, a_in, preferred_element_type=F32)
    ).astype(BF16)
    both = reduce_over_dp(down, up).reshape(2, count, rank, -1)
    return input_grad, both[0], both[1]


def solution(mesh):
    tok = P(("groups", "dp", "adapter"), None)
    return jax.shard_map(
        shards,
        mesh=mesh,
        in_specs=(tok, tok, tok, tok, P("adapter", None, None), P("adapter", None, None)),
        out_specs=(
            tok,
            P(("groups", "adapter"), None, "dp"),
            P(("groups", "adapter"), None, "dp"),
        ),
        check_vma=False,
    )
```

time: 241 us -> 65.8 us (0.27)
  local copies, waits for them, and re-layouts: 66.2 us -> 0.82 us
  waiting for transfers between devices: 85.8 us -> 26.9 us
  other arithmetic: 23.9 us -> 1.21 us
  blocking collectives: 22.1 us -> 0 us
  between operations: 14.2 us -> 0.72 us
  starting transfers between devices: 7.05 us -> 13.1 us
    reduce_scatter x2 -> x0, waiting for transfers between devices: 79.7 us -> none  [the longest x1 69.6 us: shards(): lax.psum_scatter(down_piece, 'dp', scatter_dimension=2, tiled=True)]
    gather x4 -> x0, local copies, waits for them, and re-layouts: 43.9 us -> none  [the longest x2 20.5 us: shards(): jnp.take(flat_back, slot_index, axis=0).reshape(tok_count, top_count, width)]
    ppermute x0 -> x12, waiting for transfers between devices: none -> 26.9 us  [the longest x3 15.5 us: reduce_over_dp(): lax.ppermute(term.astype(BF16), 'dp', [(i, i ^ 2 * step) for i in range(r...]
    all_to_all x2 -> x0, blocking collectives: 22.1 us -> none  [the longest x1 11.3 us: shards(): lax.all_to_all(slots_input, 'adapter', split_axis=0, concat_axis=0, tiled...]
    mul x5 -> x0, local copies, waits for them, and re-layouts: 16.8 us -> none  [the longest x3 16.5 us: shards(): router_gate_weight[:, :, None]]
    ppermute x0 -> x12, starting transfers between devices: none -> 13.1 us  [the longest x4 7.09 us: reduce_over_dp(): came = lax.ppermute(send, 'dp', [(i, i ^ 1) for i in range(replicas)])]
    reduce_sum x3 -> x1, other arithmetic: 10.9 us -> 0.78 us  [routed_weights(): jnp.sum(jnp.where(ids[:, :, None] == column, gates[:, :, None], 0.0), axi...]
    all_to_all x1 -> x0, starting transfers between devices: 6.97 us -> none  [shards(): lax.all_to_all(row_gradients, 'adapter', split_axis=0, concat_axis=0, til...]
  transfers between devices with their start and end apart: 3 -> 12, of which waited for: 3 -> 6; matrix products, arithmetic and copies ran while one was open for 19% -> 36% of each run, Pallas kernels for 0% -> 0%
where the time goes in v1:
time: 65.8 us; the launch traced here: 65.5 us
  waiting for transfers between devices  26.9 us (41%)
  matrix products  22.7 us (34%)
  starting transfers between devices  13.1 us (20%)
  other arithmetic  1.21 us (2%)
  local copies, waits for them, and re-layouts  0.82 us (1%)
  between operations  0.72 us (1%)
    ppermute x3, waiting for transfers between devices, reduce_over_dp(): lax.ppermute(term.astype(BF16), 'dp', [(i, i ^ 2 * step) for i in range(r...  15.5 us
    dot_general x4, matrix products, outer(): lax.dot_general(left, right, (((0,), (0,)), ((), ())), preferred_element_...  14.5 us
    ppermute x4, waiting for transfers between devices, reduce_over_dp(): came = lax.ppermute(send, 'dp', [(i, i ^ 1) for i in range(replicas)])  11.4 us
    ppermute x4, starting transfers between devices, reduce_over_dp(): came = lax.ppermute(send, 'dp', [(i, i ^ 1) for i in range(replicas)])  7.09 us
    ppermute x3, starting transfers between devices, reduce_over_dp(): lax.ppermute(term.astype(BF16), 'dp', [(i, i ^ 2 * step) for i in range(r...  4.79 us
    dot_general x2, matrix products, low(): lax.dot_general(rows, factor, (((1,), (1,)), ((), ())), preferred_element...  4.5 us
    dot_general x1, matrix products, shards(): jnp.dot(low_grad_back, a_in, preferred_element_type=F32)  3.1 us
  transfers between devices with their start and end apart: 12, of which 6 were waited for; matrix products, arithmetic and copies ran while one was open for 36% of the time, Pallas kernels for 0%

profile of v1, /device:TPU:0, one launch (start us, length us, event | category | flops | bytes accessed | tf_op | source)
XLA Modules:
  0.0 65.5 jit_solution(10175191420983455372)
XLA Ops:
  0.6 0.0 copy-start
  0.6 0.0 copy-start.1
  0.7 0.5 collective-permute-start
  1.2 0.1 collective-permute-start.4
  1.3 0.8 %select_reduce_fusion = (f32[128,4]{0,1:T(4,128)S(1)}, f32[128,4]{0,1:T(4,128)S(1)}) fusion(f32[128,2]{0,1:T(2,128)} %param.9, s32[128,2]{0,1:T(2,128)} %param.8, s32[4]{0:T(128)S(1)} %get-tuple-element.14, s32[4]{0:T(128)S(1)} %get-tuple-element.15), kind=kLoop, calls=%fused_computation.43 | loop fusion | flops 5120 | bytes 6176 | tf_op jit(solution)/shard_map/reduce_sum | solution.py:13
  2.0 0.5 collective-permute-start.1
  2.5 0.1 collective-permute-start.3
  2.6 0.0 copy-done
  2.6 2.2 %fusion.3 = bf16[128,64]{0,1:T(8,128)(2,1)S(1)} fusion(f32[128,64]{0,1:T(8,128)S(1)} %bitcast.30, bf16[128,7168]{1,0:T(8,128)(2,1)} %param.7, bf16[64,7168]{1,0:T(8,128)(2,1)S(1)} %bitcast.24), kind=kOutput, calls=%fused_computation.26 | convolution fusion | flops 117456896 | bytes 2801664 | tf_op jit(solution)/shard_map/dot_general | solution.py:55
  4.9 0.0 copy-done.1
  4.9 4.8 %fusion.7 = f32[64,7168]{1,0:T(8,128)} fusion(bf16[128,7168]{1,0:T(8,128)(2,1)} %param.7, f32[128,64]{0,1:T(8,128)S(1)} %bitcast.31, bf16[128,7168]{1,0:T(8,128)(2,1)} %param.6, bf16[64,7168]{1,0:T(8,128)(2,1)S(1)} %bitcast.27), kind=kOutput, calls=%fused_computation.30 | convolution fusion | flops 234897408 | bytes 6455296 | tf_op jit(solution)/shard_map/dot_general | solution.py:59
  9.7 3.1 %fusion.18 = f32[64,7168]{1,0:T(8,128)} fusion(bf16[128,64]{0,1:T(8,128)(2,1)S(1)} %fusion.3, bf16[128,7168]{1,0:T(8,128)(2,1)} %param.6), kind=kOutput, calls=%fused_computation.49 | convolution fusion | flops 117440512 | bytes 3686400 | tf_op jit(solution)/shard_map/dot_general | solution.py:59
  12.8 0.0 collective-permute-done.1
  12.8 0.0 collective-permute-done
  12.8 2.2 %fusion.4 = bf16[128,64]{0,1:T(8,128)(2,1)S(1)} fusion(f32[128,64]{0,1:T(8,128)S(1)} %collective-permute-done.1, bf16[128,7168]{1,0:T(8,128)(2,1)} %collective-permute-done, bf16[64,7168]{1,0:T(8,128)(2,1)S(1)} %bitcast.25), kind=kOutput, calls=%fused_computation.27 | convolution fusion | flops 117456896 | bytes 2801664 | tf_op jit(solution)/shard_map/dot_general | solution.py:55
  15.1 0.0 collective-permute-done.4
  15.1 4.1 %fusion.2 = bf16[64,7168]{1,0:T(8,128)(2,1)S(1)} fusion(f32[64,7168]{1,0:T(8,128)} %fusion.7, bf16[128,7168]{1,0:T(8,128)(2,1)} %collective-permute-done, f32[128,64]{0,1:T(8,128)S(1)} %collective-permute-done.1, bf16[128,7168]{1,0:T(8,128)(2,1)} %collective-permute-done.4, bf16[64,7168]{1,0:T(8,128)(2,1)S(1)} %bitcast.28), kind=kOutput, calls=%fused_computation.5 | convolution fusion | flops 235814912 | bytes 7372800 | tf_op jit(solution)/shard_map/dot_general | solution.py:59
  19.2 2.4 %fusion.1 = bf16[64,7168]{1,0:T(8,128)(2,1)S(1)} fusion(f32[64,7168]{1,0:T(8,128)} %fusion.18, bf16[128,64]{0,1:T(8,128)(2,1)S(1)} %fusion.4, bf16[128,7168]{1,0:T(8,128)(2,1)} %collective-permute-done.4), kind=kOutput, calls=%fused_computation.4 | convolution fusion | flops 118358016 | bytes 4603904 | tf_op jit(solution)/shard_map/dot_general | solution.py:59
  21.7 0.1 fusion.10
  21.8 3.0 %collective-permute-start.5 = (bf16[128,896]{1,0:T(8,128)(2,1)S(1)}, bf16[128,896]{1,0:T(8,128)(2,1)S(1)}, u32[]{:S(2)}, u32[]{:S(2)}) collective-permute-start(bf16[128,896]{1,0:T(8,128)(2,1)S(1)} %get-tuple-element.8), channel_id=1, source_target_pairs={{0,2},{2,0},{4,6},{6,4},{8,10},{10,8},{12,14},{14,12},{1,3},{3,1},... | collective-permute-start | bytes 688136 | tf_op jit(solution)/shard_map/ppermute | solution.py:31
  24.8 0.1 collective-permute-start.7
  24.8 1.9 %collective-permute-start.9 = (bf16[128,896]{1,0:T(8,128)(2,1)S(1)}, bf16[128,896]{1,0:T(8,128)(2,1)S(1)}, u32[]{:S(2)}, u32[]{:S(2)}) collective-permute-start(bf16[128,896]{1,0:T(8,128)(2,1)S(1)} %get-tuple-element.10), channel_id=1, source_target_pairs={{0,2},{2,0},{4,6},{6,4},{8,10},{10,8},{12,14},{14,12},{1,3},{3,1},... | collective-permute-start | bytes 688136 | tf_op jit(solution)/shard_map/ppermute | solution.py:31
  26.8 0.7 %fusion.17 = f32[128,7168]{1,0:T(8,128)S(1)} fusion(bf16[128,64]{0,1:T(8,128)(2,1)S(1)} %fusion.3, bf16[64,7168]{1,0:T(8,128)(2,1)S(1)} %bitcast.29), kind=kOutput, calls=%fused_computation.48 | convolution fusion | flops 117440512 | bytes 4603904 | tf_op jit(solution)/shard_map/dot_general | solution.py:69
  27.5 0.1 collective-permute-start.2
  27.5 3.6 %collective-permute-done.5 = bf16[128,896]{1,0:T(8,128)(2,1)S(1)} collective-permute-done((bf16[128,896]{1,0:T(8,128)(2,1)S(1)}, bf16[128,896]{1,0:T(8,128)(2,1)S(1)}, u32[]{:S(2)}, u32[]{:S(2)}) %collective-permute-start.5) | collective-permute-done | bytes 229408 | tf_op jit(solution)/shard_map/ppermute | solution.py:31
  31.2 2.1 %collective-permute-start.11 = (bf16[128,896]{1,0:T(8,128)(2,1)S(1)}, bf16[128,896]{1,0:T(8,128)(2,1)S(1)}, u32[]{:S(2)}, u32[]{:S(2)}) collective-permute-start(bf16[128,896]{1,0:T(8,128)(2,1)S(1)} %get-tuple-element.11), channel_id=1, source_target_pairs={{0,2},{2,0},{4,6},{6,4},{8,10},{10,8},{12,14},{14,12},{1,3},{3,1},... | collective-permute-start | bytes 688136 | tf_op jit(solution)/shard_map/ppermute | solution.py:31
  33.2 2.9 %collective-permute-done.7 = bf16[128,896]{1,0:T(8,128)(2,1)S(1)} collective-permute-done((bf16[128,896]{1,0:T(8,128)(2,1)S(1)}, bf16[128,896]{1,0:T(8,128)(2,1)S(1)}, u32[]{:S(2)}, u32[]{:S(2)}) %collective-permute-start.7) | collective-permute-done | bytes 229408 | tf_op jit(solution)/shard_map/ppermute | solution.py:31
  36.1 4.9 %collective-permute-done.9 = bf16[128,896]{1,0:T(8,128)(2,1)S(1)} collective-permute-done((bf16[128,896]{1,0:T(8,128)(2,1)S(1)}, bf16[128,896]{1,0:T(8,128)(2,1)S(1)}, u32[]{:S(2)}, u32[]{:S(2)}) %collective-permute-start.9) | collective-permute-done | bytes 229408 | tf_op jit(solution)/shard_map/ppermute | solution.py:31
  41.0 0.2 add_convert_fusion.2
  41.2 2.2 %collective-permute-start.10 = (bf16[128,896]{1,0:T(8,128)(2,1)S(1)}, bf16[128,896]{1,0:T(8,128)(2,1)S(1)}, u32[]{:S(2)}, u32[]{:S(2)}) collective-permute-start(bf16[128,896]{1,0:T(8,128)(2,1)S(1)} %get-tuple-element.7), channel_id=1, source_target_pairs={{0,4},{2,6},{4,0},{6,2},{8,12},{10,14},{12,8},{14,10},{1,5},{3,7},... | collective-permute-start | bytes 688136 | tf_op jit(solution)/shard_map/ppermute | solution.py:34
  43.4 2.5 %collective-permute-start.6 = (bf16[128,896]{1,0:T(8,128)(2,1)S(1)}, bf16[128,896]{1,0:T(8,128)(2,1)S(1)}, u32[]{:S(2)}, u32[]{:S(2)}) collective-permute-start(bf16[128,896]{1,0:T(8,128)(2,1)S(1)} %get-tuple-element.5), channel_id=1, source_target_pairs={{0,12},{2,14},{4,8},{6,10},{8,4},{10,6},{12,0},{14,2},{1,13},{3,15... | collective-permute-start | bytes 688136 | tf_op jit(solution)/shard_map/ppermute | solution.py:34
  45.9 0.0 collective-permute-done.3
  45.9 0.1 collective-permute-start.8
  46.0 0.0 collective-permute-done.2
  46.0 3.1 %fusion = bf16[128,7168]{1,0:T(8,128)(2,1)} fusion(f32[128,7168]{1,0:T(8,128)S(1)} %fusion.17, bf16[128,64]{0,1:T(8,128)(2,1)S(1)} %collective-permute-done.2, bf16[64,7168]{1,0:T(8,128)(2,1)} %collective-permute-done.3), kind=kOutput, calls=%fused_computation.1 | convolution fusion | flops 119275520 | bytes 6438912 | tf_op jit(solution)/shard_map/dot_general | solution.py:70
  49.1 0.0 collective-permute-done.11
  49.1 0.4 collective-permute-done.10
  49.5 7.6 %collective-permute-done.6 = bf16[128,896]{1,0:T(8,128)(2,1)S(1)} collective-permute-done((bf16[128,896]{1,0:T(8,128)(2,1)S(1)}, bf16[128,896]{1,0:T(8,128)(2,1)S(1)}, u32[]{:S(2)}, u32[]{:S(2)}) %collective-permute-start.6) | collective-permute-done | bytes 229408 | tf_op jit(solution)/shard_map/ppermute | solution.py:34
  57.1 7.5 %collective-permute-done.8 = bf16[128,896]{1,0:T(8,128)(2,1)S(1)} collective-permute-done((bf16[128,896]{1,0:T(8,128)(2,1)S(1)}, bf16[128,896]{1,0:T(8,128)(2,1)S(1)}, u32[]{:S(2)}, u32[]{:S(2)}) %collective-permute-start.8) | collective-permute-done | bytes 229408 | tf_op jit(solution)/shard_map/ppermute | solution.py:34
  64.6 0.1 add_add_fusion
  64.7 0.8 %fusion.16 = (f32[64,896]{1,0:T(8,128)}, f32[64,896]{1,0:T(8,128)}) fusion(f32[128,896]{1,0:T(8,128)S(1)} %add_add_fusion), kind=kLoop, calls=%fused_computation.47 | loop fusion | bytes 917504 | tf_op jit(solution)/shard_map/slice | solution.py:73
  (3 shorter events, 0.0 us)
Async XLA Ops:
  0.6 2.0 %copy-start = (bf16[4,16,7168]{2,1,0:T(8,128)(2,1)S(1)}, bf16[4,16,7168]{2,1,0:T(8,128)(2,1)}, u32[]{:S(2)}) copy-start(bf16[4,16,7168]{2,1,0:T(8,128)(2,1)} %param.11) | copy-start | bytes 2752516
  0.6 4.2 %copy-start.1 = (bf16[4,16,7168]{2,1,0:T(8,128)(2,1)S(1)}, bf16[4,16,7168]{2,1,0:T(8,128)(2,1)}, u32[]{:S(2)}) copy-start(bf16[4,16,7168]{2,1,0:T(8,128)(2,1)} %param.10) | copy-start | bytes 2752516
  0.7 12.2 %collective-permute-start = (bf16[128,7168]{1,0:T(8,128)(2,1)}, bf16[128,7168]{1,0:T(8,128)(2,1)}, u32[]{:S(2)}, u32[]{:S(2)}) collective-permute-start(bf16[128,7168]{1,0:T(8,128)(2,1)} %param.7), channel_id=1, source_target_pairs={{0,1},{1,0},{2,3},{3,2},{4,5},{5,4},{6,7},{7,6},{8,9},{9,8},{10,11... | collective-permute-start | bytes 5505032 | tf_op jit(solution)/shard_map/ppermute | solution.py:50
  1.2 13.9 %collective-permute-start.4 = (bf16[128,7168]{1,0:T(8,128)(2,1)}, bf16[128,7168]{1,0:T(8,128)(2,1)}, u32[]{:S(2)}, u32[]{:S(2)}) collective-permute-start(bf16[128,7168]{1,0:T(8,128)(2,1)} %param.6), channel_id=1, source_target_pairs={{0,1},{1,0},{2,3},{3,2},{4,5},{5,4},{6,7},{7,6},{8,9},{9,8},{10,11... | collective-permute-start | bytes 5505032 | tf_op jit(solution)/shard_map/ppermute | solution.py:51
  2.0 10.8 %collective-permute-start.1 = (f32[128,64]{0,1:T(8,128)S(1)}, f32[128,64]{0,1:T(8,128)S(1)}, u32[]{:S(2)}, u32[]{:S(2)}) collective-permute-start(f32[128,64]{0,1:T(8,128)S(1)} %bitcast.34), channel_id=1, source_target_pairs={{0,1},{1,0},{2,3},{3,2},{4,5},{5,4},{6,7},{7,6},{8,9},{9,8},{10,11... | collective-permute-start | bytes 98312 | tf_op jit(solution)/shard_map/ppermute | solution.py:49
  2.5 43.3 %collective-permute-start.3 = (bf16[64,7168]{1,0:T(8,128)(2,1)}, bf16[64,7168]{1,0:T(8,128)(2,1)}, u32[]{:S(2)}, u32[]{:S(2)}) collective-permute-start(bf16[64,7168]{1,0:T(8,128)(2,1)} %bitcast.26), channel_id=1, source_target_pairs={{0,1},{1,0},{2,3},{3,2},{4,5},{5,4},{6,7},{7,6},{8,9},{9,8},{10,11... | collective-permute-start | bytes 2752520 | tf_op jit(solution)/shard_map/ppermute | solution.py:52
  21.8 9.4 %collective-permute-start.5 = (bf16[128,896]{1,0:T(8,128)(2,1)S(1)}, bf16[128,896]{1,0:T(8,128)(2,1)S(1)}, u32[]{:S(2)}, u32[]{:S(2)}) collective-permute-start(bf16[128,896]{1,0:T(8,128)(2,1)S(1)} %get-tuple-element.8), channel_id=1, source_target_pairs={{0,2},{2,0},{4,6},{6,4},{8,10},{10,8},{12,14},{14,12},{1,3},{3,1},... | collective-permute-start | bytes 688136 | tf_op jit(solution)/shard_map/ppermute | solution.py:31
  24.8 11.3 %collective-permute-start.7 = (bf16[128,896]{1,0:T(8,128)(2,1)S(1)}, bf16[128,896]{1,0:T(8,128)(2,1)S(1)}, u32[]{:S(2)}, u32[]{:S(2)}) collective-permute-start(bf16[128,896]{1,0:T(8,128)(2,1)S(1)} %get-tuple-element.9), channel_id=1, source_target_pairs={{0,2},{2,0},{4,6},{6,4},{8,10},{10,8},{12,14},{14,12},{1,3},{3,1},... | collective-permute-start | bytes 688136 | tf_op jit(solution)/shard_map/ppermute | solution.py:31
  24.8 16.2 %collective-permute-start.9 = (bf16[128,896]{1,0:T(8,128)(2,1)S(1)}, bf16[128,896]{1,0:T(8,128)(2,1)S(1)}, u32[]{:S(2)}, u32[]{:S(2)}) collective-permute-start(bf16[128,896]{1,0:T(8,128)(2,1)S(1)} %get-tuple-element.10), channel_id=1, source_target_pairs={{0,2},{2,0},{4,6},{6,4},{8,10},{10,8},{12,14},{14,12},{1,3},{3,1},... | collective-permute-start | bytes 688136 | tf_op jit(solution)/shard_map/ppermute | solution.py:31
  27.5 18.5 %collective-permute-start.2 = (bf16[128,64]{0,1:T(8,128)(2,1)S(1)}, bf16[128,64]{0,1:T(8,128)(2,1)S(1)}, u32[]{:S(2)}, u32[]{:S(2)}) collective-permute-start(bf16[128,64]{0,1:T(8,128)(2,1)S(1)} %fusion.4), channel_id=1, source_target_pairs={{0,1},{1,0},{2,3},{3,2},{4,5},{5,4},{6,7},{7,6},{8,9},{9,8},{10,11... | collective-permute-start | bytes 49160 | tf_op jit(solution)/shard_map/ppermute | solution.py:67
  31.2 17.9 %collective-permute-start.11 = (bf16[128,896]{1,0:T(8,128)(2,1)S(1)}, bf16[128,896]{1,0:T(8,128)(2,1)S(1)}, u32[]{:S(2)}, u32[]{:S(2)}) collective-permute-start(bf16[128,896]{1,0:T(8,128)(2,1)S(1)} %get-tuple-element.11), channel_id=1, source_target_pairs={{0,2},{2,0},{4,6},{6,4},{8,10},{10,8},{12,14},{14,12},{1,3},{3,1},... | collective-permute-start | bytes 688136 | tf_op jit(solution)/shard_map/ppermute | solution.py:31
  41.2 8.3 %collective-permute-start.10 = (bf16[128,896]{1,0:T(8,128)(2,1)S(1)}, bf16[128,896]{1,0:T(8,128)(2,1)S(1)}, u32[]{:S(2)}, u32[]{:S(2)}) collective-permute-start(bf16[128,896]{1,0:T(8,128)(2,1)S(1)} %get-tuple-element.7), channel_id=1, source_target_pairs={{0,4},{2,6},{4,0},{6,2},{8,12},{10,14},{12,8},{14,10},{1,5},{3,7},... | collective-permute-start | bytes 688136 | tf_op jit(solution)/shard_map/ppermute | solution.py:34
  43.4 13.7 %collective-permute-start.6 = (bf16[128,896]{1,0:T(8,128)(2,1)S(1)}, bf16[128,896]{1,0:T(8,128)(2,1)S(1)}, u32[]{:S(2)}, u32[]{:S(2)}) collective-permute-start(bf16[128,896]{1,0:T(8,128)(2,1)S(1)} %get-tuple-element.5), channel_id=1, source_target_pairs={{0,12},{2,14},{4,8},{6,10},{8,4},{10,6},{12,0},{14,2},{1,13},{3,15... | collective-permute-start | bytes 688136 | tf_op jit(solution)/shard_map/ppermute | solution.py:34
  45.9 18.7 %collective-permute-start.8 = (bf16[128,896]{1,0:T(8,128)(2,1)S(1)}, bf16[128,896]{1,0:T(8,128)(2,1)S(1)}, u32[]{:S(2)}, u32[]{:S(2)}) collective-permute-start(bf16[128,896]{1,0:T(8,128)(2,1)S(1)} %get-tuple-element.6), channel_id=1, source_target_pairs={{0,8},{2,10},{4,12},{6,14},{8,0},{10,2},{12,4},{14,6},{1,9},{3,11}... | collective-permute-start | bytes 688136 | tf_op jit(solution)/shard_map/ppermute | solution.py:34

commit v2 on v1

v2 whole, which is shorter than its diff:
```python
import functools

import jax
import jax.numpy as jnp
from jax import lax
from jax.experimental import pallas as pl
from jax.experimental.pallas import tpu as pltpu
from jax.sharding import PartitionSpec as P

BF16 = jnp.bfloat16
F32 = jnp.float32
SWAP = [(0, 1), (1, 0)]
VMEM_LIMIT = 40 * 1024 * 1024
NT = (((1,), (1,)), ((), ()))
TN = (((0,), (0,)), ((), ()))


def params():
    return pltpu.CompilerParams(vmem_limit_bytes=VMEM_LIMIT)


def cost(flops, moved):
    return pl.CostEstimate(flops=int(flops), bytes_accessed=int(moved), transcendentals=0)


def whole(shape):
    return pl.BlockSpec(shape, lambda *_: (0,) * len(shape))


def steps_of(width):
    for steps in (4, 7, 2):
        if width % (steps * 128) == 0:
            return steps
    return 1


def gate_columns(core_ref, ids, gates, rows, rank):
    adapter = lax.broadcasted_iota(jnp.int32, (rows, ids.shape[1]), 0) // rank
    adapter = adapter + core_ref[0] * (rows // rank)
    total = jnp.zeros((rows, ids.shape[1]), F32)
    for k in range(ids.shape[0]):
        total = total + jnp.where(ids[k : k + 1, :] == adapter, gates[k : k + 1, :], 0.0)
    return total


def low_kernel(rank, count, core_ref, ids_ref, gates_ref, *refs):
    pairs, outs, sums = refs[: 2 * count], refs[2 * count : 3 * count], refs[3 * count :]
    step = pl.program_id(0)
    for j in range(count):
        part = lax.dot_general(
            pairs[2 * j][...], pairs[2 * j + 1][...], NT, preferred_element_type=F32
        )

        @pl.when(step == 0)
        def _():
            sums[j][...] = part

        @pl.when(step > 0)
        def _():
            sums[j][...] += part

    @pl.when(step == pl.num_programs(0) - 1)
    def _():
        weight = gate_columns(core_ref, ids_ref[...], gates_ref[...], sums[0].shape[0], rank)
        for j in range(count):
            outs[j][...] = (sums[j][...] * weight).astype(BF16)


def low_products(core, ids, gates, rank, *pairs):
    count = len(pairs)
    rows, width = pairs[0][0].shape
    tokens = pairs[0][1].shape[0]
    steps = steps_of(width)
    tile = width // steps
    along = lambda extent: pl.BlockSpec((extent, tile), lambda s, *_: (0, s))
    return pl.pallas_call(
        functools.partial(low_kernel, rank, count),
        grid_spec=pltpu.PrefetchScalarGridSpec(
            num_scalar_prefetch=1,
            grid=(steps,),
            in_specs=[whole(ids.shape), whole(gates.shape)] + [along(rows), along(tokens)] * count,
            out_specs=[whole((rows, tokens))] * count,
            scratch_shapes=[pltpu.VMEM((rows, tokens), F32)] * count,
        ),
        out_shape=[jax.ShapeDtypeStruct((rows, tokens), BF16)] * count,
        compiler_params=params(),
        cost_estimate=cost(
            2 * count * rows * tokens * width, count * 2 * (rows + tokens) * width
        ),
    )(core, ids, gates, *(array for pair in pairs for array in pair))


def piece_kernel(block, where_ref, lg_ref, lgi_ref, la_ref, lai_ref, x_ref, xi_ref, g_ref, gi_ref,
                 send_ref, keep_ref):
    near = where_ref[1]
    rows = lg_ref.shape[0]

    def columns(start):
        cols = pl.ds(pl.multiple_of(start, 128), block)
        dot = functools.partial(jnp.dot, preferred_element_type=F32)
        down = dot(lg_ref[...], x_ref[:, cols]) + dot(lgi_ref[...], xi_ref[:, cols])
        up = dot(la_ref[...], g_ref[:, cols]) + dot(lai_ref[...], gi_ref[:, cols])
        return down, up

    down, up = columns((1 - near) * block)
    send_ref[:rows, :] = down.astype(BF16)
    send_ref[rows:, :] = up.astype(BF16)
    down, up = columns(near * block)
    keep_ref[:rows, :] = down
    keep_ref[rows:, :] = up


def piece(where, low, x, x_in, g, g_in, block):
    rows = low[0].shape[0]
    tokens = x.shape[0]
    tall = pl.BlockSpec((tokens, 2 * block), lambda s, where: (0, where[0]))
    return pl.pallas_call(
        functools.partial(piece_kernel, block),
        grid_spec=pltpu.PrefetchScalarGridSpec(
            num_scalar_prefetch=1,
            grid=(1,),
            in_specs=[whole(low[0].shape)] * 4 + [tall] * 4,
            out_specs=[whole((2 * rows, block))] * 2,
        ),
        out_shape=[
            jax.ShapeDtypeStruct((2 * rows, block), BF16),
            jax.ShapeDtypeStruct((2 * rows, block), F32),
        ],
        compiler_params=params(),
        cost_estimate=cost(
            16 * rows * tokens * block, 16 * tokens * block + 12 * rows * block
        ),
    )(where, *low, x, x_in, g, g_in)


def add_kernel(keep_ref, came_ref, out_ref):
    out_ref[...] = (keep_ref[...] + came_ref[...].astype(F32)).astype(out_ref.dtype)


def add(keep, came):
    return pl.pallas_call(
        add_kernel,
        out_shape=jax.ShapeDtypeStruct(keep.shape, BF16),
        compiler_params=params(),
        cost_estimate=cost(keep.size, 8 * keep.size),
    )(keep, came)


def last_kernel(count, keep_ref, *refs):
    came, (down_ref, up_ref) = refs[:count], refs[count:]
    total = keep_ref[...]
    for ref in came:
        total = total + ref[...].astype(F32)
    rows = down_ref.shape[0]
    down_ref[...] = total[:rows]
    up_ref[...] = total[rows:]


def last(keep, came):
    rows, block = keep.shape[0] // 2, keep.shape[1]
    return pl.pallas_call(
        functools.partial(last_kernel, len(came)),
        out_shape=[jax.ShapeDtypeStruct((rows, block), F32)] * 2,
        compiler_params=params(),
        cost_estimate=cost(keep.size * len(came), keep.size * (8 + 2 * len(came))),
    )(keep, *came)


def input_kernel(lg_ref, lgo_ref, a_ref, ao_ref, out_ref):
    dot = functools.partial(lax.dot_general, dimension_numbers=TN, preferred_element_type=F32)
    out_ref[...] = (dot(lg_ref[...], a_ref[...]) + dot(lgo_ref[...], ao_ref[...])).astype(BF16)


def input_gradient(low_own, low_other, a, a_other):
    rows, tokens = low_own.shape
    width = a.shape[1]
    steps = steps_of(width)
    tile = width // steps
    return pl.pallas_call(
        input_kernel,
        grid=(steps,),
        in_specs=[whole((rows, tokens))] * 2 + [pl.BlockSpec((rows, tile), lambda s: (0, s))] * 2,
        out_specs=pl.BlockSpec((tokens, tile), lambda s: (0, s)),
        out_shape=jax.ShapeDtypeStruct((tokens, width), BF16),
        compiler_params=params(),
        cost_estimate=cost(4 * rows * tokens * width, 2 * (2 * rows + tokens) * width),
    )(low_own, low_other, a, a_other)


def shards(x, g, ids, gates, down_w, up_w):
    tokens, width = x.shape
    count, rank, _ = down_w.shape
    rows = count * rank
    replicas = lax.axis_size("dp")
    block = width // replicas
    core = lax.axis_index("adapter").astype(jnp.int32).reshape(1)
    a = down_w.reshape(rows, width)
    b = up_w.reshape(rows, width)
    ids, gates = ids.T, gates.T
    swap = lambda array: lax.ppermute(array, "adapter", SWAP)
    g_in, x_in, ids_in, gates_in, a_in = swap(g), swap(x), swap(ids), swap(gates), swap(a)

    lg, la = low_products(core, ids, gates, rank, (b, g), (a, x))
    (lg_in,) = low_products(core, ids_in, gates_in, rank, (b, g_in))
    (la_in,) = low_products(core, ids_in, gates_in, rank, (a, x_in))

    lg_back = swap(lg_in)
    low = (lg, lg_in, la, la_in)
    if replicas >= 2 and replicas & (replicas - 1) == 0 and block % 128 == 0:
        me = lax.axis_index("dp").astype(jnp.int32)
        far, near = me // 2, me % 2
        came = []
        for step in reversed(range(replicas // 2)):
            where = jnp.stack([far ^ step, near])
            send, keep = piece(where, low, x, x_in, g, g_in, block)
            got = lax.ppermute(send, "dp", [(i, i ^ 1) for i in range(replicas)])
            if step:
                term = add(keep, got)
                perm = [(i, i ^ (2 * step)) for i in range(replicas)]
                came.append(lax.ppermute(term, "dp", perm))
            else:
                came.append(got)
        down, up = last(keep, came)
    else:
        dot = functools.partial(jnp.dot, preferred_element_type=F32)
        both = jnp.concatenate([dot(lg, x) + dot(lg_in, x_in), dot(la, g) + dot(la_in, g_in)], axis=0)
        both = lax.psum_scatter(both, "dp", scatter_dimension=1, tiled=True)
        down, up = both[:rows], both[rows:]
    input_grad = input_gradient(lg, lg_back, a, a_in)
    return input_grad, down.reshape(count, rank, block), up.reshape(count, rank, block)


def solution(mesh):
    tok = P(("groups", "dp", "adapter"), None)
    return jax.shard_map(
        shards,
        mesh=mesh,
        in_specs=(tok, tok, tok, tok, P("adapter", None, None), P("adapter", None, None)),
        out_specs=(
            tok,
            P(("groups", "adapter"), None, "dp"),
            P(("groups", "adapter"), None, "dp"),
        ),
        check_vma=False,
    )
```

time: 65.8 us -> 56.3 us (0.86)
  the two profiles are of different devices: /device:TPU:0 before, /device:TPU:22 now
where the time goes in v2:
time: 56.3 us; the launch traced here: 55.7 us
  Pallas kernels  20.3 us (36%)
  waiting for transfers between devices  19.7 us (35%)
  starting transfers between devices  8.03 us (14%)
  local copies, waits for them, and re-layouts  6.73 us (12%)
  between operations  0.81 us (1%)
    ppermute x3, waiting for transfers between devices, shards(): came.append(lax.ppermute(term, 'dp', perm))  13 us
    pallas_call x4, Pallas kernels, piece(): pl.pallas_call(functools.partial(piece_kernel, block), grid_spec=pltpu.Pr...  8.34 us
    pallas_call x3, Pallas kernels, low_products(): pl.pallas_call(functools.partial(low_kernel, rank, count), grid_spec=pltp...  8.05 us
    unnamed x20, local copies, waits for them, and re-layouts  6.73 us
    ppermute x4, waiting for transfers between devices, shards(): got = lax.ppermute(send, 'dp', [(i, i ^ 1) for i in range(replicas)])  5.59 us
    ppermute x4, starting transfers between devices, shards(): got = lax.ppermute(send, 'dp', [(i, i ^ 1) for i in range(replicas)])  4.31 us
    pallas_call x1, Pallas kernels, input_gradient(): pl.pallas_call(input_kernel, grid=(steps,), in_specs=[whole((rows, tokens...  2.93 us
    ppermute x3, starting transfers between devices, shards(): came.append(lax.ppermute(term, 'dp', perm))  2.56 us
  transfers between devices with their start and end apart: 13, of which 5 were waited for; matrix products, arithmetic and copies ran while one was open for 0% of the time, Pallas kernels for 35%

profile of v2, /device:TPU:22, one launch (start us, length us, event | category | flops | bytes accessed | tf_op | source)
XLA Modules:
  0.0 55.7 jit_solution(13072153620908846419)
XLA Ops:
  0.6 0.1 collective-permute-start.5
  0.7 0.5 collective-permute-start.2
  1.2 0.1 collective-permute-start.4
  1.3 0.4 collective-permute-start
  1.7 0.1 collective-permute-start.1
  1.8 0.1 pad_add_fusion.2
  1.9 0.1 pad_add_fusion
  1.9 1.5 %copy-done = bf16[128,7168]{1,0:T(8,128)(2,1)S(1)} copy-done((bf16[128,7168]{1,0:T(8,128)(2,1)S(1)}, bf16[128,7168]{1,0:T(8,128)(2,1)}, u32[]{:S(2)}) %copy-start) | copy-done | bytes 1835032
  3.5 1.5 %copy-done.2 = bf16[128,7168]{1,0:T(8,128)(2,1)S(1)} copy-done((bf16[128,7168]{1,0:T(8,128)(2,1)S(1)}, bf16[128,7168]{1,0:T(8,128)(2,1)}, u32[]{:S(2)}) %copy-start.2) | copy-done | bytes 1835032
  5.0 1.2 %copy-done.4 = bf16[4,16,7168]{2,1,0:T(8,128)(2,1)S(1)} copy-done((bf16[4,16,7168]{2,1,0:T(8,128)(2,1)S(1)}, bf16[4,16,7168]{2,1,0:T(8,128)(2,1)}, u32[]{:S(2)}) %copy-start.4) | copy-done | bytes 917528
  6.1 1.2 %copy-done.6 = bf16[4,16,7168]{2,1,0:T(8,128)(2,1)S(1)} copy-done((bf16[4,16,7168]{2,1,0:T(8,128)(2,1)S(1)}, bf16[4,16,7168]{2,1,0:T(8,128)(2,1)}, u32[]{:S(2)}) %copy-start.6) | copy-done | bytes 917528
  7.3 0.7 %copy-done.8 = s32[128,2]{0,1:T(2,128)S(1)} copy-done((s32[128,2]{0,1:T(2,128)S(1)}, s32[128,2]{0,1:T(2,128)}, u32[]{:S(2)}) %copy-start.8) | copy-done | bytes 1048
  8.0 0.7 %copy-done.9 = f32[128,2]{0,1:T(2,128)S(1)} copy-done((f32[128,2]{0,1:T(2,128)S(1)}, f32[128,2]{0,1:T(2,128)}, u32[]{:S(2)}) %copy-start.9) | copy-done | bytes 1048
  8.7 3.4 %shard_map.85 = (bf16[64,128]{1,0:T(8,128)(2,1)S(1)}, bf16[64,128]{1,0:T(8,128)(2,1)S(1)}) custom-call(s32[1]{0:T(128)} %bitcast.core_ref, s32[2,128]{1,0:T(2,128)S(1)} %bitcast.19, f32[2,128]{1,0:T(2,128)S(1)} %bitcast.21, bf16[64,7168]{1,0:T(8,128)(2,1)S(1)} %bitcast.16, bf16[128,7168]{1,0:T(8,128)(2,1)S(1)} %copy-done, bf16[64,7168]{1,0:T(8,128)(2,1)S(1)} %bitcast.13, ...), custom_call_target="tpu_custom_call" | custom-call | flops 234881024 | bytes 5505024 | tf_op jit(solution)/shard_map/pallas_call | solution.py:76
  12.1 0.0 copy-start.7
  12.1 0.0 collective-permute-done.ids_ref
  12.1 0.0 collective-permute-done.1.gates_ref
  12.1 0.0 collective-permute-done.5.refs_1_.xi_ref
  12.1 0.0 copy-done.5
  12.2 0.0 copy-start.3
  12.2 1.4 %shard_map.88.lai_ref = bf16[64,128]{1,0:T(8,128)(2,1)S(1)} custom-call(s32[1]{0:T(128)} %bitcast.core_ref, s32[2,128]{1,0:T(2,128)S(1)} %collective-permute-done.ids_ref, f32[2,128]{1,0:T(2,128)S(1)} %collective-permute-done.1.gates_ref, bf16[64,7168]{1,0:T(8,128)(2,1)S(1)} %bitcast.14, bf16[128,7168]{1,0:T(8,128)(2,1)S(1)} %collective-permute-done.5.refs_1_.xi_ref), custom_call_target="tpu_custom_call" | custom-call | flops 117440512 | bytes 2752512 | tf_op jit(solution)/shard_map/pallas_call | solution.py:76
  13.6 0.0 copy-start.1
  13.6 0.0 collective-permute-done.2.refs_1_.gi_ref
  13.6 0.0 copy-done.7
  13.7 3.2 %shard_map.86.lgi_ref = bf16[64,128]{1,0:T(8,128)(2,1)S(1)} custom-call(s32[1]{0:T(128)} %bitcast.core_ref, s32[2,128]{1,0:T(2,128)S(1)} %collective-permute-done.ids_ref, f32[2,128]{1,0:T(2,128)S(1)} %collective-permute-done.1.gates_ref, bf16[64,7168]{1,0:T(8,128)(2,1)S(1)} %bitcast.17, bf16[128,7168]{1,0:T(8,128)(2,1)} %collective-permute-done.2.refs_1_.gi_ref), custom_call_target="tpu_custom_call" | custom-call | flops 117440512 | bytes 2752512 | tf_op jit(solution)/shard_map/pallas_call | solution.py:76
  16.9 2.1 %shard_map.94 = (bf16[128,896]{1,0:T(8,128)(2,1)S(1)}, f32[128,896]{1,0:T(8,128)S(1)}) custom-call(s32[2]{0:T(128)S(1)} %get-tuple-element.30.where_ref, bf16[64,128]{1,0:T(8,128)(2,1)S(1)} %get-tuple-element.15.lg_ref, bf16[64,128]{1,0:T(8,128)(2,1)S(1)} %shard_map.86.lgi_ref, bf16[64,128]{1,0:T(8,128)(2,1)S(1)} %get-tuple-element.16.la_ref, ...), custom_call_target="tpu_custom_call" | custom-call | flops 117440512 | bytes 2523136 | tf_op jit(solution)/shard_map/pallas_call | solution.py:117
  19.0 0.6 %collective-permute-start.10 = (bf16[128,896]{1,0:T(8,128)(2,1)S(1)}, bf16[128,896]{1,0:T(8,128)(2,1)S(1)}, u32[]{:S(2)}, u32[]{:S(2)}) collective-permute-start(bf16[128,896]{1,0:T(8,128)(2,1)S(1)} %get-tuple-element.23), channel_id=1, source_target_pairs={{0,2},{2,0},{4,6},{6,4},{8,10},{10,8},{12,14},{14,12},{1,3},{3,1},... | collective-permute-start | bytes 688136 | tf_op jit(solution)/shard_map/ppermute | solution.py:216
  19.5 2.1 %shard_map.92 = (bf16[128,896]{1,0:T(8,128)(2,1)S(1)}, f32[128,896]{1,0:T(8,128)S(1)}) custom-call(s32[2]{0:T(128)S(1)} %get-tuple-element.29.where_ref, bf16[64,128]{1,0:T(8,128)(2,1)S(1)} %get-tuple-element.15.lg_ref, bf16[64,128]{1,0:T(8,128)(2,1)S(1)} %shard_map.86.lgi_ref, bf16[64,128]{1,0:T(8,128)(2,1)S(1)} %get-tuple-element.16.la_ref, ...), custom_call_target="tpu_custom_call" | custom-call | flops 117440512 | bytes 2523136 | tf_op jit(solution)/shard_map/pallas_call | solution.py:117
  21.6 1.6 %collective-permute-start.8 = (bf16[128,896]{1,0:T(8,128)(2,1)S(1)}, bf16[128,896]{1,0:T(8,128)(2,1)S(1)}, u32[]{:S(2)}, u32[]{:S(2)}) collective-permute-start(bf16[128,896]{1,0:T(8,128)(2,1)S(1)} %get-tuple-element.21), channel_id=1, source_target_pairs={{0,2},{2,0},{4,6},{6,4},{8,10},{10,8},{12,14},{14,12},{1,3},{3,1},... | collective-permute-start | bytes 688136 | tf_op jit(solution)/shard_map/ppermute | solution.py:216
  23.2 2.1 %shard_map.90 = (bf16[128,896]{1,0:T(8,128)(2,1)S(1)}, f32[128,896]{1,0:T(8,128)S(1)}) custom-call(s32[2]{0:T(128)S(1)} %get-tuple-element.28.where_ref, bf16[64,128]{1,0:T(8,128)(2,1)S(1)} %get-tuple-element.15.lg_ref, bf16[64,128]{1,0:T(8,128)(2,1)S(1)} %shard_map.86.lgi_ref, bf16[64,128]{1,0:T(8,128)(2,1)S(1)} %get-tuple-element.16.la_ref, ...), custom_call_target="tpu_custom_call" | custom-call | flops 117440512 | bytes 2523136 | tf_op jit(solution)/shard_map/pallas_call | solution.py:117
  25.3 0.6 %collective-permute-start.6 = (bf16[128,896]{1,0:T(8,128)(2,1)S(1)}, bf16[128,896]{1,0:T(8,128)(2,1)S(1)}, u32[]{:S(2)}, u32[]{:S(2)}) collective-permute-start(bf16[128,896]{1,0:T(8,128)(2,1)S(1)} %get-tuple-element.19), channel_id=1, source_target_pairs={{0,2},{2,0},{4,6},{6,4},{8,10},{10,8},{12,14},{14,12},{1,3},{3,1},... | collective-permute-start | bytes 688136 | tf_op jit(solution)/shard_map/ppermute | solution.py:216
  25.9 2.1 %shard_map.89 = (bf16[128,896]{1,0:T(8,128)(2,1)S(1)}, f32[128,896]{1,0:T(8,128)S(1)}) custom-call(s32[2]{0:T(128)S(1)} %get-tuple-element.27.where_ref, bf16[64,128]{1,0:T(8,128)(2,1)S(1)} %get-tuple-element.15.lg_ref, bf16[64,128]{1,0:T(8,128)(2,1)S(1)} %shard_map.86.lgi_ref, bf16[64,128]{1,0:T(8,128)(2,1)S(1)} %get-tuple-element.16.la_ref, ...), custom_call_target="tpu_custom_call" | custom-call | flops 117440512 | bytes 2523136 | tf_op jit(solution)/shard_map/pallas_call | solution.py:117
  28.0 1.6 %collective-permute-start.12 = (bf16[128,896]{1,0:T(8,128)(2,1)S(1)}, bf16[128,896]{1,0:T(8,128)(2,1)S(1)}, u32[]{:S(2)}, u32[]{:S(2)}) collective-permute-start(bf16[128,896]{1,0:T(8,128)(2,1)S(1)} %get-tuple-element.24), channel_id=1, source_target_pairs={{0,2},{2,0},{4,6},{6,4},{8,10},{10,8},{12,14},{14,12},{1,3},{3,1},... | collective-permute-start | bytes 688136 | tf_op jit(solution)/shard_map/ppermute | solution.py:216
  29.5 0.0 collective-permute-done.10.came_ref
  29.6 1.6 %collective-permute-start.11 = (bf16[128,896]{1,0:T(8,128)(2,1)S(1)}, bf16[128,896]{1,0:T(8,128)(2,1)S(1)}, u32[]{:S(2)}, u32[]{:S(2)}) collective-permute-start(bf16[128,896]{1,0:T(8,128)(2,1)S(1)} %shard_map.95), channel_id=1, source_target_pairs={{0,4},{2,6},{4,0},{6,2},{8,12},{10,14},{12,8},{14,10},{1,5},{3,7},... | collective-permute-start | bytes 688136 | tf_op jit(solution)/shard_map/ppermute | solution.py:220
  31.2 1.1 %collective-permute-done.8.came_ref = bf16[128,896]{1,0:T(8,128)(2,1)S(1)} collective-permute-done((bf16[128,896]{1,0:T(8,128)(2,1)S(1)}, bf16[128,896]{1,0:T(8,128)(2,1)S(1)}, u32[]{:S(2)}, u32[]{:S(2)}) %collective-permute-start.8) | collective-permute-done | bytes 229408 | tf_op jit(solution)/shard_map/ppermute | solution.py:216
  32.4 0.4 collective-permute-start.9
  32.8 4.5 %collective-permute-done.6.came_ref = bf16[128,896]{1,0:T(8,128)(2,1)S(1)} collective-permute-done((bf16[128,896]{1,0:T(8,128)(2,1)S(1)}, bf16[128,896]{1,0:T(8,128)(2,1)S(1)}, u32[]{:S(2)}, u32[]{:S(2)}) %collective-permute-start.6) | collective-permute-done | bytes 229408 | tf_op jit(solution)/shard_map/ppermute | solution.py:216
  37.3 0.5 collective-permute-start.7
  37.8 0.0 collective-permute-done.4.ao_ref
  37.8 0.0 collective-permute-start.3
  37.8 1.2 %collective-permute-done.3.lgo_ref = bf16[64,128]{1,0:T(8,128)(2,1)S(1)} collective-permute-done((bf16[64,128]{1,0:T(8,128)(2,1)S(1)}, bf16[64,128]{1,0:T(8,128)(2,1)S(1)}, u32[]{:S(2)}, u32[]{:S(2)}) %collective-permute-start.3) | collective-permute-done | bytes 16416 | tf_op jit(solution)/shard_map/ppermute | solution.py:200
  39.0 2.9 %shard_map.87 = bf16[128,7168]{1,0:T(8,128)(2,1)} custom-call(bf16[64,128]{1,0:T(8,128)(2,1)S(1)} %get-tuple-element.15.lg_ref, bf16[64,128]{1,0:T(8,128)(2,1)S(1)} %collective-permute-done.3.lgo_ref, bf16[64,7168]{1,0:T(8,128)(2,1)S(1)} %bitcast.15, bf16[64,7168]{1,0:T(8,128)(2,1)S(1)} %collective-permute-done.4.ao_ref), custom_call_target="tpu_custom_call" | custom-call | flops 234881024 | bytes 3670016 | tf_op jit(solution)/shard_map/pallas_call | solution.py:179
  41.9 0.0 collective-permute-done.12.refs_3_
  41.9 0.0 collective-permute-done.11.refs_2_
  41.9 6.5 %collective-permute-done.9.refs_1_ = bf16[128,896]{1,0:T(8,128)(2,1)S(1)} collective-permute-done((bf16[128,896]{1,0:T(8,128)(2,1)S(1)}, bf16[128,896]{1,0:T(8,128)(2,1)S(1)}, u32[]{:S(2)}, u32[]{:S(2)}) %collective-permute-start.9) | collective-permute-done | bytes 229408 | tf_op jit(solution)/shard_map/ppermute | solution.py:220
  48.5 6.4 %collective-permute-done.7.refs_0_ = bf16[128,896]{1,0:T(8,128)(2,1)S(1)} collective-permute-done((bf16[128,896]{1,0:T(8,128)(2,1)S(1)}, bf16[128,896]{1,0:T(8,128)(2,1)S(1)}, u32[]{:S(2)}, u32[]{:S(2)}) %collective-permute-start.7) | collective-permute-done | bytes 229408 | tf_op jit(solution)/shard_map/ppermute | solution.py:220
  54.9 0.8 %shard_map.96 = (f32[64,896]{1,0:T(8,128)}, f32[64,896]{1,0:T(8,128)}) custom-call(f32[128,896]{1,0:T(8,128)S(1)} %get-tuple-element.17.keep_ref, bf16[128,896]{1,0:T(8,128)(2,1)S(1)} %collective-permute-done.7.refs_0_, bf16[128,896]{1,0:T(8,128)(2,1)S(1)} %collective-permute-done.9.refs_1_, bf16[128,896]{1,0:T(8,128)(2,1)S(1)} %collective-permute-done.11.refs_2_, ...), custom_call_target="tpu_custom_call" | custom-call | flops 458752 | bytes 1835008 | tf_op jit(solution)/shard_map/pallas_call | solution.py:161
  (12 shorter events, 0.1 us)
Async XLA Ops:
  0.6 11.5 %collective-permute-start.5 = (bf16[128,7168]{1,0:T(8,128)(2,1)}, bf16[128,7168]{1,0:T(8,128)(2,1)S(1)}, u32[]{:S(2)}, u32[]{:S(2)}) collective-permute-start(bf16[128,7168]{1,0:T(8,128)(2,1)} %x_ref.7), channel_id=1, source_target_pairs={{0,1},{1,0},{2,3},{3,2},{4,5},{5,4},{6,7},{7,6},{8,9},{9,8},{10,11... | collective-permute-start | bytes 5505032 | tf_op jit(solution)/shard_map/ppermute | solution.py:200
  0.7 12.9 %collective-permute-start.2 = (bf16[128,7168]{1,0:T(8,128)(2,1)}, bf16[128,7168]{1,0:T(8,128)(2,1)}, u32[]{:S(2)}, u32[]{:S(2)}) collective-permute-start(bf16[128,7168]{1,0:T(8,128)(2,1)} %g_ref.7), channel_id=1, source_target_pairs={{0,1},{1,0},{2,3},{3,2},{4,5},{5,4},{6,7},{7,6},{8,9},{9,8},{10,11... | collective-permute-start | bytes 5505032 | tf_op jit(solution)/shard_map/ppermute | solution.py:200
  1.2 36.6 %collective-permute-start.4 = (bf16[64,7168]{1,0:T(8,128)(2,1)}, bf16[64,7168]{1,0:T(8,128)(2,1)S(1)}, u32[]{:S(2)}, u32[]{:S(2)}) collective-permute-start(bf16[64,7168]{1,0:T(8,128)(2,1)} %bitcast.12), channel_id=1, source_target_pairs={{0,1},{1,0},{2,3},{3,2},{4,5},{5,4},{6,7},{7,6},{8,9},{9,8},{10,11... | collective-permute-start | bytes 2752520 | tf_op jit(solution)/shard_map/ppermute | solution.py:200
  1.3 10.8 %collective-permute-start = (s32[2,128]{1,0:T(2,128)}, s32[2,128]{1,0:T(2,128)S(1)}, u32[]{:S(2)}, u32[]{:S(2)}) collective-permute-start(s32[2,128]{1,0:T(2,128)} %bitcast.18), channel_id=1, source_target_pairs={{0,1},{1,0},{2,3},{3,2},{4,5},{5,4},{6,7},{7,6},{8,9},{9,8},{10,11... | collective-permute-start | bytes 3080 | tf_op jit(solution)/shard_map/ppermute | solution.py:200
  1.7 10.4 %collective-permute-start.1 = (f32[2,128]{1,0:T(2,128)}, f32[2,128]{1,0:T(2,128)S(1)}, u32[]{:S(2)}, u32[]{:S(2)}) collective-permute-start(f32[2,128]{1,0:T(2,128)} %bitcast.20), channel_id=1, source_target_pairs={{0,1},{1,0},{2,3},{3,2},{4,5},{5,4},{6,7},{7,6},{8,9},{9,8},{10,11... | collective-permute-start | bytes 3080 | tf_op jit(solution)/shard_map/ppermute | solution.py:200
  1.9 1.5 %copy-start = (bf16[128,7168]{1,0:T(8,128)(2,1)S(1)}, bf16[128,7168]{1,0:T(8,128)(2,1)}, u32[]{:S(2)}) copy-start(bf16[128,7168]{1,0:T(8,128)(2,1)} %g_ref.7) | copy-start | bytes 5505028
  3.4 1.5 %copy-start.2 = (bf16[128,7168]{1,0:T(8,128)(2,1)S(1)}, bf16[128,7168]{1,0:T(8,128)(2,1)}, u32[]{:S(2)}) copy-start(bf16[128,7168]{1,0:T(8,128)(2,1)} %x_ref.7) | copy-start | bytes 5505028
  4.9 1.2 %copy-start.4 = (bf16[4,16,7168]{2,1,0:T(8,128)(2,1)S(1)}, bf16[4,16,7168]{2,1,0:T(8,128)(2,1)}, u32[]{:S(2)}) copy-start(bf16[4,16,7168]{2,1,0:T(8,128)(2,1)} %param.10) | copy-start | bytes 2752516
  6.1 1.2 %copy-start.6 = (bf16[4,16,7168]{2,1,0:T(8,128)(2,1)S(1)}, bf16[4,16,7168]{2,1,0:T(8,128)(2,1)}, u32[]{:S(2)}) copy-start(bf16[4,16,7168]{2,1,0:T(8,128)(2,1)} %param.11) | copy-start | bytes 2752516
  7.3 0.7 %copy-start.8 = (s32[128,2]{0,1:T(2,128)S(1)}, s32[128,2]{0,1:T(2,128)}, u32[]{:S(2)}) copy-start(s32[128,2]{0,1:T(2,128)} %param.8) | copy-start | bytes 3076
  8.0 0.7 %copy-start.9 = (f32[128,2]{0,1:T(2,128)S(1)}, f32[128,2]{0,1:T(2,128)}, u32[]{:S(2)}) copy-start(f32[128,2]{0,1:T(2,128)} %param.9) | copy-start | bytes 3076
  8.7 3.5 %copy-start.5 = (bf16[4,16,7168]{2,1,0:T(8,128)(2,1)S(1)}, bf16[4,16,7168]{2,1,0:T(8,128)(2,1)}, u32[]{:S(2)}) copy-start(bf16[4,16,7168]{2,1,0:T(8,128)(2,1)} %param.10) | copy-start | bytes 2752516
  12.1 1.5 %copy-start.7 = (bf16[4,16,7168]{2,1,0:T(8,128)(2,1)S(1)}, bf16[4,16,7168]{2,1,0:T(8,128)(2,1)}, u32[]{:S(2)}) copy-start(bf16[4,16,7168]{2,1,0:T(8,128)(2,1)} %param.11) | copy-start | bytes 2752516
  12.2 4.7 %copy-start.3 = (bf16[128,7168]{1,0:T(8,128)(2,1)S(1)}, bf16[128,7168]{1,0:T(8,128)(2,1)}, u32[]{:S(2)}) copy-start(bf16[128,7168]{1,0:T(8,128)(2,1)} %x_ref.7) | copy-start | bytes 5505028
  13.6 3.2 %copy-start.1 = (bf16[128,7168]{1,0:T(8,128)(2,1)S(1)}, bf16[128,7168]{1,0:T(8,128)(2,1)}, u32[]{:S(2)}) copy-start(bf16[128,7168]{1,0:T(8,128)(2,1)} %g_ref.7) | copy-start | bytes 5505028
  19.0 10.6 %collective-permute-start.10 = (bf16[128,896]{1,0:T(8,128)(2,1)S(1)}, bf16[128,896]{1,0:T(8,128)(2,1)S(1)}, u32[]{:S(2)}, u32[]{:S(2)}) collective-permute-start(bf16[128,896]{1,0:T(8,128)(2,1)S(1)} %get-tuple-element.23), channel_id=1, source_target_pairs={{0,2},{2,0},{4,6},{6,4},{8,10},{10,8},{12,14},{14,12},{1,3},{3,1},... | collective-permute-start | bytes 688136 | tf_op jit(solution)/shard_map/ppermute | solution.py:216
  21.6 10.7 %collective-permute-start.8 = (bf16[128,896]{1,0:T(8,128)(2,1)S(1)}, bf16[128,896]{1,0:T(8,128)(2,1)S(1)}, u32[]{:S(2)}, u32[]{:S(2)}) collective-permute-start(bf16[128,896]{1,0:T(8,128)(2,1)S(1)} %get-tuple-element.21), channel_id=1, source_target_pairs={{0,2},{2,0},{4,6},{6,4},{8,10},{10,8},{12,14},{14,12},{1,3},{3,1},... | collective-permute-start | bytes 688136 | tf_op jit(solution)/shard_map/ppermute | solution.py:216
  25.3 12.0 %collective-permute-start.6 = (bf16[128,896]{1,0:T(8,128)(2,1)S(1)}, bf16[128,896]{1,0:T(8,128)(2,1)S(1)}, u32[]{:S(2)}, u32[]{:S(2)}) collective-permute-start(bf16[128,896]{1,0:T(8,128)(2,1)S(1)} %get-tuple-element.19), channel_id=1, source_target_pairs={{0,2},{2,0},{4,6},{6,4},{8,10},{10,8},{12,14},{14,12},{1,3},{3,1},... | collective-permute-start | bytes 688136 | tf_op jit(solution)/shard_map/ppermute | solution.py:216
  28.0 14.0 %collective-permute-start.12 = (bf16[128,896]{1,0:T(8,128)(2,1)S(1)}, bf16[128,896]{1,0:T(8,128)(2,1)S(1)}, u32[]{:S(2)}, u32[]{:S(2)}) collective-permute-start(bf16[128,896]{1,0:T(8,128)(2,1)S(1)} %get-tuple-element.24), channel_id=1, source_target_pairs={{0,2},{2,0},{4,6},{6,4},{8,10},{10,8},{12,14},{14,12},{1,3},{3,1},... | collective-permute-start | bytes 688136 | tf_op jit(solution)/shard_map/ppermute | solution.py:216
  29.6 12.4 %collective-permute-start.11 = (bf16[128,896]{1,0:T(8,128)(2,1)S(1)}, bf16[128,896]{1,0:T(8,128)(2,1)S(1)}, u32[]{:S(2)}, u32[]{:S(2)}) collective-permute-start(bf16[128,896]{1,0:T(8,128)(2,1)S(1)} %shard_map.95), channel_id=1, source_target_pairs={{0,4},{2,6},{4,0},{6,2},{8,12},{10,14},{12,8},{14,10},{1,5},{3,7},... | collective-permute-start | bytes 688136 | tf_op jit(solution)/shard_map/ppermute | solution.py:220
  32.4 16.1 %collective-permute-start.9 = (bf16[128,896]{1,0:T(8,128)(2,1)S(1)}, bf16[128,896]{1,0:T(8,128)(2,1)S(1)}, u32[]{:S(2)}, u32[]{:S(2)}) collective-permute-start(bf16[128,896]{1,0:T(8,128)(2,1)S(1)} %shard_map.93), channel_id=1, source_target_pairs={{0,8},{2,10},{4,12},{6,14},{8,0},{10,2},{12,4},{14,6},{1,9},{3,11}... | collective-permute-start | bytes 688136 | tf_op jit(solution)/shard_map/ppermute | solution.py:220
  37.3 17.6 %collective-permute-start.7 = (bf16[128,896]{1,0:T(8,128)(2,1)S(1)}, bf16[128,896]{1,0:T(8,128)(2,1)S(1)}, u32[]{:S(2)}, u32[]{:S(2)}) collective-permute-start(bf16[128,896]{1,0:T(8,128)(2,1)S(1)} %shard_map.91), channel_id=1, source_target_pairs={{0,12},{2,14},{4,8},{6,10},{8,4},{10,6},{12,0},{14,2},{1,13},{3,15... | collective-permute-start | bytes 688136 | tf_op jit(solution)/shard_map/ppermute | solution.py:220
  37.8 1.2 %collective-permute-start.3 = (bf16[64,128]{1,0:T(8,128)(2,1)S(1)}, bf16[64,128]{1,0:T(8,128)(2,1)S(1)}, u32[]{:S(2)}, u32[]{:S(2)}) collective-permute-start(bf16[64,128]{1,0:T(8,128)(2,1)S(1)} %shard_map.86.lgi_ref), channel_id=1, source_target_pairs={{0,1},{1,0},{2,3},{3,2},{4,5},{5,4},{6,7},{7,6},{8,9},{9,8},{10,11... | collective-permute-start | bytes 49160 | tf_op jit(solution)/shard_map/ppermute | solution.py:200

commit v3 on v1

v3 whole, which is shorter than its diff:
```python
import functools

import jax
import jax.numpy as jnp
from jax import lax
from jax.experimental import pallas as pl
from jax.experimental.pallas import tpu as pltpu
from jax.sharding import PartitionSpec as P

BF16 = jnp.bfloat16
F32 = jnp.float32
SWAP = [(0, 1), (1, 0)]
VMEM_LIMIT = 12 * 1024 * 1024
HOLD_LIMIT = 50 * 1024 * 1024
VECTORS = pl.BlockSpec(memory_space=pltpu.VMEM)
ANYWHERE = pl.BlockSpec(memory_space=pl.ANY)
SCALARS = pl.BlockSpec(memory_space=pltpu.SMEM)
NT = (((1,), (1,)), ((), ()))
TN = (((0,), (0,)), ((), ()))


def params(limit=VMEM_LIMIT):
    return pltpu.CompilerParams(vmem_limit_bytes=limit)


def cost(flops, moved):
    return pl.CostEstimate(flops=int(flops), bytes_accessed=int(moved), transcendentals=0)


def steps_of(width):
    for steps in (4, 7, 2):
        if width % (steps * 128) == 0:
            return steps
    return 1


def hold_kernel(*refs):
    count = len(refs) // 2
    sources, targets, sems = refs[:count], refs[count:-1], refs[-1]
    copies = [
        pltpu.make_async_copy(source.at[:, cols], target.at[:, cols], sems.at[i, j])
        for i, (source, target) in enumerate(zip(sources, targets))
        for j, cols in enumerate(tiles(source.shape[1]))
    ]
    for copy in copies:
        copy.start()
    for copy in copies:
        copy.wait()


def hold(*arrays):
    return pl.pallas_call(
        hold_kernel,
        in_specs=[ANYWHERE] * len(arrays),
        out_specs=[VECTORS] * len(arrays),
        out_shape=[jax.ShapeDtypeStruct(array.shape, array.dtype) for array in arrays],
        scratch_shapes=[pltpu.SemaphoreType.DMA((len(arrays), steps_of(arrays[0].shape[1])))],
        compiler_params=params(HOLD_LIMIT),
        cost_estimate=cost(0, sum(4 * array.size for array in arrays)),
        name="hold",
    )(*arrays)


def tiles(width):
    count = steps_of(width)
    return [pl.ds(j * (width // count), width // count) for j in range(count)]


def gate_columns(core, ids, gates, rows, rank):
    total = rows // rank
    row = lax.broadcasted_iota(jnp.int32, (rows, ids.shape[1]), 0)
    adapter = (row // rank + core * (total // 2)) % total
    weight = jnp.zeros((rows, ids.shape[1]), F32)
    for k in range(ids.shape[0]):
        weight = weight + jnp.where(ids[k : k + 1, :] == adapter, gates[k : k + 1, :], 0.0)
    return weight


def store_products(where_ref, at, blocks, lows, outers, send_ref, keep_ref):
    wide = send_ref.shape[1] // blocks
    rows = send_ref.shape[0] // 2
    for j in range(blocks):
        cols = pl.ds(pl.multiple_of(where_ref[at + j] * wide, 128), wide)
        into = pl.ds(j * wide, wide)
        for i, (low, outer) in enumerate(zip(lows, outers)):
            product = jnp.dot(low, outer[:, cols], preferred_element_type=F32).astype(BF16)
            out = pl.ds(i * rows, rows)
            send_ref[out, into] = product[:rows]
            keep_ref[out, into] = product[rows:]


def low_kernel(rank, core_ref, where_ref, ids_ref, gates_ref, b_ref, b_in_ref, a_ref, a_in_ref, g_ref, x_ref,
               lg_ref, la_ref, send_ref, keep_ref):
    rows, width = b_ref.shape
    weight = gate_columns(1 - core_ref[0], ids_ref[...], gates_ref[...], 2 * rows, rank)
    lows = []
    for other, own, tokens, out in ((b_in_ref, b_ref, g_ref, lg_ref), (a_in_ref, a_ref, x_ref, la_ref)):
        sums = [jnp.zeros((rows, tokens.shape[0]), F32)] * 2
        for cols in tiles(width):
            for i, factor in enumerate((other, own)):
                sums[i] = sums[i] + lax.dot_general(
                    factor[:, cols], tokens[:, cols], NT, preferred_element_type=F32
                )
        lows.append((jnp.concatenate(sums, axis=0) * weight).astype(BF16))
        out[...] = lows[-1]
    store_products(where_ref, 0, 1, lows, (x_ref, g_ref), send_ref, keep_ref)


def low_products(core, where, ids, gates, rank, b, b_in, a, a_in, g, x, wide):
    rows, width = b.shape
    tokens = x.shape[0]
    return pl.pallas_call(
        functools.partial(low_kernel, rank),
        in_specs=[SCALARS] * 2 + [VECTORS] * 8,
        out_specs=[VECTORS] * 4,
        out_shape=[jax.ShapeDtypeStruct((2 * rows, tokens), BF16)] * 2
        + [jax.ShapeDtypeStruct((2 * rows, wide), BF16)] * 2,
        compiler_params=params(),
        cost_estimate=cost(8 * rows * tokens * (width + wide), 4 * (2 * rows + tokens) * width),
        name="low",
    )(core, where, ids, gates, b, b_in, a, a_in, g, x)


def rest_kernel(blocks, where_ref, lg_ref, la_ref, x_ref, g_ref, send_ref, keep_ref):
    lows = (lg_ref[...], la_ref[...])
    store_products(where_ref, 1, blocks, lows, (x_ref, g_ref), send_ref, keep_ref)


def rest_products(where, lg, la, x, g, blocks, wide):
    rows = lg.shape[0]
    return pl.pallas_call(
        functools.partial(rest_kernel, blocks),
        in_specs=[SCALARS] + [VECTORS] * 4,
        out_specs=[VECTORS] * 2,
        out_shape=[jax.ShapeDtypeStruct((rows, blocks * wide), BF16)] * 2,
        compiler_params=params(),
        cost_estimate=cost(4 * rows * x.shape[0] * blocks * wide, 8 * rows * blocks * wide),
        name="rest",
    )(where, lg, la, x, g)


def fold_kernel(block, at, where_ref, keep_ref, came_ref, after_ref, send_ref, own_ref):
    near = where_ref[where_ref.shape[0] - 1]
    for place, out in ((1 - near, send_ref), (near, own_ref)):
        cols = pl.ds(pl.multiple_of((2 * at + place) * block, 128), block)
        out[...] = (keep_ref[:, cols].astype(F32) + came_ref[:, cols].astype(F32)).astype(out.dtype)


def fold(where, block, at, keep, came, after):
    rows = keep.shape[0]
    return pl.pallas_call(
        functools.partial(fold_kernel, block, at),
        in_specs=[SCALARS] + [VECTORS] * 2 + [ANYWHERE],
        out_specs=[VECTORS] * 2,
        out_shape=[
            jax.ShapeDtypeStruct((rows, block), BF16),
            jax.ShapeDtypeStruct((rows, block), F32),
        ],
        compiler_params=params(),
        cost_estimate=cost(2 * rows * block, 14 * rows * block),
        name="fold",
    )(where, keep, came, after)


def add_kernel(keep_ref, came_ref, out_ref):
    out_ref[...] = (keep_ref[...] + came_ref[...].astype(F32)).astype(out_ref.dtype)


def add(keep, came):
    return pl.pallas_call(
        add_kernel,
        out_shape=jax.ShapeDtypeStruct(keep.shape, BF16),
        compiler_params=params(),
        cost_estimate=cost(keep.size, 8 * keep.size),
        name="add",
    )(keep, came)


def last_kernel(keep_ref, *refs):
    came, (down_ref, up_ref) = refs[:-2], refs[-2:]
    rows = down_ref.shape[0]
    for half, out in ((0, down_ref), (1, up_ref)):
        own = pl.ds(half * rows, rows)
        total = keep_ref[own, :]
        at = 0
        while at < len(came):
            whole = came[at].shape[0] > rows
            total = total + (came[at][own, :] if whole else came[at + half][...]).astype(F32)
            at += 1 if whole else 2
        out[...] = total


def last(keep, came):
    rows, block = keep.shape[0] // 2, keep.shape[1]
    return pl.pallas_call(
        last_kernel,
        in_specs=[VECTORS] * (1 + len(came)),
        out_specs=[VECTORS] * 2,
        out_shape=[jax.ShapeDtypeStruct((rows, block), F32)] * 2,
        compiler_params=params(),
        cost_estimate=cost(keep.size * len(came), keep.size * (8 + 2 * len(came))),
        name="last",
    )(keep, *came)


def input_kernel(low_ref, own_ref, other_ref, out_ref):
    tile = out_ref.shape[1]
    rows = own_ref.shape[0]
    cols = pl.ds(pl.multiple_of(pl.program_id(0) * tile, 128), tile)
    dot = functools.partial(lax.dot_general, dimension_numbers=TN, preferred_element_type=F32)
    out_ref[...] = (
        dot(low_ref[:rows], other_ref[:, cols]) + dot(low_ref[rows:], own_ref[:, cols])
    ).astype(BF16)


def input_gradient(low, own, other):
    tokens = low.shape[1]
    rows, width = own.shape
    steps = steps_of(width)
    tile = width // steps
    return pl.pallas_call(
        input_kernel,
        grid=(steps,),
        in_specs=[VECTORS] * 3,
        out_specs=pl.BlockSpec((tokens, tile), lambda s: (0, s)),
        out_shape=jax.ShapeDtypeStruct((tokens, width), BF16),
        compiler_params=params(),
        cost_estimate=cost(4 * rows * tokens * width, 2 * (2 * rows + tokens) * width),
        name="input",
    )(low, own, other)


def shards(x, g, ids, gates, down_w, up_w):
    tokens, width = x.shape
    count, rank, _ = down_w.shape
    rows = count * rank
    replicas = lax.axis_size("dp")
    block = width // replicas
    core = lax.axis_index("adapter").astype(jnp.int32).reshape(1)
    a = down_w.reshape(rows, width)
    b = up_w.reshape(rows, width)
    ids, gates = ids.T, gates.T
    swap = lambda array: lax.ppermute(array, "adapter", SWAP)
    b_in = swap(b)
    me = lax.axis_index("dp").astype(jnp.int32)
    far, near = me // 2, me % 2
    flip = lambda array, by: lax.ppermute(array, "dp", [(i, i ^ by) for i in range(replicas)])
    steps = replicas // 2
    if steps < 2 or replicas & (replicas - 1) or block % 128:
        return plain(core, ids, gates, rank, x, g, a, b, swap(a), b_in, swap)

    a_in = swap(a)
    g_held, x_held = hold(g, x)
    order = list(reversed(range(steps)))
    where = jnp.stack([far ^ step for step in order] + [near])
    lg, la, pair, keep = low_products(
        core, where, ids, gates, rank, b, b_in, a, a_in, g_held, x_held, 2 * block
    )
    rest_pair, rest_keep = rest_products(where, lg, la, x_held, g_held, steps - 1, 2 * block)
    terms = (keep, swap(pair)), (rest_keep, swap(rest_pair))
    came = []
    send = la
    for i, step in enumerate(order):
        send, own = fold(where, block, max(i - 1, 0), *terms[min(i, 1)], send)
        got = flip(send, 1)
        came.append(flip(add(own, got), 2 * step) if step else got)
    input_grad = input_gradient(lg, a, a_in)
    input_grad, came[-1] = lax.optimization_barrier((input_grad, came[-1]))
    down, up = last(own, came)
    return input_grad, down.reshape(count, rank, block), up.reshape(count, rank, block)


def plain(core, ids, gates, rank, x, g, a, b, a_in, b_in, swap):
    rows = a.shape[0]
    dot = functools.partial(lax.dot_general, preferred_element_type=F32)
    weight = gate_columns(core[0], ids, gates, 2 * rows, rank)
    both_a, both_b = jnp.concatenate([a, a_in]), jnp.concatenate([b, b_in])
    lg = (dot(both_b, g, NT) * weight).astype(BF16)
    la = (dot(both_a, x, NT) * weight).astype(BF16)
    input_grad = dot(lg, both_a, TN).astype(BF16)
    down = jnp.dot(lg, x, preferred_element_type=F32)
    up = jnp.dot(la, g, preferred_element_type=F32)
    own = jnp.concatenate([down[:rows], up[:rows]])
    other = jnp.concatenate([down[rows:], up[rows:]]).astype(BF16)
    total = lax.psum_scatter(
        own + swap(other).astype(F32), "dp", scatter_dimension=1, tiled=True
    ).reshape(2, rows // rank, rank, -1)
    return input_grad, total[0], total[1]


def solution(mesh):
    tok = P(("groups", "dp", "adapter"), None)
    return jax.shard_map(
        shards,
        mesh=mesh,
        in_specs=(tok, tok, tok, tok, P("adapter", None, None), P("adapter", None, None)),
        out_specs=(
            tok,
            P(("groups", "adapter"), None, "dp"),
            P(("groups", "adapter"), None, "dp"),
        ),
        check_vma=False,
    )
```

time: 65.8 us -> 50.8 us (0.77)
  matrix products: 22.7 us -> 0 us
  Pallas kernels: 0 us -> 15.4 us
  waiting for transfers between devices: 26.9 us -> 14.6 us
  local copies, waits for them, and re-layouts: 0.82 us -> 3.99 us
  starting transfers between devices: 13.1 us -> 15.8 us
  other arithmetic: 1.21 us -> 0 us
    dot_general x8 -> x0, matrix products: 22.7 us -> none  [the longest x4 14.5 us: outer(): lax.dot_general(left, right, (((0,), (0,)), ((), ())), preferred_element_...]
    pallas_call x0 -> x12, Pallas kernels: none -> 15.4 us  [the longest x1 4.32 us: low_products(): pl.pallas_call(functools.partial(low_kernel, rank), in_specs=[SCALARS] *...]
    ppermute x12 -> x11, waiting for transfers between devices: 26.9 us -> 14.6 us  [the longest x7 11.1 us: shards(): lax.ppermute(array, 'dp', [(i, i ^ by) for i in range(replicas)])]
    unnamed x4 -> x12, local copies, waits for them, and re-layouts: 0.02 us -> 3.91 us
    ppermute x12 -> x11, starting transfers between devices: 13.1 us -> 15.8 us  [the longest x7 14.6 us: shards(): lax.ppermute(array, 'dp', [(i, i ^ by) for i in range(replicas)])]
    slice x1 -> x0, local copies, waits for them, and re-layouts: 0.8 us -> none  [shards(): return (input_grad, both[0], both[1])]
    reduce_sum x1 -> x0, other arithmetic: 0.78 us -> none  [routed_weights(): jnp.sum(jnp.where(ids[:, :, None] == column, gates[:, :, None], 0.0), axi...]
  transfers between devices with their start and end apart: 12 -> 11, of which waited for: 6 -> 5; matrix products, arithmetic and copies ran while one was open for 36% -> 0% of each run, Pallas kernels for 0% -> 18%
where the time goes in v3:
time: 50.8 us; the launch traced here: 50.5 us
  starting transfers between devices  15.8 us (31%)
  Pallas kernels  15.4 us (30%)
  waiting for transfers between devices  14.6 us (29%)
  local copies, waits for them, and re-layouts  3.99 us (8%)
  between operations  0.72 us (1%)
    ppermute x7, starting transfers between devices, shards(): lax.ppermute(array, 'dp', [(i, i ^ by) for i in range(replicas)])  14.6 us
    ppermute x7, waiting for transfers between devices, shards(): lax.ppermute(array, 'dp', [(i, i ^ by) for i in range(replicas)])  11.1 us
    pallas_call x1, Pallas kernels, low_products(): pl.pallas_call(functools.partial(low_kernel, rank), in_specs=[SCALARS] *...  4.32 us
    pallas_call x1, Pallas kernels, input_gradient(): pl.pallas_call(input_kernel, grid=(steps,), in_specs=[VECTORS] * 3, out_s...  3.98 us
    unnamed x12, local copies, waits for them, and re-layouts  3.91 us
    ppermute x4, waiting for transfers between devices, shards(): swap = lambda array: lax.ppermute(array, 'adapter', SWAP)  3.48 us
    pallas_call x4, Pallas kernels, fold(): pl.pallas_call(functools.partial(fold_kernel, block, at), in_specs=[SCALA...  2.61 us
    pallas_call x1, Pallas kernels, hold(): pl.pallas_call(hold_kernel, in_specs=[ANYWHERE] * len(arrays), out_specs=...  2.14 us
  transfers between devices with their start and end apart: 11, of which 5 were waited for; matrix products, arithmetic and copies ran while one was open for 0% of the time, Pallas kernels for 18%

profile of v3, /device:TPU:0, one launch (start us, length us, event | category | flops | bytes accessed | tf_op | source)
XLA Modules:
  0.0 50.5 jit_solution(11658207636303565428)
XLA Ops:
  0.6 0.5 %collective-permute-start.1 = (bf16[64,7168]{1,0:T(8,128)(2,1)}, bf16[64,7168]{1,0:T(8,128)(2,1)}, u32[]{:S(2)}, u32[]{:S(2)}) collective-permute-start(bf16[64,7168]{1,0:T(8,128)(2,1)} %bitcast.12), channel_id=1, source_target_pairs={{0,1},{1,0},{2,3},{3,2},{4,5},{5,4},{6,7},{7,6},{8,9},{9,8},{10,11... | collective-permute-start | bytes 2752520 | tf_op jit(solution)/shard_map/ppermute | solution.py:243
  1.1 0.1 collective-permute-start
  1.2 0.0 copy-start.2
  1.2 0.0 copy-start.4
  1.2 0.0 copy-start.5
  1.2 2.1 %hold.1 = (bf16[128,7168]{1,0:T(8,128)(2,1)S(1)}, bf16[128,7168]{1,0:T(8,128)(2,1)S(1)}) custom-call(bf16[128,7168]{1,0:T(8,128)(2,1)} %refs_0_.1, bf16[128,7168]{1,0:T(8,128)(2,1)} %refs_1_.1), custom_call_target="tpu_custom_call" | custom-call | bytes 7340032 | tf_op jit(solution)/shard_map/hold/pallas_call | solution.py:52
  3.4 0.0 copy-start
  3.4 1.2 %copy-done = bf16[128,7168]{1,0:T(8,128)(2,1)} copy-done((bf16[128,7168]{1,0:T(8,128)(2,1)}, bf16[128,7168]{1,0:T(8,128)(2,1)S(1)}, u32[]{:S(2)}) %copy-start) | copy-done | bytes 1835032
  4.6 0.1 stack.23.where_ref
  4.7 0.0 collective-permute-done.1.a_in_ref.other_ref
  4.7 0.2 collective-permute-done.b_in_ref
  4.9 0.0 copy-done.2
  4.9 0.0 copy-done.4
  4.9 0.0 copy-done.5
  4.9 0.0 copy-start.1
  4.9 1.5 %copy-done.1 = bf16[128,7168]{1,0:T(8,128)(2,1)S(1)} copy-done((bf16[128,7168]{1,0:T(8,128)(2,1)S(1)}, bf16[128,7168]{1,0:T(8,128)(2,1)}, u32[]{:S(2)}) %copy-start.1) | copy-done | bytes 1835032
  6.4 0.0 copy-start.3
  6.4 1.2 %copy-done.3 = bf16[4,16,7168]{2,1,0:T(8,128)(2,1)S(1)} copy-done((bf16[4,16,7168]{2,1,0:T(8,128)(2,1)S(1)}, bf16[4,16,7168]{2,1,0:T(8,128)(2,1)}, u32[]{:S(2)}) %copy-start.3) | copy-done | bytes 917528
  7.6 4.3 %low.1 = (bf16[128,128]{1,0:T(8,128)(2,1)S(1)}, bf16[128,128]{1,0:T(8,128)(2,1)S(1)}, bf16[128,1792]{1,0:T(8,128)(2,1)S(1)}, bf16[128,1792]{1,0:T(8,128)(2,1)S(1)}) custom-call(s32[1]{0:T(128)} %bitcast.core_ref, s32[5]{0:T(128)S(1)} %stack.23.where_ref, s32[2,128]{1,0:T(2,128)S(1)} %bitcast.17, f32[2,128]{1,0:T(2,128)S(1)} %bitcast.18, ...), custom_call_target="tpu_custom_call" | custom-call | flops 587202560 | bytes 7340032 | tf_op jit(solution)/shard_map/low/pallas_call | solution.py:112
  11.9 1.4 %rest.1 = (bf16[128,5376]{1,0:T(8,128)(2,1)S(1)}, bf16[128,5376]{1,0:T(8,128)(2,1)S(1)}) custom-call(s32[5]{0:T(128)S(1)} %stack.23.where_ref, bf16[128,128]{1,0:T(8,128)(2,1)S(1)} %get-tuple-element.25.low_ref.lg_ref, bf16[128,128]{1,0:T(8,128)(2,1)S(1)} %get-tuple-element.26.la_ref.after_ref, bf16[128,7168]{1,0:T(8,128)(2,1)S(1)} %copy-done.1, ...), custom_call_target="tpu_custom_call" | custom-call | flops 352321536 | bytes 5505024 | tf_op jit(solution)/shard_map/rest/pallas_call | solution.py:131
  13.3 0.4 collective-permute-start.2
  13.8 0.1 collective-permute-start.3
  13.9 3.3 %collective-permute-done.3.came_ref = bf16[128,1792]{1,0:T(8,128)(2,1)S(1)} collective-permute-done((bf16[128,1792]{1,0:T(8,128)(2,1)S(1)}, bf16[128,1792]{1,0:T(8,128)(2,1)S(1)}, u32[]{:S(2)}, u32[]{:S(2)}) %collective-permute-start.3) | collective-permute-done | bytes 458784 | tf_op jit(solution)/shard_map/ppermute | solution.py:243
  17.2 0.7 %fold.4 = (bf16[128,896]{1,0:T(8,128)(2,1)S(1)}, f32[128,896]{1,0:T(8,128)S(1)}) custom-call(s32[5]{0:T(128)S(1)} %stack.23.where_ref, bf16[128,1792]{1,0:T(8,128)(2,1)S(1)} %get-tuple-element.29.keep_ref, bf16[128,1792]{1,0:T(8,128)(2,1)S(1)} %collective-permute-done.3.came_ref, bf16[128,128]{1,0:T(8,128)(2,1)S(1)} %get-tuple-element.26.la_ref.after_ref), custom_call_target="tpu_custom_call" | custom-call | flops 229376 | bytes 1605632 | tf_op jit(solution)/shard_map/fold/pallas_call | solution.py:151
  17.9 3.0 %collective-permute-start.5 = (bf16[128,896]{1,0:T(8,128)(2,1)S(1)}, bf16[128,896]{1,0:T(8,128)(2,1)S(1)}, u32[]{:S(2)}, u32[]{:S(2)}) collective-permute-start(bf16[128,896]{1,0:T(8,128)(2,1)S(1)} %get-tuple-element.31.after_ref), channel_id=1, source_target_pairs={{0,2},{2,0},{4,6},{6,4},{8,10},{10,8},{12,14},{14,12},{1,3},{3,1},... | collective-permute-start | bytes 688136 | tf_op jit(solution)/shard_map/ppermute | solution.py:247
  20.8 0.0 collective-permute-done.2.came_ref
  20.8 0.6 %fold.5 = (bf16[128,896]{1,0:T(8,128)(2,1)S(1)}, f32[128,896]{1,0:T(8,128)S(1)}) custom-call(s32[5]{0:T(128)S(1)} %stack.23.where_ref, bf16[128,5376]{1,0:T(8,128)(2,1)S(1)} %get-tuple-element.27.keep_ref, bf16[128,5376]{1,0:T(8,128)(2,1)S(1)} %collective-permute-done.2.came_ref, bf16[128,896]{1,0:T(8,128)(2,1)S(1)} %get-tuple-element.31.after_ref), custom_call_target="tpu_custom_call" | custom-call | flops 229376 | bytes 1605632 | tf_op jit(solution)/shard_map/fold/pallas_call | solution.py:151
  21.5 0.6 %fold.6 = (bf16[128,896]{1,0:T(8,128)(2,1)S(1)}, f32[128,896]{1,0:T(8,128)S(1)}) custom-call(s32[5]{0:T(128)S(1)} %stack.23.where_ref, bf16[128,5376]{1,0:T(8,128)(2,1)S(1)} %get-tuple-element.27.keep_ref, bf16[128,5376]{1,0:T(8,128)(2,1)S(1)} %collective-permute-done.2.came_ref, bf16[128,896]{1,0:T(8,128)(2,1)S(1)} %get-tuple-element.32.after_ref), custom_call_target="tpu_custom_call" | custom-call | flops 229376 | bytes 1605632 | tf_op jit(solution)/shard_map/fold/pallas_call | solution.py:151
  22.1 0.1 collective-permute-start.9
  22.2 2.0 %collective-permute-start.7 = (bf16[128,896]{1,0:T(8,128)(2,1)S(1)}, bf16[128,896]{1,0:T(8,128)(2,1)S(1)}, u32[]{:S(2)}, u32[]{:S(2)}) collective-permute-start(bf16[128,896]{1,0:T(8,128)(2,1)S(1)} %get-tuple-element.32.after_ref), channel_id=1, source_target_pairs={{0,2},{2,0},{4,6},{6,4},{8,10},{10,8},{12,14},{14,12},{1,3},{3,1},... | collective-permute-start | bytes 688136 | tf_op jit(solution)/shard_map/ppermute | solution.py:247
  24.2 3.0 %collective-permute-done.5.came_ref = bf16[128,896]{1,0:T(8,128)(2,1)S(1)} collective-permute-done((bf16[128,896]{1,0:T(8,128)(2,1)S(1)}, bf16[128,896]{1,0:T(8,128)(2,1)S(1)}, u32[]{:S(2)}, u32[]{:S(2)}) %collective-permute-start.5) | collective-permute-done | bytes 229408 | tf_op jit(solution)/shard_map/ppermute | solution.py:247
  27.2 0.1 add.9
  27.3 4.2 %collective-permute-start.6 = (bf16[128,896]{1,0:T(8,128)(2,1)S(1)}, bf16[128,896]{1,0:T(8,128)(2,1)S(1)}, u32[]{:S(2)}, u32[]{:S(2)}) collective-permute-start(bf16[128,896]{1,0:T(8,128)(2,1)S(1)} %add.9), channel_id=1, source_target_pairs={{0,12},{2,14},{4,8},{6,10},{8,4},{10,6},{12,0},{14,2},{1,13},{3,15... | collective-permute-start | bytes 688136 | tf_op jit(solution)/shard_map/ppermute | solution.py:247
  31.5 0.6 %fold.7 = (bf16[128,896]{1,0:T(8,128)(2,1)S(1)}, f32[128,896]{1,0:T(8,128)S(1)}) custom-call(s32[5]{0:T(128)S(1)} %stack.23.where_ref, bf16[128,5376]{1,0:T(8,128)(2,1)S(1)} %get-tuple-element.27.keep_ref, bf16[128,5376]{1,0:T(8,128)(2,1)S(1)} %collective-permute-done.2.came_ref, bf16[128,896]{1,0:T(8,128)(2,1)S(1)} %get-tuple-element.33.after_ref), custom_call_target="tpu_custom_call" | custom-call | flops 229376 | bytes 1605632 | tf_op jit(solution)/shard_map/fold/pallas_call | solution.py:151
  32.1 1.6 %collective-permute-start.4 = (bf16[128,896]{1,0:T(8,128)(2,1)S(1)}, bf16[128,896]{1,0:T(8,128)(2,1)S(1)}, u32[]{:S(2)}, u32[]{:S(2)}) collective-permute-start(bf16[128,896]{1,0:T(8,128)(2,1)S(1)} %get-tuple-element.34), channel_id=1, source_target_pairs={{0,2},{2,0},{4,6},{6,4},{8,10},{10,8},{12,14},{14,12},{1,3},{3,1},... | collective-permute-start | bytes 688136 | tf_op jit(solution)/shard_map/ppermute | solution.py:247
  33.7 0.0 collective-permute-done.9.came_ref
  33.8 0.6 %collective-permute-start.10 = (bf16[128,896]{1,0:T(8,128)(2,1)S(1)}, bf16[128,896]{1,0:T(8,128)(2,1)S(1)}, u32[]{:S(2)}, u32[]{:S(2)}) collective-permute-start(bf16[128,896]{1,0:T(8,128)(2,1)S(1)} %add.11), channel_id=1, source_target_pairs={{0,4},{2,6},{4,0},{6,2},{8,12},{10,14},{12,8},{14,10},{1,5},{3,7},... | collective-permute-start | bytes 688136 | tf_op jit(solution)/shard_map/ppermute | solution.py:247
  34.3 2.7 %collective-permute-done.7.came_ref = bf16[128,896]{1,0:T(8,128)(2,1)S(1)} collective-permute-done((bf16[128,896]{1,0:T(8,128)(2,1)S(1)}, bf16[128,896]{1,0:T(8,128)(2,1)S(1)}, u32[]{:S(2)}, u32[]{:S(2)}) %collective-permute-start.7) | collective-permute-done | bytes 229408 | tf_op jit(solution)/shard_map/ppermute | solution.py:247
  37.1 3.2 %collective-permute-start.8 = (bf16[128,896]{1,0:T(8,128)(2,1)S(1)}, bf16[128,896]{1,0:T(8,128)(2,1)S(1)}, u32[]{:S(2)}, u32[]{:S(2)}) collective-permute-start(bf16[128,896]{1,0:T(8,128)(2,1)S(1)} %add.10), channel_id=1, source_target_pairs={{0,8},{2,10},{4,12},{6,14},{8,0},{10,2},{12,4},{14,6},{1,9},{3,11}... | collective-permute-start | bytes 688136 | tf_op jit(solution)/shard_map/ppermute | solution.py:247
  40.3 4.0 %input.1 = bf16[128,7168]{1,0:T(8,128)(2,1)} custom-call(bf16[128,128]{1,0:T(8,128)(2,1)S(1)} %get-tuple-element.25.low_ref.lg_ref, bf16[64,7168]{1,0:T(8,128)(2,1)S(1)} %bitcast.14, bf16[64,7168]{1,0:T(8,128)(2,1)} %collective-permute-done.1.a_in_ref.other_ref), custom_call_target="tpu_custom_call" | custom-call | flops 234881024 | bytes 3670016 | tf_op jit(solution)/shard_map/input/pallas_call | solution.py:221
  44.3 0.0 collective-permute-done.4.refs_3_
  44.3 0.0 collective-permute-done.6.refs_0_
  44.3 0.0 collective-permute-done.10.refs_2_
  44.3 5.4 %collective-permute-done.8.refs_1_ = bf16[128,896]{1,0:T(8,128)(2,1)S(1)} collective-permute-done((bf16[128,896]{1,0:T(8,128)(2,1)S(1)}, bf16[128,896]{1,0:T(8,128)(2,1)S(1)}, u32[]{:S(2)}, u32[]{:S(2)}) %collective-permute-start.8) | collective-permute-done | bytes 229408 | tf_op jit(solution)/shard_map/ppermute | solution.py:247
  49.7 0.8 %last.1 = (f32[64,896]{1,0:T(8,128)}, f32[64,896]{1,0:T(8,128)}) custom-call(f32[128,896]{1,0:T(8,128)S(1)} %get-tuple-element.36.keep_ref, bf16[128,896]{1,0:T(8,128)(2,1)S(1)} %collective-permute-done.6.refs_0_, bf16[128,896]{1,0:T(8,128)(2,1)S(1)} %collective-permute-done.8.refs_1_, bf16[128,896]{1,0:T(8,128)(2,1)S(1)} %collective-permute-done.10.refs_2_, ...), custom_call_target="tpu_custom_call" | custom-call | flops 458752 | bytes 1835008 | tf_op jit(solution)/shard_map/last/pallas_call | solution.py:195
  (2 shorter events, 0.1 us)
Async XLA Ops:
  0.6 4.1 %collective-permute-start.1 = (bf16[64,7168]{1,0:T(8,128)(2,1)}, bf16[64,7168]{1,0:T(8,128)(2,1)}, u32[]{:S(2)}, u32[]{:S(2)}) collective-permute-start(bf16[64,7168]{1,0:T(8,128)(2,1)} %bitcast.12), channel_id=1, source_target_pairs={{0,1},{1,0},{2,3},{3,2},{4,5},{5,4},{6,7},{7,6},{8,9},{9,8},{10,11... | collective-permute-start | bytes 2752520 | tf_op jit(solution)/shard_map/ppermute | solution.py:243
  1.1 3.8 %collective-permute-start = (bf16[64,7168]{1,0:T(8,128)(2,1)}, bf16[64,7168]{1,0:T(8,128)(2,1)}, u32[]{:S(2)}, u32[]{:S(2)}) collective-permute-start(bf16[64,7168]{1,0:T(8,128)(2,1)} %bitcast.15), channel_id=1, source_target_pairs={{0,1},{1,0},{2,3},{3,2},{4,5},{5,4},{6,7},{7,6},{8,9},{9,8},{10,11... | collective-permute-start | bytes 2752520 | tf_op jit(solution)/shard_map/ppermute | solution.py:243
  1.2 3.7 %copy-start.2 = (bf16[4,16,7168]{2,1,0:T(8,128)(2,1)S(1)}, bf16[4,16,7168]{2,1,0:T(8,128)(2,1)}, u32[]{:S(2)}) copy-start(bf16[4,16,7168]{2,1,0:T(8,128)(2,1)} %param.10) | copy-start | bytes 2752516
  1.2 3.7 %copy-start.4 = (s32[128,2]{0,1:T(2,128)S(1)}, s32[128,2]{0,1:T(2,128)}, u32[]{:S(2)}) copy-start(s32[128,2]{0,1:T(2,128)} %param.8) | copy-start | bytes 3076
  1.2 3.7 %copy-start.5 = (f32[128,2]{0,1:T(2,128)S(1)}, f32[128,2]{0,1:T(2,128)}, u32[]{:S(2)}) copy-start(f32[128,2]{0,1:T(2,128)} %param.9) | copy-start | bytes 3076
  3.4 1.2 %copy-start = (bf16[128,7168]{1,0:T(8,128)(2,1)}, bf16[128,7168]{1,0:T(8,128)(2,1)S(1)}, u32[]{:S(2)}) copy-start(bf16[128,7168]{1,0:T(8,128)(2,1)S(1)} %get-tuple-element.24.x_ref) | copy-start | bytes 5505028
  4.9 1.5 %copy-start.1 = (bf16[128,7168]{1,0:T(8,128)(2,1)S(1)}, bf16[128,7168]{1,0:T(8,128)(2,1)}, u32[]{:S(2)}) copy-start(bf16[128,7168]{1,0:T(8,128)(2,1)} %copy-done) | copy-start | bytes 5505028
  6.4 1.2 %copy-start.3 = (bf16[4,16,7168]{2,1,0:T(8,128)(2,1)S(1)}, bf16[4,16,7168]{2,1,0:T(8,128)(2,1)}, u32[]{:S(2)}) copy-start(bf16[4,16,7168]{2,1,0:T(8,128)(2,1)} %param.11) | copy-start | bytes 2752516
  13.3 7.5 %collective-permute-start.2 = (bf16[128,5376]{1,0:T(8,128)(2,1)S(1)}, bf16[128,5376]{1,0:T(8,128)(2,1)S(1)}, u32[]{:S(2)}, u32[]{:S(2)}) collective-permute-start(bf16[128,5376]{1,0:T(8,128)(2,1)S(1)} %get-tuple-element.28), channel_id=1, source_target_pairs={{0,1},{1,0},{2,3},{3,2},{4,5},{5,4},{6,7},{7,6},{8,9},{9,8},{10,11... | collective-permute-start | bytes 4128776 | tf_op jit(solution)/shard_map/ppermute | solution.py:243
  13.8 3.4 %collective-permute-start.3 = (bf16[128,1792]{1,0:T(8,128)(2,1)S(1)}, bf16[128,1792]{1,0:T(8,128)(2,1)S(1)}, u32[]{:S(2)}, u32[]{:S(2)}) collective-permute-start(bf16[128,1792]{1,0:T(8,128)(2,1)S(1)} %get-tuple-element.30), channel_id=1, source_target_pairs={{0,1},{1,0},{2,3},{3,2},{4,5},{5,4},{6,7},{7,6},{8,9},{9,8},{10,11... | collective-permute-start | bytes 1376264 | tf_op jit(solution)/shard_map/ppermute | solution.py:243
  17.9 9.3 %collective-permute-start.5 = (bf16[128,896]{1,0:T(8,128)(2,1)S(1)}, bf16[128,896]{1,0:T(8,128)(2,1)S(1)}, u32[]{:S(2)}, u32[]{:S(2)}) collective-permute-start(bf16[128,896]{1,0:T(8,128)(2,1)S(1)} %get-tuple-element.31.after_ref), channel_id=1, source_target_pairs={{0,2},{2,0},{4,6},{6,4},{8,10},{10,8},{12,14},{14,12},{1,3},{3,1},... | collective-permute-start | bytes 688136 | tf_op jit(solution)/shard_map/ppermute | solution.py:247
  22.1 11.6 %collective-permute-start.9 = (bf16[128,896]{1,0:T(8,128)(2,1)S(1)}, bf16[128,896]{1,0:T(8,128)(2,1)S(1)}, u32[]{:S(2)}, u32[]{:S(2)}) collective-permute-start(bf16[128,896]{1,0:T(8,128)(2,1)S(1)} %get-tuple-element.33.after_ref), channel_id=1, source_target_pairs={{0,2},{2,0},{4,6},{6,4},{8,10},{10,8},{12,14},{14,12},{1,3},{3,1},... | collective-permute-start | bytes 688136 | tf_op jit(solution)/shard_map/ppermute | solution.py:247
  22.2 14.8 %collective-permute-start.7 = (bf16[128,896]{1,0:T(8,128)(2,1)S(1)}, bf16[128,896]{1,0:T(8,128)(2,1)S(1)}, u32[]{:S(2)}, u32[]{:S(2)}) collective-permute-start(bf16[128,896]{1,0:T(8,128)(2,1)S(1)} %get-tuple-element.32.after_ref), channel_id=1, source_target_pairs={{0,2},{2,0},{4,6},{6,4},{8,10},{10,8},{12,14},{14,12},{1,3},{3,1},... | collective-permute-start | bytes 688136 | tf_op jit(solution)/shard_map/ppermute | solution.py:247
  27.3 17.0 %collective-permute-start.6 = (bf16[128,896]{1,0:T(8,128)(2,1)S(1)}, bf16[128,896]{1,0:T(8,128)(2,1)S(1)}, u32[]{:S(2)}, u32[]{:S(2)}) collective-permute-start(bf16[128,896]{1,0:T(8,128)(2,1)S(1)} %add.9), channel_id=1, source_target_pairs={{0,12},{2,14},{4,8},{6,10},{8,4},{10,6},{12,0},{14,2},{1,13},{3,15... | collective-permute-start | bytes 688136 | tf_op jit(solution)/shard_map/ppermute | solution.py:247
  32.1 12.1 %collective-permute-start.4 = (bf16[128,896]{1,0:T(8,128)(2,1)S(1)}, bf16[128,896]{1,0:T(8,128)(2,1)S(1)}, u32[]{:S(2)}, u32[]{:S(2)}) collective-permute-start(bf16[128,896]{1,0:T(8,128)(2,1)S(1)} %get-tuple-element.34), channel_id=1, source_target_pairs={{0,2},{2,0},{4,6},{6,4},{8,10},{10,8},{12,14},{14,12},{1,3},{3,1},... | collective-permute-start | bytes 688136 | tf_op jit(solution)/shard_map/ppermute | solution.py:247
  33.8 10.5 %collective-permute-start.10 = (bf16[128,896]{1,0:T(8,128)(2,1)S(1)}, bf16[128,896]{1,0:T(8,128)(2,1)S(1)}, u32[]{:S(2)}, u32[]{:S(2)}) collective-permute-start(bf16[128,896]{1,0:T(8,128)(2,1)S(1)} %add.11), channel_id=1, source_target_pairs={{0,4},{2,6},{4,0},{6,2},{8,12},{10,14},{12,8},{14,10},{1,5},{3,7},... | collective-permute-start | bytes 688136 | tf_op jit(solution)/shard_map/ppermute | solution.py:247
  37.1 12.6 %collective-permute-start.8 = (bf16[128,896]{1,0:T(8,128)(2,1)S(1)}, bf16[128,896]{1,0:T(8,128)(2,1)S(1)}, u32[]{:S(2)}, u32[]{:S(2)}) collective-permute-start(bf16[128,896]{1,0:T(8,128)(2,1)S(1)} %add.10), channel_id=1, source_target_pairs={{0,8},{2,10},{4,12},{6,14},{8,0},{10,2},{12,4},{14,6},{1,9},{3,11}... | collective-permute-start | bytes 688136 | tf_op jit(solution)/shard_map/ppermute | solution.py:247

commit v4 on v3

--- a/solution.py
+++ b/solution.py
@@ -11,7 +11,7 @@
 F32 = jnp.float32
 SWAP = [(0, 1), (1, 0)]
 VMEM_LIMIT = 12 * 1024 * 1024
-HOLD_LIMIT = 50 * 1024 * 1024
+OWN_LIMIT = 48 * 1024 * 1024
 VECTORS = pl.BlockSpec(memory_space=pltpu.VMEM)
 ANYWHERE = pl.BlockSpec(memory_space=pl.ANY)
 SCALARS = pl.BlockSpec(memory_space=pltpu.SMEM)
@@ -34,31 +34,46 @@
     return 1
 
 
-def hold_kernel(*refs):
-    count = len(refs) // 2
-    sources, targets, sems = refs[:count], refs[count:-1], refs[-1]
+def own_kernel(b_hbm, g_hbm, a_hbm, x_hbm, grad_ref, act_ref, g_ref, x_ref, b, a, sems):
+    width = g_ref.shape[1]
+    halves = ((b_hbm, b, g_hbm, g_ref, grad_ref), (a_hbm, a, x_hbm, x_ref, act_ref))
     copies = [
-        pltpu.make_async_copy(source.at[:, cols], target.at[:, cols], sems.at[i, j])
-        for i, (source, target) in enumerate(zip(sources, targets))
-        for j, cols in enumerate(tiles(source.shape[1]))
+        [
+            pltpu.make_async_copy(source.at[:, cols], target.at[:, cols], sems.at[half, i, j])
+            for i, (source, target) in enumerate((refs[:2], refs[2:4]))
+        ]
+        for half, refs in enumerate(halves)
+        for j, cols in enumerate(tiles(width))
     ]
-    for copy in copies:
-        copy.start()
-    for copy in copies:
-        copy.wait()
-
-
-def hold(*arrays):
-    return pl.pallas_call(
-        hold_kernel,
-        in_specs=[ANYWHERE] * len(arrays),
-        out_specs=[VECTORS] * len(arrays),
-        out_shape=[jax.ShapeDtypeStruct(array.shape, array.dtype) for array in arrays],
-        scratch_shapes=[pltpu.SemaphoreType.DMA((len(arrays), steps_of(arrays[0].shape[1])))],
-        compiler_params=params(HOLD_LIMIT),
-        cost_estimate=cost(0, sum(4 * array.size for array in arrays)),
-        name="hold",
-    )(*arrays)
+    for pair in copies:
+        for copy in pair:
+            copy.start()
+    for half, (_, factor, _, tokens, out) in enumerate(halves):
+        total = jnp.zeros(out.shape, F32)
+        for j, cols in enumerate(tiles(width)):
+            for copy in copies[half * len(tiles(width)) + j]:
+                copy.wait()
+            total = total + lax.dot_general(
+                factor[:, cols], tokens[:, cols], NT, preferred_element_type=F32
+            )
+        out[...] = total
+
+
+def own_products(b, g, a, x):
+    rows, width = b.shape
+    tokens = x.shape[0]
+    return pl.pallas_call(
+        own_kernel,
+        in_specs=[ANYWHERE] * 4,
+        out_specs=[VECTORS] * 4,
+        out_shape=[jax.ShapeDtypeStruct((rows, tokens), F32)] * 2
+        + [jax.ShapeDtypeStruct((tokens, width), BF16)] * 2,
+        scratch_shapes=[pltpu.VMEM(b.shape, BF16)] * 2
+        + [pltpu.SemaphoreType.DMA((2, 2, steps_of(width)))],
+        compiler_params=params(OWN_LIMIT),
+        cost_estimate=cost(4 * rows * tokens * width, 4 * (rows + tokens) * width),
+        name="own",
+    )(b, g, a, x)
 
 
 def tiles(width):
@@ -89,25 +104,24 @@
             keep_ref[out, into] = product[rows:]
 
 
-def low_kernel(rank, core_ref, where_ref, ids_ref, gates_ref, b_ref, b_in_ref, a_ref, a_in_ref, g_ref, x_ref,
+def low_kernel(rank, core_ref, where_ref, ids_ref, gates_ref, grad_ref, act_ref, b_ref, a_ref, g_ref, x_ref,
                lg_ref, la_ref, send_ref, keep_ref):
     rows, width = b_ref.shape
     weight = gate_columns(1 - core_ref[0], ids_ref[...], gates_ref[...], 2 * rows, rank)
     lows = []
-    for other, own, tokens, out in ((b_in_ref, b_ref, g_ref, lg_ref), (a_in_ref, a_ref, x_ref, la_ref)):
-        sums = [jnp.zeros((rows, tokens.shape[0]), F32)] * 2
+    for own, factor, tokens, out in ((grad_ref, b_ref, g_ref, lg_ref), (act_ref, a_ref, x_ref, la_ref)):
+        total = jnp.zeros(own.shape, F32)
         for cols in tiles(width):
-            for i, factor in enumerate((other, own)):
-                sums[i] = sums[i] + lax.dot_general(
-                    factor[:, cols], tokens[:, cols], NT, preferred_element_type=F32
-                )
-        lows.append((jnp.concatenate(sums, axis=0) * weight).astype(BF16))
+            total = total + lax.dot_general(
+                factor[:, cols], tokens[:, cols], NT, preferred_element_type=F32
+            )
+        lows.append((jnp.concatenate([total, own[...]], axis=0) * weight).astype(BF16))
         out[...] = lows[-1]
     store_products(where_ref, 0, 1, lows, (x_ref, g_ref), send_ref, keep_ref)
 
 
-def low_products(core, where, ids, gates, rank, b, b_in, a, a_in, g, x, wide):
-    rows, width = b.shape
+def low_products(core, where, ids, gates, rank, grad, act, b_in, a_in, g, x, wide):
+    rows, width = b_in.shape
     tokens = x.shape[0]
     return pl.pallas_call(
         functools.partial(low_kernel, rank),
@@ -116,41 +130,56 @@
         out_shape=[jax.ShapeDtypeStruct((2 * rows, tokens), BF16)] * 2
         + [jax.ShapeDtypeStruct((2 * rows, wide), BF16)] * 2,
         compiler_params=params(),
-        cost_estimate=cost(8 * rows * tokens * (width + wide), 4 * (2 * rows + tokens) * width),
+        cost_estimate=cost(4 * rows * tokens * (width + 2 * wide), 4 * (rows + tokens) * width),
         name="low",
-    )(core, where, ids, gates, b, b_in, a, a_in, g, x)
-
-
-def rest_kernel(blocks, where_ref, lg_ref, la_ref, x_ref, g_ref, send_ref, keep_ref):
+    )(core, where, ids, gates, grad, act, b_in, a_in, g, x)
+
+
+def rest_kernel(blocks, block, where_ref, kept_ref, came_ref, lg_ref, la_ref, x_ref, g_ref, *outs):
+    send_ref, keep_ref, outs = outs[0], outs[1], outs[2:]
+    near = where_ref[blocks + 1]
+    rows = kept_ref.shape[0] * 2 // len(outs)
+    for i in range(len(outs) // 2):
+        part = pl.ds(i * rows, rows)
+        for place, out in ((1 - near, outs[2 * i]), (near, outs[2 * i + 1])):
+            cols = pl.ds(pl.multiple_of(place * block, 128), block)
+            total = kept_ref[part, cols].astype(F32) + came_ref[part, cols].astype(F32)
+            out[...] = total.astype(out.dtype)
     lows = (lg_ref[...], la_ref[...])
     store_products(where_ref, 1, blocks, lows, (x_ref, g_ref), send_ref, keep_ref)
 
 
-def rest_products(where, lg, la, x, g, blocks, wide):
+def rest_products(where, kept, came, lg, la, x, g, blocks, block, parts):
     rows = lg.shape[0]
-    return pl.pallas_call(
-        functools.partial(rest_kernel, blocks),
-        in_specs=[SCALARS] + [VECTORS] * 4,
-        out_specs=[VECTORS] * 2,
-        out_shape=[jax.ShapeDtypeStruct((rows, blocks * wide), BF16)] * 2,
-        compiler_params=params(),
-        cost_estimate=cost(4 * rows * x.shape[0] * blocks * wide, 8 * rows * blocks * wide),
+    wide = 2 * blocks * block
+    return pl.pallas_call(
+        functools.partial(rest_kernel, blocks, block),
+        in_specs=[SCALARS] + [VECTORS] * 6,
+        out_specs=[VECTORS] * (2 + 2 * parts),
+        out_shape=[jax.ShapeDtypeStruct((rows, wide), BF16)] * 2
+        + [
+            jax.ShapeDtypeStruct((rows // parts, block), BF16),
+            jax.ShapeDtypeStruct((rows // parts, block), F32),
+        ]
+        * parts,
+        compiler_params=params(),
+        cost_estimate=cost(2 * rows * x.shape[0] * wide, 4 * rows * wide),
         name="rest",
-    )(where, lg, la, x, g)
-
-
-def fold_kernel(block, at, where_ref, keep_ref, came_ref, after_ref, send_ref, own_ref):
+    )(where, kept, came, lg, la, x, g)
+
+
+def fold_kernel(block, at, where_ref, keep_ref, came_ref, send_ref, own_ref):
     near = where_ref[where_ref.shape[0] - 1]
     for place, out in ((1 - near, send_ref), (near, own_ref)):
         cols = pl.ds(pl.multiple_of((2 * at + place) * block, 128), block)
         out[...] = (keep_ref[:, cols].astype(F32) + came_ref[:, cols].astype(F32)).astype(out.dtype)
 
 
-def fold(where, block, at, keep, came, after):
+def fold(where, block, at, keep, came):
     rows = keep.shape[0]
     return pl.pallas_call(
         functools.partial(fold_kernel, block, at),
-        in_specs=[SCALARS] + [VECTORS] * 2 + [ANYWHERE],
+        in_specs=[SCALARS] + [VECTORS] * 2,
         out_specs=[VECTORS] * 2,
         out_shape=[
             jax.ShapeDtypeStruct((rows, block), BF16),
@@ -159,7 +188,7 @@
         compiler_params=params(),
         cost_estimate=cost(2 * rows * block, 14 * rows * block),
         name="fold",
-    )(where, keep, came, after)
+    )(where, keep, came)
 
 
 def add_kernel(keep_ref, came_ref, out_ref):
@@ -250,18 +279,21 @@
         return plain(core, ids, gates, rank, x, g, a, b, swap(a), b_in, swap)
 
     a_in = swap(a)
-    g_held, x_held = hold(g, x)
+    grad, act, g_held, x_held = own_products(b, g, a, x)
     order = list(reversed(range(steps)))
     where = jnp.stack([far ^ step for step in order] + [near])
     lg, la, pair, keep = low_products(
-        core, where, ids, gates, rank, b, b_in, a, a_in, g_held, x_held, 2 * block
+        core, where, ids, gates, rank, grad, act, b_in, a_in, g_held, x_held, 2 * block
     )
-    rest_pair, rest_keep = rest_products(where, lg, la, x_held, g_held, steps - 1, 2 * block)
-    terms = (keep, swap(pair)), (rest_keep, swap(rest_pair))
-    came = []
-    send = la
-    for i, step in enumerate(order):
-        send, own = fold(where, block, max(i - 1, 0), *terms[min(i, 1)], send)
+    rest_pair, rest_keep, *first = rest_products(
+        where, keep, swap(pair), lg, la, x_held, g_held, steps - 1, block, 1
+    )
+    rest_came = swap(rest_pair)
+    came = [
+        flip(add(own, flip(send, 1)), 2 * order[0]) for send, own in zip(first[::2], first[1::2])
+    ]
+    for i, step in enumerate(order[1:]):
+        send, own = fold(where, block, i, rest_keep, rest_came)
         got = flip(send, 1)
         came.append(flip(add(own, got), 2 * step) if step else got)
     input_grad = input_gradient(lg, a, a_in)

time: 50.8 us -> 46.6 us (0.917)
  Pallas kernels: 15.4 us -> 13.2 us
  local copies, waits for them, and re-layouts: 3.99 us -> 2.45 us
  waiting for transfers between devices: 14.6 us -> 13.4 us
  starting transfers between devices: 15.8 us -> 16.6 us
    pallas_call x1, Pallas kernels: 4.32 us -> 2.28 us  [low_products(): pl.pallas_call(functools.partial(low_kernel, rank), in_specs=[SCALARS] *...]
    ppermute x4, waiting for transfers between devices: 3.48 us -> 1.54 us  [shards(): swap = lambda array: lax.ppermute(array, 'adapter', SWAP)]
    pallas_call x2, Pallas kernels: 3.55 us -> 5.21 us  [the longest x1 3.64 us: own_products(): pl.pallas_call(own_kernel, in_specs=[ANYWHERE] * 4, out_specs=[VECTORS] *...]
    unnamed x12 -> x8, local copies, waits for them, and re-layouts: 3.91 us -> 2.36 us
    pallas_call x1, Pallas kernels: 3.98 us -> 2.81 us  [input_gradient(): pl.pallas_call(input_kernel, grid=(steps,), in_specs=[VECTORS] * 3, out_s...]
    ppermute x7, waiting for transfers between devices: 11.1 us -> 11.8 us  [shards(): lax.ppermute(array, 'dp', [(i, i ^ by) for i in range(replicas)])]
    pallas_call x4 -> x3, Pallas kernels: 2.61 us -> 1.94 us  [fold(): pl.pallas_call(functools.partial(fold_kernel, block, at), in_specs=[SCALA...]
where the time goes in v4:
time: 46.6 us; the launch traced here: 46.4 us
  starting transfers between devices  16.6 us (36%)
  waiting for transfers between devices  13.4 us (29%)
  Pallas kernels  13.2 us (28%)
  local copies, waits for them, and re-layouts  2.45 us (5%)
  between operations  0.73 us (2%)
    ppermute x7, starting transfers between devices, shards(): lax.ppermute(array, 'dp', [(i, i ^ by) for i in range(replicas)])  15.1 us
    ppermute x7, waiting for transfers between devices, shards(): lax.ppermute(array, 'dp', [(i, i ^ by) for i in range(replicas)])  11.8 us
    pallas_call x1, Pallas kernels, own_products(): pl.pallas_call(own_kernel, in_specs=[ANYWHERE] * 4, out_specs=[VECTORS] *...  3.64 us
    pallas_call x1, Pallas kernels, input_gradient(): pl.pallas_call(input_kernel, grid=(steps,), in_specs=[VECTORS] * 3, out_s...  2.81 us
    unnamed x8, local copies, waits for them, and re-layouts  2.36 us
    pallas_call x1, Pallas kernels, low_products(): pl.pallas_call(functools.partial(low_kernel, rank), in_specs=[SCALARS] *...  2.28 us
    pallas_call x3, Pallas kernels, fold(): pl.pallas_call(functools.partial(fold_kernel, block, at), in_specs=[SCALA...  1.94 us
    pallas_call x1, Pallas kernels, rest_products(): pl.pallas_call(functools.partial(rest_kernel, blocks, block), in_specs=[S...  1.57 us
  transfers between devices with their start and end apart: 11, of which 5 were waited for; matrix products, arithmetic and copies ran while one was open for 0% of the time, Pallas kernels for 18%

profile of v4, /device:TPU:0, one launch (start us, length us, event | category | flops | bytes accessed | tf_op | source)
XLA Modules:
  0.0 46.4 jit_solution(5442830994712862255)
XLA Ops:
  0.6 0.5 %collective-permute-start.1 = (bf16[64,7168]{1,0:T(8,128)(2,1)}, bf16[64,7168]{1,0:T(8,128)(2,1)S(1)}, u32[]{:S(2)}, u32[]{:S(2)}) collective-permute-start(bf16[64,7168]{1,0:T(8,128)(2,1)} %bitcast.12), channel_id=1, source_target_pairs={{0,1},{1,0},{2,3},{3,2},{4,5},{5,4},{6,7},{7,6},{8,9},{9,8},{10,11... | collective-permute-start | bytes 2752520 | tf_op jit(solution)/shard_map/ppermute | solution.py:272
  1.1 0.1 collective-permute-start
  1.2 0.1 stack.23.where_ref
  1.3 0.0 copy-start
  1.3 1.2 %copy-done = bf16[4,16,7168]{2,1,0:T(8,128)(2,1)S(1)} copy-done((bf16[4,16,7168]{2,1,0:T(8,128)(2,1)S(1)}, bf16[4,16,7168]{2,1,0:T(8,128)(2,1)}, u32[]{:S(2)}) %copy-start) | copy-done | bytes 917528
  2.5 0.0 copy-start.1
  2.5 1.2 %copy-done.1 = bf16[4,16,7168]{2,1,0:T(8,128)(2,1)S(1)} copy-done((bf16[4,16,7168]{2,1,0:T(8,128)(2,1)S(1)}, bf16[4,16,7168]{2,1,0:T(8,128)(2,1)}, u32[]{:S(2)}) %copy-start.1) | copy-done | bytes 917528
  3.7 0.0 copy-start.2
  3.7 0.0 copy-start.3
  3.7 3.6 %own.1 = (f32[64,128]{1,0:T(8,128)S(1)}, f32[64,128]{1,0:T(8,128)S(1)}, bf16[128,7168]{1,0:T(8,128)(2,1)S(1)}, bf16[128,7168]{1,0:T(8,128)(2,1)S(1)}) custom-call(bf16[64,7168]{1,0:T(8,128)(2,1)S(1)} %bitcast.16, bf16[128,7168]{1,0:T(8,128)(2,1)} %g_hbm.1, bf16[64,7168]{1,0:T(8,128)(2,1)S(1)} %bitcast.13, bf16[128,7168]{1,0:T(8,128)(2,1)} %x_hbm.1), custom_call_target="tpu_custom_call" | custom-call | flops 234881024 | bytes 5505024 | tf_op jit(solution)/shard_map/own/pallas_call | solution.py:65
  7.3 0.0 collective-permute-done.1.a_ref.other_ref
  7.3 0.0 collective-permute-done.b_ref
  7.3 0.0 copy-done.2
  7.4 0.0 copy-done.3
  7.4 2.3 %low.1 = (bf16[128,128]{1,0:T(8,128)(2,1)S(1)}, bf16[128,128]{1,0:T(8,128)(2,1)S(1)}, bf16[128,1792]{1,0:T(8,128)(2,1)S(1)}, bf16[128,1792]{1,0:T(8,128)(2,1)S(1)}) custom-call(s32[1]{0:T(128)} %bitcast.core_ref, s32[5]{0:T(128)S(1)} %stack.23.where_ref, s32[2,128]{1,0:T(2,128)S(1)} %bitcast.17, f32[2,128]{1,0:T(2,128)S(1)} %bitcast.18, ...), custom_call_target="tpu_custom_call" | custom-call | flops 352321536 | bytes 5505024 | tf_op jit(solution)/shard_map/low/pallas_call | solution.py:126
  9.6 0.5 %collective-permute-start.2 = (bf16[128,1792]{1,0:T(8,128)(2,1)S(1)}, bf16[128,1792]{1,0:T(8,128)(2,1)S(1)}, u32[]{:S(2)}, u32[]{:S(2)}) collective-permute-start(bf16[128,1792]{1,0:T(8,128)(2,1)S(1)} %get-tuple-element.31), channel_id=1, source_target_pairs={{0,1},{1,0},{2,3},{3,2},{4,5},{5,4},{6,7},{7,6},{8,9},{9,8},{10,11... | collective-permute-start | bytes 1376264 | tf_op jit(solution)/shard_map/ppermute | solution.py:272
  10.1 1.4 %collective-permute-done.2.came_ref = bf16[128,1792]{1,0:T(8,128)(2,1)S(1)} collective-permute-done((bf16[128,1792]{1,0:T(8,128)(2,1)S(1)}, bf16[128,1792]{1,0:T(8,128)(2,1)S(1)}, u32[]{:S(2)}, u32[]{:S(2)}) %collective-permute-start.2) | collective-permute-done | bytes 458784 | tf_op jit(solution)/shard_map/ppermute | solution.py:272
  11.6 1.6 %rest.1 = (bf16[128,5376]{1,0:T(8,128)(2,1)S(1)}, bf16[128,5376]{1,0:T(8,128)(2,1)S(1)}, bf16[128,896]{1,0:T(8,128)(2,1)S(1)}, f32[128,896]{1,0:T(8,128)S(1)}) custom-call(s32[5]{0:T(128)S(1)} %stack.23.where_ref, bf16[128,1792]{1,0:T(8,128)(2,1)S(1)} %get-tuple-element.30.kept_ref, bf16[128,1792]{1,0:T(8,128)(2,1)S(1)} %collective-permute-done.2.came_ref, ...), custom_call_target="tpu_custom_call" | custom-call | flops 176160768 | bytes 2752512 | tf_op jit(solution)/shard_map/rest/pallas_call | solution.py:155
  13.2 0.4 collective-permute-start.3
  13.6 2.7 %collective-permute-start.5 = (bf16[128,896]{1,0:T(8,128)(2,1)S(1)}, bf16[128,896]{1,0:T(8,128)(2,1)S(1)}, u32[]{:S(2)}, u32[]{:S(2)}) collective-permute-start(bf16[128,896]{1,0:T(8,128)(2,1)S(1)} %get-tuple-element.39), channel_id=1, source_target_pairs={{0,2},{2,0},{4,6},{6,4},{8,10},{10,8},{12,14},{14,12},{1,3},{3,1},... | collective-permute-start | bytes 688136 | tf_op jit(solution)/shard_map/ppermute | solution.py:276
  16.3 0.1 collective-permute-done.3.came_ref
  16.4 0.6 %fold.5 = (bf16[128,896]{1,0:T(8,128)(2,1)S(1)}, f32[128,896]{1,0:T(8,128)S(1)}) custom-call(s32[5]{0:T(128)S(1)} %stack.23.where_ref, bf16[128,5376]{1,0:T(8,128)(2,1)S(1)} %get-tuple-element.33.keep_ref, bf16[128,5376]{1,0:T(8,128)(2,1)S(1)} %collective-permute-done.3.came_ref), custom_call_target="tpu_custom_call" | custom-call | flops 229376 | bytes 1605632 | tf_op jit(solution)/shard_map/fold/pallas_call | solution.py:180
  17.0 2.9 %collective-permute-start.9 = (bf16[128,896]{1,0:T(8,128)(2,1)S(1)}, bf16[128,896]{1,0:T(8,128)(2,1)S(1)}, u32[]{:S(2)}, u32[]{:S(2)}) collective-permute-start(bf16[128,896]{1,0:T(8,128)(2,1)S(1)} %get-tuple-element.43), channel_id=1, source_target_pairs={{0,2},{2,0},{4,6},{6,4},{8,10},{10,8},{12,14},{14,12},{1,3},{3,1},... | collective-permute-start | bytes 688136 | tf_op jit(solution)/shard_map/ppermute | solution.py:276
  20.0 0.6 %fold.4 = (bf16[128,896]{1,0:T(8,128)(2,1)S(1)}, f32[128,896]{1,0:T(8,128)S(1)}) custom-call(s32[5]{0:T(128)S(1)} %stack.23.where_ref, bf16[128,5376]{1,0:T(8,128)(2,1)S(1)} %get-tuple-element.33.keep_ref, bf16[128,5376]{1,0:T(8,128)(2,1)S(1)} %collective-permute-done.3.came_ref), custom_call_target="tpu_custom_call" | custom-call | flops 229376 | bytes 1605632 | tf_op jit(solution)/shard_map/fold/pallas_call | solution.py:180
  20.6 0.1 collective-permute-start.7
  20.7 2.0 %collective-permute-done.5.came_ref = bf16[128,896]{1,0:T(8,128)(2,1)S(1)} collective-permute-done((bf16[128,896]{1,0:T(8,128)(2,1)S(1)}, bf16[128,896]{1,0:T(8,128)(2,1)S(1)}, u32[]{:S(2)}, u32[]{:S(2)}) %collective-permute-start.5) | collective-permute-done | bytes 229408 | tf_op jit(solution)/shard_map/ppermute | solution.py:276
  22.7 0.1 add.9
  22.8 4.1 %collective-permute-start.6 = (bf16[128,896]{1,0:T(8,128)(2,1)S(1)}, bf16[128,896]{1,0:T(8,128)(2,1)S(1)}, u32[]{:S(2)}, u32[]{:S(2)}) collective-permute-start(bf16[128,896]{1,0:T(8,128)(2,1)S(1)} %add.9), channel_id=1, source_target_pairs={{0,12},{2,14},{4,8},{6,10},{8,4},{10,6},{12,0},{14,2},{1,13},{3,15... | collective-permute-start | bytes 688136 | tf_op jit(solution)/shard_map/ppermute | solution.py:276
  26.9 0.6 %fold.3 = (bf16[128,896]{1,0:T(8,128)(2,1)S(1)}, f32[128,896]{1,0:T(8,128)S(1)}) custom-call(s32[5]{0:T(128)S(1)} %stack.23.where_ref, bf16[128,5376]{1,0:T(8,128)(2,1)S(1)} %get-tuple-element.33.keep_ref, bf16[128,5376]{1,0:T(8,128)(2,1)S(1)} %collective-permute-done.3.came_ref), custom_call_target="tpu_custom_call" | custom-call | flops 229376 | bytes 1605632 | tf_op jit(solution)/shard_map/fold/pallas_call | solution.py:180
  27.5 1.6 %collective-permute-start.4 = (bf16[128,896]{1,0:T(8,128)(2,1)S(1)}, bf16[128,896]{1,0:T(8,128)(2,1)S(1)}, u32[]{:S(2)}, u32[]{:S(2)}) collective-permute-start(bf16[128,896]{1,0:T(8,128)(2,1)S(1)} %get-tuple-element.35), channel_id=1, source_target_pairs={{0,2},{2,0},{4,6},{6,4},{8,10},{10,8},{12,14},{14,12},{1,3},{3,1},... | collective-permute-start | bytes 688136 | tf_op jit(solution)/shard_map/ppermute | solution.py:276
  29.1 0.0 collective-permute-done.9.came_ref
  29.1 0.1 add.11
  29.2 0.6 %collective-permute-start.10 = (bf16[128,896]{1,0:T(8,128)(2,1)S(1)}, bf16[128,896]{1,0:T(8,128)(2,1)S(1)}, u32[]{:S(2)}, u32[]{:S(2)}) collective-permute-start(bf16[128,896]{1,0:T(8,128)(2,1)S(1)} %add.11), channel_id=1, source_target_pairs={{0,4},{2,6},{4,0},{6,2},{8,12},{10,14},{12,8},{14,10},{1,5},{3,7},... | collective-permute-start | bytes 688136 | tf_op jit(solution)/shard_map/ppermute | solution.py:276
  29.8 2.8 %collective-permute-done.7.came_ref = bf16[128,896]{1,0:T(8,128)(2,1)S(1)} collective-permute-done((bf16[128,896]{1,0:T(8,128)(2,1)S(1)}, bf16[128,896]{1,0:T(8,128)(2,1)S(1)}, u32[]{:S(2)}, u32[]{:S(2)}) %collective-permute-start.7) | collective-permute-done | bytes 229408 | tf_op jit(solution)/shard_map/ppermute | solution.py:276
  32.6 3.1 %collective-permute-start.8 = (bf16[128,896]{1,0:T(8,128)(2,1)S(1)}, bf16[128,896]{1,0:T(8,128)(2,1)S(1)}, u32[]{:S(2)}, u32[]{:S(2)}) collective-permute-start(bf16[128,896]{1,0:T(8,128)(2,1)S(1)} %add.10), channel_id=1, source_target_pairs={{0,8},{2,10},{4,12},{6,14},{8,0},{10,2},{12,4},{14,6},{1,9},{3,11}... | collective-permute-start | bytes 688136 | tf_op jit(solution)/shard_map/ppermute | solution.py:276
  35.7 2.8 %input.1 = bf16[128,7168]{1,0:T(8,128)(2,1)} custom-call(bf16[128,128]{1,0:T(8,128)(2,1)S(1)} %get-tuple-element.29.low_ref.lg_ref, bf16[64,7168]{1,0:T(8,128)(2,1)S(1)} %bitcast.14, bf16[64,7168]{1,0:T(8,128)(2,1)S(1)} %collective-permute-done.1.a_ref.other_ref), custom_call_target="tpu_custom_call" | custom-call | flops 234881024 | bytes 3670016 | tf_op jit(solution)/shard_map/input/pallas_call | solution.py:250
  38.5 0.0 collective-permute-done.4.refs_3_
  38.5 0.0 collective-permute-done.6.refs_0_
  38.5 0.0 collective-permute-done.10.refs_2_
  38.5 7.0 %collective-permute-done.8.refs_1_ = bf16[128,896]{1,0:T(8,128)(2,1)S(1)} collective-permute-done((bf16[128,896]{1,0:T(8,128)(2,1)S(1)}, bf16[128,896]{1,0:T(8,128)(2,1)S(1)}, u32[]{:S(2)}, u32[]{:S(2)}) %collective-permute-start.8) | collective-permute-done | bytes 229408 | tf_op jit(solution)/shard_map/ppermute | solution.py:276
  45.6 0.8 %last.1 = (f32[64,896]{1,0:T(8,128)}, f32[64,896]{1,0:T(8,128)}) custom-call(f32[128,896]{1,0:T(8,128)S(1)} %get-tuple-element.37.keep_ref, bf16[128,896]{1,0:T(8,128)(2,1)S(1)} %collective-permute-done.6.refs_0_, bf16[128,896]{1,0:T(8,128)(2,1)S(1)} %collective-permute-done.8.refs_1_, bf16[128,896]{1,0:T(8,128)(2,1)S(1)} %collective-permute-done.10.refs_2_, ...), custom_call_target="tpu_custom_call" | custom-call | flops 458752 | bytes 1835008 | tf_op jit(solution)/shard_map/last/pallas_call | solution.py:224
  (1 shorter events, 0.0 us)
Async XLA Ops:
  0.6 6.7 %collective-permute-start.1 = (bf16[64,7168]{1,0:T(8,128)(2,1)}, bf16[64,7168]{1,0:T(8,128)(2,1)S(1)}, u32[]{:S(2)}, u32[]{:S(2)}) collective-permute-start(bf16[64,7168]{1,0:T(8,128)(2,1)} %bitcast.12), channel_id=1, source_target_pairs={{0,1},{1,0},{2,3},{3,2},{4,5},{5,4},{6,7},{7,6},{8,9},{9,8},{10,11... | collective-permute-start | bytes 2752520 | tf_op jit(solution)/shard_map/ppermute | solution.py:272
  1.1 6.2 %collective-permute-start = (bf16[64,7168]{1,0:T(8,128)(2,1)}, bf16[64,7168]{1,0:T(8,128)(2,1)S(1)}, u32[]{:S(2)}, u32[]{:S(2)}) collective-permute-start(bf16[64,7168]{1,0:T(8,128)(2,1)} %bitcast.15), channel_id=1, source_target_pairs={{0,1},{1,0},{2,3},{3,2},{4,5},{5,4},{6,7},{7,6},{8,9},{9,8},{10,11... | collective-permute-start | bytes 2752520 | tf_op jit(solution)/shard_map/ppermute | solution.py:272
  1.3 1.2 %copy-start = (bf16[4,16,7168]{2,1,0:T(8,128)(2,1)S(1)}, bf16[4,16,7168]{2,1,0:T(8,128)(2,1)}, u32[]{:S(2)}) copy-start(bf16[4,16,7168]{2,1,0:T(8,128)(2,1)} %param.10) | copy-start | bytes 2752516
  2.5 1.2 %copy-start.1 = (bf16[4,16,7168]{2,1,0:T(8,128)(2,1)S(1)}, bf16[4,16,7168]{2,1,0:T(8,128)(2,1)}, u32[]{:S(2)}) copy-start(bf16[4,16,7168]{2,1,0:T(8,128)(2,1)} %param.11) | copy-start | bytes 2752516
  3.7 3.7 %copy-start.2 = (s32[128,2]{0,1:T(2,128)S(1)}, s32[128,2]{0,1:T(2,128)}, u32[]{:S(2)}) copy-start(s32[128,2]{0,1:T(2,128)} %param.8) | copy-start | bytes 3076
  3.7 3.7 %copy-start.3 = (f32[128,2]{0,1:T(2,128)S(1)}, f32[128,2]{0,1:T(2,128)}, u32[]{:S(2)}) copy-start(f32[128,2]{0,1:T(2,128)} %param.9) | copy-start | bytes 3076
  9.6 1.9 %collective-permute-start.2 = (bf16[128,1792]{1,0:T(8,128)(2,1)S(1)}, bf16[128,1792]{1,0:T(8,128)(2,1)S(1)}, u32[]{:S(2)}, u32[]{:S(2)}) collective-permute-start(bf16[128,1792]{1,0:T(8,128)(2,1)S(1)} %get-tuple-element.31), channel_id=1, source_target_pairs={{0,1},{1,0},{2,3},{3,2},{4,5},{5,4},{6,7},{7,6},{8,9},{9,8},{10,11... | collective-permute-start | bytes 1376264 | tf_op jit(solution)/shard_map/ppermute | solution.py:272
  13.2 3.2 %collective-permute-start.3 = (bf16[128,5376]{1,0:T(8,128)(2,1)S(1)}, bf16[128,5376]{1,0:T(8,128)(2,1)S(1)}, u32[]{:S(2)}, u32[]{:S(2)}) collective-permute-start(bf16[128,5376]{1,0:T(8,128)(2,1)S(1)} %get-tuple-element.34), channel_id=1, source_target_pairs={{0,1},{1,0},{2,3},{3,2},{4,5},{5,4},{6,7},{7,6},{8,9},{9,8},{10,11... | collective-permute-start | bytes 4128776 | tf_op jit(solution)/shard_map/ppermute | solution.py:272
  13.6 9.1 %collective-permute-start.5 = (bf16[128,896]{1,0:T(8,128)(2,1)S(1)}, bf16[128,896]{1,0:T(8,128)(2,1)S(1)}, u32[]{:S(2)}, u32[]{:S(2)}) collective-permute-start(bf16[128,896]{1,0:T(8,128)(2,1)S(1)} %get-tuple-element.39), channel_id=1, source_target_pairs={{0,2},{2,0},{4,6},{6,4},{8,10},{10,8},{12,14},{14,12},{1,3},{3,1},... | collective-permute-start | bytes 688136 | tf_op jit(solution)/shard_map/ppermute | solution.py:276
  17.0 12.1 %collective-permute-start.9 = (bf16[128,896]{1,0:T(8,128)(2,1)S(1)}, bf16[128,896]{1,0:T(8,128)(2,1)S(1)}, u32[]{:S(2)}, u32[]{:S(2)}) collective-permute-start(bf16[128,896]{1,0:T(8,128)(2,1)S(1)} %get-tuple-element.43), channel_id=1, source_target_pairs={{0,2},{2,0},{4,6},{6,4},{8,10},{10,8},{12,14},{14,12},{1,3},{3,1},... | collective-permute-start | bytes 688136 | tf_op jit(solution)/shard_map/ppermute | solution.py:276
  20.6 11.9 %collective-permute-start.7 = (bf16[128,896]{1,0:T(8,128)(2,1)S(1)}, bf16[128,896]{1,0:T(8,128)(2,1)S(1)}, u32[]{:S(2)}, u32[]{:S(2)}) collective-permute-start(bf16[128,896]{1,0:T(8,128)(2,1)S(1)} %get-tuple-element.41), channel_id=1, source_target_pairs={{0,2},{2,0},{4,6},{6,4},{8,10},{10,8},{12,14},{14,12},{1,3},{3,1},... | collective-permute-start | bytes 688136 | tf_op jit(solution)/shard_map/ppermute | solution.py:276
  22.8 15.8 %collective-permute-start.6 = (bf16[128,896]{1,0:T(8,128)(2,1)S(1)}, bf16[128,896]{1,0:T(8,128)(2,1)S(1)}, u32[]{:S(2)}, u32[]{:S(2)}) collective-permute-start(bf16[128,896]{1,0:T(8,128)(2,1)S(1)} %add.9), channel_id=1, source_target_pairs={{0,12},{2,14},{4,8},{6,10},{8,4},{10,6},{12,0},{14,2},{1,13},{3,15... | collective-permute-start | bytes 688136 | tf_op jit(solution)/shard_map/ppermute | solution.py:276
  27.5 11.0 %collective-permute-start.4 = (bf16[128,896]{1,0:T(8,128)(2,1)S(1)}, bf16[128,896]{1,0:T(8,128)(2,1)S(1)}, u32[]{:S(2)}, u32[]{:S(2)}) collective-permute-start(bf16[128,896]{1,0:T(8,128)(2,1)S(1)} %get-tuple-element.35), channel_id=1, source_target_pairs={{0,2},{2,0},{4,6},{6,4},{8,10},{10,8},{12,14},{14,12},{1,3},{3,1},... | collective-permute-start | bytes 688136 | tf_op jit(solution)/shard_map/ppermute | solution.py:276
  29.2 9.3 %collective-permute-start.10 = (bf16[128,896]{1,0:T(8,128)(2,1)S(1)}, bf16[128,896]{1,0:T(8,128)(2,1)S(1)}, u32[]{:S(2)}, u32[]{:S(2)}) collective-permute-start(bf16[128,896]{1,0:T(8,128)(2,1)S(1)} %add.11), channel_id=1, source_target_pairs={{0,4},{2,6},{4,0},{6,2},{8,12},{10,14},{12,8},{14,10},{1,5},{3,7},... | collective-permute-start | bytes 688136 | tf_op jit(solution)/shard_map/ppermute | solution.py:276
  32.6 13.0 %collective-permute-start.8 = (bf16[128,896]{1,0:T(8,128)(2,1)S(1)}, bf16[128,896]{1,0:T(8,128)(2,1)S(1)}, u32[]{:S(2)}, u32[]{:S(2)}) collective-permute-start(bf16[128,896]{1,0:T(8,128)(2,1)S(1)} %add.10), channel_id=1, source_target_pairs={{0,8},{2,10},{4,12},{6,14},{8,0},{10,2},{12,4},{14,6},{1,9},{3,11}... | collective-permute-start | bytes 688136 | tf_op jit(solution)/shard_map/ppermute | solution.py:276

commit v5 on v4

--- a/solution.py
+++ b/solution.py
@@ -11,7 +11,7 @@
 F32 = jnp.float32
 SWAP = [(0, 1), (1, 0)]
 VMEM_LIMIT = 12 * 1024 * 1024
-OWN_LIMIT = 48 * 1024 * 1024
+OWN_LIMIT = 49 * 1024 * 1024
 VECTORS = pl.BlockSpec(memory_space=pltpu.VMEM)
 ANYWHERE = pl.BlockSpec(memory_space=pl.ANY)
 SCALARS = pl.BlockSpec(memory_space=pltpu.SMEM)
@@ -34,46 +34,45 @@
     return 1
 
 
-def own_kernel(b_hbm, g_hbm, a_hbm, x_hbm, grad_ref, act_ref, g_ref, x_ref, b, a, sems):
+def own_kernel(b_hbm, g_hbm, x_hbm, grad_ref, g_ref, x_ref, b, sems):
     width = g_ref.shape[1]
-    halves = ((b_hbm, b, g_hbm, g_ref, grad_ref), (a_hbm, a, x_hbm, x_ref, act_ref))
+    arrays = ((b_hbm, b), (g_hbm, g_ref), (x_hbm, x_ref))
     copies = [
         [
-            pltpu.make_async_copy(source.at[:, cols], target.at[:, cols], sems.at[half, i, j])
-            for i, (source, target) in enumerate((refs[:2], refs[2:4]))
+            pltpu.make_async_copy(source.at[:, cols], target.at[:, cols], sems.at[i, j])
+            for j, cols in enumerate(tiles(width))
         ]
-        for half, refs in enumerate(halves)
-        for j, cols in enumerate(tiles(width))
+        for i, (source, target) in enumerate(arrays)
     ]
-    for pair in copies:
-        for copy in pair:
-            copy.start()
-    for half, (_, factor, _, tokens, out) in enumerate(halves):
-        total = jnp.zeros(out.shape, F32)
-        for j, cols in enumerate(tiles(width)):
-            for copy in copies[half * len(tiles(width)) + j]:
-                copy.wait()
-            total = total + lax.dot_general(
-                factor[:, cols], tokens[:, cols], NT, preferred_element_type=F32
-            )
-        out[...] = total
-
-
-def own_products(b, g, a, x):
+    for j in range(len(copies[0])):
+        copies[0][j].start()
+        copies[1][j].start()
+    for copy in copies[2]:
+        copy.start()
+    total = jnp.zeros(grad_ref.shape, F32)
+    for j, cols in enumerate(tiles(width)):
+        copies[0][j].wait()
+        copies[1][j].wait()
+        total = total + lax.dot_general(b[:, cols], g_ref[:, cols], NT, preferred_element_type=F32)
+    grad_ref[...] = total
+    for copy in copies[2]:
+        copy.wait()
+
+
+def own_products(b, g, x):
     rows, width = b.shape
     tokens = x.shape[0]
     return pl.pallas_call(
         own_kernel,
-        in_specs=[ANYWHERE] * 4,
-        out_specs=[VECTORS] * 4,
-        out_shape=[jax.ShapeDtypeStruct((rows, tokens), F32)] * 2
+        in_specs=[ANYWHERE] * 3,
+        out_specs=[VECTORS] * 3,
+        out_shape=[jax.ShapeDtypeStruct((rows, tokens), F32)]
         + [jax.ShapeDtypeStruct((tokens, width), BF16)] * 2,
-        scratch_shapes=[pltpu.VMEM(b.shape, BF16)] * 2
-        + [pltpu.SemaphoreType.DMA((2, 2, steps_of(width)))],
+        scratch_shapes=[pltpu.VMEM(b.shape, BF16), pltpu.SemaphoreType.DMA((3, steps_of(width)))],
         compiler_params=params(OWN_LIMIT),
-        cost_estimate=cost(4 * rows * tokens * width, 4 * (rows + tokens) * width),
+        cost_estimate=cost(2 * rows * tokens * width, 4 * (rows + tokens) * width),
         name="own",
-    )(b, g, a, x)
+    )(b, g, x)
 
 
 def tiles(width):
@@ -104,23 +103,28 @@
             keep_ref[out, into] = product[rows:]
 
 
-def low_kernel(rank, core_ref, where_ref, ids_ref, gates_ref, grad_ref, act_ref, b_ref, a_ref, g_ref, x_ref,
+def factor_sum(factor, tokens):
+    total = jnp.zeros((factor.shape[0], tokens.shape[0]), F32)
+    for cols in tiles(factor.shape[1]):
+        total = total + lax.dot_general(
+            factor[:, cols], tokens[:, cols], NT, preferred_element_type=F32
+        )
+    return total
+
+
+def low_kernel(rank, core_ref, where_ref, ids_ref, gates_ref, grad_ref, b_ref, a_ref, a_in_ref, g_ref, x_ref,
                lg_ref, la_ref, send_ref, keep_ref):
-    rows, width = b_ref.shape
-    weight = gate_columns(1 - core_ref[0], ids_ref[...], gates_ref[...], 2 * rows, rank)
-    lows = []
-    for own, factor, tokens, out in ((grad_ref, b_ref, g_ref, lg_ref), (act_ref, a_ref, x_ref, la_ref)):
-        total = jnp.zeros(own.shape, F32)
-        for cols in tiles(width):
-            total = total + lax.dot_general(
-                factor[:, cols], tokens[:, cols], NT, preferred_element_type=F32
-            )
-        lows.append((jnp.concatenate([total, own[...]], axis=0) * weight).astype(BF16))
-        out[...] = lows[-1]
+    weight = gate_columns(1 - core_ref[0], ids_ref[...], gates_ref[...], 2 * b_ref.shape[0], rank)
+    sums = (
+        [factor_sum(b_ref, g_ref), grad_ref[...]],
+        [factor_sum(a_in_ref, x_ref), factor_sum(a_ref, x_ref)],
+    )
+    lows = [(jnp.concatenate(pair, axis=0) * weight).astype(BF16) for pair in sums]
+    lg_ref[...], la_ref[...] = lows
     store_products(where_ref, 0, 1, lows, (x_ref, g_ref), send_ref, keep_ref)
 
 
-def low_products(core, where, ids, gates, rank, grad, act, b_in, a_in, g, x, wide):
+def low_products(core, where, ids, gates, rank, grad, b_in, a, a_in, g, x, wide):
     rows, width = b_in.shape
     tokens = x.shape[0]
     return pl.pallas_call(
@@ -132,7 +136,7 @@
         compiler_params=params(),
         cost_estimate=cost(4 * rows * tokens * (width + 2 * wide), 4 * (rows + tokens) * width),
         name="low",
-    )(core, where, ids, gates, grad, act, b_in, a_in, g, x)
+    )(core, where, ids, gates, grad, b_in, a, a_in, g, x)
 
 
 def rest_kernel(blocks, block, where_ref, kept_ref, came_ref, lg_ref, la_ref, x_ref, g_ref, *outs):
@@ -205,31 +209,42 @@
     )(keep, came)
 
 
-def last_kernel(keep_ref, *refs):
-    came, (down_ref, up_ref) = refs[:-2], refs[-2:]
+def total_kernel(keep_ref, *refs):
+    total = keep_ref[...]
+    for ref in refs[:-1]:
+        total = total + ref[...].astype(F32)
+    refs[-1][...] = total
+
+
+def total(keep, came):
+    return pl.pallas_call(
+        total_kernel,
+        in_specs=[VECTORS] * (1 + len(came)),
+        out_specs=VECTORS,
+        out_shape=jax.ShapeDtypeStruct(keep.shape, F32),
+        compiler_params=params(),
+        cost_estimate=cost(keep.size * len(came), keep.size * (8 + 2 * len(came))),
+        name="total",
+    )(keep, *came)
+
+
+def last_kernel(total_ref, came_ref, down_ref, up_ref):
     rows = down_ref.shape[0]
-    for half, out in ((0, down_ref), (1, up_ref)):
-        own = pl.ds(half * rows, rows)
-        total = keep_ref[own, :]
-        at = 0
-        while at < len(came):
-            whole = came[at].shape[0] > rows
-            total = total + (came[at][own, :] if whole else came[at + half][...]).astype(F32)
-            at += 1 if whole else 2
-        out[...] = total
-
-
-def last(keep, came):
-    rows, block = keep.shape[0] // 2, keep.shape[1]
+    down_ref[...] = total_ref[:rows] + came_ref[:rows].astype(F32)
+    up_ref[...] = total_ref[rows:] + came_ref[rows:].astype(F32)
+
+
+def last(total, came):
+    rows, block = total.shape[0] // 2, total.shape[1]
     return pl.pallas_call(
         last_kernel,
-        in_specs=[VECTORS] * (1 + len(came)),
+        in_specs=[VECTORS] * 2,
         out_specs=[VECTORS] * 2,
         out_shape=[jax.ShapeDtypeStruct((rows, block), F32)] * 2,
         compiler_params=params(),
-        cost_estimate=cost(keep.size * len(came), keep.size * (8 + 2 * len(came))),
+        cost_estimate=cost(came.size, 10 * came.size),
         name="last",
-    )(keep, *came)
+    )(total, came)
 
 
 def input_kernel(low_ref, own_ref, other_ref, out_ref):
@@ -279,26 +294,31 @@
         return plain(core, ids, gates, rank, x, g, a, b, swap(a), b_in, swap)
 
     a_in = swap(a)
-    grad, act, g_held, x_held = own_products(b, g, a, x)
+    grad, g_held, x_held = own_products(b, g, x)
     order = list(reversed(range(steps)))
     where = jnp.stack([far ^ step for step in order] + [near])
     lg, la, pair, keep = low_products(
-        core, where, ids, gates, rank, grad, act, b_in, a_in, g_held, x_held, 2 * block
+        core, where, ids, gates, rank, grad, b_in, a, a_in, g_held, x_held, 2 * block
     )
     rest_pair, rest_keep, *first = rest_products(
         where, keep, swap(pair), lg, la, x_held, g_held, steps - 1, block, 1
     )
     rest_came = swap(rest_pair)
-    came = [
-        flip(add(own, flip(send, 1)), 2 * order[0]) for send, own in zip(first[::2], first[1::2])
-    ]
-    for i, step in enumerate(order[1:]):
-        send, own = fold(where, block, i, rest_keep, rest_came)
+    send, own = first
+    came = []
+    for i, step in enumerate(order):
+        if i:
+            send, own = fold(where, block, i - 1, rest_keep, rest_came)
         got = flip(send, 1)
-        came.append(flip(add(own, got), 2 * step) if step else got)
+        if step == 0:
+            came.append(got)
+        elif step == 1:
+            nearest = flip(add(own, got), 2)
+        else:
+            came.append(flip(add(own, got), 2 * step))
     input_grad = input_gradient(lg, a, a_in)
     input_grad, came[-1] = lax.optimization_barrier((input_grad, came[-1]))
-    down, up = last(own, came)
+    down, up = last(total(own, came), nearest)
     return input_grad, down.reshape(count, rank, block), up.reshape(count, rank, block)
 
 

time: 46.6 us -> 45.3 us (0.972)
  local copies, waits for them, and re-layouts: 2.45 us -> 1.27 us
    unnamed x8, local copies, waits for them, and re-layouts: 2.36 us -> 1.19 us
    pallas_call x2 -> x3, Pallas kernels: 4.48 us -> 3.53 us  [the longest x1 2.62 us: own_products(): pl.pallas_call(own_kernel, in_specs=[ANYWHERE] * 3, out_specs=[VECTORS] *...]
    pallas_call x1, Pallas kernels: 2.28 us -> 3.09 us  [low_products(): pl.pallas_call(functools.partial(low_kernel, rank), in_specs=[SCALARS] *...]
  transfers between devices with their start and end apart: 11 -> 11, of which waited for: 5 -> 5; matrix products, arithmetic and copies ran while one was open for 0% -> 0% of each run, Pallas kernels for 18% -> 17%
where the time goes in v5:
time: 45.3 us; the launch traced here: 45.1 us
  starting transfers between devices  16.6 us (37%)
  waiting for transfers between devices  13.3 us (29%)
  Pallas kernels  13.1 us (29%)
  local copies, waits for them, and re-layouts  1.27 us (3%)
  between operations  0.75 us (2%)
    ppermute x7, starting transfers between devices, shards(): lax.ppermute(array, 'dp', [(i, i ^ by) for i in range(replicas)])  15.1 us
    ppermute x7, waiting for transfers between devices, shards(): lax.ppermute(array, 'dp', [(i, i ^ by) for i in range(replicas)])  11.8 us
    pallas_call x1, Pallas kernels, low_products(): pl.pallas_call(functools.partial(low_kernel, rank), in_specs=[SCALARS] *...  3.09 us
    pallas_call x1, Pallas kernels, input_gradient(): pl.pallas_call(input_kernel, grid=(steps,), in_specs=[VECTORS] * 3, out_s...  2.82 us
    pallas_call x1, Pallas kernels, own_products(): pl.pallas_call(own_kernel, in_specs=[ANYWHERE] * 3, out_specs=[VECTORS] *...  2.62 us
    pallas_call x3, Pallas kernels, fold(): pl.pallas_call(functools.partial(fold_kernel, block, at), in_specs=[SCALA...  1.94 us
    pallas_call x1, Pallas kernels, rest_products(): pl.pallas_call(functools.partial(rest_kernel, blocks, block), in_specs=[S...  1.57 us
    ppermute x4, waiting for transfers between devices, shards(): swap = lambda array: lax.ppermute(array, 'adapter', SWAP)  1.54 us
  transfers between devices with their start and end apart: 11, of which 5 were waited for; matrix products, arithmetic and copies ran while one was open for 0% of the time, Pallas kernels for 17%

profile of v5, /device:TPU:0, one launch (start us, length us, event | category | flops | bytes accessed | tf_op | source)
XLA Modules:
  0.0 45.1 jit_solution(11312545626309512925)
XLA Ops:
  0.6 0.5 %collective-permute-start.1 = (bf16[64,7168]{1,0:T(8,128)(2,1)}, bf16[64,7168]{1,0:T(8,128)(2,1)S(1)}, u32[]{:S(2)}, u32[]{:S(2)}) collective-permute-start(bf16[64,7168]{1,0:T(8,128)(2,1)} %bitcast.12), channel_id=1, source_target_pairs={{0,1},{1,0},{2,3},{3,2},{4,5},{5,4},{6,7},{7,6},{8,9},{9,8},{10,11... | collective-permute-start | bytes 2752520 | tf_op jit(solution)/shard_map/ppermute | solution.py:287
  1.1 0.1 collective-permute-start
  1.2 0.1 stack.23.where_ref
  1.3 0.0 copy-start.1
  1.3 1.2 %copy-done.1 = bf16[4,16,7168]{2,1,0:T(8,128)(2,1)S(1)} copy-done((bf16[4,16,7168]{2,1,0:T(8,128)(2,1)S(1)}, bf16[4,16,7168]{2,1,0:T(8,128)(2,1)}, u32[]{:S(2)}) %copy-start.1) | copy-done | bytes 917528
  2.5 0.0 copy-start
  2.5 0.0 copy-start.2
  2.5 0.0 copy-start.3
  2.5 2.6 %own.1 = (f32[64,128]{1,0:T(8,128)S(1)}, bf16[128,7168]{1,0:T(8,128)(2,1)S(1)}, bf16[128,7168]{1,0:T(8,128)(2,1)S(1)}) custom-call(bf16[64,7168]{1,0:T(8,128)(2,1)S(1)} %bitcast.16, bf16[128,7168]{1,0:T(8,128)(2,1)} %g_hbm.1, bf16[128,7168]{1,0:T(8,128)(2,1)} %x_hbm.1), custom_call_target="tpu_custom_call" | custom-call | flops 117440512 | bytes 5505024 | tf_op jit(solution)/shard_map/own/pallas_call | solution.py:65
  5.1 0.0 collective-permute-done.1.a_in_ref.other_ref
  5.1 0.0 collective-permute-done.b_ref
  5.1 0.0 copy-done
  5.2 0.0 copy-done.2
  5.2 0.0 copy-done.3
  5.2 3.1 %low.1 = (bf16[128,128]{1,0:T(8,128)(2,1)S(1)}, bf16[128,128]{1,0:T(8,128)(2,1)S(1)}, bf16[128,1792]{1,0:T(8,128)(2,1)S(1)}, bf16[128,1792]{1,0:T(8,128)(2,1)S(1)}) custom-call(s32[1]{0:T(128)} %bitcast.core_ref, s32[5]{0:T(128)S(1)} %stack.23.where_ref, s32[2,128]{1,0:T(2,128)S(1)} %bitcast.17, f32[2,128]{1,0:T(2,128)S(1)} %bitcast.18, ...), custom_call_target="tpu_custom_call" | custom-call | flops 352321536 | bytes 5505024 | tf_op jit(solution)/shard_map/low/pallas_call | solution.py:130
  8.3 0.5 %collective-permute-start.2 = (bf16[128,1792]{1,0:T(8,128)(2,1)S(1)}, bf16[128,1792]{1,0:T(8,128)(2,1)S(1)}, u32[]{:S(2)}, u32[]{:S(2)}) collective-permute-start(bf16[128,1792]{1,0:T(8,128)(2,1)S(1)} %get-tuple-element.29), channel_id=1, source_target_pairs={{0,1},{1,0},{2,3},{3,2},{4,5},{5,4},{6,7},{7,6},{8,9},{9,8},{10,11... | collective-permute-start | bytes 1376264 | tf_op jit(solution)/shard_map/ppermute | solution.py:287
  8.8 1.4 %collective-permute-done.2.came_ref = bf16[128,1792]{1,0:T(8,128)(2,1)S(1)} collective-permute-done((bf16[128,1792]{1,0:T(8,128)(2,1)S(1)}, bf16[128,1792]{1,0:T(8,128)(2,1)S(1)}, u32[]{:S(2)}, u32[]{:S(2)}) %collective-permute-start.2) | collective-permute-done | bytes 458784 | tf_op jit(solution)/shard_map/ppermute | solution.py:287
  10.2 1.6 %rest.1 = (bf16[128,5376]{1,0:T(8,128)(2,1)S(1)}, bf16[128,5376]{1,0:T(8,128)(2,1)S(1)}, bf16[128,896]{1,0:T(8,128)(2,1)S(1)}, f32[128,896]{1,0:T(8,128)S(1)}) custom-call(s32[5]{0:T(128)S(1)} %stack.23.where_ref, bf16[128,1792]{1,0:T(8,128)(2,1)S(1)} %get-tuple-element.28.kept_ref, bf16[128,1792]{1,0:T(8,128)(2,1)S(1)} %collective-permute-done.2.came_ref, ...), custom_call_target="tpu_custom_call" | custom-call | flops 176160768 | bytes 2752512 | tf_op jit(solution)/shard_map/rest/pallas_call | solution.py:159
  11.8 0.4 collective-permute-start.3
  12.2 2.7 %collective-permute-start.5 = (bf16[128,896]{1,0:T(8,128)(2,1)S(1)}, bf16[128,896]{1,0:T(8,128)(2,1)S(1)}, u32[]{:S(2)}, u32[]{:S(2)}) collective-permute-start(bf16[128,896]{1,0:T(8,128)(2,1)S(1)} %get-tuple-element.37), channel_id=1, source_target_pairs={{0,2},{2,0},{4,6},{6,4},{8,10},{10,8},{12,14},{14,12},{1,3},{3,1},... | collective-permute-start | bytes 688136 | tf_op jit(solution)/shard_map/ppermute | solution.py:291
  14.9 0.1 collective-permute-done.3.came_ref
  15.0 0.6 %fold.4 = (bf16[128,896]{1,0:T(8,128)(2,1)S(1)}, f32[128,896]{1,0:T(8,128)S(1)}) custom-call(s32[5]{0:T(128)S(1)} %stack.23.where_ref, bf16[128,5376]{1,0:T(8,128)(2,1)S(1)} %get-tuple-element.31.keep_ref, bf16[128,5376]{1,0:T(8,128)(2,1)S(1)} %collective-permute-done.3.came_ref), custom_call_target="tpu_custom_call" | custom-call | flops 229376 | bytes 1605632 | tf_op jit(solution)/shard_map/fold/pallas_call | solution.py:184
  15.6 3.0 %collective-permute-start.7 = (bf16[128,896]{1,0:T(8,128)(2,1)S(1)}, bf16[128,896]{1,0:T(8,128)(2,1)S(1)}, u32[]{:S(2)}, u32[]{:S(2)}) collective-permute-start(bf16[128,896]{1,0:T(8,128)(2,1)S(1)} %get-tuple-element.39), channel_id=1, source_target_pairs={{0,2},{2,0},{4,6},{6,4},{8,10},{10,8},{12,14},{14,12},{1,3},{3,1},... | collective-permute-start | bytes 688136 | tf_op jit(solution)/shard_map/ppermute | solution.py:291
  18.6 0.6 %fold.5 = (bf16[128,896]{1,0:T(8,128)(2,1)S(1)}, f32[128,896]{1,0:T(8,128)S(1)}) custom-call(s32[5]{0:T(128)S(1)} %stack.23.where_ref, bf16[128,5376]{1,0:T(8,128)(2,1)S(1)} %get-tuple-element.31.keep_ref, bf16[128,5376]{1,0:T(8,128)(2,1)S(1)} %collective-permute-done.3.came_ref), custom_call_target="tpu_custom_call" | custom-call | flops 229376 | bytes 1605632 | tf_op jit(solution)/shard_map/fold/pallas_call | solution.py:184
  19.2 0.1 collective-permute-start.9
  19.3 2.0 %collective-permute-done.5.came_ref = bf16[128,896]{1,0:T(8,128)(2,1)S(1)} collective-permute-done((bf16[128,896]{1,0:T(8,128)(2,1)S(1)}, bf16[128,896]{1,0:T(8,128)(2,1)S(1)}, u32[]{:S(2)}, u32[]{:S(2)}) %collective-permute-start.5) | collective-permute-done | bytes 229408 | tf_op jit(solution)/shard_map/ppermute | solution.py:291
  21.3 0.1 add.9
  21.4 4.1 %collective-permute-start.6 = (bf16[128,896]{1,0:T(8,128)(2,1)S(1)}, bf16[128,896]{1,0:T(8,128)(2,1)S(1)}, u32[]{:S(2)}, u32[]{:S(2)}) collective-permute-start(bf16[128,896]{1,0:T(8,128)(2,1)S(1)} %add.9), channel_id=1, source_target_pairs={{0,12},{2,14},{4,8},{6,10},{8,4},{10,6},{12,0},{14,2},{1,13},{3,15... | collective-permute-start | bytes 688136 | tf_op jit(solution)/shard_map/ppermute | solution.py:291
  25.5 0.6 %fold.3 = (bf16[128,896]{1,0:T(8,128)(2,1)S(1)}, f32[128,896]{1,0:T(8,128)S(1)}) custom-call(s32[5]{0:T(128)S(1)} %stack.23.where_ref, bf16[128,5376]{1,0:T(8,128)(2,1)S(1)} %get-tuple-element.31.keep_ref, bf16[128,5376]{1,0:T(8,128)(2,1)S(1)} %collective-permute-done.3.came_ref), custom_call_target="tpu_custom_call" | custom-call | flops 229376 | bytes 1605632 | tf_op jit(solution)/shard_map/fold/pallas_call | solution.py:184
  26.2 1.6 %collective-permute-start.4 = (bf16[128,896]{1,0:T(8,128)(2,1)S(1)}, bf16[128,896]{1,0:T(8,128)(2,1)S(1)}, u32[]{:S(2)}, u32[]{:S(2)}) collective-permute-start(bf16[128,896]{1,0:T(8,128)(2,1)S(1)} %get-tuple-element.33), channel_id=1, source_target_pairs={{0,2},{2,0},{4,6},{6,4},{8,10},{10,8},{12,14},{14,12},{1,3},{3,1},... | collective-permute-start | bytes 688136 | tf_op jit(solution)/shard_map/ppermute | solution.py:291
  27.7 0.0 collective-permute-done.7.came_ref
  27.7 0.1 add.10
  27.8 1.6 %collective-permute-start.8 = (bf16[128,896]{1,0:T(8,128)(2,1)S(1)}, bf16[128,896]{1,0:T(8,128)(2,1)S(1)}, u32[]{:S(2)}, u32[]{:S(2)}) collective-permute-start(bf16[128,896]{1,0:T(8,128)(2,1)S(1)} %add.10), channel_id=1, source_target_pairs={{0,8},{2,10},{4,12},{6,14},{8,0},{10,2},{12,4},{14,6},{1,9},{3,11}... | collective-permute-start | bytes 688136 | tf_op jit(solution)/shard_map/ppermute | solution.py:291
  29.4 1.7 %collective-permute-done.9.came_ref = bf16[128,896]{1,0:T(8,128)(2,1)S(1)} collective-permute-done((bf16[128,896]{1,0:T(8,128)(2,1)S(1)}, bf16[128,896]{1,0:T(8,128)(2,1)S(1)}, u32[]{:S(2)}, u32[]{:S(2)}) %collective-permute-start.9) | collective-permute-done | bytes 229408 | tf_op jit(solution)/shard_map/ppermute | solution.py:291
  31.2 0.1 add.11
  31.2 2.1 %collective-permute-start.10 = (bf16[128,896]{1,0:T(8,128)(2,1)S(1)}, bf16[128,896]{1,0:T(8,128)(2,1)S(1)}, u32[]{:S(2)}, u32[]{:S(2)}) collective-permute-start(bf16[128,896]{1,0:T(8,128)(2,1)S(1)} %add.11), channel_id=1, source_target_pairs={{0,4},{2,6},{4,0},{6,2},{8,12},{10,14},{12,8},{14,10},{1,5},{3,7},... | collective-permute-start | bytes 688136 | tf_op jit(solution)/shard_map/ppermute | solution.py:291
  33.3 2.8 %input.1 = bf16[128,7168]{1,0:T(8,128)(2,1)} custom-call(bf16[128,128]{1,0:T(8,128)(2,1)S(1)} %get-tuple-element.27.low_ref.lg_ref, bf16[64,7168]{1,0:T(8,128)(2,1)S(1)} %bitcast.14, bf16[64,7168]{1,0:T(8,128)(2,1)S(1)} %collective-permute-done.1.a_in_ref.other_ref), custom_call_target="tpu_custom_call" | custom-call | flops 234881024 | bytes 3670016 | tf_op jit(solution)/shard_map/input/pallas_call | solution.py:265
  36.1 0.0 collective-permute-done.4.refs_2_
  36.1 0.0 collective-permute-done.6.refs_0_
  36.1 8.0 %collective-permute-done.8.refs_1_ = bf16[128,896]{1,0:T(8,128)(2,1)S(1)} collective-permute-done((bf16[128,896]{1,0:T(8,128)(2,1)S(1)}, bf16[128,896]{1,0:T(8,128)(2,1)S(1)}, u32[]{:S(2)}, u32[]{:S(2)}) %collective-permute-start.8) | collective-permute-done | bytes 229408 | tf_op jit(solution)/shard_map/ppermute | solution.py:291
  44.2 0.1 total.1.total_ref
  44.3 0.0 collective-permute-done.10.came_ref
  44.3 0.8 %last.1 = (f32[64,896]{1,0:T(8,128)}, f32[64,896]{1,0:T(8,128)}) custom-call(f32[128,896]{1,0:T(8,128)S(1)} %total.1.total_ref, bf16[128,896]{1,0:T(8,128)(2,1)S(1)} %collective-permute-done.10.came_ref), custom_call_target="tpu_custom_call" | custom-call | flops 114688 | bytes 1146880 | tf_op jit(solution)/shard_map/last/pallas_call | solution.py:239
Async XLA Ops:
  0.6 4.5 %collective-permute-start.1 = (bf16[64,7168]{1,0:T(8,128)(2,1)}, bf16[64,7168]{1,0:T(8,128)(2,1)S(1)}, u32[]{:S(2)}, u32[]{:S(2)}) collective-permute-start(bf16[64,7168]{1,0:T(8,128)(2,1)} %bitcast.12), channel_id=1, source_target_pairs={{0,1},{1,0},{2,3},{3,2},{4,5},{5,4},{6,7},{7,6},{8,9},{9,8},{10,11... | collective-permute-start | bytes 2752520 | tf_op jit(solution)/shard_map/ppermute | solution.py:287
  1.1 4.0 %collective-permute-start = (bf16[64,7168]{1,0:T(8,128)(2,1)}, bf16[64,7168]{1,0:T(8,128)(2,1)S(1)}, u32[]{:S(2)}, u32[]{:S(2)}) collective-permute-start(bf16[64,7168]{1,0:T(8,128)(2,1)} %bitcast.15), channel_id=1, source_target_pairs={{0,1},{1,0},{2,3},{3,2},{4,5},{5,4},{6,7},{7,6},{8,9},{9,8},{10,11... | collective-permute-start | bytes 2752520 | tf_op jit(solution)/shard_map/ppermute | solution.py:287
  1.3 1.2 %copy-start.1 = (bf16[4,16,7168]{2,1,0:T(8,128)(2,1)S(1)}, bf16[4,16,7168]{2,1,0:T(8,128)(2,1)}, u32[]{:S(2)}) copy-start(bf16[4,16,7168]{2,1,0:T(8,128)(2,1)} %param.11) | copy-start | bytes 2752516
  2.5 2.7 %copy-start = (bf16[4,16,7168]{2,1,0:T(8,128)(2,1)S(1)}, bf16[4,16,7168]{2,1,0:T(8,128)(2,1)}, u32[]{:S(2)}) copy-start(bf16[4,16,7168]{2,1,0:T(8,128)(2,1)} %param.10) | copy-start | bytes 2752516
  2.5 2.7 %copy-start.2 = (s32[128,2]{0,1:T(2,128)S(1)}, s32[128,2]{0,1:T(2,128)}, u32[]{:S(2)}) copy-start(s32[128,2]{0,1:T(2,128)} %param.8) | copy-start | bytes 3076
  2.5 2.7 %copy-start.3 = (f32[128,2]{0,1:T(2,128)S(1)}, f32[128,2]{0,1:T(2,128)}, u32[]{:S(2)}) copy-start(f32[128,2]{0,1:T(2,128)} %param.9) | copy-start | bytes 3076
  8.3 1.9 %collective-permute-start.2 = (bf16[128,1792]{1,0:T(8,128)(2,1)S(1)}, bf16[128,1792]{1,0:T(8,128)(2,1)S(1)}, u32[]{:S(2)}, u32[]{:S(2)}) collective-permute-start(bf16[128,1792]{1,0:T(8,128)(2,1)S(1)} %get-tuple-element.29), channel_id=1, source_target_pairs={{0,1},{1,0},{2,3},{3,2},{4,5},{5,4},{6,7},{7,6},{8,9},{9,8},{10,11... | collective-permute-start | bytes 1376264 | tf_op jit(solution)/shard_map/ppermute | solution.py:287
  11.8 3.2 %collective-permute-start.3 = (bf16[128,5376]{1,0:T(8,128)(2,1)S(1)}, bf16[128,5376]{1,0:T(8,128)(2,1)S(1)}, u32[]{:S(2)}, u32[]{:S(2)}) collective-permute-start(bf16[128,5376]{1,0:T(8,128)(2,1)S(1)} %get-tuple-element.32), channel_id=1, source_target_pairs={{0,1},{1,0},{2,3},{3,2},{4,5},{5,4},{6,7},{7,6},{8,9},{9,8},{10,11... | collective-permute-start | bytes 4128776 | tf_op jit(solution)/shard_map/ppermute | solution.py:287
  12.2 9.1 %collective-permute-start.5 = (bf16[128,896]{1,0:T(8,128)(2,1)S(1)}, bf16[128,896]{1,0:T(8,128)(2,1)S(1)}, u32[]{:S(2)}, u32[]{:S(2)}) collective-permute-start(bf16[128,896]{1,0:T(8,128)(2,1)S(1)} %get-tuple-element.37), channel_id=1, source_target_pairs={{0,2},{2,0},{4,6},{6,4},{8,10},{10,8},{12,14},{14,12},{1,3},{3,1},... | collective-permute-start | bytes 688136 | tf_op jit(solution)/shard_map/ppermute | solution.py:291
  15.6 12.1 %collective-permute-start.7 = (bf16[128,896]{1,0:T(8,128)(2,1)S(1)}, bf16[128,896]{1,0:T(8,128)(2,1)S(1)}, u32[]{:S(2)}, u32[]{:S(2)}) collective-permute-start(bf16[128,896]{1,0:T(8,128)(2,1)S(1)} %get-tuple-element.39), channel_id=1, source_target_pairs={{0,2},{2,0},{4,6},{6,4},{8,10},{10,8},{12,14},{14,12},{1,3},{3,1},... | collective-permute-start | bytes 688136 | tf_op jit(solution)/shard_map/ppermute | solution.py:291
  19.2 11.9 %collective-permute-start.9 = (bf16[128,896]{1,0:T(8,128)(2,1)S(1)}, bf16[128,896]{1,0:T(8,128)(2,1)S(1)}, u32[]{:S(2)}, u32[]{:S(2)}) collective-permute-start(bf16[128,896]{1,0:T(8,128)(2,1)S(1)} %get-tuple-element.42), channel_id=1, source_target_pairs={{0,2},{2,0},{4,6},{6,4},{8,10},{10,8},{12,14},{14,12},{1,3},{3,1},... | collective-permute-start | bytes 688136 | tf_op jit(solution)/shard_map/ppermute | solution.py:291
  21.4 14.7 %collective-permute-start.6 = (bf16[128,896]{1,0:T(8,128)(2,1)S(1)}, bf16[128,896]{1,0:T(8,128)(2,1)S(1)}, u32[]{:S(2)}, u32[]{:S(2)}) collective-permute-start(bf16[128,896]{1,0:T(8,128)(2,1)S(1)} %add.9), channel_id=1, source_target_pairs={{0,12},{2,14},{4,8},{6,10},{8,4},{10,6},{12,0},{14,2},{1,13},{3,15... | collective-permute-start | bytes 688136 | tf_op jit(solution)/shard_map/ppermute | solution.py:291
  26.2 10.0 %collective-permute-start.4 = (bf16[128,896]{1,0:T(8,128)(2,1)S(1)}, bf16[128,896]{1,0:T(8,128)(2,1)S(1)}, u32[]{:S(2)}, u32[]{:S(2)}) collective-permute-start(bf16[128,896]{1,0:T(8,128)(2,1)S(1)} %get-tuple-element.33), channel_id=1, source_target_pairs={{0,2},{2,0},{4,6},{6,4},{8,10},{10,8},{12,14},{14,12},{1,3},{3,1},... | collective-permute-start | bytes 688136 | tf_op jit(solution)/shard_map/ppermute | solution.py:291
  27.8 16.4 %collective-permute-start.8 = (bf16[128,896]{1,0:T(8,128)(2,1)S(1)}, bf16[128,896]{1,0:T(8,128)(2,1)S(1)}, u32[]{:S(2)}, u32[]{:S(2)}) collective-permute-start(bf16[128,896]{1,0:T(8,128)(2,1)S(1)} %add.10), channel_id=1, source_target_pairs={{0,8},{2,10},{4,12},{6,14},{8,0},{10,2},{12,4},{14,6},{1,9},{3,11}... | collective-permute-start | bytes 688136 | tf_op jit(solution)/shard_map/ppermute | solution.py:291
  31.2 13.1 %collective-permute-start.10 = (bf16[128,896]{1,0:T(8,128)(2,1)S(1)}, bf16[128,896]{1,0:T(8,128)(2,1)S(1)}, u32[]{:S(2)}, u32[]{:S(2)}) collective-permute-start(bf16[128,896]{1,0:T(8,128)(2,1)S(1)} %add.11), channel_id=1, source_target_pairs={{0,4},{2,6},{4,0},{6,2},{8,12},{10,14},{12,8},{14,10},{1,5},{3,7},... | collective-permute-start | bytes 688136 | tf_op jit(solution)/shard_map/ppermute | solution.py:291

commit v6 on v5

--- a/solution.py
+++ b/solution.py
@@ -195,56 +195,88 @@
     )(where, keep, came)
 
 
-def add_kernel(keep_ref, came_ref, out_ref):
-    out_ref[...] = (keep_ref[...] + came_ref[...].astype(F32)).astype(out_ref.dtype)
-
-
-def add(keep, came):
+def add_kernel(keep_ref, *refs):
+    came, out_ref = refs[:-1], refs[-1]
+    total = keep_ref[...]
+    for ref in came:
+        total = total + ref[...].astype(F32)
+    out_ref[...] = total.astype(out_ref.dtype)
+
+
+def add(keep, *came):
     return pl.pallas_call(
         add_kernel,
+        in_specs=[VECTORS] * (1 + len(came)),
+        out_specs=VECTORS,
         out_shape=jax.ShapeDtypeStruct(keep.shape, BF16),
         compiler_params=params(),
         cost_estimate=cost(keep.size, 8 * keep.size),
         name="add",
+    )(keep, *came)
+
+
+def halves_kernel(keep_ref, came_ref, *outs):
+    rows = outs[0].shape[0]
+    for half, out in enumerate(outs):
+        part = pl.ds(half * rows, rows)
+        out[...] = (keep_ref[part, :] + came_ref[part, :].astype(F32)).astype(out.dtype)
+
+
+def add_halves(keep, came, dtypes):
+    rows, block = keep.shape[0] // 2, keep.shape[1]
+    return pl.pallas_call(
+        halves_kernel,
+        in_specs=[VECTORS] * 2,
+        out_specs=[VECTORS] * 2,
+        out_shape=[jax.ShapeDtypeStruct((rows, block), dtype) for dtype in dtypes],
+        compiler_params=params(),
+        cost_estimate=cost(keep.size, 9 * keep.size),
+        name="halves",
     )(keep, came)
 
 
-def total_kernel(keep_ref, *refs):
-    total = keep_ref[...]
-    for ref in refs[:-1]:
-        total = total + ref[...].astype(F32)
-    refs[-1][...] = total
-
-
-def total(keep, came):
-    return pl.pallas_call(
-        total_kernel,
+def total_kernel(both, downs, keep_ref, *refs):
+    came, outs = refs[: len(refs) - 2], refs[len(refs) - 2 :]
+    rows = outs[0].shape[0]
+    for half, out in enumerate(outs):
+        part = pl.ds(half * rows, rows)
+        total = keep_ref[part, :]
+        for ref in came[:both]:
+            total = total + ref[part, :].astype(F32)
+        for ref in came[both:][slice(downs) if half == 0 else slice(downs, None)]:
+            total = total + ref[...].astype(F32)
+        out[...] = total
+
+
+def total(keep, both, downs, ups):
+    rows, block = keep.shape[0] // 2, keep.shape[1]
+    came = [*both, *downs, *ups]
+    return pl.pallas_call(
+        functools.partial(total_kernel, len(both), len(downs)),
         in_specs=[VECTORS] * (1 + len(came)),
-        out_specs=VECTORS,
-        out_shape=jax.ShapeDtypeStruct(keep.shape, F32),
+        out_specs=[VECTORS] * 2,
+        out_shape=[jax.ShapeDtypeStruct((rows, block), F32)] * 2,
         compiler_params=params(),
         cost_estimate=cost(keep.size * len(came), keep.size * (8 + 2 * len(came))),
         name="total",
     )(keep, *came)
 
 
-def last_kernel(total_ref, came_ref, down_ref, up_ref):
-    rows = down_ref.shape[0]
-    down_ref[...] = total_ref[:rows] + came_ref[:rows].astype(F32)
-    up_ref[...] = total_ref[rows:] + came_ref[rows:].astype(F32)
-
-
-def last(total, came):
-    rows, block = total.shape[0] // 2, total.shape[1]
+def last_kernel(down_in, up_in, down_came, up_came, down_ref, up_ref):
+    down_ref[...] = down_in[...] + down_came[...].astype(F32)
+    up_ref[...] = up_in[...] + up_came[...].astype(F32)
+
+
+def last(down, up, down_came, up_came):
     return pl.pallas_call(
         last_kernel,
-        in_specs=[VECTORS] * 2,
+        in_specs=[VECTORS] * 4,
         out_specs=[VECTORS] * 2,
-        out_shape=[jax.ShapeDtypeStruct((rows, block), F32)] * 2,
-        compiler_params=params(),
-        cost_estimate=cost(came.size, 10 * came.size),
+        out_shape=[jax.ShapeDtypeStruct(down.shape, F32)] * 2,
+        compiler_params=params(),
+        cost_estimate=cost(down.size, 10 * down.size),
         name="last",
-    )(total, came)
+    )(down, up, down_came, up_came)
 
 
 def input_kernel(low_ref, own_ref, other_ref, out_ref):
@@ -305,20 +337,26 @@
     )
     rest_came = swap(rest_pair)
     send, own = first
-    came = []
+    both, downs, ups = [], [], []
     for i, step in enumerate(order):
         if i:
             send, own = fold(where, block, i - 1, rest_keep, rest_came)
         got = flip(send, 1)
         if step == 0:
-            came.append(got)
+            both.append(got)
         elif step == 1:
-            nearest = flip(add(own, got), 2)
+            nearest = [flip(half, 2) for half in add_halves(own, got, (BF16, BF16))]
+        elif steps != 4:
+            both.append(flip(add(own, got), 2 * step))
+        elif step == 3:
+            passed = [flip(half, 2) for half in add_halves(own, got, (BF16, BF16))]
         else:
-            came.append(flip(add(own, got), 2 * step))
+            mine = add_halves(own, got, (F32, F32))
+            for half, came, into in zip(mine, passed, (downs, ups)):
+                into.append(flip(add(half, came), 4))
     input_grad = input_gradient(lg, a, a_in)
-    input_grad, came[-1] = lax.optimization_barrier((input_grad, came[-1]))
-    down, up = last(total(own, came), nearest)
+    input_grad, both[-1] = lax.optimization_barrier((input_grad, both[-1]))
+    down, up = last(*total(own, both, downs, ups), *nearest)
     return input_grad, down.reshape(count, rank, block), up.reshape(count, rank, block)
 
 

time: 45.3 us -> 42.5 us (0.938); the launches traced: 45.1 us -> 41.8 us
  waiting for transfers between devices: 13.3 us -> 9.3 us
  starting transfers between devices: 16.6 us -> 17.4 us
    ppermute x7 -> x10, waiting for transfers between devices: 11.8 us -> 7.77 us  [shards(): lax.ppermute(array, 'dp', [(i, i ^ by) for i in range(replicas)])]
    ppermute x7 -> x10, starting transfers between devices: 15.1 us -> 15.9 us  [shards(): lax.ppermute(array, 'dp', [(i, i ^ by) for i in range(replicas)])]
    pallas_call x5 -> x7, Pallas kernels: 1.08 us -> 1.05 us  [the longest x1 0.8 us: last(): pl.pallas_call(last_kernel, in_specs=[VECTORS] * 4, out_specs=[VECTORS] *...]
  transfers between devices with their start and end apart: 11 -> 14, of which waited for: 5 -> 9; matrix products, arithmetic and copies ran while one was open for 0% -> 0% of each run, Pallas kernels for 17% -> 18%
where the time goes in v6:
time: 42.5 us; the launch traced here: 41.8 us
  starting transfers between devices  17.4 us (41%)
  Pallas kernels  13.1 us (31%)
  waiting for transfers between devices  9.3 us (22%)
  local copies, waits for them, and re-layouts  1.27 us (3%)
  between operations  0.75 us (2%)
    ppermute x10, starting transfers between devices, shards(): lax.ppermute(array, 'dp', [(i, i ^ by) for i in range(replicas)])  15.9 us
    ppermute x10, waiting for transfers between devices, shards(): lax.ppermute(array, 'dp', [(i, i ^ by) for i in range(replicas)])  7.77 us
    pallas_call x1, Pallas kernels, low_products(): pl.pallas_call(functools.partial(low_kernel, rank), in_specs=[SCALARS] *...  3.09 us
    pallas_call x1, Pallas kernels, input_gradient(): pl.pallas_call(input_kernel, grid=(steps,), in_specs=[VECTORS] * 3, out_s...  2.81 us
    pallas_call x1, Pallas kernels, own_products(): pl.pallas_call(own_kernel, in_specs=[ANYWHERE] * 3, out_specs=[VECTORS] *...  2.62 us
    pallas_call x3, Pallas kernels, fold(): pl.pallas_call(functools.partial(fold_kernel, block, at), in_specs=[SCALA...  1.94 us
    pallas_call x1, Pallas kernels, rest_products(): pl.pallas_call(functools.partial(rest_kernel, blocks, block), in_specs=[S...  1.57 us
    ppermute x4, waiting for transfers between devices, shards(): swap = lambda array: lax.ppermute(array, 'adapter', SWAP)  1.54 us
  transfers between devices with their start and end apart: 14, of which 9 were waited for; matrix products, arithmetic and copies ran while one was open for 0% of the time, Pallas kernels for 18%

profile of v6, /device:TPU:0, one launch (start us, length us, event | category | flops | bytes accessed | tf_op | source)
XLA Modules:
  0.0 41.8 jit_solution(11053045391905512654)
XLA Ops:
  0.6 0.5 %collective-permute-start.1 = (bf16[64,7168]{1,0:T(8,128)(2,1)}, bf16[64,7168]{1,0:T(8,128)(2,1)S(1)}, u32[]{:S(2)}, u32[]{:S(2)}) collective-permute-start(bf16[64,7168]{1,0:T(8,128)(2,1)} %bitcast.12), channel_id=1, source_target_pairs={{0,1},{1,0},{2,3},{3,2},{4,5},{5,4},{6,7},{7,6},{8,9},{9,8},{10,11... | collective-permute-start | bytes 2752520 | tf_op jit(solution)/shard_map/ppermute | solution.py:319
  1.1 0.1 collective-permute-start
  1.2 0.1 stack.23.where_ref
  1.3 0.0 copy-start.1
  1.3 1.2 %copy-done.1 = bf16[4,16,7168]{2,1,0:T(8,128)(2,1)S(1)} copy-done((bf16[4,16,7168]{2,1,0:T(8,128)(2,1)S(1)}, bf16[4,16,7168]{2,1,0:T(8,128)(2,1)}, u32[]{:S(2)}) %copy-start.1) | copy-done | bytes 917528
  2.5 0.0 copy-start
  2.5 0.0 copy-start.2
  2.5 0.0 copy-start.3
  2.5 2.6 %own.1 = (f32[64,128]{1,0:T(8,128)S(1)}, bf16[128,7168]{1,0:T(8,128)(2,1)S(1)}, bf16[128,7168]{1,0:T(8,128)(2,1)S(1)}) custom-call(bf16[64,7168]{1,0:T(8,128)(2,1)S(1)} %bitcast.16, bf16[128,7168]{1,0:T(8,128)(2,1)} %g_hbm.1, bf16[128,7168]{1,0:T(8,128)(2,1)} %x_hbm.1), custom_call_target="tpu_custom_call" | custom-call | flops 117440512 | bytes 5505024 | tf_op jit(solution)/shard_map/own/pallas_call | solution.py:65
  5.1 0.0 collective-permute-done.1.a_in_ref.other_ref
  5.1 0.0 collective-permute-done.b_ref
  5.1 0.0 copy-done
  5.2 0.0 copy-done.2
  5.2 0.0 copy-done.3
  5.2 3.1 %low.1 = (bf16[128,128]{1,0:T(8,128)(2,1)S(1)}, bf16[128,128]{1,0:T(8,128)(2,1)S(1)}, bf16[128,1792]{1,0:T(8,128)(2,1)S(1)}, bf16[128,1792]{1,0:T(8,128)(2,1)S(1)}) custom-call(s32[1]{0:T(128)} %bitcast.core_ref, s32[5]{0:T(128)S(1)} %stack.23.where_ref, s32[2,128]{1,0:T(2,128)S(1)} %bitcast.17, f32[2,128]{1,0:T(2,128)S(1)} %bitcast.18, ...), custom_call_target="tpu_custom_call" | custom-call | flops 352321536 | bytes 5505024 | tf_op jit(solution)/shard_map/low/pallas_call | solution.py:130
  8.3 0.5 %collective-permute-start.2 = (bf16[128,1792]{1,0:T(8,128)(2,1)S(1)}, bf16[128,1792]{1,0:T(8,128)(2,1)S(1)}, u32[]{:S(2)}, u32[]{:S(2)}) collective-permute-start(bf16[128,1792]{1,0:T(8,128)(2,1)S(1)} %get-tuple-element.37), channel_id=1, source_target_pairs={{0,1},{1,0},{2,3},{3,2},{4,5},{5,4},{6,7},{7,6},{8,9},{9,8},{10,11... | collective-permute-start | bytes 1376264 | tf_op jit(solution)/shard_map/ppermute | solution.py:319
  8.8 1.4 %collective-permute-done.2.came_ref = bf16[128,1792]{1,0:T(8,128)(2,1)S(1)} collective-permute-done((bf16[128,1792]{1,0:T(8,128)(2,1)S(1)}, bf16[128,1792]{1,0:T(8,128)(2,1)S(1)}, u32[]{:S(2)}, u32[]{:S(2)}) %collective-permute-start.2) | collective-permute-done | bytes 458784 | tf_op jit(solution)/shard_map/ppermute | solution.py:319
  10.2 1.6 %rest.1 = (bf16[128,5376]{1,0:T(8,128)(2,1)S(1)}, bf16[128,5376]{1,0:T(8,128)(2,1)S(1)}, bf16[128,896]{1,0:T(8,128)(2,1)S(1)}, f32[128,896]{1,0:T(8,128)S(1)}) custom-call(s32[5]{0:T(128)S(1)} %stack.23.where_ref, bf16[128,1792]{1,0:T(8,128)(2,1)S(1)} %get-tuple-element.36.kept_ref, bf16[128,1792]{1,0:T(8,128)(2,1)S(1)} %collective-permute-done.2.came_ref, ...), custom_call_target="tpu_custom_call" | custom-call | flops 176160768 | bytes 2752512 | tf_op jit(solution)/shard_map/rest/pallas_call | solution.py:159
  11.8 0.4 %collective-permute-start.3 = (bf16[128,5376]{1,0:T(8,128)(2,1)S(1)}, bf16[128,5376]{1,0:T(8,128)(2,1)S(1)}, u32[]{:S(2)}, u32[]{:S(2)}) collective-permute-start(bf16[128,5376]{1,0:T(8,128)(2,1)S(1)} %get-tuple-element.40), channel_id=1, source_target_pairs={{0,1},{1,0},{2,3},{3,2},{4,5},{5,4},{6,7},{7,6},{8,9},{9,8},{10,11... | collective-permute-start | bytes 4128776 | tf_op jit(solution)/shard_map/ppermute | solution.py:319
  12.2 2.7 %collective-permute-start.6 = (bf16[128,896]{1,0:T(8,128)(2,1)S(1)}, bf16[128,896]{1,0:T(8,128)(2,1)S(1)}, u32[]{:S(2)}, u32[]{:S(2)}) collective-permute-start(bf16[128,896]{1,0:T(8,128)(2,1)S(1)} %get-tuple-element.49), channel_id=1, source_target_pairs={{0,2},{2,0},{4,6},{6,4},{8,10},{10,8},{12,14},{14,12},{1,3},{3,1},... | collective-permute-start | bytes 688136 | tf_op jit(solution)/shard_map/ppermute | solution.py:323
  14.9 0.1 collective-permute-done.3.came_ref
  15.0 0.6 %fold.4 = (bf16[128,896]{1,0:T(8,128)(2,1)S(1)}, f32[128,896]{1,0:T(8,128)S(1)}) custom-call(s32[5]{0:T(128)S(1)} %stack.23.where_ref, bf16[128,5376]{1,0:T(8,128)(2,1)S(1)} %get-tuple-element.39.keep_ref, bf16[128,5376]{1,0:T(8,128)(2,1)S(1)} %collective-permute-done.3.came_ref), custom_call_target="tpu_custom_call" | custom-call | flops 229376 | bytes 1605632 | tf_op jit(solution)/shard_map/fold/pallas_call | solution.py:184
  15.6 3.0 %collective-permute-start.5 = (bf16[128,896]{1,0:T(8,128)(2,1)S(1)}, bf16[128,896]{1,0:T(8,128)(2,1)S(1)}, u32[]{:S(2)}, u32[]{:S(2)}) collective-permute-start(bf16[128,896]{1,0:T(8,128)(2,1)S(1)} %get-tuple-element.46), channel_id=1, source_target_pairs={{0,2},{2,0},{4,6},{6,4},{8,10},{10,8},{12,14},{14,12},{1,3},{3,1},... | collective-permute-start | bytes 688136 | tf_op jit(solution)/shard_map/ppermute | solution.py:323
  18.6 0.6 %fold.5 = (bf16[128,896]{1,0:T(8,128)(2,1)S(1)}, f32[128,896]{1,0:T(8,128)S(1)}) custom-call(s32[5]{0:T(128)S(1)} %stack.23.where_ref, bf16[128,5376]{1,0:T(8,128)(2,1)S(1)} %get-tuple-element.39.keep_ref, bf16[128,5376]{1,0:T(8,128)(2,1)S(1)} %collective-permute-done.3.came_ref), custom_call_target="tpu_custom_call" | custom-call | flops 229376 | bytes 1605632 | tf_op jit(solution)/shard_map/fold/pallas_call | solution.py:184
  19.2 0.1 collective-permute-start.11
  19.3 2.0 %collective-permute-done.6.came_ref = bf16[128,896]{1,0:T(8,128)(2,1)S(1)} collective-permute-done((bf16[128,896]{1,0:T(8,128)(2,1)S(1)}, bf16[128,896]{1,0:T(8,128)(2,1)S(1)}, u32[]{:S(2)}, u32[]{:S(2)}) %collective-permute-start.6) | collective-permute-done | bytes 229408 | tf_op jit(solution)/shard_map/ppermute | solution.py:323
  21.4 2.1 %collective-permute-start.9 = (bf16[64,896]{1,0:T(8,128)(2,1)S(1)}, bf16[64,896]{1,0:T(8,128)(2,1)S(1)}, u32[]{:S(2)}, u32[]{:S(2)}) collective-permute-start(bf16[64,896]{1,0:T(8,128)(2,1)S(1)} %get-tuple-element.52), channel_id=1, source_target_pairs={{0,4},{2,6},{4,0},{6,2},{8,12},{10,14},{12,8},{14,10},{1,5},{3,7},... | collective-permute-start | bytes 344072 | tf_op jit(solution)/shard_map/ppermute | solution.py:323
  23.5 0.1 collective-permute-start.7
  23.5 0.6 %fold.3 = (bf16[128,896]{1,0:T(8,128)(2,1)S(1)}, f32[128,896]{1,0:T(8,128)S(1)}) custom-call(s32[5]{0:T(128)S(1)} %stack.23.where_ref, bf16[128,5376]{1,0:T(8,128)(2,1)S(1)} %get-tuple-element.39.keep_ref, bf16[128,5376]{1,0:T(8,128)(2,1)S(1)} %collective-permute-done.3.came_ref), custom_call_target="tpu_custom_call" | custom-call | flops 229376 | bytes 1605632 | tf_op jit(solution)/shard_map/fold/pallas_call | solution.py:184
  24.2 2.0 %collective-permute-start.4 = (bf16[128,896]{1,0:T(8,128)(2,1)S(1)}, bf16[128,896]{1,0:T(8,128)(2,1)S(1)}, u32[]{:S(2)}, u32[]{:S(2)}) collective-permute-start(bf16[128,896]{1,0:T(8,128)(2,1)S(1)} %get-tuple-element.41), channel_id=1, source_target_pairs={{0,2},{2,0},{4,6},{6,4},{8,10},{10,8},{12,14},{14,12},{1,3},{3,1},... | collective-permute-start | bytes 688136 | tf_op jit(solution)/shard_map/ppermute | solution.py:323
  26.2 0.1 collective-permute-done.5.came_ref
  26.3 1.0 %collective-permute-done.9.refs_0_ = bf16[64,896]{1,0:T(8,128)(2,1)S(1)} collective-permute-done((bf16[64,896]{1,0:T(8,128)(2,1)S(1)}, bf16[64,896]{1,0:T(8,128)(2,1)S(1)}, u32[]{:S(2)}, u32[]{:S(2)}) %collective-permute-start.9) | collective-permute-done | bytes 114720 | tf_op jit(solution)/shard_map/ppermute | solution.py:323
  27.3 2.7 %collective-permute-start.10 = (bf16[64,896]{1,0:T(8,128)(2,1)S(1)}, bf16[64,896]{1,0:T(8,128)(2,1)S(1)}, u32[]{:S(2)}, u32[]{:S(2)}) collective-permute-start(bf16[64,896]{1,0:T(8,128)(2,1)S(1)} %add.9), channel_id=1, source_target_pairs={{0,8},{2,10},{4,12},{6,14},{8,0},{10,2},{12,4},{14,6},{1,9},{3,11}... | collective-permute-start | bytes 344072 | tf_op jit(solution)/shard_map/ppermute | solution.py:323
  29.9 0.0 collective-permute-done.7.refs_0_
  30.0 1.3 %collective-permute-start.8 = (bf16[64,896]{1,0:T(8,128)(2,1)S(1)}, bf16[64,896]{1,0:T(8,128)(2,1)S(1)}, u32[]{:S(2)}, u32[]{:S(2)}) collective-permute-start(bf16[64,896]{1,0:T(8,128)(2,1)S(1)} %add.8), channel_id=1, source_target_pairs={{0,8},{2,10},{4,12},{6,14},{8,0},{10,2},{12,4},{14,6},{1,9},{3,11}... | collective-permute-start | bytes 344072 | tf_op jit(solution)/shard_map/ppermute | solution.py:323
  31.2 0.0 collective-permute-done.11.came_ref
  31.2 0.1 halves.5
  31.3 2.0 %collective-permute-start.12 = (bf16[64,896]{1,0:T(8,128)(2,1)S(1)}, bf16[64,896]{1,0:T(8,128)(2,1)S(1)}, u32[]{:S(2)}, u32[]{:S(2)}) collective-permute-start(bf16[64,896]{1,0:T(8,128)(2,1)S(1)} %get-tuple-element.57), channel_id=1, source_target_pairs={{0,4},{2,6},{4,0},{6,2},{8,12},{10,14},{12,8},{14,10},{1,5},{3,7},... | collective-permute-start | bytes 344072 | tf_op jit(solution)/shard_map/ppermute | solution.py:323
  33.3 0.1 collective-permute-start.13
  33.4 2.8 %input.1 = bf16[128,7168]{1,0:T(8,128)(2,1)} custom-call(bf16[128,128]{1,0:T(8,128)(2,1)S(1)} %get-tuple-element.35.low_ref.lg_ref, bf16[64,7168]{1,0:T(8,128)(2,1)S(1)} %bitcast.14, bf16[64,7168]{1,0:T(8,128)(2,1)S(1)} %collective-permute-done.1.a_in_ref.other_ref), custom_call_target="tpu_custom_call" | custom-call | flops 234881024 | bytes 3670016 | tf_op jit(solution)/shard_map/input/pallas_call | solution.py:297
  36.2 0.0 collective-permute-done.4.refs_0_
  36.2 1.8 %collective-permute-done.10.refs_2_ = bf16[64,896]{1,0:T(8,128)(2,1)S(1)} collective-permute-done((bf16[64,896]{1,0:T(8,128)(2,1)S(1)}, bf16[64,896]{1,0:T(8,128)(2,1)S(1)}, u32[]{:S(2)}, u32[]{:S(2)}) %collective-permute-start.10) | collective-permute-done | bytes 114720 | tf_op jit(solution)/shard_map/ppermute | solution.py:323
  38.0 1.3 %collective-permute-done.8.refs_1_ = bf16[64,896]{1,0:T(8,128)(2,1)S(1)} collective-permute-done((bf16[64,896]{1,0:T(8,128)(2,1)S(1)}, bf16[64,896]{1,0:T(8,128)(2,1)S(1)}, u32[]{:S(2)}, u32[]{:S(2)}) %collective-permute-start.8) | collective-permute-done | bytes 114720 | tf_op jit(solution)/shard_map/ppermute | solution.py:323
  39.2 0.1 total.1
  39.3 0.4 %collective-permute-done.12.down_came = bf16[64,896]{1,0:T(8,128)(2,1)S(1)} collective-permute-done((bf16[64,896]{1,0:T(8,128)(2,1)S(1)}, bf16[64,896]{1,0:T(8,128)(2,1)S(1)}, u32[]{:S(2)}, u32[]{:S(2)}) %collective-permute-start.12) | collective-permute-done | bytes 114720 | tf_op jit(solution)/shard_map/ppermute | solution.py:323
  39.7 1.2 %collective-permute-done.13.up_came = bf16[64,896]{1,0:T(8,128)(2,1)S(1)} collective-permute-done((bf16[64,896]{1,0:T(8,128)(2,1)S(1)}, bf16[64,896]{1,0:T(8,128)(2,1)S(1)}, u32[]{:S(2)}, u32[]{:S(2)}) %collective-permute-start.13) | collective-permute-done | bytes 114720 | tf_op jit(solution)/shard_map/ppermute | solution.py:323
  41.0 0.8 %last.1 = (f32[64,896]{1,0:T(8,128)}, f32[64,896]{1,0:T(8,128)}) custom-call(f32[64,896]{1,0:T(8,128)S(1)} %get-tuple-element.53.down_in, f32[64,896]{1,0:T(8,128)S(1)} %get-tuple-element.54.up_in, bf16[64,896]{1,0:T(8,128)(2,1)S(1)} %collective-permute-done.12.down_came, bf16[64,896]{1,0:T(8,128)(2,1)S(1)} %collective-permute-done.13.up_came), custom_call_target="tpu_custom_call" | custom-call | flops 57344 | bytes 573440 | tf_op jit(solution)/shard_map/last/pallas_call | solution.py:271
  (4 shorter events, 0.1 us)
Async XLA Ops:
  0.6 4.5 %collective-permute-start.1 = (bf16[64,7168]{1,0:T(8,128)(2,1)}, bf16[64,7168]{1,0:T(8,128)(2,1)S(1)}, u32[]{:S(2)}, u32[]{:S(2)}) collective-permute-start(bf16[64,7168]{1,0:T(8,128)(2,1)} %bitcast.12), channel_id=1, source_target_pairs={{0,1},{1,0},{2,3},{3,2},{4,5},{5,4},{6,7},{7,6},{8,9},{9,8},{10,11... | collective-permute-start | bytes 2752520 | tf_op jit(solution)/shard_map/ppermute | solution.py:319
  1.1 4.0 %collective-permute-start = (bf16[64,7168]{1,0:T(8,128)(2,1)}, bf16[64,7168]{1,0:T(8,128)(2,1)S(1)}, u32[]{:S(2)}, u32[]{:S(2)}) collective-permute-start(bf16[64,7168]{1,0:T(8,128)(2,1)} %bitcast.15), channel_id=1, source_target_pairs={{0,1},{1,0},{2,3},{3,2},{4,5},{5,4},{6,7},{7,6},{8,9},{9,8},{10,11... | collective-permute-start | bytes 2752520 | tf_op jit(solution)/shard_map/ppermute | solution.py:319
  1.3 1.2 %copy-start.1 = (bf16[4,16,7168]{2,1,0:T(8,128)(2,1)S(1)}, bf16[4,16,7168]{2,1,0:T(8,128)(2,1)}, u32[]{:S(2)}) copy-start(bf16[4,16,7168]{2,1,0:T(8,128)(2,1)} %param.11) | copy-start | bytes 2752516
  2.5 2.7 %copy-start = (bf16[4,16,7168]{2,1,0:T(8,128)(2,1)S(1)}, bf16[4,16,7168]{2,1,0:T(8,128)(2,1)}, u32[]{:S(2)}) copy-start(bf16[4,16,7168]{2,1,0:T(8,128)(2,1)} %param.10) | copy-start | bytes 2752516
  2.5 2.7 %copy-start.2 = (s32[128,2]{0,1:T(2,128)S(1)}, s32[128,2]{0,1:T(2,128)}, u32[]{:S(2)}) copy-start(s32[128,2]{0,1:T(2,128)} %param.8) | copy-start | bytes 3076
  2.5 2.7 %copy-start.3 = (f32[128,2]{0,1:T(2,128)S(1)}, f32[128,2]{0,1:T(2,128)}, u32[]{:S(2)}) copy-start(f32[128,2]{0,1:T(2,128)} %param.9) | copy-start | bytes 3076
  8.3 1.9 %collective-permute-start.2 = (bf16[128,1792]{1,0:T(8,128)(2,1)S(1)}, bf16[128,1792]{1,0:T(8,128)(2,1)S(1)}, u32[]{:S(2)}, u32[]{:S(2)}) collective-permute-start(bf16[128,1792]{1,0:T(8,128)(2,1)S(1)} %get-tuple-element.37), channel_id=1, source_target_pairs={{0,1},{1,0},{2,3},{3,2},{4,5},{5,4},{6,7},{7,6},{8,9},{9,8},{10,11... | collective-permute-start | bytes 1376264 | tf_op jit(solution)/shard_map/ppermute | solution.py:319
  11.8 3.2 %collective-permute-start.3 = (bf16[128,5376]{1,0:T(8,128)(2,1)S(1)}, bf16[128,5376]{1,0:T(8,128)(2,1)S(1)}, u32[]{:S(2)}, u32[]{:S(2)}) collective-permute-start(bf16[128,5376]{1,0:T(8,128)(2,1)S(1)} %get-tuple-element.40), channel_id=1, source_target_pairs={{0,1},{1,0},{2,3},{3,2},{4,5},{5,4},{6,7},{7,6},{8,9},{9,8},{10,11... | collective-permute-start | bytes 4128776 | tf_op jit(solution)/shard_map/ppermute | solution.py:319
  12.2 9.1 %collective-permute-start.6 = (bf16[128,896]{1,0:T(8,128)(2,1)S(1)}, bf16[128,896]{1,0:T(8,128)(2,1)S(1)}, u32[]{:S(2)}, u32[]{:S(2)}) collective-permute-start(bf16[128,896]{1,0:T(8,128)(2,1)S(1)} %get-tuple-element.49), channel_id=1, source_target_pairs={{0,2},{2,0},{4,6},{6,4},{8,10},{10,8},{12,14},{14,12},{1,3},{3,1},... | collective-permute-start | bytes 688136 | tf_op jit(solution)/shard_map/ppermute | solution.py:323
  15.6 10.6 %collective-permute-start.5 = (bf16[128,896]{1,0:T(8,128)(2,1)S(1)}, bf16[128,896]{1,0:T(8,128)(2,1)S(1)}, u32[]{:S(2)}, u32[]{:S(2)}) collective-permute-start(bf16[128,896]{1,0:T(8,128)(2,1)S(1)} %get-tuple-element.46), channel_id=1, source_target_pairs={{0,2},{2,0},{4,6},{6,4},{8,10},{10,8},{12,14},{14,12},{1,3},{3,1},... | collective-permute-start | bytes 688136 | tf_op jit(solution)/shard_map/ppermute | solution.py:323
  19.2 12.0 %collective-permute-start.11 = (bf16[128,896]{1,0:T(8,128)(2,1)S(1)}, bf16[128,896]{1,0:T(8,128)(2,1)S(1)}, u32[]{:S(2)}, u32[]{:S(2)}) collective-permute-start(bf16[128,896]{1,0:T(8,128)(2,1)S(1)} %get-tuple-element.56), channel_id=1, source_target_pairs={{0,2},{2,0},{4,6},{6,4},{8,10},{10,8},{12,14},{14,12},{1,3},{3,1},... | collective-permute-start | bytes 688136 | tf_op jit(solution)/shard_map/ppermute | solution.py:323
  21.4 5.9 %collective-permute-start.9 = (bf16[64,896]{1,0:T(8,128)(2,1)S(1)}, bf16[64,896]{1,0:T(8,128)(2,1)S(1)}, u32[]{:S(2)}, u32[]{:S(2)}) collective-permute-start(bf16[64,896]{1,0:T(8,128)(2,1)S(1)} %get-tuple-element.52), channel_id=1, source_target_pairs={{0,4},{2,6},{4,0},{6,2},{8,12},{10,14},{12,8},{14,10},{1,5},{3,7},... | collective-permute-start | bytes 344072 | tf_op jit(solution)/shard_map/ppermute | solution.py:323
  23.5 6.5 %collective-permute-start.7 = (bf16[64,896]{1,0:T(8,128)(2,1)S(1)}, bf16[64,896]{1,0:T(8,128)(2,1)S(1)}, u32[]{:S(2)}, u32[]{:S(2)}) collective-permute-start(bf16[64,896]{1,0:T(8,128)(2,1)S(1)} %get-tuple-element.50), channel_id=1, source_target_pairs={{0,4},{2,6},{4,0},{6,2},{8,12},{10,14},{12,8},{14,10},{1,5},{3,7},... | collective-permute-start | bytes 344072 | tf_op jit(solution)/shard_map/ppermute | solution.py:323
  24.2 12.0 %collective-permute-start.4 = (bf16[128,896]{1,0:T(8,128)(2,1)S(1)}, bf16[128,896]{1,0:T(8,128)(2,1)S(1)}, u32[]{:S(2)}, u32[]{:S(2)}) collective-permute-start(bf16[128,896]{1,0:T(8,128)(2,1)S(1)} %get-tuple-element.41), channel_id=1, source_target_pairs={{0,2},{2,0},{4,6},{6,4},{8,10},{10,8},{12,14},{14,12},{1,3},{3,1},... | collective-permute-start | bytes 688136 | tf_op jit(solution)/shard_map/ppermute | solution.py:323
  27.3 10.7 %collective-permute-start.10 = (bf16[64,896]{1,0:T(8,128)(2,1)S(1)}, bf16[64,896]{1,0:T(8,128)(2,1)S(1)}, u32[]{:S(2)}, u32[]{:S(2)}) collective-permute-start(bf16[64,896]{1,0:T(8,128)(2,1)S(1)} %add.9), channel_id=1, source_target_pairs={{0,8},{2,10},{4,12},{6,14},{8,0},{10,2},{12,4},{14,6},{1,9},{3,11}... | collective-permute-start | bytes 344072 | tf_op jit(solution)/shard_map/ppermute | solution.py:323
  30.0 9.3 %collective-permute-start.8 = (bf16[64,896]{1,0:T(8,128)(2,1)S(1)}, bf16[64,896]{1,0:T(8,128)(2,1)S(1)}, u32[]{:S(2)}, u32[]{:S(2)}) collective-permute-start(bf16[64,896]{1,0:T(8,128)(2,1)S(1)} %add.8), channel_id=1, source_target_pairs={{0,8},{2,10},{4,12},{6,14},{8,0},{10,2},{12,4},{14,6},{1,9},{3,11}... | collective-permute-start | bytes 344072 | tf_op jit(solution)/shard_map/ppermute | solution.py:323
  31.3 8.4 %collective-permute-start.12 = (bf16[64,896]{1,0:T(8,128)(2,1)S(1)}, bf16[64,896]{1,0:T(8,128)(2,1)S(1)}, u32[]{:S(2)}, u32[]{:S(2)}) collective-permute-start(bf16[64,896]{1,0:T(8,128)(2,1)S(1)} %get-tuple-element.57), channel_id=1, source_target_pairs={{0,4},{2,6},{4,0},{6,2},{8,12},{10,14},{12,8},{14,10},{1,5},{3,7},... | collective-permute-start | bytes 344072 | tf_op jit(solution)/shard_map/ppermute | solution.py:323
  33.3 7.7 %collective-permute-start.13 = (bf16[64,896]{1,0:T(8,128)(2,1)S(1)}, bf16[64,896]{1,0:T(8,128)(2,1)S(1)}, u32[]{:S(2)}, u32[]{:S(2)}) collective-permute-start(bf16[64,896]{1,0:T(8,128)(2,1)S(1)} %get-tuple-element.58), channel_id=1, source_target_pairs={{0,4},{2,6},{4,0},{6,2},{8,12},{10,14},{12,8},{14,10},{1,5},{3,7},... | collective-permute-start | bytes 344072 | tf_op jit(solution)/shard_map/ppermute | solution.py:323

commit v7 on v6

--- a/solution.py
+++ b/solution.py
@@ -11,7 +11,7 @@
 F32 = jnp.float32
 SWAP = [(0, 1), (1, 0)]
 VMEM_LIMIT = 12 * 1024 * 1024
-OWN_LIMIT = 49 * 1024 * 1024
+HOLD_LIMIT = 50 * 1024 * 1024
 VECTORS = pl.BlockSpec(memory_space=pltpu.VMEM)
 ANYWHERE = pl.BlockSpec(memory_space=pl.ANY)
 SCALARS = pl.BlockSpec(memory_space=pltpu.SMEM)
@@ -34,45 +34,29 @@
     return 1
 
 
-def own_kernel(b_hbm, g_hbm, x_hbm, grad_ref, g_ref, x_ref, b, sems):
-    width = g_ref.shape[1]
-    arrays = ((b_hbm, b), (g_hbm, g_ref), (x_hbm, x_ref))
+def hold_kernel(g_hbm, x_hbm, g_ref, x_ref, sems):
     copies = [
-        [
-            pltpu.make_async_copy(source.at[:, cols], target.at[:, cols], sems.at[i, j])
-            for j, cols in enumerate(tiles(width))
-        ]
-        for i, (source, target) in enumerate(arrays)
+        pltpu.make_async_copy(source.at[:, cols], target.at[:, cols], sems.at[i, j])
+        for i, (source, target) in enumerate(((g_hbm, g_ref), (x_hbm, x_ref)))
+        for j, cols in enumerate(tiles(g_ref.shape[1]))
     ]
-    for j in range(len(copies[0])):
-        copies[0][j].start()
-        copies[1][j].start()
-    for copy in copies[2]:
+    for copy in copies:
         copy.start()
-    total = jnp.zeros(grad_ref.shape, F32)
-    for j, cols in enumerate(tiles(width)):
-        copies[0][j].wait()
-        copies[1][j].wait()
-        total = total + lax.dot_general(b[:, cols], g_ref[:, cols], NT, preferred_element_type=F32)
-    grad_ref[...] = total
-    for copy in copies[2]:
+    for copy in copies:
         copy.wait()
 
 
-def own_products(b, g, x):
-    rows, width = b.shape
-    tokens = x.shape[0]
-    return pl.pallas_call(
-        own_kernel,
-        in_specs=[ANYWHERE] * 3,
-        out_specs=[VECTORS] * 3,
-        out_shape=[jax.ShapeDtypeStruct((rows, tokens), F32)]
-        + [jax.ShapeDtypeStruct((tokens, width), BF16)] * 2,
-        scratch_shapes=[pltpu.VMEM(b.shape, BF16), pltpu.SemaphoreType.DMA((3, steps_of(width)))],
-        compiler_params=params(OWN_LIMIT),
-        cost_estimate=cost(2 * rows * tokens * width, 4 * (rows + tokens) * width),
-        name="own",
-    )(b, g, x)
+def hold(g, x):
+    return pl.pallas_call(
+        hold_kernel,
+        in_specs=[ANYWHERE] * 2,
+        out_specs=[VECTORS] * 2,
+        out_shape=[jax.ShapeDtypeStruct(x.shape, BF16)] * 2,
+        scratch_shapes=[pltpu.SemaphoreType.DMA((2, steps_of(x.shape[1])))],
+        compiler_params=params(HOLD_LIMIT),
+        cost_estimate=cost(128 * x.size, 8 * x.size),
+        name="hold",
+    )(g, x)
 
 
 def tiles(width):
@@ -103,28 +87,24 @@
             keep_ref[out, into] = product[rows:]
 
 
-def factor_sum(factor, tokens):
-    total = jnp.zeros((factor.shape[0], tokens.shape[0]), F32)
-    for cols in tiles(factor.shape[1]):
-        total = total + lax.dot_general(
-            factor[:, cols], tokens[:, cols], NT, preferred_element_type=F32
-        )
+def factor_sum(tokens, *factors):
+    total = 0.0
+    for cols in tiles(tokens.shape[1]):
+        rows = jnp.concatenate([factor[:, cols] for factor in factors], axis=0)
+        total = total + lax.dot_general(rows, tokens[:, cols], NT, preferred_element_type=F32)
     return total
 
 
-def low_kernel(rank, core_ref, where_ref, ids_ref, gates_ref, grad_ref, b_ref, a_ref, a_in_ref, g_ref, x_ref,
+def low_kernel(rank, core_ref, where_ref, ids_ref, gates_ref, b_ref, b_in_ref, a_ref, a_in_ref, g_ref, x_ref,
                lg_ref, la_ref, send_ref, keep_ref):
     weight = gate_columns(1 - core_ref[0], ids_ref[...], gates_ref[...], 2 * b_ref.shape[0], rank)
-    sums = (
-        [factor_sum(b_ref, g_ref), grad_ref[...]],
-        [factor_sum(a_in_ref, x_ref), factor_sum(a_ref, x_ref)],
-    )
-    lows = [(jnp.concatenate(pair, axis=0) * weight).astype(BF16) for pair in sums]
+    sums = factor_sum(g_ref, b_in_ref, b_ref), factor_sum(x_ref, a_in_ref, a_ref)
+    lows = [(rows * weight).astype(BF16) for rows in sums]
     lg_ref[...], la_ref[...] = lows
     store_products(where_ref, 0, 1, lows, (x_ref, g_ref), send_ref, keep_ref)
 
 
-def low_products(core, where, ids, gates, rank, grad, b_in, a, a_in, g, x, wide):
+def low_products(core, where, ids, gates, rank, b, b_in, a, a_in, g, x, wide):
     rows, width = b_in.shape
     tokens = x.shape[0]
     return pl.pallas_call(
@@ -136,7 +116,7 @@
         compiler_params=params(),
         cost_estimate=cost(4 * rows * tokens * (width + 2 * wide), 4 * (rows + tokens) * width),
         name="low",
-    )(core, where, ids, gates, grad, b_in, a, a_in, g, x)
+    )(core, where, ids, gates, b, b_in, a, a_in, g, x)
 
 
 def rest_kernel(blocks, block, where_ref, kept_ref, came_ref, lg_ref, la_ref, x_ref, g_ref, *outs):
@@ -262,21 +242,20 @@
     )(keep, *came)
 
 
-def last_kernel(down_in, up_in, down_came, up_came, down_ref, up_ref):
-    down_ref[...] = down_in[...] + down_came[...].astype(F32)
-    up_ref[...] = up_in[...] + up_came[...].astype(F32)
-
-
-def last(down, up, down_came, up_came):
+def last_kernel(total_ref, came_ref, out_ref):
+    out_ref[...] = total_ref[...] + came_ref[...].astype(F32)
+
+
+def last(total, came):
     return pl.pallas_call(
         last_kernel,
-        in_specs=[VECTORS] * 4,
-        out_specs=[VECTORS] * 2,
-        out_shape=[jax.ShapeDtypeStruct(down.shape, F32)] * 2,
-        compiler_params=params(),
-        cost_estimate=cost(down.size, 10 * down.size),
+        in_specs=[VECTORS] * 2,
+        out_specs=VECTORS,
+        out_shape=jax.ShapeDtypeStruct(total.shape, F32),
+        compiler_params=params(),
+        cost_estimate=cost(total.size, 10 * total.size),
         name="last",
-    )(down, up, down_came, up_came)
+    )(total, came)
 
 
 def input_kernel(low_ref, own_ref, other_ref, out_ref):
@@ -326,11 +305,11 @@
         return plain(core, ids, gates, rank, x, g, a, b, swap(a), b_in, swap)
 
     a_in = swap(a)
-    grad, g_held, x_held = own_products(b, g, x)
+    g_held, x_held = hold(g, x)
     order = list(reversed(range(steps)))
     where = jnp.stack([far ^ step for step in order] + [near])
     lg, la, pair, keep = low_products(
-        core, where, ids, gates, rank, grad, b_in, a, a_in, g_held, x_held, 2 * block
+        core, where, ids, gates, rank, b, b_in, a, a_in, g_held, x_held, 2 * block
     )
     rest_pair, rest_keep, *first = rest_products(
         where, keep, swap(pair), lg, la, x_held, g_held, steps - 1, block, 1
@@ -356,7 +335,7 @@
                 into.append(flip(add(half, came), 4))
     input_grad = input_gradient(lg, a, a_in)
     input_grad, both[-1] = lax.optimization_barrier((input_grad, both[-1]))
-    down, up = last(*total(own, both, downs, ups), *nearest)
+    down, up = (last(*pair) for pair in zip(total(own, both, downs, ups), nearest))
     return input_grad, down.reshape(count, rank, block), up.reshape(count, rank, block)
 
 

time: 42.5 us -> 40.9 us (0.962)
  local copies, waits for them, and re-layouts: 1.27 us -> 0.1 us
  Pallas kernels: 13.1 us -> 12.2 us
  waiting for transfers between devices: 9.3 us -> 9.82 us
    ppermute x4, waiting for transfers between devices: 1.54 us -> 2.78 us  [shards(): swap = lambda array: lax.ppermute(array, 'adapter', SWAP)]
    unnamed x8, local copies, waits for them, and re-layouts: 1.19 us -> 0.01 us
    pallas_call x1, Pallas kernels: 3.09 us -> 2 us  [low_products(): pl.pallas_call(functools.partial(low_kernel, rank), in_specs=[SCALARS] *...]
    ppermute x10, waiting for transfers between devices: 7.77 us -> 7.04 us  [shards(): lax.ppermute(array, 'dp', [(i, i ^ by) for i in range(replicas)])]
    pallas_call x2 -> x3, Pallas kernels: 3.42 us -> 3.61 us  [the longest x1 2.2 us: hold(): pl.pallas_call(hold_kernel, in_specs=[ANYWHERE] * 2, out_specs=[VECTORS]...]
  transfers between devices with their start and end apart: 14 -> 14, of which waited for: 9 -> 10; matrix products, arithmetic and copies ran while one was open for 0% -> 0% of each run, Pallas kernels for 18% -> 20%
where the time goes in v7:
time: 40.9 us; the launch traced here: 40.2 us
  starting transfers between devices  17.3 us (42%)
  Pallas kernels  12.2 us (30%)
  waiting for transfers between devices  9.82 us (24%)
  between operations  0.73 us (2%)
    ppermute x10, starting transfers between devices, shards(): lax.ppermute(array, 'dp', [(i, i ^ by) for i in range(replicas)])  15.9 us
    ppermute x10, waiting for transfers between devices, shards(): lax.ppermute(array, 'dp', [(i, i ^ by) for i in range(replicas)])  7.04 us
    pallas_call x1, Pallas kernels, input_gradient(): pl.pallas_call(input_kernel, grid=(steps,), in_specs=[VECTORS] * 3, out_s...  2.81 us
    ppermute x4, waiting for transfers between devices, shards(): swap = lambda array: lax.ppermute(array, 'adapter', SWAP)  2.78 us
    pallas_call x1, Pallas kernels, hold(): pl.pallas_call(hold_kernel, in_specs=[ANYWHERE] * 2, out_specs=[VECTORS]...  2.2 us
    pallas_call x1, Pallas kernels, low_products(): pl.pallas_call(functools.partial(low_kernel, rank), in_specs=[SCALARS] *...  2 us
    pallas_call x3, Pallas kernels, fold(): pl.pallas_call(functools.partial(fold_kernel, block, at), in_specs=[SCALA...  1.94 us
    pallas_call x1, Pallas kernels, rest_products(): pl.pallas_call(functools.partial(rest_kernel, blocks, block), in_specs=[S...  1.57 us
  transfers between devices with their start and end apart: 14, of which 10 were waited for; matrix products, arithmetic and copies ran while one was open for 0% of the time, Pallas kernels for 20%

profile of v7, /device:TPU:0, one launch (start us, length us, event | category | flops | bytes accessed | tf_op | source)
XLA Modules:
  0.0 40.2 jit_solution(14765070133592694847)
XLA Ops:
  0.6 0.5 %collective-permute-start.1 = (bf16[64,7168]{1,0:T(8,128)(2,1)}, bf16[64,7168]{1,0:T(8,128)(2,1)S(1)}, u32[]{:S(2)}, u32[]{:S(2)}) collective-permute-start(bf16[64,7168]{1,0:T(8,128)(2,1)} %bitcast.12), channel_id=1, source_target_pairs={{0,1},{1,0},{2,3},{3,2},{4,5},{5,4},{6,7},{7,6},{8,9},{9,8},{10,11... | collective-permute-start | bytes 2752520 | tf_op jit(solution)/shard_map/ppermute | solution.py:298
  1.1 0.1 collective-permute-start
  1.2 0.1 stack.23.where_ref
  1.3 0.0 copy-start
  1.3 0.0 copy-start.1
  1.3 0.0 copy-start.2
  1.3 0.0 copy-start.3
  1.3 2.2 %hold.1 = (bf16[128,7168]{1,0:T(8,128)(2,1)S(1)}, bf16[128,7168]{1,0:T(8,128)(2,1)S(1)}) custom-call(bf16[128,7168]{1,0:T(8,128)(2,1)} %g_hbm.1, bf16[128,7168]{1,0:T(8,128)(2,1)} %x_hbm.1), custom_call_target="tpu_custom_call" | custom-call | flops 117440512 | bytes 7340032 | tf_op jit(solution)/shard_map/hold/pallas_call | solution.py:50
  3.5 0.0 collective-permute-done.1.a_in_ref.other_ref
  3.5 1.2 %collective-permute-done.b_in_ref = bf16[64,7168]{1,0:T(8,128)(2,1)S(1)} collective-permute-done((bf16[64,7168]{1,0:T(8,128)(2,1)}, bf16[64,7168]{1,0:T(8,128)(2,1)S(1)}, u32[]{:S(2)}, u32[]{:S(2)}) %collective-permute-start) | collective-permute-done | bytes 917536 | tf_op jit(solution)/shard_map/ppermute | solution.py:298
  4.8 0.0 copy-done
  4.8 0.0 copy-done.1
  4.8 0.0 copy-done.2
  4.8 0.0 copy-done.3
  4.8 2.0 %low.1 = (bf16[128,128]{1,0:T(8,128)(2,1)S(1)}, bf16[128,128]{1,0:T(8,128)(2,1)S(1)}, bf16[128,1792]{1,0:T(8,128)(2,1)S(1)}, bf16[128,1792]{1,0:T(8,128)(2,1)S(1)}) custom-call(s32[1]{0:T(128)} %bitcast.core_ref, s32[5]{0:T(128)S(1)} %stack.23.where_ref, s32[2,128]{1,0:T(2,128)S(1)} %bitcast.17, f32[2,128]{1,0:T(2,128)S(1)} %bitcast.18, ...), custom_call_target="tpu_custom_call" | custom-call | flops 352321536 | bytes 5505024 | tf_op jit(solution)/shard_map/low/pallas_call | solution.py:110
  6.8 0.4 %collective-permute-start.2 = (bf16[128,1792]{1,0:T(8,128)(2,1)S(1)}, bf16[128,1792]{1,0:T(8,128)(2,1)S(1)}, u32[]{:S(2)}, u32[]{:S(2)}) collective-permute-start(bf16[128,1792]{1,0:T(8,128)(2,1)S(1)} %get-tuple-element.33), channel_id=1, source_target_pairs={{0,1},{1,0},{2,3},{3,2},{4,5},{5,4},{6,7},{7,6},{8,9},{9,8},{10,11... | collective-permute-start | bytes 1376264 | tf_op jit(solution)/shard_map/ppermute | solution.py:298
  7.2 1.5 %collective-permute-done.2.came_ref = bf16[128,1792]{1,0:T(8,128)(2,1)S(1)} collective-permute-done((bf16[128,1792]{1,0:T(8,128)(2,1)S(1)}, bf16[128,1792]{1,0:T(8,128)(2,1)S(1)}, u32[]{:S(2)}, u32[]{:S(2)}) %collective-permute-start.2) | collective-permute-done | bytes 458784 | tf_op jit(solution)/shard_map/ppermute | solution.py:298
  8.7 1.6 %rest.1 = (bf16[128,5376]{1,0:T(8,128)(2,1)S(1)}, bf16[128,5376]{1,0:T(8,128)(2,1)S(1)}, bf16[128,896]{1,0:T(8,128)(2,1)S(1)}, f32[128,896]{1,0:T(8,128)S(1)}) custom-call(s32[5]{0:T(128)S(1)} %stack.23.where_ref, bf16[128,1792]{1,0:T(8,128)(2,1)S(1)} %get-tuple-element.32.kept_ref, bf16[128,1792]{1,0:T(8,128)(2,1)S(1)} %collective-permute-done.2.came_ref, ...), custom_call_target="tpu_custom_call" | custom-call | flops 176160768 | bytes 2752512 | tf_op jit(solution)/shard_map/rest/pallas_call | solution.py:139
  10.2 0.4 %collective-permute-start.3 = (bf16[128,5376]{1,0:T(8,128)(2,1)S(1)}, bf16[128,5376]{1,0:T(8,128)(2,1)S(1)}, u32[]{:S(2)}, u32[]{:S(2)}) collective-permute-start(bf16[128,5376]{1,0:T(8,128)(2,1)S(1)} %get-tuple-element.36), channel_id=1, source_target_pairs={{0,1},{1,0},{2,3},{3,2},{4,5},{5,4},{6,7},{7,6},{8,9},{9,8},{10,11... | collective-permute-start | bytes 4128776 | tf_op jit(solution)/shard_map/ppermute | solution.py:298
  10.7 2.7 %collective-permute-start.6 = (bf16[128,896]{1,0:T(8,128)(2,1)S(1)}, bf16[128,896]{1,0:T(8,128)(2,1)S(1)}, u32[]{:S(2)}, u32[]{:S(2)}) collective-permute-start(bf16[128,896]{1,0:T(8,128)(2,1)S(1)} %get-tuple-element.45), channel_id=1, source_target_pairs={{0,2},{2,0},{4,6},{6,4},{8,10},{10,8},{12,14},{14,12},{1,3},{3,1},... | collective-permute-start | bytes 688136 | tf_op jit(solution)/shard_map/ppermute | solution.py:302
  13.3 0.1 collective-permute-done.3.came_ref
  13.4 0.6 %fold.4 = (bf16[128,896]{1,0:T(8,128)(2,1)S(1)}, f32[128,896]{1,0:T(8,128)S(1)}) custom-call(s32[5]{0:T(128)S(1)} %stack.23.where_ref, bf16[128,5376]{1,0:T(8,128)(2,1)S(1)} %get-tuple-element.35.keep_ref, bf16[128,5376]{1,0:T(8,128)(2,1)S(1)} %collective-permute-done.3.came_ref), custom_call_target="tpu_custom_call" | custom-call | flops 229376 | bytes 1605632 | tf_op jit(solution)/shard_map/fold/pallas_call | solution.py:164
  14.1 2.9 %collective-permute-start.5 = (bf16[128,896]{1,0:T(8,128)(2,1)S(1)}, bf16[128,896]{1,0:T(8,128)(2,1)S(1)}, u32[]{:S(2)}, u32[]{:S(2)}) collective-permute-start(bf16[128,896]{1,0:T(8,128)(2,1)S(1)} %get-tuple-element.42), channel_id=1, source_target_pairs={{0,2},{2,0},{4,6},{6,4},{8,10},{10,8},{12,14},{14,12},{1,3},{3,1},... | collective-permute-start | bytes 688136 | tf_op jit(solution)/shard_map/ppermute | solution.py:302
  17.0 0.6 %fold.5 = (bf16[128,896]{1,0:T(8,128)(2,1)S(1)}, f32[128,896]{1,0:T(8,128)S(1)}) custom-call(s32[5]{0:T(128)S(1)} %stack.23.where_ref, bf16[128,5376]{1,0:T(8,128)(2,1)S(1)} %get-tuple-element.35.keep_ref, bf16[128,5376]{1,0:T(8,128)(2,1)S(1)} %collective-permute-done.3.came_ref), custom_call_target="tpu_custom_call" | custom-call | flops 229376 | bytes 1605632 | tf_op jit(solution)/shard_map/fold/pallas_call | solution.py:164
  17.7 0.1 collective-permute-start.11
  17.8 2.0 %collective-permute-done.6.came_ref = bf16[128,896]{1,0:T(8,128)(2,1)S(1)} collective-permute-done((bf16[128,896]{1,0:T(8,128)(2,1)S(1)}, bf16[128,896]{1,0:T(8,128)(2,1)S(1)}, u32[]{:S(2)}, u32[]{:S(2)}) %collective-permute-start.6) | collective-permute-done | bytes 229408 | tf_op jit(solution)/shard_map/ppermute | solution.py:302
  19.8 2.1 %collective-permute-start.9 = (bf16[64,896]{1,0:T(8,128)(2,1)S(1)}, bf16[64,896]{1,0:T(8,128)(2,1)S(1)}, u32[]{:S(2)}, u32[]{:S(2)}) collective-permute-start(bf16[64,896]{1,0:T(8,128)(2,1)S(1)} %get-tuple-element.48), channel_id=1, source_target_pairs={{0,4},{2,6},{4,0},{6,2},{8,12},{10,14},{12,8},{14,10},{1,5},{3,7},... | collective-permute-start | bytes 344072 | tf_op jit(solution)/shard_map/ppermute | solution.py:302
  21.9 0.1 collective-permute-start.7
  22.0 0.6 %fold.3 = (bf16[128,896]{1,0:T(8,128)(2,1)S(1)}, f32[128,896]{1,0:T(8,128)S(1)}) custom-call(s32[5]{0:T(128)S(1)} %stack.23.where_ref, bf16[128,5376]{1,0:T(8,128)(2,1)S(1)} %get-tuple-element.35.keep_ref, bf16[128,5376]{1,0:T(8,128)(2,1)S(1)} %collective-permute-done.3.came_ref), custom_call_target="tpu_custom_call" | custom-call | flops 229376 | bytes 1605632 | tf_op jit(solution)/shard_map/fold/pallas_call | solution.py:164
  22.7 2.0 %collective-permute-start.4 = (bf16[128,896]{1,0:T(8,128)(2,1)S(1)}, bf16[128,896]{1,0:T(8,128)(2,1)S(1)}, u32[]{:S(2)}, u32[]{:S(2)}) collective-permute-start(bf16[128,896]{1,0:T(8,128)(2,1)S(1)} %get-tuple-element.37), channel_id=1, source_target_pairs={{0,2},{2,0},{4,6},{6,4},{8,10},{10,8},{12,14},{14,12},{1,3},{3,1},... | collective-permute-start | bytes 688136 | tf_op jit(solution)/shard_map/ppermute | solution.py:302
  24.6 0.1 collective-permute-done.5.came_ref
  24.7 1.0 %collective-permute-done.9.refs_0_ = bf16[64,896]{1,0:T(8,128)(2,1)S(1)} collective-permute-done((bf16[64,896]{1,0:T(8,128)(2,1)S(1)}, bf16[64,896]{1,0:T(8,128)(2,1)S(1)}, u32[]{:S(2)}, u32[]{:S(2)}) %collective-permute-start.9) | collective-permute-done | bytes 114720 | tf_op jit(solution)/shard_map/ppermute | solution.py:302
  25.7 2.7 %collective-permute-start.10 = (bf16[64,896]{1,0:T(8,128)(2,1)S(1)}, bf16[64,896]{1,0:T(8,128)(2,1)S(1)}, u32[]{:S(2)}, u32[]{:S(2)}) collective-permute-start(bf16[64,896]{1,0:T(8,128)(2,1)S(1)} %add.9), channel_id=1, source_target_pairs={{0,8},{2,10},{4,12},{6,14},{8,0},{10,2},{12,4},{14,6},{1,9},{3,11}... | collective-permute-start | bytes 344072 | tf_op jit(solution)/shard_map/ppermute | solution.py:302
  28.4 0.0 collective-permute-done.7.refs_0_
  28.4 1.3 %collective-permute-start.8 = (bf16[64,896]{1,0:T(8,128)(2,1)S(1)}, bf16[64,896]{1,0:T(8,128)(2,1)S(1)}, u32[]{:S(2)}, u32[]{:S(2)}) collective-permute-start(bf16[64,896]{1,0:T(8,128)(2,1)S(1)} %add.8), channel_id=1, source_target_pairs={{0,8},{2,10},{4,12},{6,14},{8,0},{10,2},{12,4},{14,6},{1,9},{3,11}... | collective-permute-start | bytes 344072 | tf_op jit(solution)/shard_map/ppermute | solution.py:302
  29.7 0.0 collective-permute-done.11.came_ref
  29.7 0.1 halves.5
  29.8 2.0 %collective-permute-start.12 = (bf16[64,896]{1,0:T(8,128)(2,1)S(1)}, bf16[64,896]{1,0:T(8,128)(2,1)S(1)}, u32[]{:S(2)}, u32[]{:S(2)}) collective-permute-start(bf16[64,896]{1,0:T(8,128)(2,1)S(1)} %get-tuple-element.52), channel_id=1, source_target_pairs={{0,4},{2,6},{4,0},{6,2},{8,12},{10,14},{12,8},{14,10},{1,5},{3,7},... | collective-permute-start | bytes 344072 | tf_op jit(solution)/shard_map/ppermute | solution.py:302
  31.8 0.1 collective-permute-start.13
  31.9 2.8 %input.1 = bf16[128,7168]{1,0:T(8,128)(2,1)} custom-call(bf16[128,128]{1,0:T(8,128)(2,1)S(1)} %get-tuple-element.31.low_ref.lg_ref, bf16[64,7168]{1,0:T(8,128)(2,1)S(1)} %bitcast.14, bf16[64,7168]{1,0:T(8,128)(2,1)S(1)} %collective-permute-done.1.a_in_ref.other_ref), custom_call_target="tpu_custom_call" | custom-call | flops 234881024 | bytes 3670016 | tf_op jit(solution)/shard_map/input/pallas_call | solution.py:276
  34.7 0.0 collective-permute-done.4.refs_0_
  34.7 1.8 %collective-permute-done.10.refs_2_ = bf16[64,896]{1,0:T(8,128)(2,1)S(1)} collective-permute-done((bf16[64,896]{1,0:T(8,128)(2,1)S(1)}, bf16[64,896]{1,0:T(8,128)(2,1)S(1)}, u32[]{:S(2)}, u32[]{:S(2)}) %collective-permute-start.10) | collective-permute-done | bytes 114720 | tf_op jit(solution)/shard_map/ppermute | solution.py:302
  36.4 1.3 %collective-permute-done.8.refs_1_ = bf16[64,896]{1,0:T(8,128)(2,1)S(1)} collective-permute-done((bf16[64,896]{1,0:T(8,128)(2,1)S(1)}, bf16[64,896]{1,0:T(8,128)(2,1)S(1)}, u32[]{:S(2)}, u32[]{:S(2)}) %collective-permute-start.8) | collective-permute-done | bytes 114720 | tf_op jit(solution)/shard_map/ppermute | solution.py:302
  37.7 0.1 total.1
  37.8 0.4 %collective-permute-done.12.came_ref = bf16[64,896]{1,0:T(8,128)(2,1)S(1)} collective-permute-done((bf16[64,896]{1,0:T(8,128)(2,1)S(1)}, bf16[64,896]{1,0:T(8,128)(2,1)S(1)}, u32[]{:S(2)}, u32[]{:S(2)}) %collective-permute-start.12) | collective-permute-done | bytes 114720 | tf_op jit(solution)/shard_map/ppermute | solution.py:302
  38.2 0.7 %last.2 = f32[64,896]{1,0:T(8,128)} custom-call(f32[64,896]{1,0:T(8,128)S(1)} %get-tuple-element.49.total_ref, bf16[64,896]{1,0:T(8,128)(2,1)S(1)} %collective-permute-done.12.came_ref), custom_call_target="tpu_custom_call" | custom-call | flops 57344 | bytes 573440 | tf_op jit(solution)/shard_map/last/pallas_call | solution.py:250
  38.9 0.5 %collective-permute-done.13.came_ref = bf16[64,896]{1,0:T(8,128)(2,1)S(1)} collective-permute-done((bf16[64,896]{1,0:T(8,128)(2,1)S(1)}, bf16[64,896]{1,0:T(8,128)(2,1)S(1)}, u32[]{:S(2)}, u32[]{:S(2)}) %collective-permute-start.13) | collective-permute-done | bytes 114720 | tf_op jit(solution)/shard_map/ppermute | solution.py:302
  39.4 0.7 %last.3 = f32[64,896]{1,0:T(8,128)} custom-call(f32[64,896]{1,0:T(8,128)S(1)} %get-tuple-element.53.total_ref, bf16[64,896]{1,0:T(8,128)(2,1)S(1)} %collective-permute-done.13.came_ref), custom_call_target="tpu_custom_call" | custom-call | flops 57344 | bytes 573440 | tf_op jit(solution)/shard_map/last/pallas_call | solution.py:250
  (4 shorter events, 0.1 us)
Async XLA Ops:
  0.6 2.9 %collective-permute-start.1 = (bf16[64,7168]{1,0:T(8,128)(2,1)}, bf16[64,7168]{1,0:T(8,128)(2,1)S(1)}, u32[]{:S(2)}, u32[]{:S(2)}) collective-permute-start(bf16[64,7168]{1,0:T(8,128)(2,1)} %bitcast.12), channel_id=1, source_target_pairs={{0,1},{1,0},{2,3},{3,2},{4,5},{5,4},{6,7},{7,6},{8,9},{9,8},{10,11... | collective-permute-start | bytes 2752520 | tf_op jit(solution)/shard_map/ppermute | solution.py:298
  1.1 3.6 %collective-permute-start = (bf16[64,7168]{1,0:T(8,128)(2,1)}, bf16[64,7168]{1,0:T(8,128)(2,1)S(1)}, u32[]{:S(2)}, u32[]{:S(2)}) collective-permute-start(bf16[64,7168]{1,0:T(8,128)(2,1)} %bitcast.15), channel_id=1, source_target_pairs={{0,1},{1,0},{2,3},{3,2},{4,5},{5,4},{6,7},{7,6},{8,9},{9,8},{10,11... | collective-permute-start | bytes 2752520 | tf_op jit(solution)/shard_map/ppermute | solution.py:298
  1.3 3.5 %copy-start = (bf16[4,16,7168]{2,1,0:T(8,128)(2,1)S(1)}, bf16[4,16,7168]{2,1,0:T(8,128)(2,1)}, u32[]{:S(2)}) copy-start(bf16[4,16,7168]{2,1,0:T(8,128)(2,1)} %param.10) | copy-start | bytes 2752516
  1.3 3.5 %copy-start.1 = (bf16[4,16,7168]{2,1,0:T(8,128)(2,1)S(1)}, bf16[4,16,7168]{2,1,0:T(8,128)(2,1)}, u32[]{:S(2)}) copy-start(bf16[4,16,7168]{2,1,0:T(8,128)(2,1)} %param.11) | copy-start | bytes 2752516
  1.3 3.5 %copy-start.2 = (s32[128,2]{0,1:T(2,128)S(1)}, s32[128,2]{0,1:T(2,128)}, u32[]{:S(2)}) copy-start(s32[128,2]{0,1:T(2,128)} %param.8) | copy-start | bytes 3076
  1.3 3.5 %copy-start.3 = (f32[128,2]{0,1:T(2,128)S(1)}, f32[128,2]{0,1:T(2,128)}, u32[]{:S(2)}) copy-start(f32[128,2]{0,1:T(2,128)} %param.9) | copy-start | bytes 3076
  6.8 1.9 %collective-permute-start.2 = (bf16[128,1792]{1,0:T(8,128)(2,1)S(1)}, bf16[128,1792]{1,0:T(8,128)(2,1)S(1)}, u32[]{:S(2)}, u32[]{:S(2)}) collective-permute-start(bf16[128,1792]{1,0:T(8,128)(2,1)S(1)} %get-tuple-element.33), channel_id=1, source_target_pairs={{0,1},{1,0},{2,3},{3,2},{4,5},{5,4},{6,7},{7,6},{8,9},{9,8},{10,11... | collective-permute-start | bytes 1376264 | tf_op jit(solution)/shard_map/ppermute | solution.py:298
  10.2 3.2 %collective-permute-start.3 = (bf16[128,5376]{1,0:T(8,128)(2,1)S(1)}, bf16[128,5376]{1,0:T(8,128)(2,1)S(1)}, u32[]{:S(2)}, u32[]{:S(2)}) collective-permute-start(bf16[128,5376]{1,0:T(8,128)(2,1)S(1)} %get-tuple-element.36), channel_id=1, source_target_pairs={{0,1},{1,0},{2,3},{3,2},{4,5},{5,4},{6,7},{7,6},{8,9},{9,8},{10,11... | collective-permute-start | bytes 4128776 | tf_op jit(solution)/shard_map/ppermute | solution.py:298
  10.7 9.1 %collective-permute-start.6 = (bf16[128,896]{1,0:T(8,128)(2,1)S(1)}, bf16[128,896]{1,0:T(8,128)(2,1)S(1)}, u32[]{:S(2)}, u32[]{:S(2)}) collective-permute-start(bf16[128,896]{1,0:T(8,128)(2,1)S(1)} %get-tuple-element.45), channel_id=1, source_target_pairs={{0,2},{2,0},{4,6},{6,4},{8,10},{10,8},{12,14},{14,12},{1,3},{3,1},... | collective-permute-start | bytes 688136 | tf_op jit(solution)/shard_map/ppermute | solution.py:302
  14.1 10.6 %collective-permute-start.5 = (bf16[128,896]{1,0:T(8,128)(2,1)S(1)}, bf16[128,896]{1,0:T(8,128)(2,1)S(1)}, u32[]{:S(2)}, u32[]{:S(2)}) collective-permute-start(bf16[128,896]{1,0:T(8,128)(2,1)S(1)} %get-tuple-element.42), channel_id=1, source_target_pairs={{0,2},{2,0},{4,6},{6,4},{8,10},{10,8},{12,14},{14,12},{1,3},{3,1},... | collective-permute-start | bytes 688136 | tf_op jit(solution)/shard_map/ppermute | solution.py:302
  17.7 12.0 %collective-permute-start.11 = (bf16[128,896]{1,0:T(8,128)(2,1)S(1)}, bf16[128,896]{1,0:T(8,128)(2,1)S(1)}, u32[]{:S(2)}, u32[]{:S(2)}) collective-permute-start(bf16[128,896]{1,0:T(8,128)(2,1)S(1)} %get-tuple-element.51), channel_id=1, source_target_pairs={{0,2},{2,0},{4,6},{6,4},{8,10},{10,8},{12,14},{14,12},{1,3},{3,1},... | collective-permute-start | bytes 688136 | tf_op jit(solution)/shard_map/ppermute | solution.py:302
  19.8 5.9 %collective-permute-start.9 = (bf16[64,896]{1,0:T(8,128)(2,1)S(1)}, bf16[64,896]{1,0:T(8,128)(2,1)S(1)}, u32[]{:S(2)}, u32[]{:S(2)}) collective-permute-start(bf16[64,896]{1,0:T(8,128)(2,1)S(1)} %get-tuple-element.48), channel_id=1, source_target_pairs={{0,4},{2,6},{4,0},{6,2},{8,12},{10,14},{12,8},{14,10},{1,5},{3,7},... | collective-permute-start | bytes 344072 | tf_op jit(solution)/shard_map/ppermute | solution.py:302
  21.9 6.5 %collective-permute-start.7 = (bf16[64,896]{1,0:T(8,128)(2,1)S(1)}, bf16[64,896]{1,0:T(8,128)(2,1)S(1)}, u32[]{:S(2)}, u32[]{:S(2)}) collective-permute-start(bf16[64,896]{1,0:T(8,128)(2,1)S(1)} %get-tuple-element.46), channel_id=1, source_target_pairs={{0,4},{2,6},{4,0},{6,2},{8,12},{10,14},{12,8},{14,10},{1,5},{3,7},... | collective-permute-start | bytes 344072 | tf_op jit(solution)/shard_map/ppermute | solution.py:302
  22.7 12.0 %collective-permute-start.4 = (bf16[128,896]{1,0:T(8,128)(2,1)S(1)}, bf16[128,896]{1,0:T(8,128)(2,1)S(1)}, u32[]{:S(2)}, u32[]{:S(2)}) collective-permute-start(bf16[128,896]{1,0:T(8,128)(2,1)S(1)} %get-tuple-element.37), channel_id=1, source_target_pairs={{0,2},{2,0},{4,6},{6,4},{8,10},{10,8},{12,14},{14,12},{1,3},{3,1},... | collective-permute-start | bytes 688136 | tf_op jit(solution)/shard_map/ppermute | solution.py:302
  25.7 10.7 %collective-permute-start.10 = (bf16[64,896]{1,0:T(8,128)(2,1)S(1)}, bf16[64,896]{1,0:T(8,128)(2,1)S(1)}, u32[]{:S(2)}, u32[]{:S(2)}) collective-permute-start(bf16[64,896]{1,0:T(8,128)(2,1)S(1)} %add.9), channel_id=1, source_target_pairs={{0,8},{2,10},{4,12},{6,14},{8,0},{10,2},{12,4},{14,6},{1,9},{3,11}... | collective-permute-start | bytes 344072 | tf_op jit(solution)/shard_map/ppermute | solution.py:302
  28.4 9.3 %collective-permute-start.8 = (bf16[64,896]{1,0:T(8,128)(2,1)S(1)}, bf16[64,896]{1,0:T(8,128)(2,1)S(1)}, u32[]{:S(2)}, u32[]{:S(2)}) collective-permute-start(bf16[64,896]{1,0:T(8,128)(2,1)S(1)} %add.8), channel_id=1, source_target_pairs={{0,8},{2,10},{4,12},{6,14},{8,0},{10,2},{12,4},{14,6},{1,9},{3,11}... | collective-permute-start | bytes 344072 | tf_op jit(solution)/shard_map/ppermute | solution.py:302
  29.8 8.5 %collective-permute-start.12 = (bf16[64,896]{1,0:T(8,128)(2,1)S(1)}, bf16[64,896]{1,0:T(8,128)(2,1)S(1)}, u32[]{:S(2)}, u32[]{:S(2)}) collective-permute-start(bf16[64,896]{1,0:T(8,128)(2,1)S(1)} %get-tuple-element.52), channel_id=1, source_target_pairs={{0,4},{2,6},{4,0},{6,2},{8,12},{10,14},{12,8},{14,10},{1,5},{3,7},... | collective-permute-start | bytes 344072 | tf_op jit(solution)/shard_map/ppermute | solution.py:302
  31.8 7.7 %collective-permute-start.13 = (bf16[64,896]{1,0:T(8,128)(2,1)S(1)}, bf16[64,896]{1,0:T(8,128)(2,1)S(1)}, u32[]{:S(2)}, u32[]{:S(2)}) collective-permute-start(bf16[64,896]{1,0:T(8,128)(2,1)S(1)} %get-tuple-element.54), channel_id=1, source_target_pairs={{0,4},{2,6},{4,0},{6,2},{8,12},{10,14},{12,8},{14,10},{1,5},{3,7},... | collective-permute-start | bytes 344072 | tf_op jit(solution)/shard_map/ppermute | solution.py:302

commit v8 on v7

--- a/solution.py
+++ b/solution.py
@@ -119,37 +119,23 @@
     )(core, where, ids, gates, b, b_in, a, a_in, g, x)
 
 
-def rest_kernel(blocks, block, where_ref, kept_ref, came_ref, lg_ref, la_ref, x_ref, g_ref, *outs):
-    send_ref, keep_ref, outs = outs[0], outs[1], outs[2:]
-    near = where_ref[blocks + 1]
-    rows = kept_ref.shape[0] * 2 // len(outs)
-    for i in range(len(outs) // 2):
-        part = pl.ds(i * rows, rows)
-        for place, out in ((1 - near, outs[2 * i]), (near, outs[2 * i + 1])):
-            cols = pl.ds(pl.multiple_of(place * block, 128), block)
-            total = kept_ref[part, cols].astype(F32) + came_ref[part, cols].astype(F32)
-            out[...] = total.astype(out.dtype)
+def rest_kernel(blocks, where_ref, lg_ref, la_ref, x_ref, g_ref, *outs):
     lows = (lg_ref[...], la_ref[...])
-    store_products(where_ref, 1, blocks, lows, (x_ref, g_ref), send_ref, keep_ref)
-
-
-def rest_products(where, kept, came, lg, la, x, g, blocks, block, parts):
+    for j in range(blocks):
+        store_products(where_ref, 1 + j, 1, lows, (x_ref, g_ref), outs[2 * j], outs[2 * j + 1])
+
+
+def rest_products(where, lg, la, x, g, blocks, wide):
     rows = lg.shape[0]
-    wide = 2 * blocks * block
-    return pl.pallas_call(
-        functools.partial(rest_kernel, blocks, block),
-        in_specs=[SCALARS] + [VECTORS] * 6,
-        out_specs=[VECTORS] * (2 + 2 * parts),
-        out_shape=[jax.ShapeDtypeStruct((rows, wide), BF16)] * 2
-        + [
-            jax.ShapeDtypeStruct((rows // parts, block), BF16),
-            jax.ShapeDtypeStruct((rows // parts, block), F32),
-        ]
-        * parts,
-        compiler_params=params(),
-        cost_estimate=cost(2 * rows * x.shape[0] * wide, 4 * rows * wide),
+    return pl.pallas_call(
+        functools.partial(rest_kernel, blocks),
+        in_specs=[SCALARS] + [VECTORS] * 4,
+        out_specs=[VECTORS] * (2 * blocks),
+        out_shape=[jax.ShapeDtypeStruct((rows, wide), BF16)] * (2 * blocks),
+        compiler_params=params(),
+        cost_estimate=cost(4 * rows * x.shape[0] * blocks * wide, 8 * rows * blocks * wide),
         name="rest",
-    )(where, kept, came, lg, la, x, g)
+    )(where, lg, la, x, g)
 
 
 def fold_kernel(block, at, where_ref, keep_ref, came_ref, send_ref, own_ref):
@@ -311,15 +297,11 @@
     lg, la, pair, keep = low_products(
         core, where, ids, gates, rank, b, b_in, a, a_in, g_held, x_held, 2 * block
     )
-    rest_pair, rest_keep, *first = rest_products(
-        where, keep, swap(pair), lg, la, x_held, g_held, steps - 1, block, 1
-    )
-    rest_came = swap(rest_pair)
-    send, own = first
+    rest = rest_products(where, lg, la, x_held, g_held, steps - 1, 2 * block)
+    terms = [(keep, swap(pair))] + [(k, swap(p)) for p, k in zip(rest[::2], rest[1::2])]
     both, downs, ups = [], [], []
     for i, step in enumerate(order):
-        if i:
-            send, own = fold(where, block, i - 1, rest_keep, rest_came)
+        send, own = fold(where, block, 0, *terms[i])
         got = flip(send, 1)
         if step == 0:
             both.append(got)

time: 40.9 us -> 40.1 us (0.980); the launches traced: 40.2 us -> 39.9 us
  waiting for transfers between devices: 9.82 us -> 7.65 us
  starting transfers between devices: 17.3 us -> 18.7 us
  Pallas kernels: 12.2 us -> 12.7 us
    ppermute x4 -> x6, waiting for transfers between devices: 2.78 us -> 1.24 us  [shards(): swap = lambda array: lax.ppermute(array, 'adapter', SWAP)]
    ppermute x10, starting transfers between devices: 15.9 us -> 17 us  [shards(): lax.ppermute(array, 'dp', [(i, i ^ by) for i in range(replicas)])]
    pallas_call x3 -> x4, Pallas kernels: 1.94 us -> 2.59 us  [fold(): pl.pallas_call(functools.partial(fold_kernel, block, at), in_specs=[SCALA...]
    ppermute x10, waiting for transfers between devices: 7.04 us -> 6.41 us  [shards(): lax.ppermute(array, 'dp', [(i, i ^ by) for i in range(replicas)])]
    ppermute x4 -> x6, starting transfers between devices: 1.46 us -> 1.74 us  [shards(): swap = lambda array: lax.ppermute(array, 'adapter', SWAP)]
  transfers between devices with their start and end apart: 14 -> 16, of which waited for: 10 -> 8; matrix products, arithmetic and copies ran while one was open for 0% -> 0% of each run, Pallas kernels for 20% -> 25%
where the time goes in v8:
time: 40.1 us; the launch traced here: 39.9 us
  starting transfers between devices  18.7 us (47%)
  Pallas kernels  12.7 us (32%)
  waiting for transfers between devices  7.65 us (19%)
  between operations  0.74 us (2%)
    ppermute x10, starting transfers between devices, shards(): lax.ppermute(array, 'dp', [(i, i ^ by) for i in range(replicas)])  17 us
    ppermute x10, waiting for transfers between devices, shards(): lax.ppermute(array, 'dp', [(i, i ^ by) for i in range(replicas)])  6.41 us
    pallas_call x1, Pallas kernels, input_gradient(): pl.pallas_call(input_kernel, grid=(steps,), in_specs=[VECTORS] * 3, out_s...  2.8 us
    pallas_call x4, Pallas kernels, fold(): pl.pallas_call(functools.partial(fold_kernel, block, at), in_specs=[SCALA...  2.59 us
    pallas_call x1, Pallas kernels, hold(): pl.pallas_call(hold_kernel, in_specs=[ANYWHERE] * 2, out_specs=[VECTORS]...  2.2 us
    pallas_call x1, Pallas kernels, low_products(): pl.pallas_call(functools.partial(low_kernel, rank), in_specs=[SCALARS] *...  2 us
    ppermute x6, starting transfers between devices, shards(): swap = lambda array: lax.ppermute(array, 'adapter', SWAP)  1.74 us
    pallas_call x2, Pallas kernels, last(): pl.pallas_call(last_kernel, in_specs=[VECTORS] * 2, out_specs=VECTORS, ou...  1.43 us
  transfers between devices with their start and end apart: 16, of which 8 were waited for; matrix products, arithmetic and copies ran while one was open for 0% of the time, Pallas kernels for 25%

profile of v8, /device:TPU:0, one launch (start us, length us, event | category | flops | bytes accessed | tf_op | source)
XLA Modules:
  0.0 39.9 jit_solution(9080129599330391608)
XLA Ops:
  0.6 0.5 %collective-permute-start.1 = (bf16[64,7168]{1,0:T(8,128)(2,1)}, bf16[64,7168]{1,0:T(8,128)(2,1)S(1)}, u32[]{:S(2)}, u32[]{:S(2)}) collective-permute-start(bf16[64,7168]{1,0:T(8,128)(2,1)} %bitcast.12), channel_id=1, source_target_pairs={{0,1},{1,0},{2,3},{3,2},{4,5},{5,4},{6,7},{7,6},{8,9},{9,8},{10,11... | collective-permute-start | bytes 2752520 | tf_op jit(solution)/shard_map/ppermute | solution.py:284
  1.1 0.1 collective-permute-start
  1.2 0.1 stack.23.where_ref
  1.3 2.2 %hold.1 = (bf16[128,7168]{1,0:T(8,128)(2,1)S(1)}, bf16[128,7168]{1,0:T(8,128)(2,1)S(1)}) custom-call(bf16[128,7168]{1,0:T(8,128)(2,1)} %g_hbm.1, bf16[128,7168]{1,0:T(8,128)(2,1)} %x_hbm.1), custom_call_target="tpu_custom_call" | custom-call | flops 117440512 | bytes 7340032 | tf_op jit(solution)/shard_map/hold/pallas_call | solution.py:50
  3.5 0.0 collective-permute-done.1.a_in_ref.other_ref
  3.5 1.2 %collective-permute-done.b_in_ref = bf16[64,7168]{1,0:T(8,128)(2,1)S(1)} collective-permute-done((bf16[64,7168]{1,0:T(8,128)(2,1)}, bf16[64,7168]{1,0:T(8,128)(2,1)S(1)}, u32[]{:S(2)}, u32[]{:S(2)}) %collective-permute-start) | collective-permute-done | bytes 917536 | tf_op jit(solution)/shard_map/ppermute | solution.py:284
  4.8 0.0 copy-done
  4.8 0.0 copy-done.1
  4.8 0.0 copy-done.2
  4.8 0.0 copy-done.3
  4.8 2.0 %low.1 = (bf16[128,128]{1,0:T(8,128)(2,1)S(1)}, bf16[128,128]{1,0:T(8,128)(2,1)S(1)}, bf16[128,1792]{1,0:T(8,128)(2,1)S(1)}, bf16[128,1792]{1,0:T(8,128)(2,1)S(1)}) custom-call(s32[1]{0:T(128)} %bitcast.core_ref, s32[5]{0:T(128)S(1)} %stack.23.where_ref, s32[2,128]{1,0:T(2,128)S(1)} %bitcast.17, f32[2,128]{1,0:T(2,128)S(1)} %bitcast.18, ...), custom_call_target="tpu_custom_call" | custom-call | flops 352321536 | bytes 5505024 | tf_op jit(solution)/shard_map/low/pallas_call | solution.py:110
  6.8 0.4 %collective-permute-start.6 = (bf16[128,1792]{1,0:T(8,128)(2,1)S(1)}, bf16[128,1792]{1,0:T(8,128)(2,1)S(1)}, u32[]{:S(2)}, u32[]{:S(2)}) collective-permute-start(bf16[128,1792]{1,0:T(8,128)(2,1)S(1)} %get-tuple-element.49), channel_id=1, source_target_pairs={{0,1},{1,0},{2,3},{3,2},{4,5},{5,4},{6,7},{7,6},{8,9},{9,8},{10,11... | collective-permute-start | bytes 1376264 | tf_op jit(solution)/shard_map/ppermute | solution.py:284
  7.2 1.4 %rest.1 = (bf16[128,1792]{1,0:T(8,128)(2,1)S(1)}, bf16[128,1792]{1,0:T(8,128)(2,1)S(1)}, bf16[128,1792]{1,0:T(8,128)(2,1)S(1)}, bf16[128,1792]{1,0:T(8,128)(2,1)...) custom-call(s32[5]{0:T(128)S(1)} %stack.23.where_ref, ...), custom_call_target="tpu_custom_call" | custom-call | flops 352321536 | bytes 5505024 | tf_op jit(solution)/shard_map/rest/pallas_call | solution.py:130
  8.6 0.2 collective-permute-start.4
  8.8 0.4 collective-permute-start.12
  9.2 0.1 collective-permute-start.2
  9.4 0.0 collective-permute-done.6.came_ref
  9.4 0.6 %fold.6 = (bf16[128,896]{1,0:T(8,128)(2,1)S(1)}, f32[128,896]{1,0:T(8,128)S(1)}) custom-call(s32[5]{0:T(128)S(1)} %stack.23.where_ref, bf16[128,1792]{1,0:T(8,128)(2,1)S(1)} %get-tuple-element.48.keep_ref, bf16[128,1792]{1,0:T(8,128)(2,1)S(1)} %collective-permute-done.6.came_ref), custom_call_target="tpu_custom_call" | custom-call | flops 229376 | bytes 1605632 | tf_op jit(solution)/shard_map/fold/pallas_call | solution.py:150
  10.0 2.9 %collective-permute-start.7 = (bf16[128,896]{1,0:T(8,128)(2,1)S(1)}, bf16[128,896]{1,0:T(8,128)(2,1)S(1)}, u32[]{:S(2)}, u32[]{:S(2)}) collective-permute-start(bf16[128,896]{1,0:T(8,128)(2,1)S(1)} %get-tuple-element.51), channel_id=1, source_target_pairs={{0,2},{2,0},{4,6},{6,4},{8,10},{10,8},{12,14},{14,12},{1,3},{3,1},... | collective-permute-start | bytes 688136 | tf_op jit(solution)/shard_map/ppermute | solution.py:288
  13.0 0.0 collective-permute-done.4.came_ref
  13.0 0.6 %fold.5 = (bf16[128,896]{1,0:T(8,128)(2,1)S(1)}, f32[128,896]{1,0:T(8,128)S(1)}) custom-call(s32[5]{0:T(128)S(1)} %stack.23.where_ref, bf16[128,1792]{1,0:T(8,128)(2,1)S(1)} %get-tuple-element.43.keep_ref, bf16[128,1792]{1,0:T(8,128)(2,1)S(1)} %collective-permute-done.4.came_ref), custom_call_target="tpu_custom_call" | custom-call | flops 229376 | bytes 1605632 | tf_op jit(solution)/shard_map/fold/pallas_call | solution.py:150
  13.6 0.3 collective-permute-start.5
  13.9 0.0 collective-permute-done.12.came_ref
  13.9 0.6 %fold.7 = (bf16[128,896]{1,0:T(8,128)(2,1)S(1)}, f32[128,896]{1,0:T(8,128)S(1)}) custom-call(s32[5]{0:T(128)S(1)} %stack.23.where_ref, bf16[128,1792]{1,0:T(8,128)(2,1)S(1)} %get-tuple-element.56.keep_ref, bf16[128,1792]{1,0:T(8,128)(2,1)S(1)} %collective-permute-done.12.came_ref), custom_call_target="tpu_custom_call" | custom-call | flops 229376 | bytes 1605632 | tf_op jit(solution)/shard_map/fold/pallas_call | solution.py:150
  14.6 1.9 %collective-permute-start.13 = (bf16[128,896]{1,0:T(8,128)(2,1)S(1)}, bf16[128,896]{1,0:T(8,128)(2,1)S(1)}, u32[]{:S(2)}, u32[]{:S(2)}) collective-permute-start(bf16[128,896]{1,0:T(8,128)(2,1)S(1)} %get-tuple-element.59), channel_id=1, source_target_pairs={{0,2},{2,0},{4,6},{6,4},{8,10},{10,8},{12,14},{14,12},{1,3},{3,1},... | collective-permute-start | bytes 688136 | tf_op jit(solution)/shard_map/ppermute | solution.py:288
  16.4 0.0 collective-permute-done.2.came_ref
  16.4 0.6 %fold.4 = (bf16[128,896]{1,0:T(8,128)(2,1)S(1)}, f32[128,896]{1,0:T(8,128)S(1)}) custom-call(s32[5]{0:T(128)S(1)} %stack.23.where_ref, bf16[128,1792]{1,0:T(8,128)(2,1)S(1)} %get-tuple-element.37.keep_ref, bf16[128,1792]{1,0:T(8,128)(2,1)S(1)} %collective-permute-done.2.came_ref), custom_call_target="tpu_custom_call" | custom-call | flops 229376 | bytes 1605632 | tf_op jit(solution)/shard_map/fold/pallas_call | solution.py:150
  17.1 2.3 %collective-permute-done.7.came_ref = bf16[128,896]{1,0:T(8,128)(2,1)S(1)} collective-permute-done((bf16[128,896]{1,0:T(8,128)(2,1)S(1)}, bf16[128,896]{1,0:T(8,128)(2,1)S(1)}, u32[]{:S(2)}, u32[]{:S(2)}) %collective-permute-start.7) | collective-permute-done | bytes 229408 | tf_op jit(solution)/shard_map/ppermute | solution.py:288
  19.4 2.2 %collective-permute-start.8 = (bf16[64,896]{1,0:T(8,128)(2,1)S(1)}, bf16[64,896]{1,0:T(8,128)(2,1)S(1)}, u32[]{:S(2)}, u32[]{:S(2)}) collective-permute-start(bf16[64,896]{1,0:T(8,128)(2,1)S(1)} %get-tuple-element.52), channel_id=1, source_target_pairs={{0,4},{2,6},{4,0},{6,2},{8,12},{10,14},{12,8},{14,10},{1,5},{3,7},... | collective-permute-start | bytes 344072 | tf_op jit(solution)/shard_map/ppermute | solution.py:288
  21.6 1.5 %collective-permute-start.3 = (bf16[128,896]{1,0:T(8,128)(2,1)S(1)}, bf16[128,896]{1,0:T(8,128)(2,1)S(1)}, u32[]{:S(2)}, u32[]{:S(2)}) collective-permute-start(bf16[128,896]{1,0:T(8,128)(2,1)S(1)} %get-tuple-element.39), channel_id=1, source_target_pairs={{0,2},{2,0},{4,6},{6,4},{8,10},{10,8},{12,14},{14,12},{1,3},{3,1},... | collective-permute-start | bytes 688136 | tf_op jit(solution)/shard_map/ppermute | solution.py:288
  23.1 0.4 %collective-permute-start.10 = (bf16[64,896]{1,0:T(8,128)(2,1)S(1)}, bf16[64,896]{1,0:T(8,128)(2,1)S(1)}, u32[]{:S(2)}, u32[]{:S(2)}) collective-permute-start(bf16[64,896]{1,0:T(8,128)(2,1)S(1)} %get-tuple-element.54), channel_id=1, source_target_pairs={{0,4},{2,6},{4,0},{6,2},{8,12},{10,14},{12,8},{14,10},{1,5},{3,7},... | collective-permute-start | bytes 344072 | tf_op jit(solution)/shard_map/ppermute | solution.py:288
  23.5 0.7 %collective-permute-done.5.came_ref = bf16[128,896]{1,0:T(8,128)(2,1)S(1)} collective-permute-done((bf16[128,896]{1,0:T(8,128)(2,1)S(1)}, bf16[128,896]{1,0:T(8,128)(2,1)S(1)}, u32[]{:S(2)}, u32[]{:S(2)}) %collective-permute-start.5) | collective-permute-done | bytes 229408 | tf_op jit(solution)/shard_map/ppermute | solution.py:288
  24.3 0.9 %collective-permute-done.8.refs_0_ = bf16[64,896]{1,0:T(8,128)(2,1)S(1)} collective-permute-done((bf16[64,896]{1,0:T(8,128)(2,1)S(1)}, bf16[64,896]{1,0:T(8,128)(2,1)S(1)}, u32[]{:S(2)}, u32[]{:S(2)}) %collective-permute-start.8) | collective-permute-done | bytes 114720 | tf_op jit(solution)/shard_map/ppermute | solution.py:288
  25.2 3.4 %collective-permute-start.9 = (bf16[64,896]{1,0:T(8,128)(2,1)S(1)}, bf16[64,896]{1,0:T(8,128)(2,1)S(1)}, u32[]{:S(2)}, u32[]{:S(2)}) collective-permute-start(bf16[64,896]{1,0:T(8,128)(2,1)S(1)} %add.8), channel_id=1, source_target_pairs={{0,8},{2,10},{4,12},{6,14},{8,0},{10,2},{12,4},{14,6},{1,9},{3,11}... | collective-permute-start | bytes 344072 | tf_op jit(solution)/shard_map/ppermute | solution.py:288
  28.6 0.3 collective-permute-done.10.refs_0_
  29.0 2.2 %collective-permute-start.11 = (bf16[64,896]{1,0:T(8,128)(2,1)S(1)}, bf16[64,896]{1,0:T(8,128)(2,1)S(1)}, u32[]{:S(2)}, u32[]{:S(2)}) collective-permute-start(bf16[64,896]{1,0:T(8,128)(2,1)S(1)} %add.9), channel_id=1, source_target_pairs={{0,8},{2,10},{4,12},{6,14},{8,0},{10,2},{12,4},{14,6},{1,9},{3,11}... | collective-permute-start | bytes 344072 | tf_op jit(solution)/shard_map/ppermute | solution.py:288
  31.2 0.0 collective-permute-done.13.came_ref
  31.3 0.1 collective-permute-start.14
  31.4 2.0 %collective-permute-start.15 = (bf16[64,896]{1,0:T(8,128)(2,1)S(1)}, bf16[64,896]{1,0:T(8,128)(2,1)S(1)}, u32[]{:S(2)}, u32[]{:S(2)}) collective-permute-start(bf16[64,896]{1,0:T(8,128)(2,1)S(1)} %get-tuple-element.62), channel_id=1, source_target_pairs={{0,4},{2,6},{4,0},{6,2},{8,12},{10,14},{12,8},{14,10},{1,5},{3,7},... | collective-permute-start | bytes 344072 | tf_op jit(solution)/shard_map/ppermute | solution.py:288
  33.4 2.8 %input.1 = bf16[128,7168]{1,0:T(8,128)(2,1)} custom-call(bf16[128,128]{1,0:T(8,128)(2,1)S(1)} %get-tuple-element.35.low_ref.lg_ref, bf16[64,7168]{1,0:T(8,128)(2,1)S(1)} %bitcast.14, bf16[64,7168]{1,0:T(8,128)(2,1)S(1)} %collective-permute-done.1.a_in_ref.other_ref), custom_call_target="tpu_custom_call" | custom-call | flops 234881024 | bytes 3670016 | tf_op jit(solution)/shard_map/input/pallas_call | solution.py:262
  36.2 0.0 collective-permute-done.3.refs_0_
  36.2 0.0 collective-permute-done.9.refs_1_
  36.2 1.0 %collective-permute-done.11.refs_2_ = bf16[64,896]{1,0:T(8,128)(2,1)S(1)} collective-permute-done((bf16[64,896]{1,0:T(8,128)(2,1)S(1)}, bf16[64,896]{1,0:T(8,128)(2,1)S(1)}, u32[]{:S(2)}, u32[]{:S(2)}) %collective-permute-start.11) | collective-permute-done | bytes 114720 | tf_op jit(solution)/shard_map/ppermute | solution.py:288
  37.2 0.1 total.1
  37.2 0.7 %collective-permute-done.14.came_ref = bf16[64,896]{1,0:T(8,128)(2,1)S(1)} collective-permute-done((bf16[64,896]{1,0:T(8,128)(2,1)S(1)}, bf16[64,896]{1,0:T(8,128)(2,1)S(1)}, u32[]{:S(2)}, u32[]{:S(2)}) %collective-permute-start.14) | collective-permute-done | bytes 114720 | tf_op jit(solution)/shard_map/ppermute | solution.py:288
  38.0 0.7 %last.2 = f32[64,896]{1,0:T(8,128)} custom-call(f32[64,896]{1,0:T(8,128)S(1)} %get-tuple-element.55.total_ref, bf16[64,896]{1,0:T(8,128)(2,1)S(1)} %collective-permute-done.14.came_ref), custom_call_target="tpu_custom_call" | custom-call | flops 57344 | bytes 573440 | tf_op jit(solution)/shard_map/last/pallas_call | solution.py:236
  38.7 0.5 %collective-permute-done.15.came_ref = bf16[64,896]{1,0:T(8,128)(2,1)S(1)} collective-permute-done((bf16[64,896]{1,0:T(8,128)(2,1)S(1)}, bf16[64,896]{1,0:T(8,128)(2,1)S(1)}, u32[]{:S(2)}, u32[]{:S(2)}) %collective-permute-start.15) | collective-permute-done | bytes 114720 | tf_op jit(solution)/shard_map/ppermute | solution.py:288
  39.2 0.7 %last.3 = f32[64,896]{1,0:T(8,128)} custom-call(f32[64,896]{1,0:T(8,128)S(1)} %get-tuple-element.61.total_ref, bf16[64,896]{1,0:T(8,128)(2,1)S(1)} %collective-permute-done.15.came_ref), custom_call_target="tpu_custom_call" | custom-call | flops 57344 | bytes 573440 | tf_op jit(solution)/shard_map/last/pallas_call | solution.py:236
  (9 shorter events, 0.2 us)
Async XLA Ops:
  0.6 2.9 %collective-permute-start.1 = (bf16[64,7168]{1,0:T(8,128)(2,1)}, bf16[64,7168]{1,0:T(8,128)(2,1)S(1)}, u32[]{:S(2)}, u32[]{:S(2)}) collective-permute-start(bf16[64,7168]{1,0:T(8,128)(2,1)} %bitcast.12), channel_id=1, source_target_pairs={{0,1},{1,0},{2,3},{3,2},{4,5},{5,4},{6,7},{7,6},{8,9},{9,8},{10,11... | collective-permute-start | bytes 2752520 | tf_op jit(solution)/shard_map/ppermute | solution.py:284
  1.1 3.6 %collective-permute-start = (bf16[64,7168]{1,0:T(8,128)(2,1)}, bf16[64,7168]{1,0:T(8,128)(2,1)S(1)}, u32[]{:S(2)}, u32[]{:S(2)}) collective-permute-start(bf16[64,7168]{1,0:T(8,128)(2,1)} %bitcast.15), channel_id=1, source_target_pairs={{0,1},{1,0},{2,3},{3,2},{4,5},{5,4},{6,7},{7,6},{8,9},{9,8},{10,11... | collective-permute-start | bytes 2752520 | tf_op jit(solution)/shard_map/ppermute | solution.py:284
  1.3 3.5 %copy-start = (bf16[4,16,7168]{2,1,0:T(8,128)(2,1)S(1)}, bf16[4,16,7168]{2,1,0:T(8,128)(2,1)}, u32[]{:S(2)}) copy-start(bf16[4,16,7168]{2,1,0:T(8,128)(2,1)} %param.10) | copy-start | bytes 2752516
  1.3 3.5 %copy-start.1 = (bf16[4,16,7168]{2,1,0:T(8,128)(2,1)S(1)}, bf16[4,16,7168]{2,1,0:T(8,128)(2,1)}, u32[]{:S(2)}) copy-start(bf16[4,16,7168]{2,1,0:T(8,128)(2,1)} %param.11) | copy-start | bytes 2752516
  1.3 3.5 %copy-start.2 = (s32[128,2]{0,1:T(2,128)S(1)}, s32[128,2]{0,1:T(2,128)}, u32[]{:S(2)}) copy-start(s32[128,2]{0,1:T(2,128)} %param.8) | copy-start | bytes 3076
  1.3 3.5 %copy-start.3 = (f32[128,2]{0,1:T(2,128)S(1)}, f32[128,2]{0,1:T(2,128)}, u32[]{:S(2)}) copy-start(f32[128,2]{0,1:T(2,128)} %param.9) | copy-start | bytes 3076
  6.8 2.6 %collective-permute-start.6 = (bf16[128,1792]{1,0:T(8,128)(2,1)S(1)}, bf16[128,1792]{1,0:T(8,128)(2,1)S(1)}, u32[]{:S(2)}, u32[]{:S(2)}) collective-permute-start(bf16[128,1792]{1,0:T(8,128)(2,1)S(1)} %get-tuple-element.49), channel_id=1, source_target_pairs={{0,1},{1,0},{2,3},{3,2},{4,5},{5,4},{6,7},{7,6},{8,9},{9,8},{10,11... | collective-permute-start | bytes 1376264 | tf_op jit(solution)/shard_map/ppermute | solution.py:284
  8.6 4.3 %collective-permute-start.4 = (bf16[128,1792]{1,0:T(8,128)(2,1)S(1)}, bf16[128,1792]{1,0:T(8,128)(2,1)S(1)}, u32[]{:S(2)}, u32[]{:S(2)}) collective-permute-start(bf16[128,1792]{1,0:T(8,128)(2,1)S(1)} %get-tuple-element.44), channel_id=1, source_target_pairs={{0,1},{1,0},{2,3},{3,2},{4,5},{5,4},{6,7},{7,6},{8,9},{9,8},{10,11... | collective-permute-start | bytes 1376264 | tf_op jit(solution)/shard_map/ppermute | solution.py:284
  8.8 5.1 %collective-permute-start.12 = (bf16[128,1792]{1,0:T(8,128)(2,1)S(1)}, bf16[128,1792]{1,0:T(8,128)(2,1)S(1)}, u32[]{:S(2)}, u32[]{:S(2)}) collective-permute-start(bf16[128,1792]{1,0:T(8,128)(2,1)S(1)} %get-tuple-element.57), channel_id=1, source_target_pairs={{0,1},{1,0},{2,3},{3,2},{4,5},{5,4},{6,7},{7,6},{8,9},{9,8},{10,11... | collective-permute-start | bytes 1376264 | tf_op jit(solution)/shard_map/ppermute | solution.py:284
  9.2 7.2 %collective-permute-start.2 = (bf16[128,1792]{1,0:T(8,128)(2,1)S(1)}, bf16[128,1792]{1,0:T(8,128)(2,1)S(1)}, u32[]{:S(2)}, u32[]{:S(2)}) collective-permute-start(bf16[128,1792]{1,0:T(8,128)(2,1)S(1)} %get-tuple-element.38), channel_id=1, source_target_pairs={{0,1},{1,0},{2,3},{3,2},{4,5},{5,4},{6,7},{7,6},{8,9},{9,8},{10,11... | collective-permute-start | bytes 1376264 | tf_op jit(solution)/shard_map/ppermute | solution.py:284
  10.0 9.3 %collective-permute-start.7 = (bf16[128,896]{1,0:T(8,128)(2,1)S(1)}, bf16[128,896]{1,0:T(8,128)(2,1)S(1)}, u32[]{:S(2)}, u32[]{:S(2)}) collective-permute-start(bf16[128,896]{1,0:T(8,128)(2,1)S(1)} %get-tuple-element.51), channel_id=1, source_target_pairs={{0,2},{2,0},{4,6},{6,4},{8,10},{10,8},{12,14},{14,12},{1,3},{3,1},... | collective-permute-start | bytes 688136 | tf_op jit(solution)/shard_map/ppermute | solution.py:288
  13.6 10.6 %collective-permute-start.5 = (bf16[128,896]{1,0:T(8,128)(2,1)S(1)}, bf16[128,896]{1,0:T(8,128)(2,1)S(1)}, u32[]{:S(2)}, u32[]{:S(2)}) collective-permute-start(bf16[128,896]{1,0:T(8,128)(2,1)S(1)} %get-tuple-element.46), channel_id=1, source_target_pairs={{0,2},{2,0},{4,6},{6,4},{8,10},{10,8},{12,14},{14,12},{1,3},{3,1},... | collective-permute-start | bytes 688136 | tf_op jit(solution)/shard_map/ppermute | solution.py:288
  14.6 16.7 %collective-permute-start.13 = (bf16[128,896]{1,0:T(8,128)(2,1)S(1)}, bf16[128,896]{1,0:T(8,128)(2,1)S(1)}, u32[]{:S(2)}, u32[]{:S(2)}) collective-permute-start(bf16[128,896]{1,0:T(8,128)(2,1)S(1)} %get-tuple-element.59), channel_id=1, source_target_pairs={{0,2},{2,0},{4,6},{6,4},{8,10},{10,8},{12,14},{14,12},{1,3},{3,1},... | collective-permute-start | bytes 688136 | tf_op jit(solution)/shard_map/ppermute | solution.py:288
  19.4 5.8 %collective-permute-start.8 = (bf16[64,896]{1,0:T(8,128)(2,1)S(1)}, bf16[64,896]{1,0:T(8,128)(2,1)S(1)}, u32[]{:S(2)}, u32[]{:S(2)}) collective-permute-start(bf16[64,896]{1,0:T(8,128)(2,1)S(1)} %get-tuple-element.52), channel_id=1, source_target_pairs={{0,4},{2,6},{4,0},{6,2},{8,12},{10,14},{12,8},{14,10},{1,5},{3,7},... | collective-permute-start | bytes 344072 | tf_op jit(solution)/shard_map/ppermute | solution.py:288
  21.6 14.6 %collective-permute-start.3 = (bf16[128,896]{1,0:T(8,128)(2,1)S(1)}, bf16[128,896]{1,0:T(8,128)(2,1)S(1)}, u32[]{:S(2)}, u32[]{:S(2)}) collective-permute-start(bf16[128,896]{1,0:T(8,128)(2,1)S(1)} %get-tuple-element.39), channel_id=1, source_target_pairs={{0,2},{2,0},{4,6},{6,4},{8,10},{10,8},{12,14},{14,12},{1,3},{3,1},... | collective-permute-start | bytes 688136 | tf_op jit(solution)/shard_map/ppermute | solution.py:288
  23.1 5.9 %collective-permute-start.10 = (bf16[64,896]{1,0:T(8,128)(2,1)S(1)}, bf16[64,896]{1,0:T(8,128)(2,1)S(1)}, u32[]{:S(2)}, u32[]{:S(2)}) collective-permute-start(bf16[64,896]{1,0:T(8,128)(2,1)S(1)} %get-tuple-element.54), channel_id=1, source_target_pairs={{0,4},{2,6},{4,0},{6,2},{8,12},{10,14},{12,8},{14,10},{1,5},{3,7},... | collective-permute-start | bytes 344072 | tf_op jit(solution)/shard_map/ppermute | solution.py:288
  25.2 11.0 %collective-permute-start.9 = (bf16[64,896]{1,0:T(8,128)(2,1)S(1)}, bf16[64,896]{1,0:T(8,128)(2,1)S(1)}, u32[]{:S(2)}, u32[]{:S(2)}) collective-permute-start(bf16[64,896]{1,0:T(8,128)(2,1)S(1)} %add.8), channel_id=1, source_target_pairs={{0,8},{2,10},{4,12},{6,14},{8,0},{10,2},{12,4},{14,6},{1,9},{3,11}... | collective-permute-start | bytes 344072 | tf_op jit(solution)/shard_map/ppermute | solution.py:288
  29.0 8.2 %collective-permute-start.11 = (bf16[64,896]{1,0:T(8,128)(2,1)S(1)}, bf16[64,896]{1,0:T(8,128)(2,1)S(1)}, u32[]{:S(2)}, u32[]{:S(2)}) collective-permute-start(bf16[64,896]{1,0:T(8,128)(2,1)S(1)} %add.9), channel_id=1, source_target_pairs={{0,8},{2,10},{4,12},{6,14},{8,0},{10,2},{12,4},{14,6},{1,9},{3,11}... | collective-permute-start | bytes 344072 | tf_op jit(solution)/shard_map/ppermute | solution.py:288
  31.3 6.7 %collective-permute-start.14 = (bf16[64,896]{1,0:T(8,128)(2,1)S(1)}, bf16[64,896]{1,0:T(8,128)(2,1)S(1)}, u32[]{:S(2)}, u32[]{:S(2)}) collective-permute-start(bf16[64,896]{1,0:T(8,128)(2,1)S(1)} %get-tuple-element.60), channel_id=1, source_target_pairs={{0,4},{2,6},{4,0},{6,2},{8,12},{10,14},{12,8},{14,10},{1,5},{3,7},... | collective-permute-start | bytes 344072 | tf_op jit(solution)/shard_map/ppermute | solution.py:288
  31.4 7.8 %collective-permute-start.15 = (bf16[64,896]{1,0:T(8,128)(2,1)S(1)}, bf16[64,896]{1,0:T(8,128)(2,1)S(1)}, u32[]{:S(2)}, u32[]{:S(2)}) collective-permute-start(bf16[64,896]{1,0:T(8,128)(2,1)S(1)} %get-tuple-element.62), channel_id=1, source_target_pairs={{0,4},{2,6},{4,0},{6,2},{8,12},{10,14},{12,8},{14,10},{1,5},{3,7},... | collective-permute-start | bytes 344072 | tf_op jit(solution)/shard_map/ppermute | solution.py:288

commit v9 on v8

--- a/solution.py
+++ b/solution.py
@@ -14,7 +14,6 @@
 HOLD_LIMIT = 50 * 1024 * 1024
 VECTORS = pl.BlockSpec(memory_space=pltpu.VMEM)
 ANYWHERE = pl.BlockSpec(memory_space=pl.ANY)
-SCALARS = pl.BlockSpec(memory_space=pltpu.SMEM)
 NT = (((1,), (1,)), ((), ()))
 TN = (((0,), (0,)), ((), ()))
 
@@ -74,11 +73,22 @@
     return weight
 
 
-def store_products(where_ref, at, blocks, lows, outers, send_ref, keep_ref):
+class Places:
+    def __init__(self, pairs):
+        self.pairs = pairs
+
+    def far(self, j):
+        return (lax.axis_index("dp") >> 1) ^ (self.pairs - 1 - j)
+
+    def near(self):
+        return lax.axis_index("dp") & 1
+
+
+def store_products(places, at, blocks, lows, outers, send_ref, keep_ref):
     wide = send_ref.shape[1] // blocks
     rows = send_ref.shape[0] // 2
     for j in range(blocks):
-        cols = pl.ds(pl.multiple_of(where_ref[at + j] * wide, 128), wide)
+        cols = pl.ds(pl.multiple_of(places.far(at + j) * wide, 128), wide)
         into = pl.ds(j * wide, wide)
         for i, (low, outer) in enumerate(zip(lows, outers)):
             product = jnp.dot(low, outer[:, cols], preferred_element_type=F32).astype(BF16)
@@ -95,61 +105,61 @@
     return total
 
 
-def low_kernel(rank, core_ref, where_ref, ids_ref, gates_ref, b_ref, b_in_ref, a_ref, a_in_ref, g_ref, x_ref,
+def low_kernel(rank, places, ids_ref, gates_ref, b_ref, b_in_ref, a_ref, a_in_ref, g_ref, x_ref,
                lg_ref, la_ref, send_ref, keep_ref):
-    weight = gate_columns(1 - core_ref[0], ids_ref[...], gates_ref[...], 2 * b_ref.shape[0], rank)
+    weight = gate_columns(1 - lax.axis_index("adapter"), ids_ref[...], gates_ref[...], 2 * b_ref.shape[0], rank)
     sums = factor_sum(g_ref, b_in_ref, b_ref), factor_sum(x_ref, a_in_ref, a_ref)
     lows = [(rows * weight).astype(BF16) for rows in sums]
     lg_ref[...], la_ref[...] = lows
-    store_products(where_ref, 0, 1, lows, (x_ref, g_ref), send_ref, keep_ref)
-
-
-def low_products(core, where, ids, gates, rank, b, b_in, a, a_in, g, x, wide):
+    store_products(places, 0, 1, lows, (x_ref, g_ref), send_ref, keep_ref)
+
+
+def low_products(places, ids, gates, rank, b, b_in, a, a_in, g, x, wide):
     rows, width = b_in.shape
     tokens = x.shape[0]
     return pl.pallas_call(
-        functools.partial(low_kernel, rank),
-        in_specs=[SCALARS] * 2 + [VECTORS] * 8,
+        functools.partial(low_kernel, rank, places),
+        in_specs=[VECTORS] * 8,
         out_specs=[VECTORS] * 4,
         out_shape=[jax.ShapeDtypeStruct((2 * rows, tokens), BF16)] * 2
         + [jax.ShapeDtypeStruct((2 * rows, wide), BF16)] * 2,
         compiler_params=params(),
         cost_estimate=cost(4 * rows * tokens * (width + 2 * wide), 4 * (rows + tokens) * width),
         name="low",
-    )(core, where, ids, gates, b, b_in, a, a_in, g, x)
-
-
-def rest_kernel(blocks, where_ref, lg_ref, la_ref, x_ref, g_ref, *outs):
+    )(ids, gates, b, b_in, a, a_in, g, x)
+
+
+def rest_kernel(blocks, places, lg_ref, la_ref, x_ref, g_ref, *outs):
     lows = (lg_ref[...], la_ref[...])
     for j in range(blocks):
-        store_products(where_ref, 1 + j, 1, lows, (x_ref, g_ref), outs[2 * j], outs[2 * j + 1])
-
-
-def rest_products(where, lg, la, x, g, blocks, wide):
+        store_products(places, 1 + j, 1, lows, (x_ref, g_ref), outs[2 * j], outs[2 * j + 1])
+
+
+def rest_products(places, lg, la, x, g, blocks, wide):
     rows = lg.shape[0]
     return pl.pallas_call(
-        functools.partial(rest_kernel, blocks),
-        in_specs=[SCALARS] + [VECTORS] * 4,
+        functools.partial(rest_kernel, blocks, places),
+        in_specs=[VECTORS] * 4,
         out_specs=[VECTORS] * (2 * blocks),
         out_shape=[jax.ShapeDtypeStruct((rows, wide), BF16)] * (2 * blocks),
         compiler_params=params(),
         cost_estimate=cost(4 * rows * x.shape[0] * blocks * wide, 8 * rows * blocks * wide),
         name="rest",
-    )(where, lg, la, x, g)
-
-
-def fold_kernel(block, at, where_ref, keep_ref, came_ref, send_ref, own_ref):
-    near = where_ref[where_ref.shape[0] - 1]
+    )(lg, la, x, g)
+
+
+def fold_kernel(block, at, places, keep_ref, came_ref, send_ref, own_ref):
+    near = places.near()
     for place, out in ((1 - near, send_ref), (near, own_ref)):
         cols = pl.ds(pl.multiple_of((2 * at + place) * block, 128), block)
         out[...] = (keep_ref[:, cols].astype(F32) + came_ref[:, cols].astype(F32)).astype(out.dtype)
 
 
-def fold(where, block, at, keep, came):
+def fold(places, block, at, keep, came):
     rows = keep.shape[0]
     return pl.pallas_call(
-        functools.partial(fold_kernel, block, at),
-        in_specs=[SCALARS] + [VECTORS] * 2,
+        functools.partial(fold_kernel, block, at, places),
+        in_specs=[VECTORS] * 2,
         out_specs=[VECTORS] * 2,
         out_shape=[
             jax.ShapeDtypeStruct((rows, block), BF16),
@@ -158,7 +168,7 @@
         compiler_params=params(),
         cost_estimate=cost(2 * rows * block, 14 * rows * block),
         name="fold",
-    )(where, keep, came)
+    )(keep, came)
 
 
 def add_kernel(keep_ref, *refs):
@@ -277,14 +287,12 @@
     rows = count * rank
     replicas = lax.axis_size("dp")
     block = width // replicas
-    core = lax.axis_index("adapter").astype(jnp.int32).reshape(1)
+    core = lax.axis_index("adapter")
     a = down_w.reshape(rows, width)
     b = up_w.reshape(rows, width)
     ids, gates = ids.T, gates.T
     swap = lambda array: lax.ppermute(array, "adapter", SWAP)
     b_in = swap(b)
-    me = lax.axis_index("dp").astype(jnp.int32)
-    far, near = me // 2, me % 2
     flip = lambda array, by: lax.ppermute(array, "dp", [(i, i ^ by) for i in range(replicas)])
     steps = replicas // 2
     if steps < 2 or replicas & (replicas - 1) or block % 128:
@@ -293,15 +301,15 @@
     a_in = swap(a)
     g_held, x_held = hold(g, x)
     order = list(reversed(range(steps)))
-    where = jnp.stack([far ^ step for step in order] + [near])
+    places = Places(steps)
     lg, la, pair, keep = low_products(
-        core, where, ids, gates, rank, b, b_in, a, a_in, g_held, x_held, 2 * block
+        places, ids, gates, rank, b, b_in, a, a_in, g_held, x_held, 2 * block
     )
-    rest = rest_products(where, lg, la, x_held, g_held, steps - 1, 2 * block)
+    rest = rest_products(places, lg, la, x_held, g_held, steps - 1, 2 * block)
     terms = [(keep, swap(pair))] + [(k, swap(p)) for p, k in zip(rest[::2], rest[1::2])]
     both, downs, ups = [], [], []
     for i, step in enumerate(order):
-        send, own = fold(where, block, 0, *terms[i])
+        send, own = fold(places, block, 0, *terms[i])
         got = flip(send, 1)
         if step == 0:
             both.append(got)
@@ -324,7 +332,7 @@
 def plain(core, ids, gates, rank, x, g, a, b, a_in, b_in, swap):
     rows = a.shape[0]
     dot = functools.partial(lax.dot_general, preferred_element_type=F32)
-    weight = gate_columns(core[0], ids, gates, 2 * rows, rank)
+    weight = gate_columns(core, ids, gates, 2 * rows, rank)
     both_a, both_b = jnp.concatenate([a, a_in]), jnp.concatenate([b, b_in])
     lg = (dot(both_b, g, NT) * weight).astype(BF16)
     la = (dot(both_a, x, NT) * weight).astype(BF16)

time: 40.1 us -> 38.4 us (0.958)
  Pallas kernels: 12.7 us -> 9.35 us
  waiting for transfers between devices: 7.65 us -> 9.38 us
    pallas_call x6, Pallas kernels: 6 us -> 2.71 us  [the longest x1 1.45 us: low_products(): pl.pallas_call(functools.partial(low_kernel, rank, places), in_specs=[VEC...]
    ppermute x10, waiting for transfers between devices: 6.41 us -> 8.07 us  [shards(): lax.ppermute(array, 'dp', [(i, i ^ by) for i in range(replicas)])]
  transfers between devices with their start and end apart: 16 -> 16, of which waited for: 8 -> 8; matrix products, arithmetic and copies ran while one was open for 0% -> 0% of each run, Pallas kernels for 25% -> 19%
where the time goes in v9:
time: 38.4 us; the launch traced here: 38.2 us
  starting transfers between devices  18.8 us (49%)
  waiting for transfers between devices  9.38 us (24%)
  Pallas kernels  9.35 us (24%)
  between operations  0.73 us (2%)
    ppermute x10, starting transfers between devices, shards(): lax.ppermute(array, 'dp', [(i, i ^ by) for i in range(replicas)])  17 us
    ppermute x10, waiting for transfers between devices, shards(): lax.ppermute(array, 'dp', [(i, i ^ by) for i in range(replicas)])  8.07 us
    pallas_call x1, Pallas kernels, input_gradient(): pl.pallas_call(input_kernel, grid=(steps,), in_specs=[VECTORS] * 3, out_s...  2.81 us
    pallas_call x1, Pallas kernels, hold(): pl.pallas_call(hold_kernel, in_specs=[ANYWHERE] * 2, out_specs=[VECTORS]...  2.17 us
    ppermute x6, starting transfers between devices, shards(): swap = lambda array: lax.ppermute(array, 'adapter', SWAP)  1.79 us
    pallas_call x1, Pallas kernels, low_products(): pl.pallas_call(functools.partial(low_kernel, rank, places), in_specs=[VEC...  1.45 us
    pallas_call x2, Pallas kernels, last(): pl.pallas_call(last_kernel, in_specs=[VECTORS] * 2, out_specs=VECTORS, ou...  1.42 us
    ppermute x6, waiting for transfers between devices, shards(): swap = lambda array: lax.ppermute(array, 'adapter', SWAP)  1.31 us
  transfers between devices with their start and end apart: 16, of which 8 were waited for; matrix products, arithmetic and copies ran while one was open for 0% of the time, Pallas kernels for 19%

profile of v9, /device:TPU:0, one launch (start us, length us, event | category | flops | bytes accessed | tf_op | source)
XLA Modules:
  0.0 38.2 jit_solution(9473249241639025168)
XLA Ops:
  0.6 0.5 %collective-permute-start.1 = (bf16[64,7168]{1,0:T(8,128)(2,1)}, bf16[64,7168]{1,0:T(8,128)(2,1)S(1)}, u32[]{:S(2)}, u32[]{:S(2)}) collective-permute-start(bf16[64,7168]{1,0:T(8,128)(2,1)} %bitcast.6), channel_id=1, source_target_pairs={{0,1},{1,0},{2,3},{3,2},{4,5},{5,4},{6,7},{7,6},{8,9},{9,8},{10,11... | collective-permute-start | bytes 2752520 | tf_op jit(solution)/shard_map/ppermute | solution.py:294
  1.1 0.0 copy-start
  1.2 0.1 collective-permute-start
  1.3 2.2 %hold.1 = (bf16[128,7168]{1,0:T(8,128)(2,1)S(1)}, bf16[128,7168]{1,0:T(8,128)(2,1)S(1)}) custom-call(bf16[128,7168]{1,0:T(8,128)(2,1)} %g_hbm.1, bf16[128,7168]{1,0:T(8,128)(2,1)} %x_hbm.1), custom_call_target="tpu_custom_call" | custom-call | flops 117440512 | bytes 7340032 | tf_op jit(solution)/shard_map/hold/pallas_call | solution.py:49
  3.5 0.0 collective-permute-done.1.a_in_ref.other_ref
  3.5 1.3 %collective-permute-done.b_in_ref = bf16[64,7168]{1,0:T(8,128)(2,1)S(1)} collective-permute-done((bf16[64,7168]{1,0:T(8,128)(2,1)}, bf16[64,7168]{1,0:T(8,128)(2,1)S(1)}, u32[]{:S(2)}, u32[]{:S(2)}) %collective-permute-start) | collective-permute-done | bytes 917536 | tf_op jit(solution)/shard_map/ppermute | solution.py:294
  4.8 0.0 copy-done
  4.8 0.0 copy-done.1
  4.8 0.0 copy-done.2
  4.8 0.0 copy-done.3
  4.8 1.4 %low.1 = (bf16[128,128]{1,0:T(8,128)(2,1)S(1)}, bf16[128,128]{1,0:T(8,128)(2,1)S(1)}, bf16[128,1792]{1,0:T(8,128)(2,1)S(1)}, bf16[128,1792]{1,0:T(8,128)(2,1)S(1)}) custom-call(s32[2,128]{1,0:T(2,128)S(1)} %bitcast.11, f32[2,128]{1,0:T(2,128)S(1)} %bitcast.12, bf16[64,7168]{1,0:T(8,128)(2,1)S(1)} %bitcast.10, ...), custom_call_target="tpu_custom_call" | custom-call | flops 352321536 | bytes 5505024 | tf_op jit(solution)/shard_map/low/pallas_call | solution.py:120
  6.2 0.4 %collective-permute-start.6 = (bf16[128,1792]{1,0:T(8,128)(2,1)S(1)}, bf16[128,1792]{1,0:T(8,128)(2,1)S(1)}, u32[]{:S(2)}, u32[]{:S(2)}) collective-permute-start(bf16[128,1792]{1,0:T(8,128)(2,1)S(1)} %get-tuple-element.49), channel_id=1, source_target_pairs={{0,1},{1,0},{2,3},{3,2},{4,5},{5,4},{6,7},{7,6},{8,9},{9,8},{10,11... | collective-permute-start | bytes 1376264 | tf_op jit(solution)/shard_map/ppermute | solution.py:294
  6.7 0.9 %rest.1 = (bf16[128,1792]{1,0:T(8,128)(2,1)S(1)}, bf16[128,1792]{1,0:T(8,128)(2,1)S(1)}, bf16[128,1792]{1,0:T(8,128)(2,1)S(1)}, bf16[128,1792]{1,0:T(8,128)(2,1)...) custom-call(bf16[128,128]{1,0:T(8,128)(2,1)S(1)} %get-tuple-element.35.low_ref.lg_ref, ...), custom_call_target="tpu_custom_call" | custom-call | flops 352321536 | bytes 5505024 | tf_op jit(solution)/shard_map/rest/pallas_call | solution.py:140
  7.6 0.2 collective-permute-start.4
  7.7 0.4 %collective-permute-start.12 = (bf16[128,1792]{1,0:T(8,128)(2,1)S(1)}, bf16[128,1792]{1,0:T(8,128)(2,1)S(1)}, u32[]{:S(2)}, u32[]{:S(2)}) collective-permute-start(bf16[128,1792]{1,0:T(8,128)(2,1)S(1)} %get-tuple-element.57), channel_id=1, source_target_pairs={{0,1},{1,0},{2,3},{3,2},{4,5},{5,4},{6,7},{7,6},{8,9},{9,8},{10,11... | collective-permute-start | bytes 1376264 | tf_op jit(solution)/shard_map/ppermute | solution.py:294
  8.1 0.1 collective-permute-start.2
  8.3 0.0 collective-permute-done.6.came_ref
  8.3 0.1 fold.6
  8.4 3.0 %collective-permute-start.7 = (bf16[128,896]{1,0:T(8,128)(2,1)S(1)}, bf16[128,896]{1,0:T(8,128)(2,1)S(1)}, u32[]{:S(2)}, u32[]{:S(2)}) collective-permute-start(bf16[128,896]{1,0:T(8,128)(2,1)S(1)} %get-tuple-element.51), channel_id=1, source_target_pairs={{0,2},{2,0},{4,6},{6,4},{8,10},{10,8},{12,14},{14,12},{1,3},{3,1},... | collective-permute-start | bytes 688136 | tf_op jit(solution)/shard_map/ppermute | solution.py:296
  11.3 0.0 collective-permute-done.4.came_ref
  11.3 0.1 fold.5
  11.4 0.8 %collective-permute-start.5 = (bf16[128,896]{1,0:T(8,128)(2,1)S(1)}, bf16[128,896]{1,0:T(8,128)(2,1)S(1)}, u32[]{:S(2)}, u32[]{:S(2)}) collective-permute-start(bf16[128,896]{1,0:T(8,128)(2,1)S(1)} %get-tuple-element.46), channel_id=1, source_target_pairs={{0,2},{2,0},{4,6},{6,4},{8,10},{10,8},{12,14},{14,12},{1,3},{3,1},... | collective-permute-start | bytes 688136 | tf_op jit(solution)/shard_map/ppermute | solution.py:296
  12.3 0.0 collective-permute-done.12.came_ref
  12.3 0.1 fold.7
  12.4 1.3 %collective-permute-start.13 = (bf16[128,896]{1,0:T(8,128)(2,1)S(1)}, bf16[128,896]{1,0:T(8,128)(2,1)S(1)}, u32[]{:S(2)}, u32[]{:S(2)}) collective-permute-start(bf16[128,896]{1,0:T(8,128)(2,1)S(1)} %get-tuple-element.59), channel_id=1, source_target_pairs={{0,2},{2,0},{4,6},{6,4},{8,10},{10,8},{12,14},{14,12},{1,3},{3,1},... | collective-permute-start | bytes 688136 | tf_op jit(solution)/shard_map/ppermute | solution.py:296
  13.7 0.0 collective-permute-done.2.came_ref
  13.7 0.1 fold.4
  13.8 3.9 %collective-permute-done.7.came_ref = bf16[128,896]{1,0:T(8,128)(2,1)S(1)} collective-permute-done((bf16[128,896]{1,0:T(8,128)(2,1)S(1)}, bf16[128,896]{1,0:T(8,128)(2,1)S(1)}, u32[]{:S(2)}, u32[]{:S(2)}) %collective-permute-start.7) | collective-permute-done | bytes 229408 | tf_op jit(solution)/shard_map/ppermute | solution.py:296
  17.8 2.2 %collective-permute-start.8 = (bf16[64,896]{1,0:T(8,128)(2,1)S(1)}, bf16[64,896]{1,0:T(8,128)(2,1)S(1)}, u32[]{:S(2)}, u32[]{:S(2)}) collective-permute-start(bf16[64,896]{1,0:T(8,128)(2,1)S(1)} %get-tuple-element.52), channel_id=1, source_target_pairs={{0,4},{2,6},{4,0},{6,2},{8,12},{10,14},{12,8},{14,10},{1,5},{3,7},... | collective-permute-start | bytes 344072 | tf_op jit(solution)/shard_map/ppermute | solution.py:296
  20.0 1.5 %collective-permute-start.3 = (bf16[128,896]{1,0:T(8,128)(2,1)S(1)}, bf16[128,896]{1,0:T(8,128)(2,1)S(1)}, u32[]{:S(2)}, u32[]{:S(2)}) collective-permute-start(bf16[128,896]{1,0:T(8,128)(2,1)S(1)} %get-tuple-element.39), channel_id=1, source_target_pairs={{0,2},{2,0},{4,6},{6,4},{8,10},{10,8},{12,14},{14,12},{1,3},{3,1},... | collective-permute-start | bytes 688136 | tf_op jit(solution)/shard_map/ppermute | solution.py:296
  21.5 0.4 %collective-permute-start.10 = (bf16[64,896]{1,0:T(8,128)(2,1)S(1)}, bf16[64,896]{1,0:T(8,128)(2,1)S(1)}, u32[]{:S(2)}, u32[]{:S(2)}) collective-permute-start(bf16[64,896]{1,0:T(8,128)(2,1)S(1)} %get-tuple-element.54), channel_id=1, source_target_pairs={{0,4},{2,6},{4,0},{6,2},{8,12},{10,14},{12,8},{14,10},{1,5},{3,7},... | collective-permute-start | bytes 344072 | tf_op jit(solution)/shard_map/ppermute | solution.py:296
  21.9 0.7 %collective-permute-done.5.came_ref = bf16[128,896]{1,0:T(8,128)(2,1)S(1)} collective-permute-done((bf16[128,896]{1,0:T(8,128)(2,1)S(1)}, bf16[128,896]{1,0:T(8,128)(2,1)S(1)}, u32[]{:S(2)}, u32[]{:S(2)}) %collective-permute-start.5) | collective-permute-done | bytes 229408 | tf_op jit(solution)/shard_map/ppermute | solution.py:296
  22.7 0.9 %collective-permute-done.8.refs_0_ = bf16[64,896]{1,0:T(8,128)(2,1)S(1)} collective-permute-done((bf16[64,896]{1,0:T(8,128)(2,1)S(1)}, bf16[64,896]{1,0:T(8,128)(2,1)S(1)}, u32[]{:S(2)}, u32[]{:S(2)}) %collective-permute-start.8) | collective-permute-done | bytes 114720 | tf_op jit(solution)/shard_map/ppermute | solution.py:296
  23.6 3.4 %collective-permute-start.9 = (bf16[64,896]{1,0:T(8,128)(2,1)S(1)}, bf16[64,896]{1,0:T(8,128)(2,1)S(1)}, u32[]{:S(2)}, u32[]{:S(2)}) collective-permute-start(bf16[64,896]{1,0:T(8,128)(2,1)S(1)} %add.2), channel_id=1, source_target_pairs={{0,8},{2,10},{4,12},{6,14},{8,0},{10,2},{12,4},{14,6},{1,9},{3,11}... | collective-permute-start | bytes 344072 | tf_op jit(solution)/shard_map/ppermute | solution.py:296
  27.0 0.4 collective-permute-done.10.refs_0_
  27.4 2.2 %collective-permute-start.11 = (bf16[64,896]{1,0:T(8,128)(2,1)S(1)}, bf16[64,896]{1,0:T(8,128)(2,1)S(1)}, u32[]{:S(2)}, u32[]{:S(2)}) collective-permute-start(bf16[64,896]{1,0:T(8,128)(2,1)S(1)} %add.3), channel_id=1, source_target_pairs={{0,8},{2,10},{4,12},{6,14},{8,0},{10,2},{12,4},{14,6},{1,9},{3,11}... | collective-permute-start | bytes 344072 | tf_op jit(solution)/shard_map/ppermute | solution.py:296
  29.6 0.0 collective-permute-done.13.came_ref
  29.6 0.2 collective-permute-start.14
  29.8 1.9 %collective-permute-start.15 = (bf16[64,896]{1,0:T(8,128)(2,1)S(1)}, bf16[64,896]{1,0:T(8,128)(2,1)S(1)}, u32[]{:S(2)}, u32[]{:S(2)}) collective-permute-start(bf16[64,896]{1,0:T(8,128)(2,1)S(1)} %get-tuple-element.62), channel_id=1, source_target_pairs={{0,4},{2,6},{4,0},{6,2},{8,12},{10,14},{12,8},{14,10},{1,5},{3,7},... | collective-permute-start | bytes 344072 | tf_op jit(solution)/shard_map/ppermute | solution.py:296
  31.7 2.8 %input.1 = bf16[128,7168]{1,0:T(8,128)(2,1)} custom-call(bf16[128,128]{1,0:T(8,128)(2,1)S(1)} %get-tuple-element.35.low_ref.lg_ref, bf16[64,7168]{1,0:T(8,128)(2,1)S(1)} %bitcast.8, bf16[64,7168]{1,0:T(8,128)(2,1)S(1)} %collective-permute-done.1.a_in_ref.other_ref), custom_call_target="tpu_custom_call" | custom-call | flops 234881024 | bytes 3670016 | tf_op jit(solution)/shard_map/input/pallas_call | solution.py:272
  34.5 0.0 collective-permute-done.3.refs_0_
  34.5 0.0 collective-permute-done.9.refs_1_
  34.5 1.0 %collective-permute-done.11.refs_2_ = bf16[64,896]{1,0:T(8,128)(2,1)S(1)} collective-permute-done((bf16[64,896]{1,0:T(8,128)(2,1)S(1)}, bf16[64,896]{1,0:T(8,128)(2,1)S(1)}, u32[]{:S(2)}, u32[]{:S(2)}) %collective-permute-start.11) | collective-permute-done | bytes 114720 | tf_op jit(solution)/shard_map/ppermute | solution.py:296
  35.5 0.1 total.1
  35.6 0.7 %collective-permute-done.14.came_ref = bf16[64,896]{1,0:T(8,128)(2,1)S(1)} collective-permute-done((bf16[64,896]{1,0:T(8,128)(2,1)S(1)}, bf16[64,896]{1,0:T(8,128)(2,1)S(1)}, u32[]{:S(2)}, u32[]{:S(2)}) %collective-permute-start.14) | collective-permute-done | bytes 114720 | tf_op jit(solution)/shard_map/ppermute | solution.py:296
  36.3 0.7 %last.2 = f32[64,896]{1,0:T(8,128)} custom-call(f32[64,896]{1,0:T(8,128)S(1)} %get-tuple-element.55.total_ref, bf16[64,896]{1,0:T(8,128)(2,1)S(1)} %collective-permute-done.14.came_ref), custom_call_target="tpu_custom_call" | custom-call | flops 57344 | bytes 573440 | tf_op jit(solution)/shard_map/last/pallas_call | solution.py:246
  37.0 0.5 %collective-permute-done.15.came_ref = bf16[64,896]{1,0:T(8,128)(2,1)S(1)} collective-permute-done((bf16[64,896]{1,0:T(8,128)(2,1)S(1)}, bf16[64,896]{1,0:T(8,128)(2,1)S(1)}, u32[]{:S(2)}, u32[]{:S(2)}) %collective-permute-start.15) | collective-permute-done | bytes 114720 | tf_op jit(solution)/shard_map/ppermute | solution.py:296
  37.5 0.7 %last.3 = f32[64,896]{1,0:T(8,128)} custom-call(f32[64,896]{1,0:T(8,128)S(1)} %get-tuple-element.61.total_ref, bf16[64,896]{1,0:T(8,128)(2,1)S(1)} %collective-permute-done.15.came_ref), custom_call_target="tpu_custom_call" | custom-call | flops 57344 | bytes 573440 | tf_op jit(solution)/shard_map/last/pallas_call | solution.py:246
  (8 shorter events, 0.2 us)
Async XLA Ops:
  0.6 2.8 %collective-permute-start.1 = (bf16[64,7168]{1,0:T(8,128)(2,1)}, bf16[64,7168]{1,0:T(8,128)(2,1)S(1)}, u32[]{:S(2)}, u32[]{:S(2)}) collective-permute-start(bf16[64,7168]{1,0:T(8,128)(2,1)} %bitcast.6), channel_id=1, source_target_pairs={{0,1},{1,0},{2,3},{3,2},{4,5},{5,4},{6,7},{7,6},{8,9},{9,8},{10,11... | collective-permute-start | bytes 2752520 | tf_op jit(solution)/shard_map/ppermute | solution.py:294
  1.1 3.6 %copy-start = (bf16[4,16,7168]{2,1,0:T(8,128)(2,1)S(1)}, bf16[4,16,7168]{2,1,0:T(8,128)(2,1)}, u32[]{:S(2)}) copy-start(bf16[4,16,7168]{2,1,0:T(8,128)(2,1)} %param.10) | copy-start | bytes 2752516
  1.2 3.6 %copy-start.1 = (bf16[4,16,7168]{2,1,0:T(8,128)(2,1)S(1)}, bf16[4,16,7168]{2,1,0:T(8,128)(2,1)}, u32[]{:S(2)}) copy-start(bf16[4,16,7168]{2,1,0:T(8,128)(2,1)} %param.11) | copy-start | bytes 2752516
  1.2 3.6 %copy-start.2 = (s32[128,2]{0,1:T(2,128)S(1)}, s32[128,2]{0,1:T(2,128)}, u32[]{:S(2)}) copy-start(s32[128,2]{0,1:T(2,128)} %param.8) | copy-start | bytes 3076
  1.2 3.6 %copy-start.3 = (f32[128,2]{0,1:T(2,128)S(1)}, f32[128,2]{0,1:T(2,128)}, u32[]{:S(2)}) copy-start(f32[128,2]{0,1:T(2,128)} %param.9) | copy-start | bytes 3076
  1.2 3.6 %collective-permute-start = (bf16[64,7168]{1,0:T(8,128)(2,1)}, bf16[64,7168]{1,0:T(8,128)(2,1)S(1)}, u32[]{:S(2)}, u32[]{:S(2)}) collective-permute-start(bf16[64,7168]{1,0:T(8,128)(2,1)} %bitcast.9), channel_id=1, source_target_pairs={{0,1},{1,0},{2,3},{3,2},{4,5},{5,4},{6,7},{7,6},{8,9},{9,8},{10,11... | collective-permute-start | bytes 2752520 | tf_op jit(solution)/shard_map/ppermute | solution.py:294
  6.2 2.0 %collective-permute-start.6 = (bf16[128,1792]{1,0:T(8,128)(2,1)S(1)}, bf16[128,1792]{1,0:T(8,128)(2,1)S(1)}, u32[]{:S(2)}, u32[]{:S(2)}) collective-permute-start(bf16[128,1792]{1,0:T(8,128)(2,1)S(1)} %get-tuple-element.49), channel_id=1, source_target_pairs={{0,1},{1,0},{2,3},{3,2},{4,5},{5,4},{6,7},{7,6},{8,9},{9,8},{10,11... | collective-permute-start | bytes 1376264 | tf_op jit(solution)/shard_map/ppermute | solution.py:294
  7.6 3.8 %collective-permute-start.4 = (bf16[128,1792]{1,0:T(8,128)(2,1)S(1)}, bf16[128,1792]{1,0:T(8,128)(2,1)S(1)}, u32[]{:S(2)}, u32[]{:S(2)}) collective-permute-start(bf16[128,1792]{1,0:T(8,128)(2,1)S(1)} %get-tuple-element.44), channel_id=1, source_target_pairs={{0,1},{1,0},{2,3},{3,2},{4,5},{5,4},{6,7},{7,6},{8,9},{9,8},{10,11... | collective-permute-start | bytes 1376264 | tf_op jit(solution)/shard_map/ppermute | solution.py:294
  7.7 4.5 %collective-permute-start.12 = (bf16[128,1792]{1,0:T(8,128)(2,1)S(1)}, bf16[128,1792]{1,0:T(8,128)(2,1)S(1)}, u32[]{:S(2)}, u32[]{:S(2)}) collective-permute-start(bf16[128,1792]{1,0:T(8,128)(2,1)S(1)} %get-tuple-element.57), channel_id=1, source_target_pairs={{0,1},{1,0},{2,3},{3,2},{4,5},{5,4},{6,7},{7,6},{8,9},{9,8},{10,11... | collective-permute-start | bytes 1376264 | tf_op jit(solution)/shard_map/ppermute | solution.py:294
  8.1 5.6 %collective-permute-start.2 = (bf16[128,1792]{1,0:T(8,128)(2,1)S(1)}, bf16[128,1792]{1,0:T(8,128)(2,1)S(1)}, u32[]{:S(2)}, u32[]{:S(2)}) collective-permute-start(bf16[128,1792]{1,0:T(8,128)(2,1)S(1)} %get-tuple-element.38), channel_id=1, source_target_pairs={{0,1},{1,0},{2,3},{3,2},{4,5},{5,4},{6,7},{7,6},{8,9},{9,8},{10,11... | collective-permute-start | bytes 1376264 | tf_op jit(solution)/shard_map/ppermute | solution.py:294
  8.4 9.4 %collective-permute-start.7 = (bf16[128,896]{1,0:T(8,128)(2,1)S(1)}, bf16[128,896]{1,0:T(8,128)(2,1)S(1)}, u32[]{:S(2)}, u32[]{:S(2)}) collective-permute-start(bf16[128,896]{1,0:T(8,128)(2,1)S(1)} %get-tuple-element.51), channel_id=1, source_target_pairs={{0,2},{2,0},{4,6},{6,4},{8,10},{10,8},{12,14},{14,12},{1,3},{3,1},... | collective-permute-start | bytes 688136 | tf_op jit(solution)/shard_map/ppermute | solution.py:296
  11.4 11.2 %collective-permute-start.5 = (bf16[128,896]{1,0:T(8,128)(2,1)S(1)}, bf16[128,896]{1,0:T(8,128)(2,1)S(1)}, u32[]{:S(2)}, u32[]{:S(2)}) collective-permute-start(bf16[128,896]{1,0:T(8,128)(2,1)S(1)} %get-tuple-element.46), channel_id=1, source_target_pairs={{0,2},{2,0},{4,6},{6,4},{8,10},{10,8},{12,14},{14,12},{1,3},{3,1},... | collective-permute-start | bytes 688136 | tf_op jit(solution)/shard_map/ppermute | solution.py:296
  12.4 17.2 %collective-permute-start.13 = (bf16[128,896]{1,0:T(8,128)(2,1)S(1)}, bf16[128,896]{1,0:T(8,128)(2,1)S(1)}, u32[]{:S(2)}, u32[]{:S(2)}) collective-permute-start(bf16[128,896]{1,0:T(8,128)(2,1)S(1)} %get-tuple-element.59), channel_id=1, source_target_pairs={{0,2},{2,0},{4,6},{6,4},{8,10},{10,8},{12,14},{14,12},{1,3},{3,1},... | collective-permute-start | bytes 688136 | tf_op jit(solution)/shard_map/ppermute | solution.py:296
  17.8 5.8 %collective-permute-start.8 = (bf16[64,896]{1,0:T(8,128)(2,1)S(1)}, bf16[64,896]{1,0:T(8,128)(2,1)S(1)}, u32[]{:S(2)}, u32[]{:S(2)}) collective-permute-start(bf16[64,896]{1,0:T(8,128)(2,1)S(1)} %get-tuple-element.52), channel_id=1, source_target_pairs={{0,4},{2,6},{4,0},{6,2},{8,12},{10,14},{12,8},{14,10},{1,5},{3,7},... | collective-permute-start | bytes 344072 | tf_op jit(solution)/shard_map/ppermute | solution.py:296
  20.0 14.6 %collective-permute-start.3 = (bf16[128,896]{1,0:T(8,128)(2,1)S(1)}, bf16[128,896]{1,0:T(8,128)(2,1)S(1)}, u32[]{:S(2)}, u32[]{:S(2)}) collective-permute-start(bf16[128,896]{1,0:T(8,128)(2,1)S(1)} %get-tuple-element.39), channel_id=1, source_target_pairs={{0,2},{2,0},{4,6},{6,4},{8,10},{10,8},{12,14},{14,12},{1,3},{3,1},... | collective-permute-start | bytes 688136 | tf_op jit(solution)/shard_map/ppermute | solution.py:296
  21.5 5.9 %collective-permute-start.10 = (bf16[64,896]{1,0:T(8,128)(2,1)S(1)}, bf16[64,896]{1,0:T(8,128)(2,1)S(1)}, u32[]{:S(2)}, u32[]{:S(2)}) collective-permute-start(bf16[64,896]{1,0:T(8,128)(2,1)S(1)} %get-tuple-element.54), channel_id=1, source_target_pairs={{0,4},{2,6},{4,0},{6,2},{8,12},{10,14},{12,8},{14,10},{1,5},{3,7},... | collective-permute-start | bytes 344072 | tf_op jit(solution)/shard_map/ppermute | solution.py:296
  23.6 11.0 %collective-permute-start.9 = (bf16[64,896]{1,0:T(8,128)(2,1)S(1)}, bf16[64,896]{1,0:T(8,128)(2,1)S(1)}, u32[]{:S(2)}, u32[]{:S(2)}) collective-permute-start(bf16[64,896]{1,0:T(8,128)(2,1)S(1)} %add.2), channel_id=1, source_target_pairs={{0,8},{2,10},{4,12},{6,14},{8,0},{10,2},{12,4},{14,6},{1,9},{3,11}... | collective-permute-start | bytes 344072 | tf_op jit(solution)/shard_map/ppermute | solution.py:296
  27.4 8.2 %collective-permute-start.11 = (bf16[64,896]{1,0:T(8,128)(2,1)S(1)}, bf16[64,896]{1,0:T(8,128)(2,1)S(1)}, u32[]{:S(2)}, u32[]{:S(2)}) collective-permute-start(bf16[64,896]{1,0:T(8,128)(2,1)S(1)} %add.3), channel_id=1, source_target_pairs={{0,8},{2,10},{4,12},{6,14},{8,0},{10,2},{12,4},{14,6},{1,9},{3,11}... | collective-permute-start | bytes 344072 | tf_op jit(solution)/shard_map/ppermute | solution.py:296
  29.6 6.7 %collective-permute-start.14 = (bf16[64,896]{1,0:T(8,128)(2,1)S(1)}, bf16[64,896]{1,0:T(8,128)(2,1)S(1)}, u32[]{:S(2)}, u32[]{:S(2)}) collective-permute-start(bf16[64,896]{1,0:T(8,128)(2,1)S(1)} %get-tuple-element.60), channel_id=1, source_target_pairs={{0,4},{2,6},{4,0},{6,2},{8,12},{10,14},{12,8},{14,10},{1,5},{3,7},... | collective-permute-start | bytes 344072 | tf_op jit(solution)/shard_map/ppermute | solution.py:296
  29.8 7.7 %collective-permute-start.15 = (bf16[64,896]{1,0:T(8,128)(2,1)S(1)}, bf16[64,896]{1,0:T(8,128)(2,1)S(1)}, u32[]{:S(2)}, u32[]{:S(2)}) collective-permute-start(bf16[64,896]{1,0:T(8,128)(2,1)S(1)} %get-tuple-element.62), channel_id=1, source_target_pairs={{0,4},{2,6},{4,0},{6,2},{8,12},{10,14},{12,8},{14,10},{1,5},{3,7},... | collective-permute-start | bytes 344072 | tf_op jit(solution)/shard_map/ppermute | solution.py:296

commit v10 on v9

--- a/solution.py
+++ b/solution.py
@@ -105,28 +105,46 @@
     return total
 
 
-def low_kernel(rank, places, ids_ref, gates_ref, b_ref, b_in_ref, a_ref, a_in_ref, g_ref, x_ref,
-               lg_ref, la_ref, send_ref, keep_ref):
-    weight = gate_columns(1 - lax.axis_index("adapter"), ids_ref[...], gates_ref[...], 2 * b_ref.shape[0], rank)
-    sums = factor_sum(g_ref, b_in_ref, b_ref), factor_sum(x_ref, a_in_ref, a_ref)
-    lows = [(rows * weight).astype(BF16) for rows in sums]
-    lg_ref[...], la_ref[...] = lows
+def low_kernel(rank, ids_ref, gates_ref, own_ref, other_ref, tokens_ref, low_ref):
+    core = 1 - lax.axis_index("adapter")
+    weight = gate_columns(core, ids_ref[...], gates_ref[...], low_ref.shape[0], rank)
+    low_ref[...] = (factor_sum(tokens_ref, other_ref, own_ref) * weight).astype(BF16)
+
+
+def low_product(ids, gates, rank, own, other, tokens):
+    rows, width = own.shape
+    count = tokens.shape[0]
+    return pl.pallas_call(
+        functools.partial(low_kernel, rank),
+        in_specs=[VECTORS] * 5,
+        out_specs=VECTORS,
+        out_shape=jax.ShapeDtypeStruct((2 * rows, count), BF16),
+        compiler_params=params(),
+        cost_estimate=cost(4 * rows * count * width, 2 * (2 * rows + count) * width),
+        name="low",
+    )(ids, gates, own, other, tokens)
+
+
+def first_kernel(rank, places, ids_ref, gates_ref, own_ref, other_ref, la_ref, g_ref, x_ref,
+                 lg_ref, send_ref, keep_ref):
+    low_kernel(rank, ids_ref, gates_ref, own_ref, other_ref, g_ref, lg_ref)
+    lows = (lg_ref[...], la_ref[...])
     store_products(places, 0, 1, lows, (x_ref, g_ref), send_ref, keep_ref)
 
 
-def low_products(places, ids, gates, rank, b, b_in, a, a_in, g, x, wide):
-    rows, width = b_in.shape
-    tokens = x.shape[0]
-    return pl.pallas_call(
-        functools.partial(low_kernel, rank, places),
-        in_specs=[VECTORS] * 8,
-        out_specs=[VECTORS] * 4,
-        out_shape=[jax.ShapeDtypeStruct((2 * rows, tokens), BF16)] * 2
+def first_products(places, ids, gates, rank, own, other, la, g, x, wide):
+    rows, width = own.shape
+    count = x.shape[0]
+    return pl.pallas_call(
+        functools.partial(first_kernel, rank, places),
+        in_specs=[VECTORS] * 7,
+        out_specs=[VECTORS] * 3,
+        out_shape=[jax.ShapeDtypeStruct((2 * rows, count), BF16)]
         + [jax.ShapeDtypeStruct((2 * rows, wide), BF16)] * 2,
         compiler_params=params(),
-        cost_estimate=cost(4 * rows * tokens * (width + 2 * wide), 4 * (rows + tokens) * width),
-        name="low",
-    )(ids, gates, b, b_in, a, a_in, g, x)
+        cost_estimate=cost(4 * rows * count * (width + 2 * wide), 2 * (2 * rows + count) * width),
+        name="first",
+    )(ids, gates, own, other, la, g, x)
 
 
 def rest_kernel(blocks, places, lg_ref, la_ref, x_ref, g_ref, *outs):
@@ -302,8 +320,9 @@
     g_held, x_held = hold(g, x)
     order = list(reversed(range(steps)))
     places = Places(steps)
-    lg, la, pair, keep = low_products(
-        places, ids, gates, rank, b, b_in, a, a_in, g_held, x_held, 2 * block
+    la = low_product(ids, gates, rank, a, a_in, x_held)
+    lg, pair, keep = first_products(
+        places, ids, gates, rank, b, b_in, la, g_held, x_held, 2 * block
     )
     rest = rest_products(places, lg, la, x_held, g_held, steps - 1, 2 * block)
     terms = [(keep, swap(pair))] + [(k, swap(p)) for p, k in zip(rest[::2], rest[1::2])]

time: 38.4 us -> 38.4 us (level)
  waiting for transfers between devices: 9.38 us -> 8.73 us
  Pallas kernels: 9.35 us -> 9.92 us
    pallas_call x1 -> x2, Pallas kernels: 1.45 us -> 2.07 us  [the longest x1 1.43 us: first_products(): pl.pallas_call(functools.partial(first_kernel, rank, places), in_specs=[V...]
    ppermute x6, waiting for transfers between devices: 1.31 us -> 0.73 us  [shards(): swap = lambda array: lax.ppermute(array, 'adapter', SWAP)]
  transfers between devices with their start and end apart: 16 -> 16, of which waited for: 8 -> 9; matrix products, arithmetic and copies ran while one was open for 0% -> 0% of each run, Pallas kernels for 19% -> 20%
where the time goes in v10:
time: 38.4 us; the launch traced here: 38.2 us
  starting transfers between devices  18.8 us (49%)
  Pallas kernels  9.92 us (26%)
  waiting for transfers between devices  8.73 us (23%)
  between operations  0.72 us (2%)
    ppermute x10, starting transfers between devices, shards(): lax.ppermute(array, 'dp', [(i, i ^ by) for i in range(replicas)])  17.1 us
    ppermute x10, waiting for transfers between devices, shards(): lax.ppermute(array, 'dp', [(i, i ^ by) for i in range(replicas)])  8 us
    pallas_call x1, Pallas kernels, input_gradient(): pl.pallas_call(input_kernel, grid=(steps,), in_specs=[VECTORS] * 3, out_s...  2.81 us
    pallas_call x1, Pallas kernels, hold(): pl.pallas_call(hold_kernel, in_specs=[ANYWHERE] * 2, out_specs=[VECTORS]...  2.12 us
    ppermute x6, starting transfers between devices, shards(): swap = lambda array: lax.ppermute(array, 'adapter', SWAP)  1.77 us
    pallas_call x1, Pallas kernels, first_products(): pl.pallas_call(functools.partial(first_kernel, rank, places), in_specs=[V...  1.43 us
    pallas_call x2, Pallas kernels, last(): pl.pallas_call(last_kernel, in_specs=[VECTORS] * 2, out_specs=VECTORS, ou...  1.42 us
    pallas_call x1, Pallas kernels, rest_products(): pl.pallas_call(functools.partial(rest_kernel, blocks, places), in_specs=[...  0.86 us
  transfers between devices with their start and end apart: 16, of which 9 were waited for; matrix products, arithmetic and copies ran while one was open for 0% of the time, Pallas kernels for 20%

profile of v10, /device:TPU:0, one launch (start us, length us, event | category | flops | bytes accessed | tf_op | source)
XLA Modules:
  0.0 38.2 jit_solution(10067563555039101856)
XLA Ops:
  0.6 0.5 %collective-permute-start.1 = (bf16[64,7168]{1,0:T(8,128)(2,1)}, bf16[64,7168]{1,0:T(8,128)(2,1)S(1)}, u32[]{:S(2)}, u32[]{:S(2)}) collective-permute-start(bf16[64,7168]{1,0:T(8,128)(2,1)} %bitcast.6), channel_id=1, source_target_pairs={{0,1},{1,0},{2,3},{3,2},{4,5},{5,4},{6,7},{7,6},{8,9},{9,8},{10,11... | collective-permute-start | bytes 2752520 | tf_op jit(solution)/shard_map/ppermute | solution.py:312
  1.2 0.1 collective-permute-start
  1.3 2.1 %hold.1 = (bf16[128,7168]{1,0:T(8,128)(2,1)S(1)}, bf16[128,7168]{1,0:T(8,128)(2,1)S(1)}) custom-call(bf16[128,7168]{1,0:T(8,128)(2,1)} %g_hbm.1, bf16[128,7168]{1,0:T(8,128)(2,1)} %x_hbm.1), custom_call_target="tpu_custom_call" | custom-call | flops 117440512 | bytes 7340032 | tf_op jit(solution)/shard_map/hold/pallas_call | solution.py:49
  3.4 0.1 collective-permute-done.1.other_ref
  3.5 0.0 copy-done
  3.5 0.0 copy-done.2
  3.5 0.0 copy-done.3
  3.5 0.6 %low.1.la_ref = bf16[128,128]{1,0:T(8,128)(2,1)S(1)} custom-call(s32[2,128]{1,0:T(2,128)S(1)} %bitcast.11, f32[2,128]{1,0:T(2,128)S(1)} %bitcast.13, bf16[64,7168]{1,0:T(8,128)(2,1)S(1)} %bitcast.7, bf16[64,7168]{1,0:T(8,128)(2,1)S(1)} %collective-permute-done.1.other_ref, bf16[128,7168]{1,0:T(8,128)(2,1)S(1)} %get-tuple-element.32.tokens_ref.x_ref), custom_call_target="tpu_custom_call" | custom-call | flops 234881024 | bytes 3670016 | tf_op jit(solution)/shard_map/low/pallas_call | solution.py:117
  4.1 0.7 %collective-permute-done.other_ref = bf16[64,7168]{1,0:T(8,128)(2,1)S(1)} collective-permute-done((bf16[64,7168]{1,0:T(8,128)(2,1)}, bf16[64,7168]{1,0:T(8,128)(2,1)S(1)}, u32[]{:S(2)}, u32[]{:S(2)}) %collective-permute-start) | collective-permute-done | bytes 917536 | tf_op jit(solution)/shard_map/ppermute | solution.py:312
  4.8 0.0 copy-done.1
  4.8 1.4 %first.1 = (bf16[128,128]{1,0:T(8,128)(2,1)S(1)}, bf16[128,1792]{1,0:T(8,128)(2,1)S(1)}, bf16[128,1792]{1,0:T(8,128)(2,1)S(1)}) custom-call(s32[2,128]{1,0:T(2,128)S(1)} %bitcast.12, f32[2,128]{1,0:T(2,128)S(1)} %bitcast.14, bf16[64,7168]{1,0:T(8,128)(2,1)S(1)} %bitcast.10, bf16[64,7168]{1,0:T(8,128)(2,1)S(1)} %collective-permute-done.other_ref, ...), custom_call_target="tpu_custom_call" | custom-call | flops 352321536 | bytes 3670016 | tf_op jit(solution)/shard_map/first/pallas_call | solution.py:138
  6.2 0.4 %collective-permute-start.6 = (bf16[128,1792]{1,0:T(8,128)(2,1)S(1)}, bf16[128,1792]{1,0:T(8,128)(2,1)S(1)}, u32[]{:S(2)}, u32[]{:S(2)}) collective-permute-start(bf16[128,1792]{1,0:T(8,128)(2,1)S(1)} %get-tuple-element.47), channel_id=1, source_target_pairs={{0,1},{1,0},{2,3},{3,2},{4,5},{5,4},{6,7},{7,6},{8,9},{9,8},{10,11... | collective-permute-start | bytes 1376264 | tf_op jit(solution)/shard_map/ppermute | solution.py:312
  6.7 0.9 %rest.1 = (bf16[128,1792]{1,0:T(8,128)(2,1)S(1)}, bf16[128,1792]{1,0:T(8,128)(2,1)S(1)}, bf16[128,1792]{1,0:T(8,128)(2,1)S(1)}, bf16[128,1792]{1,0:T(8,128)(2,1)...) custom-call(bf16[128,128]{1,0:T(8,128)(2,1)S(1)} %get-tuple-element.34.low_ref.lg_ref, ...), custom_call_target="tpu_custom_call" | custom-call | flops 352321536 | bytes 5505024 | tf_op jit(solution)/shard_map/rest/pallas_call | solution.py:158
  7.5 0.2 collective-permute-start.4
  7.7 0.4 collective-permute-start.12
  8.1 0.1 collective-permute-start.2
  8.2 0.0 collective-permute-done.6.came_ref
  8.2 0.1 fold.6
  8.3 3.0 %collective-permute-start.7 = (bf16[128,896]{1,0:T(8,128)(2,1)S(1)}, bf16[128,896]{1,0:T(8,128)(2,1)S(1)}, u32[]{:S(2)}, u32[]{:S(2)}) collective-permute-start(bf16[128,896]{1,0:T(8,128)(2,1)S(1)} %get-tuple-element.49), channel_id=1, source_target_pairs={{0,2},{2,0},{4,6},{6,4},{8,10},{10,8},{12,14},{14,12},{1,3},{3,1},... | collective-permute-start | bytes 688136 | tf_op jit(solution)/shard_map/ppermute | solution.py:314
  11.3 0.0 collective-permute-done.4.came_ref
  11.3 0.1 fold.5
  11.4 0.8 %collective-permute-start.5 = (bf16[128,896]{1,0:T(8,128)(2,1)S(1)}, bf16[128,896]{1,0:T(8,128)(2,1)S(1)}, u32[]{:S(2)}, u32[]{:S(2)}) collective-permute-start(bf16[128,896]{1,0:T(8,128)(2,1)S(1)} %get-tuple-element.44), channel_id=1, source_target_pairs={{0,2},{2,0},{4,6},{6,4},{8,10},{10,8},{12,14},{14,12},{1,3},{3,1},... | collective-permute-start | bytes 688136 | tf_op jit(solution)/shard_map/ppermute | solution.py:314
  12.3 0.0 collective-permute-done.12.came_ref
  12.3 0.1 fold.7
  12.4 1.3 %collective-permute-start.13 = (bf16[128,896]{1,0:T(8,128)(2,1)S(1)}, bf16[128,896]{1,0:T(8,128)(2,1)S(1)}, u32[]{:S(2)}, u32[]{:S(2)}) collective-permute-start(bf16[128,896]{1,0:T(8,128)(2,1)S(1)} %get-tuple-element.57), channel_id=1, source_target_pairs={{0,2},{2,0},{4,6},{6,4},{8,10},{10,8},{12,14},{14,12},{1,3},{3,1},... | collective-permute-start | bytes 688136 | tf_op jit(solution)/shard_map/ppermute | solution.py:314
  13.7 0.0 collective-permute-done.2.came_ref
  13.7 0.1 fold.4
  13.8 3.9 %collective-permute-done.7.came_ref = bf16[128,896]{1,0:T(8,128)(2,1)S(1)} collective-permute-done((bf16[128,896]{1,0:T(8,128)(2,1)S(1)}, bf16[128,896]{1,0:T(8,128)(2,1)S(1)}, u32[]{:S(2)}, u32[]{:S(2)}) %collective-permute-start.7) | collective-permute-done | bytes 229408 | tf_op jit(solution)/shard_map/ppermute | solution.py:314
  17.7 2.2 %collective-permute-start.10 = (bf16[64,896]{1,0:T(8,128)(2,1)S(1)}, bf16[64,896]{1,0:T(8,128)(2,1)S(1)}, u32[]{:S(2)}, u32[]{:S(2)}) collective-permute-start(bf16[64,896]{1,0:T(8,128)(2,1)S(1)} %get-tuple-element.52), channel_id=1, source_target_pairs={{0,4},{2,6},{4,0},{6,2},{8,12},{10,14},{12,8},{14,10},{1,5},{3,7},... | collective-permute-start | bytes 344072 | tf_op jit(solution)/shard_map/ppermute | solution.py:314
  19.9 1.5 %collective-permute-start.3 = (bf16[128,896]{1,0:T(8,128)(2,1)S(1)}, bf16[128,896]{1,0:T(8,128)(2,1)S(1)}, u32[]{:S(2)}, u32[]{:S(2)}) collective-permute-start(bf16[128,896]{1,0:T(8,128)(2,1)S(1)} %get-tuple-element.37), channel_id=1, source_target_pairs={{0,2},{2,0},{4,6},{6,4},{8,10},{10,8},{12,14},{14,12},{1,3},{3,1},... | collective-permute-start | bytes 688136 | tf_op jit(solution)/shard_map/ppermute | solution.py:314
  21.4 0.5 %collective-permute-start.8 = (bf16[64,896]{1,0:T(8,128)(2,1)S(1)}, bf16[64,896]{1,0:T(8,128)(2,1)S(1)}, u32[]{:S(2)}, u32[]{:S(2)}) collective-permute-start(bf16[64,896]{1,0:T(8,128)(2,1)S(1)} %get-tuple-element.50), channel_id=1, source_target_pairs={{0,4},{2,6},{4,0},{6,2},{8,12},{10,14},{12,8},{14,10},{1,5},{3,7},... | collective-permute-start | bytes 344072 | tf_op jit(solution)/shard_map/ppermute | solution.py:314
  21.9 0.7 %collective-permute-done.5.came_ref = bf16[128,896]{1,0:T(8,128)(2,1)S(1)} collective-permute-done((bf16[128,896]{1,0:T(8,128)(2,1)S(1)}, bf16[128,896]{1,0:T(8,128)(2,1)S(1)}, u32[]{:S(2)}, u32[]{:S(2)}) %collective-permute-start.5) | collective-permute-done | bytes 229408 | tf_op jit(solution)/shard_map/ppermute | solution.py:314
  22.7 0.8 %collective-permute-done.10.refs_0_ = bf16[64,896]{1,0:T(8,128)(2,1)S(1)} collective-permute-done((bf16[64,896]{1,0:T(8,128)(2,1)S(1)}, bf16[64,896]{1,0:T(8,128)(2,1)S(1)}, u32[]{:S(2)}, u32[]{:S(2)}) %collective-permute-start.10) | collective-permute-done | bytes 114720 | tf_op jit(solution)/shard_map/ppermute | solution.py:314
  23.5 3.5 %collective-permute-start.11 = (bf16[64,896]{1,0:T(8,128)(2,1)S(1)}, bf16[64,896]{1,0:T(8,128)(2,1)S(1)}, u32[]{:S(2)}, u32[]{:S(2)}) collective-permute-start(bf16[64,896]{1,0:T(8,128)(2,1)S(1)} %add.3), channel_id=1, source_target_pairs={{0,8},{2,10},{4,12},{6,14},{8,0},{10,2},{12,4},{14,6},{1,9},{3,11}... | collective-permute-start | bytes 344072 | tf_op jit(solution)/shard_map/ppermute | solution.py:314
  27.0 0.3 collective-permute-done.8.refs_0_
  27.3 2.2 %collective-permute-start.9 = (bf16[64,896]{1,0:T(8,128)(2,1)S(1)}, bf16[64,896]{1,0:T(8,128)(2,1)S(1)}, u32[]{:S(2)}, u32[]{:S(2)}) collective-permute-start(bf16[64,896]{1,0:T(8,128)(2,1)S(1)} %add.2), channel_id=1, source_target_pairs={{0,8},{2,10},{4,12},{6,14},{8,0},{10,2},{12,4},{14,6},{1,9},{3,11}... | collective-permute-start | bytes 344072 | tf_op jit(solution)/shard_map/ppermute | solution.py:314
  29.6 0.0 collective-permute-done.13.came_ref
  29.6 0.1 collective-permute-start.14
  29.7 2.0 %collective-permute-start.15 = (bf16[64,896]{1,0:T(8,128)(2,1)S(1)}, bf16[64,896]{1,0:T(8,128)(2,1)S(1)}, u32[]{:S(2)}, u32[]{:S(2)}) collective-permute-start(bf16[64,896]{1,0:T(8,128)(2,1)S(1)} %get-tuple-element.60), channel_id=1, source_target_pairs={{0,4},{2,6},{4,0},{6,2},{8,12},{10,14},{12,8},{14,10},{1,5},{3,7},... | collective-permute-start | bytes 344072 | tf_op jit(solution)/shard_map/ppermute | solution.py:314
  31.7 2.8 %input.1 = bf16[128,7168]{1,0:T(8,128)(2,1)} custom-call(bf16[128,128]{1,0:T(8,128)(2,1)S(1)} %get-tuple-element.34.low_ref.lg_ref, bf16[64,7168]{1,0:T(8,128)(2,1)S(1)} %bitcast.8, bf16[64,7168]{1,0:T(8,128)(2,1)S(1)} %collective-permute-done.1.other_ref), custom_call_target="tpu_custom_call" | custom-call | flops 234881024 | bytes 3670016 | tf_op jit(solution)/shard_map/input/pallas_call | solution.py:290
  34.5 0.0 collective-permute-done.3.refs_0_
  34.5 0.0 collective-permute-done.11.refs_2_
  34.5 1.0 %collective-permute-done.9.refs_1_ = bf16[64,896]{1,0:T(8,128)(2,1)S(1)} collective-permute-done((bf16[64,896]{1,0:T(8,128)(2,1)S(1)}, bf16[64,896]{1,0:T(8,128)(2,1)S(1)}, u32[]{:S(2)}, u32[]{:S(2)}) %collective-permute-start.9) | collective-permute-done | bytes 114720 | tf_op jit(solution)/shard_map/ppermute | solution.py:314
  35.5 0.1 total.1
  35.6 0.7 %collective-permute-done.14.came_ref = bf16[64,896]{1,0:T(8,128)(2,1)S(1)} collective-permute-done((bf16[64,896]{1,0:T(8,128)(2,1)S(1)}, bf16[64,896]{1,0:T(8,128)(2,1)S(1)}, u32[]{:S(2)}, u32[]{:S(2)}) %collective-permute-start.14) | collective-permute-done | bytes 114720 | tf_op jit(solution)/shard_map/ppermute | solution.py:314
  36.3 0.7 %last.2 = f32[64,896]{1,0:T(8,128)} custom-call(f32[64,896]{1,0:T(8,128)S(1)} %get-tuple-element.53.total_ref, bf16[64,896]{1,0:T(8,128)(2,1)S(1)} %collective-permute-done.14.came_ref), custom_call_target="tpu_custom_call" | custom-call | flops 57344 | bytes 573440 | tf_op jit(solution)/shard_map/last/pallas_call | solution.py:264
  37.0 0.5 %collective-permute-done.15.came_ref = bf16[64,896]{1,0:T(8,128)(2,1)S(1)} collective-permute-done((bf16[64,896]{1,0:T(8,128)(2,1)S(1)}, bf16[64,896]{1,0:T(8,128)(2,1)S(1)}, u32[]{:S(2)}, u32[]{:S(2)}) %collective-permute-start.15) | collective-permute-done | bytes 114720 | tf_op jit(solution)/shard_map/ppermute | solution.py:314
  37.5 0.7 %last.3 = f32[64,896]{1,0:T(8,128)} custom-call(f32[64,896]{1,0:T(8,128)S(1)} %get-tuple-element.59.total_ref, bf16[64,896]{1,0:T(8,128)(2,1)S(1)} %collective-permute-done.15.came_ref), custom_call_target="tpu_custom_call" | custom-call | flops 57344 | bytes 573440 | tf_op jit(solution)/shard_map/last/pallas_call | solution.py:264
  (9 shorter events, 0.2 us)
Async XLA Ops:
  0.6 2.8 %collective-permute-start.1 = (bf16[64,7168]{1,0:T(8,128)(2,1)}, bf16[64,7168]{1,0:T(8,128)(2,1)S(1)}, u32[]{:S(2)}, u32[]{:S(2)}) collective-permute-start(bf16[64,7168]{1,0:T(8,128)(2,1)} %bitcast.6), channel_id=1, source_target_pairs={{0,1},{1,0},{2,3},{3,2},{4,5},{5,4},{6,7},{7,6},{8,9},{9,8},{10,11... | collective-permute-start | bytes 2752520 | tf_op jit(solution)/shard_map/ppermute | solution.py:312
  1.1 2.3 %copy-start = (bf16[4,16,7168]{2,1,0:T(8,128)(2,1)S(1)}, bf16[4,16,7168]{2,1,0:T(8,128)(2,1)}, u32[]{:S(2)}) copy-start(bf16[4,16,7168]{2,1,0:T(8,128)(2,1)} %param.10) | copy-start | bytes 2752516
  1.2 2.3 %copy-start.2 = (s32[128,2]{0,1:T(2,128)S(1)}, s32[128,2]{0,1:T(2,128)}, u32[]{:S(2)}) copy-start(s32[128,2]{0,1:T(2,128)} %param.8) | copy-start | bytes 3076
  1.2 2.3 %copy-start.3 = (f32[128,2]{0,1:T(2,128)S(1)}, f32[128,2]{0,1:T(2,128)}, u32[]{:S(2)}) copy-start(f32[128,2]{0,1:T(2,128)} %param.9) | copy-start | bytes 3076
  1.2 3.6 %collective-permute-start = (bf16[64,7168]{1,0:T(8,128)(2,1)}, bf16[64,7168]{1,0:T(8,128)(2,1)S(1)}, u32[]{:S(2)}, u32[]{:S(2)}) collective-permute-start(bf16[64,7168]{1,0:T(8,128)(2,1)} %bitcast.9), channel_id=1, source_target_pairs={{0,1},{1,0},{2,3},{3,2},{4,5},{5,4},{6,7},{7,6},{8,9},{9,8},{10,11... | collective-permute-start | bytes 2752520 | tf_op jit(solution)/shard_map/ppermute | solution.py:312
  3.5 1.3 %copy-start.1 = (bf16[4,16,7168]{2,1,0:T(8,128)(2,1)S(1)}, bf16[4,16,7168]{2,1,0:T(8,128)(2,1)}, u32[]{:S(2)}) copy-start(bf16[4,16,7168]{2,1,0:T(8,128)(2,1)} %param.11) | copy-start | bytes 2752516
  6.2 2.0 %collective-permute-start.6 = (bf16[128,1792]{1,0:T(8,128)(2,1)S(1)}, bf16[128,1792]{1,0:T(8,128)(2,1)S(1)}, u32[]{:S(2)}, u32[]{:S(2)}) collective-permute-start(bf16[128,1792]{1,0:T(8,128)(2,1)S(1)} %get-tuple-element.47), channel_id=1, source_target_pairs={{0,1},{1,0},{2,3},{3,2},{4,5},{5,4},{6,7},{7,6},{8,9},{9,8},{10,11... | collective-permute-start | bytes 1376264 | tf_op jit(solution)/shard_map/ppermute | solution.py:312
  7.5 3.8 %collective-permute-start.4 = (bf16[128,1792]{1,0:T(8,128)(2,1)S(1)}, bf16[128,1792]{1,0:T(8,128)(2,1)S(1)}, u32[]{:S(2)}, u32[]{:S(2)}) collective-permute-start(bf16[128,1792]{1,0:T(8,128)(2,1)S(1)} %get-tuple-element.42), channel_id=1, source_target_pairs={{0,1},{1,0},{2,3},{3,2},{4,5},{5,4},{6,7},{7,6},{8,9},{9,8},{10,11... | collective-permute-start | bytes 1376264 | tf_op jit(solution)/shard_map/ppermute | solution.py:312
  7.7 4.5 %collective-permute-start.12 = (bf16[128,1792]{1,0:T(8,128)(2,1)S(1)}, bf16[128,1792]{1,0:T(8,128)(2,1)S(1)}, u32[]{:S(2)}, u32[]{:S(2)}) collective-permute-start(bf16[128,1792]{1,0:T(8,128)(2,1)S(1)} %get-tuple-element.55), channel_id=1, source_target_pairs={{0,1},{1,0},{2,3},{3,2},{4,5},{5,4},{6,7},{7,6},{8,9},{9,8},{10,11... | collective-permute-start | bytes 1376264 | tf_op jit(solution)/shard_map/ppermute | solution.py:312
  8.1 5.6 %collective-permute-start.2 = (bf16[128,1792]{1,0:T(8,128)(2,1)S(1)}, bf16[128,1792]{1,0:T(8,128)(2,1)S(1)}, u32[]{:S(2)}, u32[]{:S(2)}) collective-permute-start(bf16[128,1792]{1,0:T(8,128)(2,1)S(1)} %get-tuple-element.36), channel_id=1, source_target_pairs={{0,1},{1,0},{2,3},{3,2},{4,5},{5,4},{6,7},{7,6},{8,9},{9,8},{10,11... | collective-permute-start | bytes 1376264 | tf_op jit(solution)/shard_map/ppermute | solution.py:312
  8.3 9.3 %collective-permute-start.7 = (bf16[128,896]{1,0:T(8,128)(2,1)S(1)}, bf16[128,896]{1,0:T(8,128)(2,1)S(1)}, u32[]{:S(2)}, u32[]{:S(2)}) collective-permute-start(bf16[128,896]{1,0:T(8,128)(2,1)S(1)} %get-tuple-element.49), channel_id=1, source_target_pairs={{0,2},{2,0},{4,6},{6,4},{8,10},{10,8},{12,14},{14,12},{1,3},{3,1},... | collective-permute-start | bytes 688136 | tf_op jit(solution)/shard_map/ppermute | solution.py:314
  11.4 11.2 %collective-permute-start.5 = (bf16[128,896]{1,0:T(8,128)(2,1)S(1)}, bf16[128,896]{1,0:T(8,128)(2,1)S(1)}, u32[]{:S(2)}, u32[]{:S(2)}) collective-permute-start(bf16[128,896]{1,0:T(8,128)(2,1)S(1)} %get-tuple-element.44), channel_id=1, source_target_pairs={{0,2},{2,0},{4,6},{6,4},{8,10},{10,8},{12,14},{14,12},{1,3},{3,1},... | collective-permute-start | bytes 688136 | tf_op jit(solution)/shard_map/ppermute | solution.py:314
  12.4 17.2 %collective-permute-start.13 = (bf16[128,896]{1,0:T(8,128)(2,1)S(1)}, bf16[128,896]{1,0:T(8,128)(2,1)S(1)}, u32[]{:S(2)}, u32[]{:S(2)}) collective-permute-start(bf16[128,896]{1,0:T(8,128)(2,1)S(1)} %get-tuple-element.57), channel_id=1, source_target_pairs={{0,2},{2,0},{4,6},{6,4},{8,10},{10,8},{12,14},{14,12},{1,3},{3,1},... | collective-permute-start | bytes 688136 | tf_op jit(solution)/shard_map/ppermute | solution.py:314
  17.7 5.7 %collective-permute-start.10 = (bf16[64,896]{1,0:T(8,128)(2,1)S(1)}, bf16[64,896]{1,0:T(8,128)(2,1)S(1)}, u32[]{:S(2)}, u32[]{:S(2)}) collective-permute-start(bf16[64,896]{1,0:T(8,128)(2,1)S(1)} %get-tuple-element.52), channel_id=1, source_target_pairs={{0,4},{2,6},{4,0},{6,2},{8,12},{10,14},{12,8},{14,10},{1,5},{3,7},... | collective-permute-start | bytes 344072 | tf_op jit(solution)/shard_map/ppermute | solution.py:314
  19.9 14.6 %collective-permute-start.3 = (bf16[128,896]{1,0:T(8,128)(2,1)S(1)}, bf16[128,896]{1,0:T(8,128)(2,1)S(1)}, u32[]{:S(2)}, u32[]{:S(2)}) collective-permute-start(bf16[128,896]{1,0:T(8,128)(2,1)S(1)} %get-tuple-element.37), channel_id=1, source_target_pairs={{0,2},{2,0},{4,6},{6,4},{8,10},{10,8},{12,14},{14,12},{1,3},{3,1},... | collective-permute-start | bytes 688136 | tf_op jit(solution)/shard_map/ppermute | solution.py:314
  21.4 5.9 %collective-permute-start.8 = (bf16[64,896]{1,0:T(8,128)(2,1)S(1)}, bf16[64,896]{1,0:T(8,128)(2,1)S(1)}, u32[]{:S(2)}, u32[]{:S(2)}) collective-permute-start(bf16[64,896]{1,0:T(8,128)(2,1)S(1)} %get-tuple-element.50), channel_id=1, source_target_pairs={{0,4},{2,6},{4,0},{6,2},{8,12},{10,14},{12,8},{14,10},{1,5},{3,7},... | collective-permute-start | bytes 344072 | tf_op jit(solution)/shard_map/ppermute | solution.py:314
  23.5 11.0 %collective-permute-start.11 = (bf16[64,896]{1,0:T(8,128)(2,1)S(1)}, bf16[64,896]{1,0:T(8,128)(2,1)S(1)}, u32[]{:S(2)}, u32[]{:S(2)}) collective-permute-start(bf16[64,896]{1,0:T(8,128)(2,1)S(1)} %add.3), channel_id=1, source_target_pairs={{0,8},{2,10},{4,12},{6,14},{8,0},{10,2},{12,4},{14,6},{1,9},{3,11}... | collective-permute-start | bytes 344072 | tf_op jit(solution)/shard_map/ppermute | solution.py:314
  27.3 8.2 %collective-permute-start.9 = (bf16[64,896]{1,0:T(8,128)(2,1)S(1)}, bf16[64,896]{1,0:T(8,128)(2,1)S(1)}, u32[]{:S(2)}, u32[]{:S(2)}) collective-permute-start(bf16[64,896]{1,0:T(8,128)(2,1)S(1)} %add.2), channel_id=1, source_target_pairs={{0,8},{2,10},{4,12},{6,14},{8,0},{10,2},{12,4},{14,6},{1,9},{3,11}... | collective-permute-start | bytes 344072 | tf_op jit(solution)/shard_map/ppermute | solution.py:314
  29.6 6.7 %collective-permute-start.14 = (bf16[64,896]{1,0:T(8,128)(2,1)S(1)}, bf16[64,896]{1,0:T(8,128)(2,1)S(1)}, u32[]{:S(2)}, u32[]{:S(2)}) collective-permute-start(bf16[64,896]{1,0:T(8,128)(2,1)S(1)} %get-tuple-element.58), channel_id=1, source_target_pairs={{0,4},{2,6},{4,0},{6,2},{8,12},{10,14},{12,8},{14,10},{1,5},{3,7},... | collective-permute-start | bytes 344072 | tf_op jit(solution)/shard_map/ppermute | solution.py:314
  29.7 7.8 %collective-permute-start.15 = (bf16[64,896]{1,0:T(8,128)(2,1)S(1)}, bf16[64,896]{1,0:T(8,128)(2,1)S(1)}, u32[]{:S(2)}, u32[]{:S(2)}) collective-permute-start(bf16[64,896]{1,0:T(8,128)(2,1)S(1)} %get-tuple-element.60), channel_id=1, source_target_pairs={{0,4},{2,6},{4,0},{6,2},{8,12},{10,14},{12,8},{14,10},{1,5},{3,7},... | collective-permute-start | bytes 344072 | tf_op jit(solution)/shard_map/ppermute | solution.py:314

commit v11 on v9

--- a/solution.py
+++ b/solution.py
@@ -238,20 +238,21 @@
     )(keep, *came)
 
 
-def last_kernel(total_ref, came_ref, out_ref):
-    out_ref[...] = total_ref[...] + came_ref[...].astype(F32)
-
-
-def last(total, came):
+def last_kernel(down_total, up_total, down_came, up_came, down_ref, up_ref):
+    down_ref[...] = down_total[...] + down_came[...].astype(F32)
+    up_ref[...] = up_total[...] + up_came[...].astype(F32)
+
+
+def last(down, up, down_came, up_came):
     return pl.pallas_call(
         last_kernel,
-        in_specs=[VECTORS] * 2,
-        out_specs=VECTORS,
-        out_shape=jax.ShapeDtypeStruct(total.shape, F32),
-        compiler_params=params(),
-        cost_estimate=cost(total.size, 10 * total.size),
+        in_specs=[VECTORS] * 4,
+        out_specs=[VECTORS] * 2,
+        out_shape=[jax.ShapeDtypeStruct(down.shape, F32)] * 2,
+        compiler_params=params(),
+        cost_estimate=cost(2 * down.size, 20 * down.size),
         name="last",
-    )(total, came)
+    )(down, up, down_came, up_came)
 
 
 def input_kernel(low_ref, own_ref, other_ref, out_ref):
@@ -325,7 +326,7 @@
                 into.append(flip(add(half, came), 4))
     input_grad = input_gradient(lg, a, a_in)
     input_grad, both[-1] = lax.optimization_barrier((input_grad, both[-1]))
-    down, up = (last(*pair) for pair in zip(total(own, both, downs, ups), nearest))
+    down, up = last(*total(own, both, downs, ups), *nearest)
     return input_grad, down.reshape(count, rank, block), up.reshape(count, rank, block)
 
 

time: 38.4 us -> 38.3 us (level)
  waiting for transfers between devices: 9.38 us -> 10.6 us
  starting transfers between devices: 18.8 us -> 18 us
  Pallas kernels: 9.35 us -> 8.72 us
    ppermute x10, waiting for transfers between devices: 8.07 us -> 9.28 us  [shards(): lax.ppermute(array, 'dp', [(i, i ^ by) for i in range(replicas)])]
    ppermute x10, starting transfers between devices: 17 us -> 16.3 us  [shards(): lax.ppermute(array, 'dp', [(i, i ^ by) for i in range(replicas)])]
    pallas_call x2 -> x1, Pallas kernels: 1.42 us -> 0.8 us  [last(): pl.pallas_call(last_kernel, in_specs=[VECTORS] * 4, out_specs=[VECTORS] *...]
  transfers between devices with their start and end apart: 16 -> 16, of which waited for: 8 -> 8; matrix products, arithmetic and copies ran while one was open for 0% -> 0% of each run, Pallas kernels for 19% -> 17%
where the time goes in v11:
time: 38.3 us; the launch traced here: 38.1 us
  starting transfers between devices  18 us (47%)
  waiting for transfers between devices  10.6 us (28%)
  Pallas kernels  8.72 us (23%)
  between operations  0.73 us (2%)
    ppermute x10, starting transfers between devices, shards(): lax.ppermute(array, 'dp', [(i, i ^ by) for i in range(replicas)])  16.3 us
    ppermute x10, waiting for transfers between devices, shards(): lax.ppermute(array, 'dp', [(i, i ^ by) for i in range(replicas)])  9.28 us
    pallas_call x1, Pallas kernels, input_gradient(): pl.pallas_call(input_kernel, grid=(steps,), in_specs=[VECTORS] * 3, out_s...  2.8 us
    pallas_call x1, Pallas kernels, hold(): pl.pallas_call(hold_kernel, in_specs=[ANYWHERE] * 2, out_specs=[VECTORS]...  2.17 us
    ppermute x6, starting transfers between devices, shards(): swap = lambda array: lax.ppermute(array, 'adapter', SWAP)  1.79 us
    pallas_call x1, Pallas kernels, low_products(): pl.pallas_call(functools.partial(low_kernel, rank, places), in_specs=[VEC...  1.45 us
    ppermute x6, waiting for transfers between devices, shards(): swap = lambda array: lax.ppermute(array, 'adapter', SWAP)  1.31 us
    pallas_call x1, Pallas kernels, rest_products(): pl.pallas_call(functools.partial(rest_kernel, blocks, places), in_specs=[...  0.87 us
  transfers between devices with their start and end apart: 16, of which 8 were waited for; matrix products, arithmetic and copies ran while one was open for 0% of the time, Pallas kernels for 17%

profile of v11, /device:TPU:0, one launch (start us, length us, event | category | flops | bytes accessed | tf_op | source)
XLA Modules:
  0.0 38.1 jit_solution(13225321214355000513)
XLA Ops:
  0.6 0.5 %collective-permute-start.1 = (bf16[64,7168]{1,0:T(8,128)(2,1)}, bf16[64,7168]{1,0:T(8,128)(2,1)S(1)}, u32[]{:S(2)}, u32[]{:S(2)}) collective-permute-start(bf16[64,7168]{1,0:T(8,128)(2,1)} %bitcast.6), channel_id=1, source_target_pairs={{0,1},{1,0},{2,3},{3,2},{4,5},{5,4},{6,7},{7,6},{8,9},{9,8},{10,11... | collective-permute-start | bytes 2752520 | tf_op jit(solution)/shard_map/ppermute | solution.py:295
  1.1 0.0 copy-start
  1.2 0.0 copy-start.1
  1.2 0.1 collective-permute-start
  1.3 2.2 %hold.1 = (bf16[128,7168]{1,0:T(8,128)(2,1)S(1)}, bf16[128,7168]{1,0:T(8,128)(2,1)S(1)}) custom-call(bf16[128,7168]{1,0:T(8,128)(2,1)} %g_hbm.1, bf16[128,7168]{1,0:T(8,128)(2,1)} %x_hbm.1), custom_call_target="tpu_custom_call" | custom-call | flops 117440512 | bytes 7340032 | tf_op jit(solution)/shard_map/hold/pallas_call | solution.py:49
  3.5 0.0 collective-permute-done.1.a_in_ref.other_ref
  3.5 1.3 %collective-permute-done.b_in_ref = bf16[64,7168]{1,0:T(8,128)(2,1)S(1)} collective-permute-done((bf16[64,7168]{1,0:T(8,128)(2,1)}, bf16[64,7168]{1,0:T(8,128)(2,1)S(1)}, u32[]{:S(2)}, u32[]{:S(2)}) %collective-permute-start) | collective-permute-done | bytes 917536 | tf_op jit(solution)/shard_map/ppermute | solution.py:295
  4.8 0.0 copy-done
  4.8 0.0 copy-done.1
  4.8 0.0 copy-done.2
  4.8 0.0 copy-done.3
  4.8 1.4 %low.1 = (bf16[128,128]{1,0:T(8,128)(2,1)S(1)}, bf16[128,128]{1,0:T(8,128)(2,1)S(1)}, bf16[128,1792]{1,0:T(8,128)(2,1)S(1)}, bf16[128,1792]{1,0:T(8,128)(2,1)S(1)}) custom-call(s32[2,128]{1,0:T(2,128)S(1)} %bitcast.11, f32[2,128]{1,0:T(2,128)S(1)} %bitcast.12, bf16[64,7168]{1,0:T(8,128)(2,1)S(1)} %bitcast.10, ...), custom_call_target="tpu_custom_call" | custom-call | flops 352321536 | bytes 5505024 | tf_op jit(solution)/shard_map/low/pallas_call | solution.py:120
  6.2 0.4 %collective-permute-start.6 = (bf16[128,1792]{1,0:T(8,128)(2,1)S(1)}, bf16[128,1792]{1,0:T(8,128)(2,1)S(1)}, u32[]{:S(2)}, u32[]{:S(2)}) collective-permute-start(bf16[128,1792]{1,0:T(8,128)(2,1)S(1)} %get-tuple-element.51), channel_id=1, source_target_pairs={{0,1},{1,0},{2,3},{3,2},{4,5},{5,4},{6,7},{7,6},{8,9},{9,8},{10,11... | collective-permute-start | bytes 1376264 | tf_op jit(solution)/shard_map/ppermute | solution.py:295
  6.7 0.9 %rest.1 = (bf16[128,1792]{1,0:T(8,128)(2,1)S(1)}, bf16[128,1792]{1,0:T(8,128)(2,1)S(1)}, bf16[128,1792]{1,0:T(8,128)(2,1)S(1)}, bf16[128,1792]{1,0:T(8,128)(2,1)...) custom-call(bf16[128,128]{1,0:T(8,128)(2,1)S(1)} %get-tuple-element.37.low_ref.lg_ref, ...), custom_call_target="tpu_custom_call" | custom-call | flops 352321536 | bytes 5505024 | tf_op jit(solution)/shard_map/rest/pallas_call | solution.py:140
  7.6 0.2 collective-permute-start.4
  7.7 0.4 %collective-permute-start.12 = (bf16[128,1792]{1,0:T(8,128)(2,1)S(1)}, bf16[128,1792]{1,0:T(8,128)(2,1)S(1)}, u32[]{:S(2)}, u32[]{:S(2)}) collective-permute-start(bf16[128,1792]{1,0:T(8,128)(2,1)S(1)} %get-tuple-element.60), channel_id=1, source_target_pairs={{0,1},{1,0},{2,3},{3,2},{4,5},{5,4},{6,7},{7,6},{8,9},{9,8},{10,11... | collective-permute-start | bytes 1376264 | tf_op jit(solution)/shard_map/ppermute | solution.py:295
  8.1 0.1 collective-permute-start.2
  8.3 0.0 collective-permute-done.6.came_ref
  8.3 0.1 fold.6
  8.4 3.0 %collective-permute-start.7 = (bf16[128,896]{1,0:T(8,128)(2,1)S(1)}, bf16[128,896]{1,0:T(8,128)(2,1)S(1)}, u32[]{:S(2)}, u32[]{:S(2)}) collective-permute-start(bf16[128,896]{1,0:T(8,128)(2,1)S(1)} %get-tuple-element.53), channel_id=1, source_target_pairs={{0,2},{2,0},{4,6},{6,4},{8,10},{10,8},{12,14},{14,12},{1,3},{3,1},... | collective-permute-start | bytes 688136 | tf_op jit(solution)/shard_map/ppermute | solution.py:297
  11.3 0.0 collective-permute-done.4.came_ref
  11.3 0.1 fold.5
  11.4 0.8 %collective-permute-start.5 = (bf16[128,896]{1,0:T(8,128)(2,1)S(1)}, bf16[128,896]{1,0:T(8,128)(2,1)S(1)}, u32[]{:S(2)}, u32[]{:S(2)}) collective-permute-start(bf16[128,896]{1,0:T(8,128)(2,1)S(1)} %get-tuple-element.48), channel_id=1, source_target_pairs={{0,2},{2,0},{4,6},{6,4},{8,10},{10,8},{12,14},{14,12},{1,3},{3,1},... | collective-permute-start | bytes 688136 | tf_op jit(solution)/shard_map/ppermute | solution.py:297
  12.3 0.0 collective-permute-done.12.came_ref
  12.3 0.1 fold.7
  12.4 1.3 %collective-permute-start.13 = (bf16[128,896]{1,0:T(8,128)(2,1)S(1)}, bf16[128,896]{1,0:T(8,128)(2,1)S(1)}, u32[]{:S(2)}, u32[]{:S(2)}) collective-permute-start(bf16[128,896]{1,0:T(8,128)(2,1)S(1)} %get-tuple-element.62), channel_id=1, source_target_pairs={{0,2},{2,0},{4,6},{6,4},{8,10},{10,8},{12,14},{14,12},{1,3},{3,1},... | collective-permute-start | bytes 688136 | tf_op jit(solution)/shard_map/ppermute | solution.py:297
  13.7 4.0 %collective-permute-done.7.came_ref = bf16[128,896]{1,0:T(8,128)(2,1)S(1)} collective-permute-done((bf16[128,896]{1,0:T(8,128)(2,1)S(1)}, bf16[128,896]{1,0:T(8,128)(2,1)S(1)}, u32[]{:S(2)}, u32[]{:S(2)}) %collective-permute-start.7) | collective-permute-done | bytes 229408 | tf_op jit(solution)/shard_map/ppermute | solution.py:297
  17.8 2.2 %collective-permute-start.8 = (bf16[64,896]{1,0:T(8,128)(2,1)S(1)}, bf16[64,896]{1,0:T(8,128)(2,1)S(1)}, u32[]{:S(2)}, u32[]{:S(2)}) collective-permute-start(bf16[64,896]{1,0:T(8,128)(2,1)S(1)} %get-tuple-element.54), channel_id=1, source_target_pairs={{0,4},{2,6},{4,0},{6,2},{8,12},{10,14},{12,8},{14,10},{1,5},{3,7},... | collective-permute-start | bytes 344072 | tf_op jit(solution)/shard_map/ppermute | solution.py:297
  20.0 0.0 collective-permute-done.2.came_ref
  20.0 0.1 fold.4
  20.1 0.1 collective-permute-start.10
  20.2 1.9 %collective-permute-start.3 = (bf16[128,896]{1,0:T(8,128)(2,1)S(1)}, bf16[128,896]{1,0:T(8,128)(2,1)S(1)}, u32[]{:S(2)}, u32[]{:S(2)}) collective-permute-start(bf16[128,896]{1,0:T(8,128)(2,1)S(1)} %get-tuple-element.41), channel_id=1, source_target_pairs={{0,2},{2,0},{4,6},{6,4},{8,10},{10,8},{12,14},{14,12},{1,3},{3,1},... | collective-permute-start | bytes 688136 | tf_op jit(solution)/shard_map/ppermute | solution.py:297
  22.1 0.5 %collective-permute-done.5.came_ref = bf16[128,896]{1,0:T(8,128)(2,1)S(1)} collective-permute-done((bf16[128,896]{1,0:T(8,128)(2,1)S(1)}, bf16[128,896]{1,0:T(8,128)(2,1)S(1)}, u32[]{:S(2)}, u32[]{:S(2)}) %collective-permute-start.5) | collective-permute-done | bytes 229408 | tf_op jit(solution)/shard_map/ppermute | solution.py:297
  22.7 0.7 %collective-permute-done.8.refs_0_ = bf16[64,896]{1,0:T(8,128)(2,1)S(1)} collective-permute-done((bf16[64,896]{1,0:T(8,128)(2,1)S(1)}, bf16[64,896]{1,0:T(8,128)(2,1)S(1)}, u32[]{:S(2)}, u32[]{:S(2)}) %collective-permute-start.8) | collective-permute-done | bytes 114720 | tf_op jit(solution)/shard_map/ppermute | solution.py:297
  23.4 2.7 %collective-permute-start.9 = (bf16[64,896]{1,0:T(8,128)(2,1)S(1)}, bf16[64,896]{1,0:T(8,128)(2,1)S(1)}, u32[]{:S(2)}, u32[]{:S(2)}) collective-permute-start(bf16[64,896]{1,0:T(8,128)(2,1)S(1)} %add.2), channel_id=1, source_target_pairs={{0,8},{2,10},{4,12},{6,14},{8,0},{10,2},{12,4},{14,6},{1,9},{3,11}... | collective-permute-start | bytes 344072 | tf_op jit(solution)/shard_map/ppermute | solution.py:297
  26.1 0.0 collective-permute-done.10.refs_0_
  26.1 2.1 %collective-permute-start.11 = (bf16[64,896]{1,0:T(8,128)(2,1)S(1)}, bf16[64,896]{1,0:T(8,128)(2,1)S(1)}, u32[]{:S(2)}, u32[]{:S(2)}) collective-permute-start(bf16[64,896]{1,0:T(8,128)(2,1)S(1)} %add.3), channel_id=1, source_target_pairs={{0,8},{2,10},{4,12},{6,14},{8,0},{10,2},{12,4},{14,6},{1,9},{3,11}... | collective-permute-start | bytes 344072 | tf_op jit(solution)/shard_map/ppermute | solution.py:297
  28.3 0.0 collective-permute-done.13.came_ref
  28.3 1.5 %collective-permute-start.14 = (bf16[64,896]{1,0:T(8,128)(2,1)S(1)}, bf16[64,896]{1,0:T(8,128)(2,1)S(1)}, u32[]{:S(2)}, u32[]{:S(2)}) collective-permute-start(bf16[64,896]{1,0:T(8,128)(2,1)S(1)} %get-tuple-element.63), channel_id=1, source_target_pairs={{0,4},{2,6},{4,0},{6,2},{8,12},{10,14},{12,8},{14,10},{1,5},{3,7},... | collective-permute-start | bytes 344072 | tf_op jit(solution)/shard_map/ppermute | solution.py:297
  29.8 0.6 %collective-permute-start.15 = (bf16[64,896]{1,0:T(8,128)(2,1)S(1)}, bf16[64,896]{1,0:T(8,128)(2,1)S(1)}, u32[]{:S(2)}, u32[]{:S(2)}) collective-permute-start(bf16[64,896]{1,0:T(8,128)(2,1)S(1)} %get-tuple-element.64), channel_id=1, source_target_pairs={{0,4},{2,6},{4,0},{6,2},{8,12},{10,14},{12,8},{14,10},{1,5},{3,7},... | collective-permute-start | bytes 344072 | tf_op jit(solution)/shard_map/ppermute | solution.py:297
  30.4 2.8 %input.1 = bf16[128,7168]{1,0:T(8,128)(2,1)} custom-call(bf16[128,128]{1,0:T(8,128)(2,1)S(1)} %get-tuple-element.37.low_ref.lg_ref, bf16[64,7168]{1,0:T(8,128)(2,1)S(1)} %bitcast.8, bf16[64,7168]{1,0:T(8,128)(2,1)S(1)} %collective-permute-done.1.a_in_ref.other_ref), custom_call_target="tpu_custom_call" | custom-call | flops 234881024 | bytes 3670016 | tf_op jit(solution)/shard_map/input/pallas_call | solution.py:273
  33.2 0.0 collective-permute-done.3.refs_0_
  33.2 1.1 %collective-permute-done.9.refs_1_ = bf16[64,896]{1,0:T(8,128)(2,1)S(1)} collective-permute-done((bf16[64,896]{1,0:T(8,128)(2,1)S(1)}, bf16[64,896]{1,0:T(8,128)(2,1)S(1)}, u32[]{:S(2)}, u32[]{:S(2)}) %collective-permute-start.9) | collective-permute-done | bytes 114720 | tf_op jit(solution)/shard_map/ppermute | solution.py:297
  34.3 1.3 %collective-permute-done.11.refs_2_ = bf16[64,896]{1,0:T(8,128)(2,1)S(1)} collective-permute-done((bf16[64,896]{1,0:T(8,128)(2,1)S(1)}, bf16[64,896]{1,0:T(8,128)(2,1)S(1)}, u32[]{:S(2)}, u32[]{:S(2)}) %collective-permute-start.11) | collective-permute-done | bytes 114720 | tf_op jit(solution)/shard_map/ppermute | solution.py:297
  35.6 0.1 total.1
  35.7 0.4 %collective-permute-done.14.down_came = bf16[64,896]{1,0:T(8,128)(2,1)S(1)} collective-permute-done((bf16[64,896]{1,0:T(8,128)(2,1)S(1)}, bf16[64,896]{1,0:T(8,128)(2,1)S(1)}, u32[]{:S(2)}, u32[]{:S(2)}) %collective-permute-start.14) | collective-permute-done | bytes 114720 | tf_op jit(solution)/shard_map/ppermute | solution.py:297
  36.1 1.2 %collective-permute-done.15.up_came = bf16[64,896]{1,0:T(8,128)(2,1)S(1)} collective-permute-done((bf16[64,896]{1,0:T(8,128)(2,1)S(1)}, bf16[64,896]{1,0:T(8,128)(2,1)S(1)}, u32[]{:S(2)}, u32[]{:S(2)}) %collective-permute-start.15) | collective-permute-done | bytes 114720 | tf_op jit(solution)/shard_map/ppermute | solution.py:297
  37.3 0.8 %last.1 = (f32[64,896]{1,0:T(8,128)}, f32[64,896]{1,0:T(8,128)}) custom-call(f32[64,896]{1,0:T(8,128)S(1)} %get-tuple-element.57.down_total, f32[64,896]{1,0:T(8,128)S(1)} %get-tuple-element.58.up_total, bf16[64,896]{1,0:T(8,128)(2,1)S(1)} %collective-permute-done.14.down_came, bf16[64,896]{1,0:T(8,128)(2,1)S(1)} %collective-permute-done.15.up_came), custom_call_target="tpu_custom_call" | custom-call | flops 114688 | bytes 1146880 | tf_op jit(solution)/shard_map/last/pallas_call | solution.py:247
  (7 shorter events, 0.2 us)
Async XLA Ops:
  0.6 2.8 %collective-permute-start.1 = (bf16[64,7168]{1,0:T(8,128)(2,1)}, bf16[64,7168]{1,0:T(8,128)(2,1)S(1)}, u32[]{:S(2)}, u32[]{:S(2)}) collective-permute-start(bf16[64,7168]{1,0:T(8,128)(2,1)} %bitcast.6), channel_id=1, source_target_pairs={{0,1},{1,0},{2,3},{3,2},{4,5},{5,4},{6,7},{7,6},{8,9},{9,8},{10,11... | collective-permute-start | bytes 2752520 | tf_op jit(solution)/shard_map/ppermute | solution.py:295
  1.1 3.6 %copy-start = (bf16[4,16,7168]{2,1,0:T(8,128)(2,1)S(1)}, bf16[4,16,7168]{2,1,0:T(8,128)(2,1)}, u32[]{:S(2)}) copy-start(bf16[4,16,7168]{2,1,0:T(8,128)(2,1)} %param.10) | copy-start | bytes 2752516
  1.2 3.6 %copy-start.1 = (bf16[4,16,7168]{2,1,0:T(8,128)(2,1)S(1)}, bf16[4,16,7168]{2,1,0:T(8,128)(2,1)}, u32[]{:S(2)}) copy-start(bf16[4,16,7168]{2,1,0:T(8,128)(2,1)} %param.11) | copy-start | bytes 2752516
  1.2 3.6 %copy-start.2 = (s32[128,2]{0,1:T(2,128)S(1)}, s32[128,2]{0,1:T(2,128)}, u32[]{:S(2)}) copy-start(s32[128,2]{0,1:T(2,128)} %param.8) | copy-start | bytes 3076
  1.2 3.6 %copy-start.3 = (f32[128,2]{0,1:T(2,128)S(1)}, f32[128,2]{0,1:T(2,128)}, u32[]{:S(2)}) copy-start(f32[128,2]{0,1:T(2,128)} %param.9) | copy-start | bytes 3076
  1.2 3.6 %collective-permute-start = (bf16[64,7168]{1,0:T(8,128)(2,1)}, bf16[64,7168]{1,0:T(8,128)(2,1)S(1)}, u32[]{:S(2)}, u32[]{:S(2)}) collective-permute-start(bf16[64,7168]{1,0:T(8,128)(2,1)} %bitcast.9), channel_id=1, source_target_pairs={{0,1},{1,0},{2,3},{3,2},{4,5},{5,4},{6,7},{7,6},{8,9},{9,8},{10,11... | collective-permute-start | bytes 2752520 | tf_op jit(solution)/shard_map/ppermute | solution.py:295
  6.2 2.0 %collective-permute-start.6 = (bf16[128,1792]{1,0:T(8,128)(2,1)S(1)}, bf16[128,1792]{1,0:T(8,128)(2,1)S(1)}, u32[]{:S(2)}, u32[]{:S(2)}) collective-permute-start(bf16[128,1792]{1,0:T(8,128)(2,1)S(1)} %get-tuple-element.51), channel_id=1, source_target_pairs={{0,1},{1,0},{2,3},{3,2},{4,5},{5,4},{6,7},{7,6},{8,9},{9,8},{10,11... | collective-permute-start | bytes 1376264 | tf_op jit(solution)/shard_map/ppermute | solution.py:295
  7.6 3.8 %collective-permute-start.4 = (bf16[128,1792]{1,0:T(8,128)(2,1)S(1)}, bf16[128,1792]{1,0:T(8,128)(2,1)S(1)}, u32[]{:S(2)}, u32[]{:S(2)}) collective-permute-start(bf16[128,1792]{1,0:T(8,128)(2,1)S(1)} %get-tuple-element.46), channel_id=1, source_target_pairs={{0,1},{1,0},{2,3},{3,2},{4,5},{5,4},{6,7},{7,6},{8,9},{9,8},{10,11... | collective-permute-start | bytes 1376264 | tf_op jit(solution)/shard_map/ppermute | solution.py:295
  7.7 4.5 %collective-permute-start.12 = (bf16[128,1792]{1,0:T(8,128)(2,1)S(1)}, bf16[128,1792]{1,0:T(8,128)(2,1)S(1)}, u32[]{:S(2)}, u32[]{:S(2)}) collective-permute-start(bf16[128,1792]{1,0:T(8,128)(2,1)S(1)} %get-tuple-element.60), channel_id=1, source_target_pairs={{0,1},{1,0},{2,3},{3,2},{4,5},{5,4},{6,7},{7,6},{8,9},{9,8},{10,11... | collective-permute-start | bytes 1376264 | tf_op jit(solution)/shard_map/ppermute | solution.py:295
  8.1 11.8 %collective-permute-start.2 = (bf16[128,1792]{1,0:T(8,128)(2,1)S(1)}, bf16[128,1792]{1,0:T(8,128)(2,1)S(1)}, u32[]{:S(2)}, u32[]{:S(2)}) collective-permute-start(bf16[128,1792]{1,0:T(8,128)(2,1)S(1)} %get-tuple-element.40), channel_id=1, source_target_pairs={{0,1},{1,0},{2,3},{3,2},{4,5},{5,4},{6,7},{7,6},{8,9},{9,8},{10,11... | collective-permute-start | bytes 1376264 | tf_op jit(solution)/shard_map/ppermute | solution.py:295
  8.4 9.4 %collective-permute-start.7 = (bf16[128,896]{1,0:T(8,128)(2,1)S(1)}, bf16[128,896]{1,0:T(8,128)(2,1)S(1)}, u32[]{:S(2)}, u32[]{:S(2)}) collective-permute-start(bf16[128,896]{1,0:T(8,128)(2,1)S(1)} %get-tuple-element.53), channel_id=1, source_target_pairs={{0,2},{2,0},{4,6},{6,4},{8,10},{10,8},{12,14},{14,12},{1,3},{3,1},... | collective-permute-start | bytes 688136 | tf_op jit(solution)/shard_map/ppermute | solution.py:297
  11.4 11.2 %collective-permute-start.5 = (bf16[128,896]{1,0:T(8,128)(2,1)S(1)}, bf16[128,896]{1,0:T(8,128)(2,1)S(1)}, u32[]{:S(2)}, u32[]{:S(2)}) collective-permute-start(bf16[128,896]{1,0:T(8,128)(2,1)S(1)} %get-tuple-element.48), channel_id=1, source_target_pairs={{0,2},{2,0},{4,6},{6,4},{8,10},{10,8},{12,14},{14,12},{1,3},{3,1},... | collective-permute-start | bytes 688136 | tf_op jit(solution)/shard_map/ppermute | solution.py:297
  12.4 15.9 %collective-permute-start.13 = (bf16[128,896]{1,0:T(8,128)(2,1)S(1)}, bf16[128,896]{1,0:T(8,128)(2,1)S(1)}, u32[]{:S(2)}, u32[]{:S(2)}) collective-permute-start(bf16[128,896]{1,0:T(8,128)(2,1)S(1)} %get-tuple-element.62), channel_id=1, source_target_pairs={{0,2},{2,0},{4,6},{6,4},{8,10},{10,8},{12,14},{14,12},{1,3},{3,1},... | collective-permute-start | bytes 688136 | tf_op jit(solution)/shard_map/ppermute | solution.py:297
  17.8 5.6 %collective-permute-start.8 = (bf16[64,896]{1,0:T(8,128)(2,1)S(1)}, bf16[64,896]{1,0:T(8,128)(2,1)S(1)}, u32[]{:S(2)}, u32[]{:S(2)}) collective-permute-start(bf16[64,896]{1,0:T(8,128)(2,1)S(1)} %get-tuple-element.54), channel_id=1, source_target_pairs={{0,4},{2,6},{4,0},{6,2},{8,12},{10,14},{12,8},{14,10},{1,5},{3,7},... | collective-permute-start | bytes 344072 | tf_op jit(solution)/shard_map/ppermute | solution.py:297
  20.1 6.0 %collective-permute-start.10 = (bf16[64,896]{1,0:T(8,128)(2,1)S(1)}, bf16[64,896]{1,0:T(8,128)(2,1)S(1)}, u32[]{:S(2)}, u32[]{:S(2)}) collective-permute-start(bf16[64,896]{1,0:T(8,128)(2,1)S(1)} %get-tuple-element.56), channel_id=1, source_target_pairs={{0,4},{2,6},{4,0},{6,2},{8,12},{10,14},{12,8},{14,10},{1,5},{3,7},... | collective-permute-start | bytes 344072 | tf_op jit(solution)/shard_map/ppermute | solution.py:297
  20.2 13.0 %collective-permute-start.3 = (bf16[128,896]{1,0:T(8,128)(2,1)S(1)}, bf16[128,896]{1,0:T(8,128)(2,1)S(1)}, u32[]{:S(2)}, u32[]{:S(2)}) collective-permute-start(bf16[128,896]{1,0:T(8,128)(2,1)S(1)} %get-tuple-element.41), channel_id=1, source_target_pairs={{0,2},{2,0},{4,6},{6,4},{8,10},{10,8},{12,14},{14,12},{1,3},{3,1},... | collective-permute-start | bytes 688136 | tf_op jit(solution)/shard_map/ppermute | solution.py:297
  23.4 10.9 %collective-permute-start.9 = (bf16[64,896]{1,0:T(8,128)(2,1)S(1)}, bf16[64,896]{1,0:T(8,128)(2,1)S(1)}, u32[]{:S(2)}, u32[]{:S(2)}) collective-permute-start(bf16[64,896]{1,0:T(8,128)(2,1)S(1)} %add.2), channel_id=1, source_target_pairs={{0,8},{2,10},{4,12},{6,14},{8,0},{10,2},{12,4},{14,6},{1,9},{3,11}... | collective-permute-start | bytes 344072 | tf_op jit(solution)/shard_map/ppermute | solution.py:297
  26.1 9.5 %collective-permute-start.11 = (bf16[64,896]{1,0:T(8,128)(2,1)S(1)}, bf16[64,896]{1,0:T(8,128)(2,1)S(1)}, u32[]{:S(2)}, u32[]{:S(2)}) collective-permute-start(bf16[64,896]{1,0:T(8,128)(2,1)S(1)} %add.3), channel_id=1, source_target_pairs={{0,8},{2,10},{4,12},{6,14},{8,0},{10,2},{12,4},{14,6},{1,9},{3,11}... | collective-permute-start | bytes 344072 | tf_op jit(solution)/shard_map/ppermute | solution.py:297
  28.3 7.8 %collective-permute-start.14 = (bf16[64,896]{1,0:T(8,128)(2,1)S(1)}, bf16[64,896]{1,0:T(8,128)(2,1)S(1)}, u32[]{:S(2)}, u32[]{:S(2)}) collective-permute-start(bf16[64,896]{1,0:T(8,128)(2,1)S(1)} %get-tuple-element.63), channel_id=1, source_target_pairs={{0,4},{2,6},{4,0},{6,2},{8,12},{10,14},{12,8},{14,10},{1,5},{3,7},... | collective-permute-start | bytes 344072 | tf_op jit(solution)/shard_map/ppermute | solution.py:297
  29.8 7.5 %collective-permute-start.15 = (bf16[64,896]{1,0:T(8,128)(2,1)S(1)}, bf16[64,896]{1,0:T(8,128)(2,1)S(1)}, u32[]{:S(2)}, u32[]{:S(2)}) collective-permute-start(bf16[64,896]{1,0:T(8,128)(2,1)S(1)} %get-tuple-element.64), channel_id=1, source_target_pairs={{0,4},{2,6},{4,0},{6,2},{8,12},{10,14},{12,8},{14,10},{1,5},{3,7},... | collective-permute-start | bytes 344072 | tf_op jit(solution)/shard_map/ppermute | solution.py:297
